TPU v7x, 32 devices: a whole 2x2x4 slice. The times are simulated.
32 devices in a mesh: groups: 2 (over y), band: 4 (over z), wt: 4 (over x, core).
Axes of the slice: x: 2, y: 2, z: 4, core: 2. Of those that a mesh axis runs over, the one named last changes fastest.
Arguments:
- prior_state: float32 [128, 16, 1024], P('groups', 'band', 'wt'), parts along dimension 0, may hold values from -6 to 6
- langevin_noise: float32 [4, 128, 16, 1024], P(None, 'groups', 'band', 'wt'), parts along dimension 1, may hold values from -6 to 6
- station_values: float32 [8192], P(('groups', 'band', 'wt')), parts along dimension 0, may hold values from -6 to 6
- entry_cell: int32 [8192], P(('groups', 'band', 'wt')), parts along dimension 0, may hold values from 0 to 65535
- entry_owner: int32 [8192], P(('groups', 'band', 'wt')), parts along dimension 0, may hold values from 0 to 3, as said below
- entry_slot: int32 [8192], P(('groups', 'band', 'wt')), parts along dimension 0, may hold values from 0 to 255
- entry_weight: float32 [8192], P(('groups', 'band', 'wt')), parts along dimension 0, may hold values from 0.25 to 1
- live_counts: int32 [32], P(('groups', 'band', 'wt')), parts along dimension 0, may hold values from 64 to 256, as said below
- lift_weight: bfloat16 [64, 256], replicated, may hold values from -0.75 to 0.75
- conv_weight: bfloat16 [9, 256, 256], replicated, may hold values from -0.125 to 0.125
- head_weight: bfloat16 [256, 64], replicated, may hold values from -0.375 to 0.375
- first_gain: float32 [256], replicated, may hold values from 0.1 to 1.9
- second_gain: float32 [256], replicated, may hold values from 0.1 to 1.9
Outputs:
- analysis_state: float32 [128, 16, 1024], P('groups', 'band', 'wt'), parts along dimension 0
- innovation: float32 [8192], P(('groups', 'band', 'wt')), parts along dimension 0
There are 2 independent parts, one for each index of `groups`. A program takes and returns all parts, laid end to end along the dimension named above; an argument that names none is the same for every part. Nothing has to cross between parts.
Inputs may be any that keep to these rules, and one draw needn't show every extreme that they name: `entry_owner`: an entry's owner band lies within 2 bands of the entry's own band; every list holds an entry at offset +2 and one at -2, clipped to the existing bands. `live_counts`: some list is full in every draw.
All inputs are finite; a program needn't handle non-finite values.
Results may differ from a plain program's by a relative error of at most 0.0014.
Values may be sent and summed in bfloat16 or wider, within the bound.
No kernel may reach another device: no remote copies, remote signals or barrier semaphores. Data moves between devices by JAX's collectives and lax.ppermute only.
A program may use at most 64 MiB of HBM per device.

v0:
```python
import math

import jax
import jax.numpy as jnp
from jax import lax
from jax.sharding import PartitionSpec as P

REACH = 2


noise_levels = (1.0, 0.6, 0.3)
obs_precision = 4.0
step_factor = 0.1


def with_halo(block, sides, width, periodic):
    for axis, dim in sides:
        count = lax.axis_size(axis)
        forward = [(i, i + 1) for i in range(count - 1)]
        if periodic:
            forward.append((count - 1, 0))
        backward = [(target, source) for source, target in forward]
        low = lax.ppermute(
            lax.slice_in_dim(block, block.shape[dim] - width, None, axis=dim), axis, forward
        )
        high = lax.ppermute(lax.slice_in_dim(block, 0, width, axis=dim), axis, backward)
        block = jnp.concatenate([low, block, high], axis=dim)
    return block


def from_behind(block, axis, distance):
    devices = range(lax.axis_size(axis))
    route = [(i - distance, i) for i in devices if i - distance in devices]
    return lax.ppermute(block, axis, route)


def rms_scale(values, gain):
    power = jnp.mean(values * values, axis=0, keepdims=True)
    return values * lax.rsqrt(power + 1e-06) * gain[:, None, None]


def widened(hidden):
    sideways = with_halo(hidden, (("wt", 2),), 1, True)
    return with_halo(sideways, (("band", 1),), 1, False)


def apply_taps(padded, kernel):
    rows = padded.shape[1] - 2
    cols = padded.shape[2] - 2
    total = jnp.zeros((kernel.shape[2], rows, cols), jnp.float32)
    for tap_index in range(9):
        row_shift, col_shift = divmod(tap_index, 3)
        window = padded[:, row_shift : row_shift + rows, col_shift : col_shift + cols]
        total = total + jnp.einsum(
            "co,chw->ohw", kernel[tap_index], window, preferred_element_type=jnp.float32
        )
    return total


def per_device(
    prior_state,
    langevin_noise,
    station_values,
    entry_cell,
    entry_owner,
    entry_slot,
    entry_weight,
    live_counts,
    lift_weight,
    conv_weight,
    head_weight,
    first_gain,
    second_gain,
):
    count = entry_cell.shape[0]
    stations = station_values.shape[0]
    alive = jnp.arange(count, dtype=jnp.int32) < live_counts[0]
    weights = jnp.where(alive, entry_weight, jnp.float32(0.0))
    my_band = lax.axis_index("band")
    offset = entry_owner - my_band + REACH
    near_index = offset * stations + entry_slot

    def evaluate(current, level):
        scaled = (current / math.sqrt(1.0 + level * level)).astype(jnp.bfloat16)
        lifted = jnp.einsum("vo,vhw->ohw", lift_weight, scaled, preferred_element_type=jnp.float32)
        first = jax.nn.silu(rms_scale(lifted, first_gain)).astype(jnp.bfloat16)
        padded = widened(first)
        mixed = lifted + apply_taps(padded, conv_weight)
        second = jax.nn.silu(rms_scale(mixed, second_gain)).astype(jnp.bfloat16)
        score = (
            jnp.einsum("co,chw->ohw", head_weight, second, preferred_element_type=jnp.float32)
            / level
        )
        values = weights * current.reshape(-1)[entry_cell]
        buffer = jnp.zeros(((2 * REACH + 1) * stations,), jnp.float32).at[near_index].add(values)
        buffer = buffer.reshape(2 * REACH + 1, stations)
        interp = buffer[REACH]
        upward = buffer[REACH + 1 :]
        downward = buffer[:REACH][::-1]
        for hop in range(REACH):
            arrived_up = from_behind(upward, "band", 1)
            arrived_down = from_behind(downward, "band", -1)
            interp = interp + arrived_up[0] + arrived_down[0]
            upward = arrived_up[1:]
            downward = arrived_down[1:]
        innov = station_values - interp
        below = []
        above = []
        lower_value = innov
        upper_value = innov
        for hop in range(REACH):
            lower_value = from_behind(lower_value, "band", 1)
            upper_value = from_behind(upper_value, "band", -1)
            below.append(lower_value)
            above.append(upper_value)
        pieces = below[::-1] + [innov] + above
        back = jnp.stack(pieces).reshape(-1)[near_index]
        adjoint = jnp.zeros((current.size,), jnp.float32).at[entry_cell].add(weights * back)
        return (score + obs_precision * adjoint.reshape(current.shape), innov)

    current = prior_state
    innov = station_values
    for section in range(2):
        upper = noise_levels[section]
        lower = noise_levels[section + 1]
        spread = upper * upper - lower * lower
        drift, innov = evaluate(current, upper)
        current = current + spread * drift + math.sqrt(spread) * langevin_noise[2 * section]
        factor = step_factor * lower * lower
        drift, innov = evaluate(current, lower)
        current = (
            current + factor * drift + math.sqrt(2.0 * factor) * langevin_noise[2 * section + 1]
        )
    return (current, innov)


def solution(mesh):
    in_specs = (
        P("groups", "band", "wt"),
        P(None, "groups", "band", "wt"),
        P(("groups", "band", "wt")),
        P(("groups", "band", "wt")),
        P(("groups", "band", "wt")),
        P(("groups", "band", "wt")),
        P(("groups", "band", "wt")),
        P(("groups", "band", "wt")),
        P(),
        P(),
        P(),
        P(),
        P(),
    )
    out_specs = (P("groups", "band", "wt"), P(("groups", "band", "wt")))
    return jax.shard_map(
        per_device, mesh=mesh, in_specs=in_specs, out_specs=out_specs, check_vma=False
    )
```

profile of v0, /device:TPU:0, one launch (start us, length us, event | category | flops | bytes accessed | tf_op | source)
XLA Modules:
  0.0 210.0 jit_solution(5459529131440576998)
XLA Ops:
  5.0 2.1 %scatter_custom_fusion = f32[1280]{0:T(1024)S(1)} fusion(s32[256]{0:T(256)S(1)} %compare_select_fusion, f32[256]{0:T(256)S(1)} %get-tuple-element.6, f32[]{:T(128)} %constant.26.clone.1), kind=kCustom, calls=%fused_computation.360 | custom fusion | flops 256 | bytes 5124 | tf_op jit(solution)/shard_map/scatter-add | solution.py:95
  8.5 5.5 %collective-permute-start.4 = (f32[2,256]{1,0:T(2,128)S(1)}, f32[2,256]{1,0:T(2,128)S(1)}, u32[]{:S(2)}, u32[]{:S(2)}) collective-permute-start(f32[2,256]{1,0:T(2,128)S(1)} %slice.441), channel_id=1, source_target_pairs={{0,4},{4,8},{8,12},{1,5},{5,9},{9,13},{2,6},{6,10},{10,14},{3,7},{... | collective-permute-start | bytes 6152 | tf_op jit(solution)/shard_map/ppermute | solution.py:34
  15.1 1.7 collective-permute-start.1
  20.5 4.5 %collective-permute-start.6 = (f32[1,256]{1,0:T(1,128)S(1)}, f32[1,256]{1,0:T(1,128)S(1)}, u32[]{:S(2)}, u32[]{:S(2)}) collective-permute-start(f32[1,256]{1,0:T(1,128)S(1)} %get-tuple-element.57), channel_id=1, source_target_pairs={{0,4},{4,8},{8,12},{1,5},{5,9},{9,13},{2,6},{6,10},{10,14},{3,7},{... | collective-permute-start | bytes 3080 | tf_op jit(solution)/shard_map/ppermute | solution.py:34
  27.6 4.8 %collective-permute-start.8 = (f32[256]{0:T(256)S(1)}, f32[256]{0:T(256)S(1)}, u32[]{:S(2)}, u32[]{:S(2)}) collective-permute-start(f32[256]{0:T(256)S(1)} %fusion.278), channel_id=1, source_target_pairs={{0,4},{4,8},{8,12},{1,5},{5,9},{9,13},{2,6},{6,10},{10,14},{3,7},{... | collective-permute-start | bytes 3080 | tf_op jit(solution)/shard_map/ppermute | solution.py:34
  33.2 3.9 %collective-permute-start.2 = (bf16[256,1,258]{0,2,1:T(8,128)(2,1)}, bf16[256,1,258]{0,2,1:T(8,128)(2,1)S(1)}, u32[]{:S(2)}, u32[]{:S(2)}) collective-permute-start(bf16[256,1,258]{0,2,1:T(8,128)(2,1)} %get-tuple-element.26), channel_id=1, source_target_pairs={{0,4},{4,8},{8,12},{1,5},{5,9},{9,13},{2,6},{6,10},{10,14},{3,7},{... | collective-permute-start | bytes 396296 | tf_op jit(solution)/shard_map/ppermute | solution.py:23
  39.8 5.2 %collective-permute-start.9 = (f32[256]{0:T(256)S(1)}, f32[256]{0:T(256)S(1)}, u32[]{:S(2)}, u32[]{:S(2)}) collective-permute-start(f32[256]{0:T(256)S(1)} %collective-permute-done.8), channel_id=1, source_target_pairs={{0,4},{4,8},{8,12},{1,5},{5,9},{9,13},{2,6},{6,10},{10,14},{3,7},{... | collective-permute-start | bytes 3080 | tf_op jit(solution)/shard_map/ppermute | solution.py:34
  48.1 2.0 scatter_custom_fusion.1
  59.9 2.1 %scatter_custom_fusion.2 = f32[1280]{0:T(1024)S(1)} fusion(s32[256]{0:T(256)S(1)} %compare_select_fusion, f32[256]{0:T(256)S(1)} %mul.312, f32[]{:T(128)} %constant.26.clone.1), kind=kCustom, calls=%fused_computation.358 | custom fusion | flops 256 | bytes 5124 | tf_op jit(solution)/shard_map/scatter-add | solution.py:95
  63.4 4.8 %collective-permute-start.16 = (f32[2,256]{1,0:T(2,128)S(1)}, f32[2,256]{1,0:T(2,128)S(1)}, u32[]{:S(2)}, u32[]{:S(2)}) collective-permute-start(f32[2,256]{1,0:T(2,128)S(1)} %slice.463), channel_id=1, source_target_pairs={{0,4},{4,8},{8,12},{1,5},{5,9},{9,13},{2,6},{6,10},{10,14},{3,7},{... | collective-permute-start | bytes 6152 | tf_op jit(solution)/shard_map/ppermute | solution.py:34
  71.2 4.8 %collective-permute-start.18 = (f32[1,256]{1,0:T(1,128)S(1)}, f32[1,256]{1,0:T(1,128)S(1)}, u32[]{:S(2)}, u32[]{:S(2)}) collective-permute-start(f32[1,256]{1,0:T(1,128)S(1)} %get-tuple-element.53), channel_id=1, source_target_pairs={{0,4},{4,8},{8,12},{1,5},{5,9},{9,13},{2,6},{6,10},{10,14},{3,7},{... | collective-permute-start | bytes 3080 | tf_op jit(solution)/shard_map/ppermute | solution.py:34
  76.1 1.7 collective-permute-start.13
  79.2 4.7 %collective-permute-start.20 = (f32[256]{0:T(256)S(1)}, f32[256]{0:T(256)S(1)}, u32[]{:S(2)}, u32[]{:S(2)}) collective-permute-start(f32[256]{0:T(256)S(1)} %fusion.274), channel_id=1, source_target_pairs={{0,4},{4,8},{8,12},{1,5},{5,9},{9,13},{2,6},{6,10},{10,14},{3,7},{... | collective-permute-start | bytes 3080 | tf_op jit(solution)/shard_map/ppermute | solution.py:34
  84.7 3.9 %collective-permute-start.14 = (bf16[256,1,258]{0,2,1:T(8,128)(2,1)}, bf16[256,1,258]{0,2,1:T(8,128)(2,1)S(1)}, u32[]{:S(2)}, u32[]{:S(2)}) collective-permute-start(bf16[256,1,258]{0,2,1:T(8,128)(2,1)} %get-tuple-element.22), channel_id=1, source_target_pairs={{0,4},{4,8},{8,12},{1,5},{5,9},{9,13},{2,6},{6,10},{10,14},{3,7},{... | collective-permute-start | bytes 396296 | tf_op jit(solution)/shard_map/ppermute | solution.py:23
  91.2 5.2 %collective-permute-start.21 = (f32[256]{0:T(256)S(1)}, f32[256]{0:T(256)S(1)}, u32[]{:S(2)}, u32[]{:S(2)}) collective-permute-start(f32[256]{0:T(256)S(1)} %collective-permute-done.20), channel_id=1, source_target_pairs={{0,4},{4,8},{8,12},{1,5},{5,9},{9,13},{2,6},{6,10},{10,14},{3,7},{... | collective-permute-start | bytes 3080 | tf_op jit(solution)/shard_map/ppermute | solution.py:34
  99.5 2.0 scatter_custom_fusion.3
  110.6 2.1 %scatter_custom_fusion.4 = f32[1280]{0:T(1024)S(1)} fusion(s32[256]{0:T(256)S(1)} %compare_select_fusion, f32[256]{0:T(256)S(1)} %mul.331, f32[]{:T(128)} %constant.26.clone.1), kind=kCustom, calls=%fused_computation.356 | custom fusion | flops 256 | bytes 5124 | tf_op jit(solution)/shard_map/scatter-add | solution.py:95
  114.1 4.7 %collective-permute-start.28 = (f32[2,256]{1,0:T(2,128)S(1)}, f32[2,256]{1,0:T(2,128)S(1)}, u32[]{:S(2)}, u32[]{:S(2)}) collective-permute-start(f32[2,256]{1,0:T(2,128)S(1)} %slice.485), channel_id=1, source_target_pairs={{0,4},{4,8},{8,12},{1,5},{5,9},{9,13},{2,6},{6,10},{10,14},{3,7},{... | collective-permute-start | bytes 6152 | tf_op jit(solution)/shard_map/ppermute | solution.py:34
  121.8 4.8 %collective-permute-start.30 = (f32[1,256]{1,0:T(1,128)S(1)}, f32[1,256]{1,0:T(1,128)S(1)}, u32[]{:S(2)}, u32[]{:S(2)}) collective-permute-start(f32[1,256]{1,0:T(1,128)S(1)} %get-tuple-element.49), channel_id=1, source_target_pairs={{0,4},{4,8},{8,12},{1,5},{5,9},{9,13},{2,6},{6,10},{10,14},{3,7},{... | collective-permute-start | bytes 3080 | tf_op jit(solution)/shard_map/ppermute | solution.py:34
  126.7 1.7 collective-permute-start.25
  129.8 4.6 %collective-permute-start.32 = (f32[256]{0:T(256)S(1)}, f32[256]{0:T(256)S(1)}, u32[]{:S(2)}, u32[]{:S(2)}) collective-permute-start(f32[256]{0:T(256)S(1)} %fusion.270), channel_id=1, source_target_pairs={{0,4},{4,8},{8,12},{1,5},{5,9},{9,13},{2,6},{6,10},{10,14},{3,7},{... | collective-permute-start | bytes 3080 | tf_op jit(solution)/shard_map/ppermute | solution.py:34
  135.1 3.9 %collective-permute-start.26 = (bf16[256,1,258]{0,2,1:T(8,128)(2,1)}, bf16[256,1,258]{0,2,1:T(8,128)(2,1)S(1)}, u32[]{:S(2)}, u32[]{:S(2)}) collective-permute-start(bf16[256,1,258]{0,2,1:T(8,128)(2,1)} %get-tuple-element.18), channel_id=1, source_target_pairs={{0,4},{4,8},{8,12},{1,5},{5,9},{9,13},{2,6},{6,10},{10,14},{3,7},{... | collective-permute-start | bytes 396296 | tf_op jit(solution)/shard_map/ppermute | solution.py:23
  141.7 5.2 %collective-permute-start.33 = (f32[256]{0:T(256)S(1)}, f32[256]{0:T(256)S(1)}, u32[]{:S(2)}, u32[]{:S(2)}) collective-permute-start(f32[256]{0:T(256)S(1)} %collective-permute-done.32), channel_id=1, source_target_pairs={{0,4},{4,8},{8,12},{1,5},{5,9},{9,13},{2,6},{6,10},{10,14},{3,7},{... | collective-permute-start | bytes 3080 | tf_op jit(solution)/shard_map/ppermute | solution.py:34
  150.0 2.2 %scatter_custom_fusion.5 = f32[65536]{0:T(1024)S(1)} fusion(s32[256]{0:T(256)S(1)} %compare_select_fusion.1, f32[256]{0:T(256)S(1)} %mul.332, f32[]{:T(128)} %constant.26.clone.1), kind=kCustom, calls=%fused_computation.296 | custom fusion | flops 256 | bytes 262148 | tf_op jit(solution)/shard_map/scatter-add | solution.py:118
  161.2 2.1 %scatter_custom_fusion.6 = f32[1280]{0:T(1024)S(1)} fusion(s32[256]{0:T(256)S(1)} %compare_select_fusion, f32[256]{0:T(256)S(1)} %mul.350, f32[]{:T(128)} %constant.26.clone.1), kind=kCustom, calls=%fused_computation.354 | custom fusion | flops 256 | bytes 5124 | tf_op jit(solution)/shard_map/scatter-add | solution.py:95
  164.8 4.8 %collective-permute-start.40 = (f32[2,256]{1,0:T(2,128)S(1)}, f32[2,256]{1,0:T(2,128)S(1)}, u32[]{:S(2)}, u32[]{:S(2)}) collective-permute-start(f32[2,256]{1,0:T(2,128)S(1)} %slice.507), channel_id=1, source_target_pairs={{0,4},{4,8},{8,12},{1,5},{5,9},{9,13},{2,6},{6,10},{10,14},{3,7},{... | collective-permute-start | bytes 6152 | tf_op jit(solution)/shard_map/ppermute | solution.py:34
  172.5 4.8 %collective-permute-start.42 = (f32[1,256]{1,0:T(1,128)S(1)}, f32[1,256]{1,0:T(1,128)S(1)}, u32[]{:S(2)}, u32[]{:S(2)}) collective-permute-start(f32[1,256]{1,0:T(1,128)S(1)} %get-tuple-element.45), channel_id=1, source_target_pairs={{0,4},{4,8},{8,12},{1,5},{5,9},{9,13},{2,6},{6,10},{10,14},{3,7},{... | collective-permute-start | bytes 3080 | tf_op jit(solution)/shard_map/ppermute | solution.py:34
  177.4 1.7 collective-permute-start.37
  180.5 4.6 %collective-permute-start.44 = (f32[256]{0:T(256)S(1)}, f32[256]{0:T(256)S(1)}, u32[]{:S(2)}, u32[]{:S(2)}) collective-permute-start(f32[256]{0:T(256)S(1)} %fusion.266), channel_id=1, source_target_pairs={{0,4},{4,8},{8,12},{1,5},{5,9},{9,13},{2,6},{6,10},{10,14},{3,7},{... | collective-permute-start | bytes 3080 | tf_op jit(solution)/shard_map/ppermute | solution.py:34
  185.8 3.9 %collective-permute-start.38 = (bf16[256,1,258]{0,2,1:T(8,128)(2,1)}, bf16[256,1,258]{0,2,1:T(8,128)(2,1)S(1)}, u32[]{:S(2)}, u32[]{:S(2)}) collective-permute-start(bf16[256,1,258]{0,2,1:T(8,128)(2,1)} %get-tuple-element.14), channel_id=1, source_target_pairs={{0,4},{4,8},{8,12},{1,5},{5,9},{9,13},{2,6},{6,10},{10,14},{3,7},{... | collective-permute-start | bytes 396296 | tf_op jit(solution)/shard_map/ppermute | solution.py:23
  192.4 5.2 %collective-permute-start.45 = (f32[256]{0:T(256)S(1)}, f32[256]{0:T(256)S(1)}, u32[]{:S(2)}, u32[]{:S(2)}) collective-permute-start(f32[256]{0:T(256)S(1)} %collective-permute-done.44), channel_id=1, source_target_pairs={{0,4},{4,8},{8,12},{1,5},{5,9},{9,13},{2,6},{6,10},{10,14},{3,7},{... | collective-permute-start | bytes 3080 | tf_op jit(solution)/shard_map/ppermute | solution.py:34
  200.7 2.0 scatter_custom_fusion.7
  (280 shorter events, 89.9 us)
Async XLA Ops:
  7.2 12.0 %collective-permute-start.5 = (f32[2,256]{1,0:T(2,128)S(1)}, f32[2,256]{1,0:T(2,128)S(1)}, u32[]{:S(2)}, u32[]{:S(2)}) collective-permute-start(f32[2,256]{1,0:T(2,128)S(1)} %rev.12), channel_id=1, source_target_pairs={{4,0},{8,4},{12,8},{5,1},{9,5},{13,9},{6,2},{10,6},{14,10},{7,3},{... | collective-permute-start | bytes 6152 | tf_op jit(solution)/shard_map/ppermute | solution.py:34
  8.5 11.9 %collective-permute-start.4 = (f32[2,256]{1,0:T(2,128)S(1)}, f32[2,256]{1,0:T(2,128)S(1)}, u32[]{:S(2)}, u32[]{:S(2)}) collective-permute-start(f32[2,256]{1,0:T(2,128)S(1)} %slice.441), channel_id=1, source_target_pairs={{0,4},{4,8},{8,12},{1,5},{5,9},{9,13},{2,6},{6,10},{10,14},{3,7},{... | collective-permute-start | bytes 6152 | tf_op jit(solution)/shard_map/ppermute | solution.py:34
  15.0 17.4 %collective-permute-start = (bf16[256,4,1]{0,2,1:T(2,128)(2,1)S(1)}, bf16[256,4,1]{0,2,1:T(2,128)(2,1)S(1)}, u32[]{:S(2)}, u32[]{:S(2)}) collective-permute-start(bf16[256,4,1]{0,2,1:T(2,128)(2,1)S(1)} %get-tuple-element.34), channel_id=1, source_target_pairs={{0,1},{1,2},{2,3},{3,0},{4,5},{5,6},{6,7},{7,4},{8,9},{9,10},{10,1... | collective-permute-start | bytes 6152 | tf_op jit(solution)/shard_map/ppermute | solution.py:23
  15.1 17.4 %collective-permute-start.1 = (bf16[256,4,1]{0,2,1:T(2,128)(2,1)S(1)}, bf16[256,4,1]{0,2,1:T(2,128)(2,1)S(1)}, u32[]{:S(2)}, u32[]{:S(2)}) collective-permute-start(bf16[256,4,1]{0,2,1:T(2,128)(2,1)S(1)} %get-tuple-element.35), channel_id=1, source_target_pairs={{1,0},{2,1},{3,2},{0,3},{5,4},{6,5},{7,6},{4,7},{9,8},{10,9},{11,1... | collective-permute-start | bytes 6152 | tf_op jit(solution)/shard_map/ppermute | solution.py:26
  26.3 12.1 %collective-permute-start.10 = (f32[256]{0:T(256)S(1)}, f32[256]{0:T(256)S(1)}, u32[]{:S(2)}, u32[]{:S(2)}) collective-permute-start(f32[256]{0:T(256)S(1)} %fusion.278), channel_id=1, source_target_pairs={{4,0},{8,4},{12,8},{5,1},{9,5},{13,9},{6,2},{10,6},{14,10},{7,3},{... | collective-permute-start | bytes 3080 | tf_op jit(solution)/shard_map/ppermute | solution.py:34
  27.6 12.1 %collective-permute-start.8 = (f32[256]{0:T(256)S(1)}, f32[256]{0:T(256)S(1)}, u32[]{:S(2)}, u32[]{:S(2)}) collective-permute-start(f32[256]{0:T(256)S(1)} %fusion.278), channel_id=1, source_target_pairs={{0,4},{4,8},{8,12},{1,5},{5,9},{9,13},{2,6},{6,10},{10,14},{3,7},{... | collective-permute-start | bytes 3080 | tf_op jit(solution)/shard_map/ppermute | solution.py:34
  33.2 18.6 %collective-permute-start.2 = (bf16[256,1,258]{0,2,1:T(8,128)(2,1)}, bf16[256,1,258]{0,2,1:T(8,128)(2,1)S(1)}, u32[]{:S(2)}, u32[]{:S(2)}) collective-permute-start(bf16[256,1,258]{0,2,1:T(8,128)(2,1)} %get-tuple-element.26), channel_id=1, source_target_pairs={{0,4},{4,8},{8,12},{1,5},{5,9},{9,13},{2,6},{6,10},{10,14},{3,7},{... | collective-permute-start | bytes 396296 | tf_op jit(solution)/shard_map/ppermute | solution.py:23
  37.1 14.7 %collective-permute-start.3 = (bf16[256,1,258]{0,2,1:T(8,128)(2,1)}, bf16[256,1,258]{0,2,1:T(8,128)(2,1)}, u32[]{:S(2)}, u32[]{:S(2)}) collective-permute-start(bf16[256,1,258]{0,2,1:T(8,128)(2,1)} %get-tuple-element.27), channel_id=1, source_target_pairs={{4,0},{8,4},{12,8},{5,1},{9,5},{13,9},{6,2},{10,6},{14,10},{7,3},{... | collective-permute-start | bytes 396296 | tf_op jit(solution)/shard_map/ppermute | solution.py:26
  38.5 7.8 %collective-permute-start.11 = (f32[256]{0:T(256)S(1)}, f32[256]{0:T(256)S(1)}, u32[]{:S(2)}, u32[]{:S(2)}) collective-permute-start(f32[256]{0:T(256)S(1)} %collective-permute-done.10), channel_id=1, source_target_pairs={{4,0},{8,4},{12,8},{5,1},{9,5},{13,9},{6,2},{10,6},{14,10},{7,3},{... | collective-permute-start | bytes 3080 | tf_op jit(solution)/shard_map/ppermute | solution.py:34
  62.1 7.8 %collective-permute-start.17 = (f32[2,256]{1,0:T(2,128)S(1)}, f32[2,256]{1,0:T(2,128)S(1)}, u32[]{:S(2)}, u32[]{:S(2)}) collective-permute-start(f32[2,256]{1,0:T(2,128)S(1)} %rev.13), channel_id=1, source_target_pairs={{4,0},{8,4},{12,8},{5,1},{9,5},{13,9},{6,2},{10,6},{14,10},{7,3},{... | collective-permute-start | bytes 6152 | tf_op jit(solution)/shard_map/ppermute | solution.py:34
  63.4 7.8 %collective-permute-start.16 = (f32[2,256]{1,0:T(2,128)S(1)}, f32[2,256]{1,0:T(2,128)S(1)}, u32[]{:S(2)}, u32[]{:S(2)}) collective-permute-start(f32[2,256]{1,0:T(2,128)S(1)} %slice.463), channel_id=1, source_target_pairs={{0,4},{4,8},{8,12},{1,5},{5,9},{9,13},{2,6},{6,10},{10,14},{3,7},{... | collective-permute-start | bytes 6152 | tf_op jit(solution)/shard_map/ppermute | solution.py:34
  69.9 7.9 %collective-permute-start.19 = (f32[1,256]{1,0:T(1,128)S(1)}, f32[1,256]{1,0:T(1,128)S(1)}, u32[]{:S(2)}, u32[]{:S(2)}) collective-permute-start(f32[1,256]{1,0:T(1,128)S(1)} %get-tuple-element.55), channel_id=1, source_target_pairs={{4,0},{8,4},{12,8},{5,1},{9,5},{13,9},{6,2},{10,6},{14,10},{7,3},{... | collective-permute-start | bytes 3080 | tf_op jit(solution)/shard_map/ppermute | solution.py:34
  76.0 7.9 %collective-permute-start.12 = (bf16[256,4,1]{0,2,1:T(2,128)(2,1)S(1)}, bf16[256,4,1]{0,2,1:T(2,128)(2,1)S(1)}, u32[]{:S(2)}, u32[]{:S(2)}) collective-permute-start(bf16[256,4,1]{0,2,1:T(2,128)(2,1)S(1)} %get-tuple-element.32), channel_id=1, source_target_pairs={{0,1},{1,2},{2,3},{3,0},{4,5},{5,6},{6,7},{7,4},{8,9},{9,10},{10,1... | collective-permute-start | bytes 6152 | tf_op jit(solution)/shard_map/ppermute | solution.py:23
  76.1 7.8 %collective-permute-start.13 = (bf16[256,4,1]{0,2,1:T(2,128)(2,1)S(1)}, bf16[256,4,1]{0,2,1:T(2,128)(2,1)S(1)}, u32[]{:S(2)}, u32[]{:S(2)}) collective-permute-start(bf16[256,4,1]{0,2,1:T(2,128)(2,1)S(1)} %get-tuple-element.33), channel_id=1, source_target_pairs={{1,0},{2,1},{3,2},{0,3},{5,4},{6,5},{7,6},{4,7},{9,8},{10,9},{11,1... | collective-permute-start | bytes 6152 | tf_op jit(solution)/shard_map/ppermute | solution.py:26
  77.9 12.1 %collective-permute-start.22 = (f32[256]{0:T(256)S(1)}, f32[256]{0:T(256)S(1)}, u32[]{:S(2)}, u32[]{:S(2)}) collective-permute-start(f32[256]{0:T(256)S(1)} %fusion.274), channel_id=1, source_target_pairs={{4,0},{8,4},{12,8},{5,1},{9,5},{13,9},{6,2},{10,6},{14,10},{7,3},{... | collective-permute-start | bytes 3080 | tf_op jit(solution)/shard_map/ppermute | solution.py:34
  79.2 12.1 %collective-permute-start.20 = (f32[256]{0:T(256)S(1)}, f32[256]{0:T(256)S(1)}, u32[]{:S(2)}, u32[]{:S(2)}) collective-permute-start(f32[256]{0:T(256)S(1)} %fusion.274), channel_id=1, source_target_pairs={{0,4},{4,8},{8,12},{1,5},{5,9},{9,13},{2,6},{6,10},{10,14},{3,7},{... | collective-permute-start | bytes 3080 | tf_op jit(solution)/shard_map/ppermute | solution.py:34
  84.7 17.7 %collective-permute-start.14 = (bf16[256,1,258]{0,2,1:T(8,128)(2,1)}, bf16[256,1,258]{0,2,1:T(8,128)(2,1)S(1)}, u32[]{:S(2)}, u32[]{:S(2)}) collective-permute-start(bf16[256,1,258]{0,2,1:T(8,128)(2,1)} %get-tuple-element.22), channel_id=1, source_target_pairs={{0,4},{4,8},{8,12},{1,5},{5,9},{9,13},{2,6},{6,10},{10,14},{3,7},{... | collective-permute-start | bytes 396296 | tf_op jit(solution)/shard_map/ppermute | solution.py:23
  88.6 13.8 %collective-permute-start.15 = (bf16[256,1,258]{0,2,1:T(8,128)(2,1)}, bf16[256,1,258]{0,2,1:T(8,128)(2,1)}, u32[]{:S(2)}, u32[]{:S(2)}) collective-permute-start(bf16[256,1,258]{0,2,1:T(8,128)(2,1)} %get-tuple-element.23), channel_id=1, source_target_pairs={{4,0},{8,4},{12,8},{5,1},{9,5},{13,9},{6,2},{10,6},{14,10},{7,3},{... | collective-permute-start | bytes 396296 | tf_op jit(solution)/shard_map/ppermute | solution.py:26
  89.9 7.8 %collective-permute-start.23 = (f32[256]{0:T(256)S(1)}, f32[256]{0:T(256)S(1)}, u32[]{:S(2)}, u32[]{:S(2)}) collective-permute-start(f32[256]{0:T(256)S(1)} %collective-permute-done.22), channel_id=1, source_target_pairs={{4,0},{8,4},{12,8},{5,1},{9,5},{13,9},{6,2},{10,6},{14,10},{7,3},{... | collective-permute-start | bytes 3080 | tf_op jit(solution)/shard_map/ppermute | solution.py:34
  120.5 7.9 %collective-permute-start.31 = (f32[1,256]{1,0:T(1,128)S(1)}, f32[1,256]{1,0:T(1,128)S(1)}, u32[]{:S(2)}, u32[]{:S(2)}) collective-permute-start(f32[1,256]{1,0:T(1,128)S(1)} %get-tuple-element.51), channel_id=1, source_target_pairs={{4,0},{8,4},{12,8},{5,1},{9,5},{13,9},{6,2},{10,6},{14,10},{7,3},{... | collective-permute-start | bytes 3080 | tf_op jit(solution)/shard_map/ppermute | solution.py:34
  128.5 11.9 %collective-permute-start.34 = (f32[256]{0:T(256)S(1)}, f32[256]{0:T(256)S(1)}, u32[]{:S(2)}, u32[]{:S(2)}) collective-permute-start(f32[256]{0:T(256)S(1)} %fusion.270), channel_id=1, source_target_pairs={{4,0},{8,4},{12,8},{5,1},{9,5},{13,9},{6,2},{10,6},{14,10},{7,3},{... | collective-permute-start | bytes 3080 | tf_op jit(solution)/shard_map/ppermute | solution.py:34
  129.8 11.9 %collective-permute-start.32 = (f32[256]{0:T(256)S(1)}, f32[256]{0:T(256)S(1)}, u32[]{:S(2)}, u32[]{:S(2)}) collective-permute-start(f32[256]{0:T(256)S(1)} %fusion.270), channel_id=1, source_target_pairs={{0,4},{4,8},{8,12},{1,5},{5,9},{9,13},{2,6},{6,10},{10,14},{3,7},{... | collective-permute-start | bytes 3080 | tf_op jit(solution)/shard_map/ppermute | solution.py:34
  135.1 17.9 %collective-permute-start.26 = (bf16[256,1,258]{0,2,1:T(8,128)(2,1)}, bf16[256,1,258]{0,2,1:T(8,128)(2,1)S(1)}, u32[]{:S(2)}, u32[]{:S(2)}) collective-permute-start(bf16[256,1,258]{0,2,1:T(8,128)(2,1)} %get-tuple-element.18), channel_id=1, source_target_pairs={{0,4},{4,8},{8,12},{1,5},{5,9},{9,13},{2,6},{6,10},{10,14},{3,7},{... | collective-permute-start | bytes 396296 | tf_op jit(solution)/shard_map/ppermute | solution.py:23
  139.1 14.0 %collective-permute-start.27 = (bf16[256,1,258]{0,2,1:T(8,128)(2,1)}, bf16[256,1,258]{0,2,1:T(8,128)(2,1)}, u32[]{:S(2)}, u32[]{:S(2)}) collective-permute-start(bf16[256,1,258]{0,2,1:T(8,128)(2,1)} %get-tuple-element.19), channel_id=1, source_target_pairs={{4,0},{8,4},{12,8},{5,1},{9,5},{13,9},{6,2},{10,6},{14,10},{7,3},{... | collective-permute-start | bytes 396296 | tf_op jit(solution)/shard_map/ppermute | solution.py:26
  140.4 7.8 %collective-permute-start.35 = (f32[256]{0:T(256)S(1)}, f32[256]{0:T(256)S(1)}, u32[]{:S(2)}, u32[]{:S(2)}) collective-permute-start(f32[256]{0:T(256)S(1)} %collective-permute-done.34), channel_id=1, source_target_pairs={{4,0},{8,4},{12,8},{5,1},{9,5},{13,9},{6,2},{10,6},{14,10},{7,3},{... | collective-permute-start | bytes 3080 | tf_op jit(solution)/shard_map/ppermute | solution.py:34
  163.5 7.8 %collective-permute-start.41 = (f32[2,256]{1,0:T(2,128)S(1)}, f32[2,256]{1,0:T(2,128)S(1)}, u32[]{:S(2)}, u32[]{:S(2)}) collective-permute-start(f32[2,256]{1,0:T(2,128)S(1)} %rev.15), channel_id=1, source_target_pairs={{4,0},{8,4},{12,8},{5,1},{9,5},{13,9},{6,2},{10,6},{14,10},{7,3},{... | collective-permute-start | bytes 6152 | tf_op jit(solution)/shard_map/ppermute | solution.py:34
  171.2 7.9 %collective-permute-start.43 = (f32[1,256]{1,0:T(1,128)S(1)}, f32[1,256]{1,0:T(1,128)S(1)}, u32[]{:S(2)}, u32[]{:S(2)}) collective-permute-start(f32[1,256]{1,0:T(1,128)S(1)} %get-tuple-element.47), channel_id=1, source_target_pairs={{4,0},{8,4},{12,8},{5,1},{9,5},{13,9},{6,2},{10,6},{14,10},{7,3},{... | collective-permute-start | bytes 3080 | tf_op jit(solution)/shard_map/ppermute | solution.py:34
  179.2 11.9 %collective-permute-start.46 = (f32[256]{0:T(256)S(1)}, f32[256]{0:T(256)S(1)}, u32[]{:S(2)}, u32[]{:S(2)}) collective-permute-start(f32[256]{0:T(256)S(1)} %fusion.266), channel_id=1, source_target_pairs={{4,0},{8,4},{12,8},{5,1},{9,5},{13,9},{6,2},{10,6},{14,10},{7,3},{... | collective-permute-start | bytes 3080 | tf_op jit(solution)/shard_map/ppermute | solution.py:34
  180.5 11.9 %collective-permute-start.44 = (f32[256]{0:T(256)S(1)}, f32[256]{0:T(256)S(1)}, u32[]{:S(2)}, u32[]{:S(2)}) collective-permute-start(f32[256]{0:T(256)S(1)} %fusion.266), channel_id=1, source_target_pairs={{0,4},{4,8},{8,12},{1,5},{5,9},{9,13},{2,6},{6,10},{10,14},{3,7},{... | collective-permute-start | bytes 3080 | tf_op jit(solution)/shard_map/ppermute | solution.py:34
  185.8 17.7 %collective-permute-start.38 = (bf16[256,1,258]{0,2,1:T(8,128)(2,1)}, bf16[256,1,258]{0,2,1:T(8,128)(2,1)S(1)}, u32[]{:S(2)}, u32[]{:S(2)}) collective-permute-start(bf16[256,1,258]{0,2,1:T(8,128)(2,1)} %get-tuple-element.14), channel_id=1, source_target_pairs={{0,4},{4,8},{8,12},{1,5},{5,9},{9,13},{2,6},{6,10},{10,14},{3,7},{... | collective-permute-start | bytes 396296 | tf_op jit(solution)/shard_map/ppermute | solution.py:23
  189.7 13.8 %collective-permute-start.39 = (bf16[256,1,258]{0,2,1:T(8,128)(2,1)}, bf16[256,1,258]{0,2,1:T(8,128)(2,1)}, u32[]{:S(2)}, u32[]{:S(2)}) collective-permute-start(bf16[256,1,258]{0,2,1:T(8,128)(2,1)} %get-tuple-element.15), channel_id=1, source_target_pairs={{4,0},{8,4},{12,8},{5,1},{9,5},{13,9},{6,2},{10,6},{14,10},{7,3},{... | collective-permute-start | bytes 396296 | tf_op jit(solution)/shard_map/ppermute | solution.py:26
  191.1 7.8 %collective-permute-start.47 = (f32[256]{0:T(256)S(1)}, f32[256]{0:T(256)S(1)}, u32[]{:S(2)}, u32[]{:S(2)}) collective-permute-start(f32[256]{0:T(256)S(1)} %collective-permute-done.46), channel_id=1, source_target_pairs={{4,0},{8,4},{12,8},{5,1},{9,5},{13,9},{6,2},{10,6},{14,10},{7,3},{... | collective-permute-start | bytes 3080 | tf_op jit(solution)/shard_map/ppermute | solution.py:34
  (49 other events, 220.7 us)
where the time goes:
time: 212 us; the launch traced here: 210 us
  starting transfers between devices  127 us (60%)
  local copies, waits for them, and re-layouts  27.6 us (13%)
  other arithmetic  27.2 us (13%)
  matrix products  24.4 us (12%)
  between operations  2.84 us (1%)
    ppermute x32, starting transfers between devices, from_behind(): return lax.ppermute(block, axis, route)  98.7 us
    dot_general x36, matrix products, apply_taps(): jnp.einsum('co,chw->ohw', kernel[tap_index], window, preferred_element_ty...  20.6 us
    ppermute x8, starting transfers between devices, with_halo(): lax.ppermute(lax.slice_in_dim(block, block.shape[dim] - width, None, axis...  15.9 us
    ppermute x8, starting transfers between devices, with_halo(): lax.ppermute(lax.slice_in_dim(block, 0, width, axis=dim), axis, backward)  12.1 us
    scatter-add x4, other arithmetic, evaluate(): jnp.zeros(((2 * REACH + 1) * stations,), jnp.float32).at[near_index]  8.41 us
    scatter-add x4, other arithmetic, evaluate(): jnp.zeros((current.size,), jnp.float32).at[entry_cell].add(weights * back)  8.27 us
    unnamed x71, local copies, waits for them, and re-layouts  8.15 us
    gather x4, local copies, waits for them, and re-layouts, evaluate(): back = jnp.stack(pieces).reshape(-1)[near_index]  6.89 us
  transfers between devices with their start and end apart: 48, of which 1 were waited for; matrix products, arithmetic and copies ran while one was open for 17% of the time, Pallas kernels for 0%

commit v1 on v0

v1 whole, which is shorter than its diff:
```python
import functools
import math

import jax
import jax.numpy as jnp
from jax import lax
from jax.experimental import pallas as pl
from jax.experimental.pallas import tpu as pltpu
from jax.sharding import PartitionSpec as P

F32 = jnp.float32
BF16 = jnp.bfloat16
REACH = 2
HALO = 4
LANES = 128
HALF = 64

noise_levels = (1.0, 0.6, 0.3)
obs_precision = 4.0
step_factor = 0.1


def sub_steps():
    steps = []
    for section in range(2):
        upper, lower = noise_levels[section], noise_levels[section + 1]
        spread = upper * upper - lower * lower
        steps.append((upper, spread, math.sqrt(spread)))
        factor = step_factor * lower * lower
        steps.append((lower, factor, math.sqrt(2.0 * factor)))
    return steps


STEPS = sub_steps()


def shrink(level):
    return 1.0 / math.sqrt(1.0 + level * level)


def vmem_call(kernel, outs, *args, scratch=()):
    args = [pltpu.with_memory_space_constraint(a, pltpu.VMEM) for a in args]
    spec = pl.BlockSpec(memory_space=pltpu.VMEM)
    return pl.pallas_call(
        kernel,
        out_shape=[pltpu.VMEM(shape, dtype) for shape, dtype in outs],
        in_specs=[spec] * len(args),
        out_specs=[spec] * len(outs),
        scratch_shapes=list(scratch),
        compiler_params=pltpu.CompilerParams(vmem_limit_bytes=48 * 2**20),
    )(*args)


def dot(a, b, ca=1, cb=0):
    return lax.dot_general(a, b, (((ca,), (cb,)), ((), ())), preferred_element_type=F32)


def pieces(x, count):
    out = []
    for _ in range(count):
        part = x.astype(BF16)
        out.append(part)
        x = x - part.astype(F32)
    return out


def iota(shape, dim):
    return lax.broadcasted_iota(jnp.int32, shape, dim).astype(F32)


def silu_norm(values, gain):
    power = jnp.mean(values * values, axis=1, keepdims=True)
    half = values * (0.5 * lax.rsqrt(power + 1e-06)) * gain
    return half + half * jnp.tanh(half)


def is_even(axis):
    return lax.rem(lax.axis_index(axis), 2) == 0


def setup_kernel(
    prior, noise, cell, owner, slot, weight, live, station,
    state_msg, entry_msg, noise_a, noise_b,
    *, lond, latb, slots, n_wt,
):
    count = cell.shape[1]
    cells = cell[...]
    lon = cells % lond
    row = (cells // lond) % latb
    variable = cells // (lond * latb)
    rv = row * prior.shape[0] + variable
    key = owner[...] * slots + slot[...]
    alive = lax.broadcasted_iota(jnp.int32, (1, count), 1) < live[...]
    weights = jnp.where(alive, weight[...], 0.0)
    mine = lax.axis_index("band") * slots + lax.broadcasted_iota(jnp.int32, (1, count), 1)
    rows = [key.astype(F32), rv.astype(F32), lon.astype(F32), weights, station[...], mine.astype(F32)]
    entry_msg[0:1] = rows[0]
    entry_msg[1:2] = rows[1]
    entry_msg[2:3] = rows[2]
    entry_msg[3:4] = rows[3]
    entry_msg[4:5] = rows[4]
    entry_msg[5:6] = rows[5]
    entry_msg[6:8] = jnp.zeros((2, count), F32)
    columns = jnp.transpose(entry_msg[...])
    rv_col, lon_col = columns[:, 1:2], columns[:, 2:3]
    one_hot = jnp.where(rv_col == iota((count, latb * prior.shape[0]), 1), 1.0, 0.0).astype(BF16)
    current = jnp.concatenate([prior[:, r, :] for r in range(latb)], axis=0)
    picked = sum(dot(one_hot, part) for part in pieces(current, 3))
    at = jnp.sum(jnp.where(lon_col == iota((count, lond), 1), picked, 0.0), axis=1, keepdims=True)
    eye = iota((count, count), 0) == iota((count, count), 1)
    entry_msg[6:7] = weights * jnp.sum(jnp.where(eye, at, 0.0), axis=0, keepdims=True)
    for r in range(latb):
        state_msg[r] = (prior[:, r, :] * shrink(STEPS[0][0])).astype(BF16)
    up = [(k, r) for k in range(3) for r in range(1 + k, latb)]
    down = [(k, r) for k in range(3) for r in range(0, latb - 1 - k)]

    @pl.when(is_even("band"))
    def _():
        for i in range(len(up)):
            noise_a[i] = noise[up[i][0], :, up[i][1], :].astype(BF16)
            noise_b[i] = noise[down[i][0], :, down[i][1], :].astype(BF16)

    @pl.when(jnp.logical_not(is_even("band")))
    def _():
        for i in range(len(up)):
            noise_a[i] = noise[down[i][0], :, down[i][1], :].astype(BF16)
            noise_b[i] = noise[up[i][0], :, up[i][1], :].astype(BF16)


def edges_into(edge_ref, state, rows, level):
    lane = lax.broadcasted_iota(jnp.int32, (1, LANES), 1)
    width = state.shape[2]
    edge = jnp.zeros(edge_ref.shape, F32)
    for r in range(rows):
        slab = state[r]
        edge = jnp.where(lane == r, slab[:, 0:1], edge)
        edge = jnp.where(lane == HALF + r, slab[:, width - 1 : width], edge)
    edge_ref[...] = (edge * shrink(level)).astype(BF16)


def extend_kernel(prior, halo_a, halo_b, state, edge, *, latb):
    grow = 1.0 / shrink(STEPS[0][0])
    for r in range(latb):
        state[HALO + r] = prior[:, r, :]

    @pl.when(is_even("band"))
    def _():
        for r in range(latb):
            state[r] = halo_b[r].astype(F32) * grow
            state[HALO + latb + r] = halo_a[r].astype(F32) * grow

    @pl.when(jnp.logical_not(is_even("band")))
    def _():
        for r in range(latb):
            state[r] = halo_a[r].astype(F32) * grow
            state[HALO + latb + r] = halo_b[r].astype(F32) * grow

    edges_into(edge, state, 2 * HALO + latb, STEPS[0][0])


def tables_kernel(*refs, n_msgs, variables, latb, lond):
    msgs = refs[:n_msgs]
    keys, cols, pick, spread = refs[n_msgs:]
    count = msgs[0].shape[1]
    high = latb * variables
    even = is_even("band")
    own = msgs[0][...]
    low = jnp.where(even, msgs[2][...], msgs[1][...])
    up = jnp.where(even, msgs[1][...], msgs[2][...])
    for i in range(n_msgs):
        keys[:, i * count : (i + 1) * count] = msgs[i][...]
    for j, msg in enumerate((own, low, up)):
        col = jnp.transpose(msg)
        block = slice(j * count, (j + 1) * count)
        key = jnp.broadcast_to(col[:, 0:1], (count, LANES))
        acc = jnp.zeros((count, LANES), F32)
        for i in range(n_msgs):
            for part in range(count // LANES):
                at = slice(part * LANES, (part + 1) * LANES)
                acc = acc + jnp.where(key == msgs[i][5:6, at], msgs[i][4:5, at], 0.0)
        cols[0, block] = key
        cols[1, block] = jnp.broadcast_to(jnp.sum(acc, axis=1, keepdims=True), (count, LANES))
        cols[2, block] = jnp.broadcast_to(col[:, 3:4], (count, LANES))
        cols[3, block] = jnp.broadcast_to(col[:, 2:3], (count, LANES))
        cols[4, block] = jnp.broadcast_to(col[:, 1:2] * lond + col[:, 2:3], (count, LANES))
        cols[5, block] = jnp.broadcast_to(col[:, 5:6], (count, LANES))
        spread[j] = jnp.where(iota((high, count), 0) == msg[1:2], 1.0, 0.0).astype(BF16)
        if j == 0:
            pick[...] = jnp.where(col[:, 1:2] == iota((count, high), 1), 1.0, 0.0).astype(BF16)


def network_kernel(*refs, step, rows, latb, gather):
    state, edge_a, edge_b, noise, halo_a, halo_b, lift, conv, head, gain_1, gain_2 = refs[:11]
    if gather:
        pick, cols, target, at_entries, firsts, lifteds, halos = refs[11:]
    else:
        target, firsts, lifteds = refs[11:]
    level, drift, kick = STEPS[step]
    scale = shrink(level)
    wide = rows + 2
    out_halo = (rows - latb) // 2
    width = state.shape[2]
    channels = lift.shape[1]
    band = lax.axis_index("band")
    north = band == 0
    south = band == lax.axis_size("band") - 1

    lane = lax.broadcasted_iota(jnp.int32, (1, LANES), 1)
    even = is_even("wt")
    from_a, from_b = edge_a[...].astype(F32), edge_b[...].astype(F32)
    right = jnp.where(even, from_a, from_b)
    left = jnp.where(even, from_b, from_a)
    edge = pltpu.roll(jnp.where(lane < HALF, right, left), HALF, 1).astype(BF16)
    edge = silu_norm(dot(edge, lift[...], 0, 0), gain_1[...])

    sub = lax.broadcasted_iota(jnp.int32, (width, 1), 0)
    for r in range(wide):
        lifted = dot((state[r] * scale).astype(BF16), lift[...], 0, 0)
        if 1 <= r <= rows:
            lifteds[(r - 1) * width : r * width] = lifted
        first = silu_norm(lifted, gain_1[...])
        before, after = edge[r : r + 1], edge[HALF + r : HALF + r + 1]
        outside = None
        if r < out_halo + 1:
            outside = north
        elif r >= out_halo + 1 + latb:
            outside = south
        if outside is not None:
            first = jnp.where(outside, 0.0, first)
            before = jnp.where(outside, 0.0, before)
            after = jnp.where(outside, 0.0, after)
        here = slice(r * width, (r + 1) * width)
        firsts[here, 0:channels] = jnp.where(sub == 0, before, pltpu.roll(first, 1, 0)).astype(BF16)
        firsts[here, channels : 2 * channels] = first.astype(BF16)
        firsts[here, 2 * channels : 3 * channels] = jnp.where(
            sub == width - 1, after, pltpu.roll(first, width - 1, 0)
        ).astype(BF16)

    mixed = lifteds[0 : rows * width]
    for p in range(3):
        mixed = mixed + dot(
            firsts[p * width : (p + rows) * width], conv[3 * channels * p : 3 * channels * (p + 1)]
        )
    second = silu_norm(mixed, gain_2[...]).astype(BF16)
    base = sum(3 - k for k in range(step))
    if out_halo:
        even_band = is_even("band")
    for i in range(rows):
        score = dot(head[...], second[i * width : (i + 1) * width], 0, 1)
        r = i - out_halo
        if 0 <= r < latb:
            draw = noise[step, :, r, :]
        else:
            a, b = halo_a[base + i % (out_halo + latb)], halo_b[base + i % (out_halo + latb)]
            draw = (jnp.where(even_band, b, a) if r < 0 else jnp.where(even_band, a, b)).astype(F32)
        target[i] = state[i + 1] + (drift / level) * score + kick * draw
    if gather:
        variables = state.shape[1]
        for r in range(latb):
            for j, part in enumerate(pieces(target[out_halo + r], 3)):
                halos[r * variables : (r + 1) * variables, j * width : (j + 1) * width] = part
        picked = dot(pick[...], halos[...])
        picked = picked[:, 0:width] + picked[:, width : 2 * width] + picked[:, 2 * width :]
        count = pick.shape[0]
        lon = jnp.concatenate([cols[3, 0:count]] * (width // LANES), axis=1)
        at = jnp.sum(jnp.where(lon == iota((count, width), 1), picked, 0.0), axis=1, keepdims=True)
        at_entries[...] = jnp.broadcast_to(at, (count, LANES))


def matching(key, keys, values):
    count = values[0].shape[1]
    acc = jnp.zeros(key.shape, F32)
    for i, row in enumerate(values):
        for part in range(count // LANES):
            at = slice(part * LANES, (part + 1) * LANES)
            known = keys[0:1, i * count + part * LANES : i * count + (part + 1) * LANES]
            acc = acc + jnp.where(key == known, row[:, at], 0.0)
    return jnp.sum(acc, axis=1, keepdims=True)


def update_kernel(*refs, step, n_msgs, rows, latb, value_row):
    target, keys, cols, spread = refs[:4]
    values = [ref[value_row : value_row + 1] for ref in refs[4 : 4 + n_msgs]]
    rest = refs[4 + n_msgs :]
    last = step == len(STEPS) - 1
    count = values[0].shape[1]
    variables, width = target.shape[1], target.shape[2]
    out_halo = (rows - latb) // 2
    strength = obs_precision * STEPS[step][1]

    def column(j):
        block = slice(j * count, (j + 1) * count)
        found = matching(cols[0, block], keys, values)
        return strength * cols[2, block] * (cols[1, block] - found)

    def spread_rows(j, column_j, rows_from, rows_to):
        block = slice(j * count, (j + 1) * count)
        lon = jnp.concatenate([cols[3, block]] * (width // LANES), axis=1)
        tall = jnp.concatenate([column_j] * (width // LANES), axis=1)
        value = jnp.where(lon == iota((count, width), 1), tall, 0.0)
        parts = jnp.concatenate(pieces(value, 2), axis=1)
        both = dot(spread[j, rows_from * variables : rows_to * variables], parts)
        return both[:, 0:width] + both[:, width:]

    mine = column(0)
    own = spread_rows(0, mine, 0, latb)
    if last:
        state, innov = rest
        for r in range(latb):
            state[:, r, :] = target[out_halo + r] + own[r * variables : (r + 1) * variables]
        found = matching(cols[5, 0:count], keys, values)
        eye = iota((count, count), 0) == iota((count, count), 1)
        innov[...] = keys[4:5, 0:count] - jnp.sum(jnp.where(eye, found, 0.0), axis=0, keepdims=True)
        return
    at_entries, state, edge, value = rest
    row_cell = keys[1:2, 0:count] * width + keys[2:3, 0:count]
    cell = jnp.concatenate([cols[4, 0:count]] * (count // LANES), axis=1)
    tall = jnp.concatenate([mine] * (count // LANES), axis=1)
    before = jnp.concatenate([at_entries[...]] * (count // LANES), axis=1)
    eye = iota((count, count), 0) == iota((count, count), 1)
    total = jnp.where(cell == row_cell, tall, 0.0) + jnp.where(eye, before, 0.0)
    value[...] = jnp.broadcast_to(
        keys[3:4, 0:count] * jnp.sum(total, axis=0, keepdims=True), value.shape
    )
    for r in range(latb):
        state[out_halo + r] = target[out_halo + r] + own[r * variables : (r + 1) * variables]
    if out_halo:
        low = spread_rows(1, column(1), latb - out_halo, latb)
        up = spread_rows(2, column(2), 0, out_halo)
        for r in range(out_halo):
            here = slice(r * variables, (r + 1) * variables)
            state[r] = target[r] + low[here]
            state[out_halo + latb + r] = target[out_halo + latb + r] + up[here]
    edges_into(edge, state, rows, STEPS[step + 1][0])


def swaps(count):
    first = [(i, i ^ 1) for i in range(count)]
    other = [(i, (i - 1) % count if i % 2 == 0 else (i + 1) % count) for i in range(count)]
    return first, other


def from_neighbours(block, axis):
    return [lax.ppermute(block, axis, route) for route in swaps(lax.axis_size(axis))]


def from_bands(block):
    count = lax.axis_size("band")
    found = [block] + from_neighbours(block, "band")
    reach = min(2 * REACH + 1, count)
    far = sorted({d % count for d in range(-reach, reach + 1)} - {0, 1, count - 1})
    for distance in far:
        route = [(i, (i + distance) % count) for i in range(count)]
        found.append(lax.ppermute(block, "band", route))
    return found


def per_device(
    prior_state, langevin_noise, station_values, entry_cell, entry_owner, entry_slot,
    entry_weight, live_counts, lift_weight, conv_weight, head_weight, first_gain, second_gain,
):
    variables, latb, lond = prior_state.shape
    count = entry_cell.shape[0]
    slots = station_values.shape[0]
    channels = lift_weight.shape[1]
    taps = conv_weight.reshape(-1, channels)
    gain_1, gain_2 = first_gain.reshape(1, -1), second_gain.reshape(1, -1)

    def row(a):
        return a.reshape(1, -1)

    noise_slabs = sum(latb - 1 - k for k in range(3))
    state_msg, entry_msg, noise_a, noise_b = vmem_call(
        functools.partial(
            setup_kernel, lond=lond, latb=latb, slots=slots, n_wt=lax.axis_size("wt")
        ),
        [
            ((latb, variables, lond), BF16),
            ((8, count), F32),
            ((noise_slabs, variables, lond), BF16),
            ((noise_slabs, variables, lond), BF16),
        ],
        prior_state, langevin_noise, row(entry_cell), row(entry_owner), row(entry_slot),
        row(entry_weight), jnp.broadcast_to(live_counts, (1, count)), row(station_values),
    )
    halos = from_neighbours(state_msg, "band")
    msgs = from_bands(entry_msg)
    route_a, route_b = swaps(lax.axis_size("band"))
    noise_halo_a = lax.ppermute(noise_a, "band", route_a)
    noise_halo_b = lax.ppermute(noise_b, "band", route_b)
    n_msgs = len(msgs)
    state, edge = vmem_call(
        functools.partial(extend_kernel, latb=latb),
        [((2 * HALO + latb, variables, lond), F32), ((variables, LANES), BF16)],
        prior_state, *halos,
    )
    edges = from_neighbours(edge, "wt")
    keys, cols, pick, spread = vmem_call(
        functools.partial(tables_kernel, n_msgs=n_msgs, variables=variables, latb=latb, lond=lond),
        [
            ((8, n_msgs * count), F32),
            ((6, 3 * count, LANES), F32),
            ((count, latb * variables), BF16),
            ((3, latb * variables, count), BF16),
        ],
        *msgs,
    )
    values, value_row = msgs, 6
    for step in range(len(STEPS)):
        last = step == len(STEPS) - 1
        rows = latb + 2 * (HALO - 1 - step)
        network_out = [((rows, variables, lond), F32)]
        network_in = [
            state, *edges, langevin_noise, noise_halo_a, noise_halo_b,
            lift_weight, taps, head_weight, gain_1, gain_2,
        ]
        scratch = [
            pltpu.VMEM(((rows + 2) * lond, 3 * channels), BF16),
            pltpu.VMEM((rows * lond, channels), F32),
        ]
        if not last:
            network_out.append(((count, LANES), F32))
            network_in += [pick, cols]
            scratch.append(pltpu.VMEM((latb * variables, 3 * lond), BF16))
        found = vmem_call(
            functools.partial(network_kernel, step=step, rows=rows, latb=latb, gather=not last),
            network_out,
            *network_in,
            scratch=scratch,
        )
        update = functools.partial(
            update_kernel, step=step, n_msgs=n_msgs, rows=rows, latb=latb, value_row=value_row
        )
        if last:
            state, innov = vmem_call(
                update,
                [((variables, latb, lond), F32), ((1, count), F32)],
                found[0], keys, cols, spread, *values,
            )
            return state, innov.reshape(-1)
        state, edge, value = vmem_call(
            update,
            [((rows, variables, lond), F32), ((variables, LANES), BF16), ((8, count), F32)],
            found[0], keys, cols, spread, *values, found[1],
        )
        values, value_row = from_bands(value), 0
        edges = from_neighbours(edge, "wt")


def solution(mesh):
    split = P(("groups", "band", "wt"))
    in_specs = (
        P("groups", "band", "wt"),
        P(None, "groups", "band", "wt"),
        split, split, split, split, split, split,
        P(), P(), P(), P(), P(),
    )
    out_specs = (P("groups", "band", "wt"), split)
    return jax.shard_map(
        per_device, mesh=mesh, in_specs=in_specs, out_specs=out_specs, check_vma=False
    )
```

time: 212 us -> 82.3 us (0.39)
  starting transfers between devices: 127 us -> 30.1 us
  other arithmetic: 27.2 us -> 0 us
  Pallas kernels: 0 us -> 25.4 us
  matrix products: 24.4 us -> 0 us
  local copies, waits for them, and re-layouts: 27.6 us -> 11.1 us
  waiting for transfers between devices: 1.38 us -> 13.7 us
    ppermute x48 -> x24, starting transfers between devices: 127 us -> 30.1 us  [the longest x18 13.6 us: from_neighbours(): lax.ppermute(block, axis, route)]
    pallas_call x0 -> x11, Pallas kernels: none -> 25.4 us  [vmem_call(): pl.pallas_call(kernel, out_shape=[pltpu.VMEM(shape, dtype) for shape, dty...]
    dot_general x44 -> x0, matrix products: 24.4 us -> none  [the longest x36 20.6 us: apply_taps(): jnp.einsum('co,chw->ohw', kernel[tap_index], window, preferred_element_ty...]
    scatter-add x8 -> x0, other arithmetic: 16.7 us -> none  [the longest x4 8.41 us: evaluate(): jnp.zeros(((2 * REACH + 1) * stations,), jnp.float32).at[near_index]]
    gather x8 -> x0, local copies, waits for them, and re-layouts: 13.8 us -> none  [the longest x4 6.89 us: evaluate(): back = jnp.stack(pieces).reshape(-1)[near_index]]
    ppermute x48 -> x24, waiting for transfers between devices: 1.38 us -> 13.7 us  [the longest x18 13.6 us: from_neighbours(): lax.ppermute(block, axis, route)]
    concatenate x4 -> x0, other arithmetic: 4.24 us -> none  [with_halo(): block = jnp.concatenate([low, block, high], axis=dim)]
    mul x4 -> x0, local copies, waits for them, and re-layouts: 3.53 us -> none  [evaluate(): return (score + obs_precision * adjoint.reshape(current.shape), innov)]
  transfers between devices with their start and end apart: 48 -> 24, of which waited for: 1 -> 4; matrix products, arithmetic and copies ran while one was open for 17% -> 1% of each run, Pallas kernels for 0% -> 18%
where the time goes in v1:
time: 82.3 us; the launch traced here: 81.8 us
  starting transfers between devices  30.1 us (37%)
  Pallas kernels  25.4 us (31%)
  waiting for transfers between devices  13.7 us (17%)
  local copies, waits for them, and re-layouts  11.1 us (13%)
  between operations  1.54 us (2%)
    pallas_call x11, Pallas kernels, vmem_call(): pl.pallas_call(kernel, out_shape=[pltpu.VMEM(shape, dtype) for shape, dty...  25.4 us
    ppermute x18, waiting for transfers between devices, from_neighbours(): lax.ppermute(block, axis, route)  13.6 us
    ppermute x18, starting transfers between devices, from_neighbours(): lax.ppermute(block, axis, route)  13.6 us
    unnamed x31, local copies, waits for them, and re-layouts  11.1 us
    ppermute x4, starting transfers between devices, from_bands(): found.append(lax.ppermute(block, 'band', route))  11 us
    ppermute x1, starting transfers between devices, per_device(): noise_halo_a = lax.ppermute(noise_a, 'band', route_a)  3.09 us
    ppermute x1, starting transfers between devices, per_device(): noise_halo_b = lax.ppermute(noise_b, 'band', route_b)  2.48 us
  transfers between devices with their start and end apart: 24, of which 4 were waited for; matrix products, arithmetic and copies ran while one was open for 1% of the time, Pallas kernels for 18%

profile of v1, /device:TPU:0, one launch (start us, length us, event | category | flops | bytes accessed | tf_op | source)
XLA Modules:
  0.0 81.8 jit_solution(10065303663089025159)
XLA Ops:
  1.3 1.2 %copy-done = f32[4,64,4,256]{3,2,1,0:T(4,128)S(1)} copy-done((f32[4,64,4,256]{3,2,1,0:T(4,128)S(1)}, f32[4,64,4,256]{3,2,1,0:T(4,128)}, u32[]{:S(2)}) %copy-start) | copy-done | bytes 1048600
  2.5 0.9 %copy-done.4 = f32[64,4,256]{2,1,0:T(4,128)S(1)} copy-done((f32[64,4,256]{2,1,0:T(4,128)S(1)}, f32[64,4,256]{2,1,0:T(4,128)}, u32[]{:S(2)}) %copy-start.4) | copy-done | bytes 262168
  6.9 1.9 %shard_map.143 = (bf16[4,64,256]{2,1,0:T(8,128)(2,1)S(1)}, f32[8,256]{1,0:T(8,128)S(1)}, bf16[6,64,256]{2,1,0:T(8,128)(2,1)S(1)}, bf16[6,64,256]{2,1,0:T(8,128)(2,1)S(1)}) custom-call(f32[64,4,256]{2,1,0:T(4,128)S(1)} %copy-done.4, f32[4,64,4,256]{3,2,1,0:T(4,128)S(1)} %copy-done, s32[1,256]{1,0:T(1,128)S(1)} %bitcast.24, s32[1,256]{1,0:T(1,128)S(1)} %bitcast.25, ...), custom_call_target="tpu_custom_call" | custom-call | tf_op jit(solution)/shard_map/pallas_call | solution.py:44
  8.8 3.1 %collective-permute-start.4 = (bf16[6,64,256]{2,1,0:T(8,128)(2,1)S(1)}, bf16[6,64,256]{2,1,0:T(8,128)(2,1)S(1)}, u32[]{:S(2)}, u32[]{:S(2)}) collective-permute-start(bf16[6,64,256]{2,1,0:T(8,128)(2,1)S(1)} %get-tuple-element.32), channel_id=1, source_target_pairs={{0,4},{4,0},{8,12},{12,8},{1,5},{5,1},{9,13},{13,9},{2,6},{6,2},{1... | collective-permute-start | bytes 589832 | tf_op jit(solution)/shard_map/ppermute | solution.py:389
  11.9 2.5 %collective-permute-start.5 = (bf16[6,64,256]{2,1,0:T(8,128)(2,1)S(1)}, bf16[6,64,256]{2,1,0:T(8,128)(2,1)S(1)}, u32[]{:S(2)}, u32[]{:S(2)}) collective-permute-start(bf16[6,64,256]{2,1,0:T(8,128)(2,1)S(1)} %get-tuple-element.33), channel_id=1, source_target_pairs={{0,12},{4,8},{8,4},{12,0},{1,13},{5,9},{9,5},{13,1},{2,14},{6,10},... | collective-permute-start | bytes 589832 | tf_op jit(solution)/shard_map/ppermute | solution.py:390
  14.4 1.3 %collective-permute-start.1 = (bf16[4,64,256]{2,1,0:T(8,128)(2,1)S(1)}, bf16[4,64,256]{2,1,0:T(8,128)(2,1)S(1)}, u32[]{:S(2)}, u32[]{:S(2)}) collective-permute-start(bf16[4,64,256]{2,1,0:T(8,128)(2,1)S(1)} %get-tuple-element.29), channel_id=1, source_target_pairs={{0,12},{4,8},{8,4},{12,0},{1,13},{5,9},{9,5},{13,1},{2,14},{6,10},... | collective-permute-start | bytes 393224 | tf_op jit(solution)/shard_map/ppermute | solution.py:344
  15.7 3.0 %collective-permute-start.8 = (f32[8,256]{1,0:T(8,128)S(1)}, f32[8,256]{1,0:T(8,128)S(1)}, u32[]{:S(2)}, u32[]{:S(2)}) collective-permute-start(f32[8,256]{1,0:T(8,128)S(1)} %get-tuple-element.34.refs_0_.refs_4_), channel_id=1, source_target_pairs={{0,8},{4,12},{8,0},{12,4},{1,9},{5,13},{9,1},{13,5},{2,10},{6,14},... | collective-permute-start | bytes 24584 | tf_op jit(solution)/shard_map/ppermute | solution.py:354
  18.8 8.4 %collective-permute-done.1.halo_b = bf16[4,64,256]{2,1,0:T(8,128)(2,1)S(1)} collective-permute-done((bf16[4,64,256]{2,1,0:T(8,128)(2,1)S(1)}, bf16[4,64,256]{2,1,0:T(8,128)(2,1)S(1)}, u32[]{:S(2)}, u32[]{:S(2)}) %collective-permute-start.1) | collective-permute-done | bytes 131104 | tf_op jit(solution)/shard_map/ppermute | solution.py:344
  27.2 1.4 %collective-permute-start.7 = (f32[8,256]{1,0:T(8,128)S(1)}, f32[8,256]{1,0:T(8,128)S(1)}, u32[]{:S(2)}, u32[]{:S(2)}) collective-permute-start(f32[8,256]{1,0:T(8,128)S(1)} %get-tuple-element.34.refs_0_.refs_4_), channel_id=1, source_target_pairs={{0,12},{4,8},{8,4},{12,0},{1,13},{5,9},{9,5},{13,1},{2,14},{6,10},... | collective-permute-start | bytes 24584 | tf_op jit(solution)/shard_map/ppermute | solution.py:344
  29.3 1.6 %collective-permute-start.2 = (bf16[64,128]{1,0:T(8,128)(2,1)S(1)}, bf16[64,128]{1,0:T(8,128)(2,1)S(1)}, u32[]{:S(2)}, u32[]{:S(2)}) collective-permute-start(bf16[64,128]{1,0:T(8,128)(2,1)S(1)} %get-tuple-element.31), channel_id=1, source_target_pairs={{0,1},{1,0},{2,3},{3,2},{4,5},{5,4},{6,7},{7,6},{8,9},{9,8},{10,11... | collective-permute-start | bytes 49160 | tf_op jit(solution)/shard_map/ppermute | solution.py:344
  30.8 1.8 %collective-permute-done.7.refs_2_.refs_6_ = f32[8,256]{1,0:T(8,128)S(1)} collective-permute-done((f32[8,256]{1,0:T(8,128)S(1)}, f32[8,256]{1,0:T(8,128)S(1)}, u32[]{:S(2)}, u32[]{:S(2)}) %collective-permute-start.7) | collective-permute-done | bytes 8224 | tf_op jit(solution)/shard_map/ppermute | solution.py:344
  32.6 1.2 %collective-permute-start.6 = (f32[8,256]{1,0:T(8,128)S(1)}, f32[8,256]{1,0:T(8,128)S(1)}, u32[]{:S(2)}, u32[]{:S(2)}) collective-permute-start(f32[8,256]{1,0:T(8,128)S(1)} %get-tuple-element.34.refs_0_.refs_4_), channel_id=1, source_target_pairs={{0,4},{4,0},{8,12},{12,8},{1,5},{5,1},{9,13},{13,9},{2,6},{6,2},{1... | collective-permute-start | bytes 24584 | tf_op jit(solution)/shard_map/ppermute | solution.py:344
  33.9 0.9 %copy.15.refs_8_ = bf16[256,64]{1,0:T(8,128)(2,1)S(1)} copy(bf16[256,64]{0,1:T(8,128)(2,1)} %param.23) | data formatting | bytes 65536 | tf_op args[10]
  34.8 1.5 %collective-permute-done.6.refs_1_.refs_5_ = f32[8,256]{1,0:T(8,128)S(1)} collective-permute-done((f32[8,256]{1,0:T(8,128)S(1)}, f32[8,256]{1,0:T(8,128)S(1)}, u32[]{:S(2)}, u32[]{:S(2)}) %collective-permute-start.6) | collective-permute-done | bytes 8224 | tf_op jit(solution)/shard_map/ppermute | solution.py:344
  36.3 1.7 %shard_map.145 = (f32[8,1024]{1,0:T(8,128)S(1)}, f32[6,768,128]{2,1,0:T(8,128)S(1)}, bf16[256,256]{1,0:T(8,128)(2,1)S(1)}, bf16[3,256,256]{2,1,0:T(8,128)(2,1)S(1)}) custom-call(f32[8,256]{1,0:T(8,128)S(1)} %get-tuple-element.34.refs_0_.refs_4_, f32[8,256]{1,0:T(8,128)S(1)} %collective-permute-done.6.refs_1_.refs_5_, ...), custom_call_target="tpu_custom_call" | custom-call | tf_op jit(solution)/shard_map/pallas_call | solution.py:44
  38.0 1.3 %copy-done.2 = bf16[9,256,256]{2,1,0:T(8,128)(2,1)S(1)} copy-done((bf16[9,256,256]{2,1,0:T(8,128)(2,1)S(1)}, bf16[9,256,256]{2,1,0:T(8,128)(2,1)}, u32[]{:S(2)}) %copy-start.2) | copy-done | bytes 1179672
  41.4 6.2 %shard_map.146 = (f32[10,64,256]{2,1,0:T(8,128)S(1)}, f32[256,128]{1,0:T(8,128)S(1)}) custom-call(f32[12,64,256]{2,1,0:T(8,128)S(1)} %get-tuple-element.30.refs_0_, bf16[64,128]{1,0:T(8,128)(2,1)S(1)} %collective-permute-done.2.refs_1_, bf16[64,128]{1,0:T(8,128)(2,1)S(1)} %collective-permute-done.3.refs_2_, f32[4,64,4,256]{3,2,1,0:T(4,128)S(1)} %copy-done.1, ...), custom_call_target="tpu_custom_call" | custom-call | tf_op jit(solution)/shard_map/pallas_call | solution.py:44
  47.6 0.9 %shard_map.147 = (f32[10,64,256]{2,1,0:T(8,128)S(1)}, bf16[64,128]{1,0:T(8,128)(2,1)S(1)}, f32[8,256]{1,0:T(8,128)S(1)}) custom-call(f32[10,64,256]{2,1,0:T(8,128)S(1)} %get-tuple-element.37.refs_0_, f32[8,1024]{1,0:T(8,128)S(1)} %get-tuple-element.38.refs_1_, f32[6,768,128]{2,1,0:T(8,128)S(1)} %get-tuple-element.36.refs_12_.refs_2_, ...), custom_call_target="tpu_custom_call" | custom-call | tf_op jit(solution)/shard_map/pallas_call | solution.py:44
  48.6 1.6 %collective-permute-start.9 = (bf16[64,128]{1,0:T(8,128)(2,1)S(1)}, bf16[64,128]{1,0:T(8,128)(2,1)S(1)}, u32[]{:S(2)}, u32[]{:S(2)}) collective-permute-start(bf16[64,128]{1,0:T(8,128)(2,1)S(1)} %get-tuple-element.42), channel_id=1, source_target_pairs={{0,1},{1,0},{2,3},{3,2},{4,5},{5,4},{6,7},{7,6},{8,9},{9,8},{10,11... | collective-permute-start | bytes 49160 | tf_op jit(solution)/shard_map/ppermute | solution.py:344
  50.2 2.0 %collective-permute-start.13 = (f32[8,256]{1,0:T(8,128)S(1)}, f32[8,256]{1,0:T(8,128)S(1)}, u32[]{:S(2)}, u32[]{:S(2)}) collective-permute-start(f32[8,256]{1,0:T(8,128)S(1)} %get-tuple-element.44.refs_4_), channel_id=1, source_target_pairs={{0,8},{4,12},{8,0},{12,4},{1,9},{5,13},{9,1},{13,5},{2,10},{6,14},... | collective-permute-start | bytes 24584 | tf_op jit(solution)/shard_map/ppermute | solution.py:354
  52.2 1.1 %collective-permute-start.12 = (f32[8,256]{1,0:T(8,128)S(1)}, f32[8,256]{1,0:T(8,128)S(1)}, u32[]{:S(2)}, u32[]{:S(2)}) collective-permute-start(f32[8,256]{1,0:T(8,128)S(1)} %get-tuple-element.44.refs_4_), channel_id=1, source_target_pairs={{0,12},{4,8},{8,4},{12,0},{1,13},{5,9},{9,5},{13,1},{2,14},{6,10},... | collective-permute-start | bytes 24584 | tf_op jit(solution)/shard_map/ppermute | solution.py:344
  53.7 5.4 %shard_map.148 = (f32[8,64,256]{2,1,0:T(8,128)S(1)}, f32[256,128]{1,0:T(8,128)S(1)}) custom-call(f32[10,64,256]{2,1,0:T(8,128)S(1)} %get-tuple-element.41.refs_0_, bf16[64,128]{1,0:T(8,128)(2,1)S(1)} %collective-permute-done.9.refs_1_, bf16[64,128]{1,0:T(8,128)(2,1)S(1)} %collective-permute-done.10.refs_2_, f32[4,64,4,256]{3,2,1,0:T(4,128)S(1)} %copy-done.1, ...), custom_call_target="tpu_custom_call" | custom-call | tf_op jit(solution)/shard_map/pallas_call | solution.py:44
  59.1 0.9 %shard_map.149 = (f32[8,64,256]{2,1,0:T(8,128)S(1)}, bf16[64,128]{1,0:T(8,128)(2,1)S(1)}, f32[8,256]{1,0:T(8,128)S(1)}) custom-call(f32[8,64,256]{2,1,0:T(8,128)S(1)} %get-tuple-element.43.refs_0_, f32[8,1024]{1,0:T(8,128)S(1)} %get-tuple-element.38.refs_1_, f32[6,768,128]{2,1,0:T(8,128)S(1)} %get-tuple-element.36.refs_12_.refs_2_, ...), custom_call_target="tpu_custom_call" | custom-call | tf_op jit(solution)/shard_map/pallas_call | solution.py:44
  60.8 2.8 %collective-permute-start.18 = (f32[8,256]{1,0:T(8,128)S(1)}, f32[8,256]{1,0:T(8,128)S(1)}, u32[]{:S(2)}, u32[]{:S(2)}) collective-permute-start(f32[8,256]{1,0:T(8,128)S(1)} %get-tuple-element.49.refs_4_), channel_id=1, source_target_pairs={{0,8},{4,12},{8,0},{12,4},{1,9},{5,13},{9,1},{13,5},{2,10},{6,14},... | collective-permute-start | bytes 24584 | tf_op jit(solution)/shard_map/ppermute | solution.py:354
  63.6 1.6 %collective-permute-start.17 = (f32[8,256]{1,0:T(8,128)S(1)}, f32[8,256]{1,0:T(8,128)S(1)}, u32[]{:S(2)}, u32[]{:S(2)}) collective-permute-start(f32[8,256]{1,0:T(8,128)S(1)} %get-tuple-element.49.refs_4_), channel_id=1, source_target_pairs={{0,12},{4,8},{8,4},{12,0},{1,13},{5,9},{9,5},{13,1},{2,14},{6,10},... | collective-permute-start | bytes 24584 | tf_op jit(solution)/shard_map/ppermute | solution.py:344
  65.2 4.1 %shard_map.150 = (f32[6,64,256]{2,1,0:T(8,128)S(1)}, f32[256,128]{1,0:T(8,128)S(1)}) custom-call(f32[8,64,256]{2,1,0:T(8,128)S(1)} %get-tuple-element.46.refs_0_, bf16[64,128]{1,0:T(8,128)(2,1)S(1)} %collective-permute-done.14.refs_1_, bf16[64,128]{1,0:T(8,128)(2,1)S(1)} %collective-permute-done.15.refs_2_, f32[4,64,4,256]{3,2,1,0:T(4,128)S(1)} %copy-done.1, ...), custom_call_target="tpu_custom_call" | custom-call | tf_op jit(solution)/shard_map/pallas_call | solution.py:44
  69.4 0.8 %shard_map.151 = (f32[6,64,256]{2,1,0:T(8,128)S(1)}, bf16[64,128]{1,0:T(8,128)(2,1)S(1)}, f32[8,256]{1,0:T(8,128)S(1)}) custom-call(f32[6,64,256]{2,1,0:T(8,128)S(1)} %get-tuple-element.48.refs_0_, f32[8,1024]{1,0:T(8,128)S(1)} %get-tuple-element.38.refs_1_, f32[6,768,128]{2,1,0:T(8,128)S(1)} %get-tuple-element.36.refs_12_.refs_2_, ...), custom_call_target="tpu_custom_call" | custom-call | tf_op jit(solution)/shard_map/pallas_call | solution.py:44
  70.3 1.3 %collective-permute-start.19 = (bf16[64,128]{1,0:T(8,128)(2,1)S(1)}, bf16[64,128]{1,0:T(8,128)(2,1)S(1)}, u32[]{:S(2)}, u32[]{:S(2)}) collective-permute-start(bf16[64,128]{1,0:T(8,128)(2,1)S(1)} %get-tuple-element.52), channel_id=1, source_target_pairs={{0,1},{1,0},{2,3},{3,2},{4,5},{5,4},{6,7},{7,6},{8,9},{9,8},{10,11... | collective-permute-start | bytes 49160 | tf_op jit(solution)/shard_map/ppermute | solution.py:344
  71.6 3.1 %collective-permute-start.23 = (f32[8,256]{1,0:T(8,128)S(1)}, f32[8,256]{1,0:T(8,128)S(1)}, u32[]{:S(2)}, u32[]{:S(2)}) collective-permute-start(f32[8,256]{1,0:T(8,128)S(1)} %get-tuple-element.53.refs_4_), channel_id=1, source_target_pairs={{0,8},{4,12},{8,0},{12,4},{1,9},{5,13},{9,1},{13,5},{2,10},{6,14},... | collective-permute-start | bytes 24584 | tf_op jit(solution)/shard_map/ppermute | solution.py:354
  74.7 1.1 %collective-permute-start.22 = (f32[8,256]{1,0:T(8,128)S(1)}, f32[8,256]{1,0:T(8,128)S(1)}, u32[]{:S(2)}, u32[]{:S(2)}) collective-permute-start(f32[8,256]{1,0:T(8,128)S(1)} %get-tuple-element.53.refs_4_), channel_id=1, source_target_pairs={{0,12},{4,8},{8,4},{12,0},{1,13},{5,9},{9,5},{13,1},{2,14},{6,10},... | collective-permute-start | bytes 24584 | tf_op jit(solution)/shard_map/ppermute | solution.py:344
  75.8 2.5 %shard_map.152.refs_0_ = f32[4,64,256]{2,1,0:T(8,128)S(1)} custom-call(f32[6,64,256]{2,1,0:T(8,128)S(1)} %get-tuple-element.51.refs_0_, bf16[64,128]{1,0:T(8,128)(2,1)S(1)} %collective-permute-done.19.refs_1_, bf16[64,128]{1,0:T(8,128)(2,1)S(1)} %collective-permute-done.20.refs_2_, f32[4,64,4,256]{3,2,1,0:T(4,128)S(1)} %copy-done.1, ...), custom_call_target="tpu_custom_call" | custom-call | tf_op jit(solution)/shard_map/pallas_call | solution.py:44
  78.3 1.8 %collective-permute-done.22.refs_6_ = f32[8,256]{1,0:T(8,128)S(1)} collective-permute-done((f32[8,256]{1,0:T(8,128)S(1)}, f32[8,256]{1,0:T(8,128)S(1)}, u32[]{:S(2)}, u32[]{:S(2)}) %collective-permute-start.22) | collective-permute-done | bytes 8224 | tf_op jit(solution)/shard_map/ppermute | solution.py:344
  (59 shorter events, 9.4 us)
Async XLA Ops:
  1.3 1.2 %copy-start = (f32[4,64,4,256]{3,2,1,0:T(4,128)S(1)}, f32[4,64,4,256]{3,2,1,0:T(4,128)}, u32[]{:S(2)}) copy-start(f32[4,64,4,256]{3,2,1,0:T(4,128)} %refs_3_.7) | copy-start | bytes 3145732
  2.5 0.9 %copy-start.4 = (f32[64,4,256]{2,1,0:T(4,128)S(1)}, f32[64,4,256]{2,1,0:T(4,128)}, u32[]{:S(2)}) copy-start(f32[64,4,256]{2,1,0:T(4,128)} %prior.3) | copy-start | bytes 786436
  4.8 0.7 copy-start.11
  6.9 31.2 %copy-start.1 = (f32[4,64,4,256]{3,2,1,0:T(4,128)S(1)}, f32[4,64,4,256]{3,2,1,0:T(4,128)}, u32[]{:S(2)}) copy-start(f32[4,64,4,256]{3,2,1,0:T(4,128)} %refs_3_.7) | copy-start | bytes 3145732
  8.8 29.2 %collective-permute-start.4 = (bf16[6,64,256]{2,1,0:T(8,128)(2,1)S(1)}, bf16[6,64,256]{2,1,0:T(8,128)(2,1)S(1)}, u32[]{:S(2)}, u32[]{:S(2)}) collective-permute-start(bf16[6,64,256]{2,1,0:T(8,128)(2,1)S(1)} %get-tuple-element.32), channel_id=1, source_target_pairs={{0,4},{4,0},{8,12},{12,8},{1,5},{5,1},{9,13},{13,9},{2,6},{6,2},{1... | collective-permute-start | bytes 589832 | tf_op jit(solution)/shard_map/ppermute | solution.py:389
  11.9 26.1 %collective-permute-start.5 = (bf16[6,64,256]{2,1,0:T(8,128)(2,1)S(1)}, bf16[6,64,256]{2,1,0:T(8,128)(2,1)S(1)}, u32[]{:S(2)}, u32[]{:S(2)}) collective-permute-start(bf16[6,64,256]{2,1,0:T(8,128)(2,1)S(1)} %get-tuple-element.33), channel_id=1, source_target_pairs={{0,12},{4,8},{8,4},{12,0},{1,13},{5,9},{9,5},{13,1},{2,14},{6,10},... | collective-permute-start | bytes 589832 | tf_op jit(solution)/shard_map/ppermute | solution.py:390
  14.4 12.8 %collective-permute-start.1 = (bf16[4,64,256]{2,1,0:T(8,128)(2,1)S(1)}, bf16[4,64,256]{2,1,0:T(8,128)(2,1)S(1)}, u32[]{:S(2)}, u32[]{:S(2)}) collective-permute-start(bf16[4,64,256]{2,1,0:T(8,128)(2,1)S(1)} %get-tuple-element.29), channel_id=1, source_target_pairs={{0,12},{4,8},{8,4},{12,0},{1,13},{5,9},{9,5},{13,1},{2,14},{6,10},... | collective-permute-start | bytes 393224 | tf_op jit(solution)/shard_map/ppermute | solution.py:344
  15.7 12.8 %collective-permute-start = (bf16[4,64,256]{2,1,0:T(8,128)(2,1)S(1)}, bf16[4,64,256]{2,1,0:T(8,128)(2,1)S(1)}, u32[]{:S(2)}, u32[]{:S(2)}) collective-permute-start(bf16[4,64,256]{2,1,0:T(8,128)(2,1)S(1)} %get-tuple-element.29), channel_id=1, source_target_pairs={{0,4},{4,0},{8,12},{12,8},{1,5},{5,1},{9,13},{13,9},{2,6},{6,2},{1... | collective-permute-start | bytes 393224 | tf_op jit(solution)/shard_map/ppermute | solution.py:344
  15.7 13.6 %collective-permute-start.8 = (f32[8,256]{1,0:T(8,128)S(1)}, f32[8,256]{1,0:T(8,128)S(1)}, u32[]{:S(2)}, u32[]{:S(2)}) collective-permute-start(f32[8,256]{1,0:T(8,128)S(1)} %get-tuple-element.34.refs_0_.refs_4_), channel_id=1, source_target_pairs={{0,8},{4,12},{8,0},{12,4},{1,9},{5,13},{9,1},{13,5},{2,10},{6,14},... | collective-permute-start | bytes 24584 | tf_op jit(solution)/shard_map/ppermute | solution.py:354
  27.2 5.4 %collective-permute-start.7 = (f32[8,256]{1,0:T(8,128)S(1)}, f32[8,256]{1,0:T(8,128)S(1)}, u32[]{:S(2)}, u32[]{:S(2)}) collective-permute-start(f32[8,256]{1,0:T(8,128)S(1)} %get-tuple-element.34.refs_0_.refs_4_), channel_id=1, source_target_pairs={{0,12},{4,8},{8,4},{12,0},{1,13},{5,9},{9,5},{13,1},{2,14},{6,10},... | collective-permute-start | bytes 24584 | tf_op jit(solution)/shard_map/ppermute | solution.py:344
  29.2 8.8 %collective-permute-start.3 = (bf16[64,128]{1,0:T(8,128)(2,1)S(1)}, bf16[64,128]{1,0:T(8,128)(2,1)S(1)}, u32[]{:S(2)}, u32[]{:S(2)}) collective-permute-start(bf16[64,128]{1,0:T(8,128)(2,1)S(1)} %get-tuple-element.31), channel_id=1, source_target_pairs={{0,3},{1,2},{2,1},{3,0},{4,7},{5,6},{6,5},{7,4},{8,11},{9,10},{10,... | collective-permute-start | bytes 49160 | tf_op jit(solution)/shard_map/ppermute | solution.py:344
  29.3 8.7 %collective-permute-start.2 = (bf16[64,128]{1,0:T(8,128)(2,1)S(1)}, bf16[64,128]{1,0:T(8,128)(2,1)S(1)}, u32[]{:S(2)}, u32[]{:S(2)}) collective-permute-start(bf16[64,128]{1,0:T(8,128)(2,1)S(1)} %get-tuple-element.31), channel_id=1, source_target_pairs={{0,1},{1,0},{2,3},{3,2},{4,5},{5,4},{6,7},{7,6},{8,9},{9,8},{10,11... | collective-permute-start | bytes 49160 | tf_op jit(solution)/shard_map/ppermute | solution.py:344
  32.6 3.7 %collective-permute-start.6 = (f32[8,256]{1,0:T(8,128)S(1)}, f32[8,256]{1,0:T(8,128)S(1)}, u32[]{:S(2)}, u32[]{:S(2)}) collective-permute-start(f32[8,256]{1,0:T(8,128)S(1)} %get-tuple-element.34.refs_0_.refs_4_), channel_id=1, source_target_pairs={{0,4},{4,0},{8,12},{12,8},{1,5},{5,1},{9,13},{13,9},{2,6},{6,2},{1... | collective-permute-start | bytes 24584 | tf_op jit(solution)/shard_map/ppermute | solution.py:344
  38.0 1.3 %copy-start.2 = (bf16[9,256,256]{2,1,0:T(8,128)(2,1)S(1)}, bf16[9,256,256]{2,1,0:T(8,128)(2,1)}, u32[]{:S(2)}) copy-start(bf16[9,256,256]{2,1,0:T(8,128)(2,1)} %param.22) | copy-start | bytes 3538948
  39.3 0.8 copy-start.5
  47.6 6.1 %copy-start.3 = (bf16[9,256,256]{2,1,0:T(8,128)(2,1)S(1)}, bf16[9,256,256]{2,1,0:T(8,128)(2,1)}, u32[]{:S(2)}) copy-start(bf16[9,256,256]{2,1,0:T(8,128)(2,1)} %param.22) | copy-start | bytes 3538948
  47.6 6.1 %copy-start.6 = (bf16[64,256]{1,0:T(8,128)(2,1)S(1)}, bf16[64,256]{1,0:T(8,128)(2,1)}, u32[]{:S(2)}) copy-start(bf16[64,256]{1,0:T(8,128)(2,1)} %refs_6_.7) | copy-start | bytes 98308
  48.5 5.2 %collective-permute-start.10 = (bf16[64,128]{1,0:T(8,128)(2,1)S(1)}, bf16[64,128]{1,0:T(8,128)(2,1)S(1)}, u32[]{:S(2)}, u32[]{:S(2)}) collective-permute-start(bf16[64,128]{1,0:T(8,128)(2,1)S(1)} %get-tuple-element.42), channel_id=1, source_target_pairs={{0,3},{1,2},{2,1},{3,0},{4,7},{5,6},{6,5},{7,4},{8,11},{9,10},{10,... | collective-permute-start | bytes 49160 | tf_op jit(solution)/shard_map/ppermute | solution.py:344
  48.6 5.1 %collective-permute-start.9 = (bf16[64,128]{1,0:T(8,128)(2,1)S(1)}, bf16[64,128]{1,0:T(8,128)(2,1)S(1)}, u32[]{:S(2)}, u32[]{:S(2)}) collective-permute-start(bf16[64,128]{1,0:T(8,128)(2,1)S(1)} %get-tuple-element.42), channel_id=1, source_target_pairs={{0,1},{1,0},{2,3},{3,2},{4,5},{5,4},{6,7},{7,6},{8,9},{9,8},{10,11... | collective-permute-start | bytes 49160 | tf_op jit(solution)/shard_map/ppermute | solution.py:344
  50.2 8.9 %collective-permute-start.13 = (f32[8,256]{1,0:T(8,128)S(1)}, f32[8,256]{1,0:T(8,128)S(1)}, u32[]{:S(2)}, u32[]{:S(2)}) collective-permute-start(f32[8,256]{1,0:T(8,128)S(1)} %get-tuple-element.44.refs_4_), channel_id=1, source_target_pairs={{0,8},{4,12},{8,0},{12,4},{1,9},{5,13},{9,1},{13,5},{2,10},{6,14},... | collective-permute-start | bytes 24584 | tf_op jit(solution)/shard_map/ppermute | solution.py:354
  52.2 6.9 %collective-permute-start.12 = (f32[8,256]{1,0:T(8,128)S(1)}, f32[8,256]{1,0:T(8,128)S(1)}, u32[]{:S(2)}, u32[]{:S(2)}) collective-permute-start(f32[8,256]{1,0:T(8,128)S(1)} %get-tuple-element.44.refs_4_), channel_id=1, source_target_pairs={{0,12},{4,8},{8,4},{12,0},{1,13},{5,9},{9,5},{13,1},{2,14},{6,10},... | collective-permute-start | bytes 24584 | tf_op jit(solution)/shard_map/ppermute | solution.py:344
  53.3 5.8 %collective-permute-start.11 = (f32[8,256]{1,0:T(8,128)S(1)}, f32[8,256]{1,0:T(8,128)S(1)}, u32[]{:S(2)}, u32[]{:S(2)}) collective-permute-start(f32[8,256]{1,0:T(8,128)S(1)} %get-tuple-element.44.refs_4_), channel_id=1, source_target_pairs={{0,4},{4,0},{8,12},{12,8},{1,5},{5,1},{9,13},{13,9},{2,6},{6,2},{1... | collective-permute-start | bytes 24584 | tf_op jit(solution)/shard_map/ppermute | solution.py:344
  60.0 5.2 %collective-permute-start.15 = (bf16[64,128]{1,0:T(8,128)(2,1)S(1)}, bf16[64,128]{1,0:T(8,128)(2,1)S(1)}, u32[]{:S(2)}, u32[]{:S(2)}) collective-permute-start(bf16[64,128]{1,0:T(8,128)(2,1)S(1)} %get-tuple-element.47), channel_id=1, source_target_pairs={{0,3},{1,2},{2,1},{3,0},{4,7},{5,6},{6,5},{7,4},{8,11},{9,10},{10,... | collective-permute-start | bytes 49160 | tf_op jit(solution)/shard_map/ppermute | solution.py:344
  60.1 5.1 %collective-permute-start.14 = (bf16[64,128]{1,0:T(8,128)(2,1)S(1)}, bf16[64,128]{1,0:T(8,128)(2,1)S(1)}, u32[]{:S(2)}, u32[]{:S(2)}) collective-permute-start(bf16[64,128]{1,0:T(8,128)(2,1)S(1)} %get-tuple-element.47), channel_id=1, source_target_pairs={{0,1},{1,0},{2,3},{3,2},{4,5},{5,4},{6,7},{7,6},{8,9},{9,8},{10,11... | collective-permute-start | bytes 49160 | tf_op jit(solution)/shard_map/ppermute | solution.py:344
  60.8 8.5 %collective-permute-start.18 = (f32[8,256]{1,0:T(8,128)S(1)}, f32[8,256]{1,0:T(8,128)S(1)}, u32[]{:S(2)}, u32[]{:S(2)}) collective-permute-start(f32[8,256]{1,0:T(8,128)S(1)} %get-tuple-element.49.refs_4_), channel_id=1, source_target_pairs={{0,8},{4,12},{8,0},{12,4},{1,9},{5,13},{9,1},{13,5},{2,10},{6,14},... | collective-permute-start | bytes 24584 | tf_op jit(solution)/shard_map/ppermute | solution.py:354
  63.6 5.7 %collective-permute-start.17 = (f32[8,256]{1,0:T(8,128)S(1)}, f32[8,256]{1,0:T(8,128)S(1)}, u32[]{:S(2)}, u32[]{:S(2)}) collective-permute-start(f32[8,256]{1,0:T(8,128)S(1)} %get-tuple-element.49.refs_4_), channel_id=1, source_target_pairs={{0,12},{4,8},{8,4},{12,0},{1,13},{5,9},{9,5},{13,1},{2,14},{6,10},... | collective-permute-start | bytes 24584 | tf_op jit(solution)/shard_map/ppermute | solution.py:344
  65.2 4.2 %collective-permute-start.16 = (f32[8,256]{1,0:T(8,128)S(1)}, f32[8,256]{1,0:T(8,128)S(1)}, u32[]{:S(2)}, u32[]{:S(2)}) collective-permute-start(f32[8,256]{1,0:T(8,128)S(1)} %get-tuple-element.49.refs_4_), channel_id=1, source_target_pairs={{0,4},{4,0},{8,12},{12,8},{1,5},{5,1},{9,13},{13,9},{2,6},{6,2},{1... | collective-permute-start | bytes 24584 | tf_op jit(solution)/shard_map/ppermute | solution.py:344
  70.2 5.6 %collective-permute-start.20 = (bf16[64,128]{1,0:T(8,128)(2,1)S(1)}, bf16[64,128]{1,0:T(8,128)(2,1)S(1)}, u32[]{:S(2)}, u32[]{:S(2)}) collective-permute-start(bf16[64,128]{1,0:T(8,128)(2,1)S(1)} %get-tuple-element.52), channel_id=1, source_target_pairs={{0,3},{1,2},{2,1},{3,0},{4,7},{5,6},{6,5},{7,4},{8,11},{9,10},{10,... | collective-permute-start | bytes 49160 | tf_op jit(solution)/shard_map/ppermute | solution.py:344
  70.3 5.5 %collective-permute-start.19 = (bf16[64,128]{1,0:T(8,128)(2,1)S(1)}, bf16[64,128]{1,0:T(8,128)(2,1)S(1)}, u32[]{:S(2)}, u32[]{:S(2)}) collective-permute-start(bf16[64,128]{1,0:T(8,128)(2,1)S(1)} %get-tuple-element.52), channel_id=1, source_target_pairs={{0,1},{1,0},{2,3},{3,2},{4,5},{5,4},{6,7},{7,6},{8,9},{9,8},{10,11... | collective-permute-start | bytes 49160 | tf_op jit(solution)/shard_map/ppermute | solution.py:344
  71.6 6.7 %collective-permute-start.23 = (f32[8,256]{1,0:T(8,128)S(1)}, f32[8,256]{1,0:T(8,128)S(1)}, u32[]{:S(2)}, u32[]{:S(2)}) collective-permute-start(f32[8,256]{1,0:T(8,128)S(1)} %get-tuple-element.53.refs_4_), channel_id=1, source_target_pairs={{0,8},{4,12},{8,0},{12,4},{1,9},{5,13},{9,1},{13,5},{2,10},{6,14},... | collective-permute-start | bytes 24584 | tf_op jit(solution)/shard_map/ppermute | solution.py:354
  74.7 5.4 %collective-permute-start.22 = (f32[8,256]{1,0:T(8,128)S(1)}, f32[8,256]{1,0:T(8,128)S(1)}, u32[]{:S(2)}, u32[]{:S(2)}) collective-permute-start(f32[8,256]{1,0:T(8,128)S(1)} %get-tuple-element.53.refs_4_), channel_id=1, source_target_pairs={{0,12},{4,8},{8,4},{12,0},{1,13},{5,9},{9,5},{13,1},{2,14},{6,10},... | collective-permute-start | bytes 24584 | tf_op jit(solution)/shard_map/ppermute | solution.py:344
  75.8 4.4 %collective-permute-start.21 = (f32[8,256]{1,0:T(8,128)S(1)}, f32[8,256]{1,0:T(8,128)S(1)}, u32[]{:S(2)}, u32[]{:S(2)}) collective-permute-start(f32[8,256]{1,0:T(8,128)S(1)} %get-tuple-element.53.refs_4_), channel_id=1, source_target_pairs={{0,4},{4,0},{8,12},{12,8},{1,5},{5,1},{9,13},{13,9},{2,6},{6,2},{1... | collective-permute-start | bytes 24584 | tf_op jit(solution)/shard_map/ppermute | solution.py:344
  (6 other events, 4.1 us)

commit v2 on v1

v2 whole, which is shorter than its diff:
```python
import functools
import math

import jax
import jax.numpy as jnp
from jax import lax
from jax.experimental import pallas as pl
from jax.experimental.pallas import tpu as pltpu
from jax.sharding import PartitionSpec as P

F32 = jnp.float32
BF16 = jnp.bfloat16
REACH = 2
HALO = 4
LANES = 128
HALF = 64
CHUNK = 4

noise_levels = (1.0, 0.6, 0.3)
obs_precision = 4.0
step_factor = 0.1


def sub_steps():
    steps = []
    for section in range(2):
        upper, lower = noise_levels[section], noise_levels[section + 1]
        spread = upper * upper - lower * lower
        steps.append((upper, spread, math.sqrt(spread)))
        factor = step_factor * lower * lower
        steps.append((lower, factor, math.sqrt(2.0 * factor)))
    return steps


STEPS = sub_steps()


def shrink(level):
    return 1.0 / math.sqrt(1.0 + level * level)


def vmem_call(kernel, outs, *args, scratch=(), scalars=0, hbm_in=0, hbm_out=False, flops=0):
    args = list(args)
    for i in range(scalars, len(args)):
        place = pltpu.HBM if i < scalars + hbm_in else pltpu.VMEM
        args[i] = pltpu.with_memory_space_constraint(args[i], place)
    smem = pl.BlockSpec(memory_space=pltpu.SMEM)
    vmem, hbm = pl.BlockSpec(memory_space=pltpu.VMEM), pl.BlockSpec(memory_space=pltpu.HBM)
    out_type = jax.ShapeDtypeStruct if hbm_out else pltpu.VMEM
    return pl.pallas_call(
        kernel,
        out_shape=[out_type(shape, dtype) for shape, dtype in outs],
        in_specs=[smem] * scalars + [hbm] * hbm_in + [vmem] * (len(args) - scalars - hbm_in),
        out_specs=[hbm if hbm_out else vmem] * len(outs),
        scratch_shapes=list(scratch),
        cost_estimate=pl.CostEstimate(flops=flops, bytes_accessed=0, transcendentals=0),
        compiler_params=pltpu.CompilerParams(vmem_limit_bytes=48 * 2**20),
    )(*args)


def dot(a, b, ca=1, cb=0):
    return lax.dot_general(a, b, (((ca,), (cb,)), ((), ())), preferred_element_type=F32)


def pieces(x, count):
    out = []
    for _ in range(count):
        part = x.astype(BF16)
        out.append(part)
        x = x - part.astype(F32)
    return out


def iota(shape, dim):
    return lax.broadcasted_iota(jnp.int32, shape, dim).astype(F32)


def silu_norm(values, gain):
    power = jnp.mean(values * values, axis=1, keepdims=True)
    half = values * (0.5 * lax.rsqrt(power + 1e-06)) * gain
    return half + half * jnp.tanh(half)


def is_even(axis):
    return lax.rem(lax.axis_index(axis), 2) == 0


def stage_kernel(*refs, n_args, slots):
    live, sources, staged = refs[0], refs[1 : 1 + n_args], refs[1 + n_args : 1 + 2 * n_args]
    msg, entry_msg, sems = refs[1 + 2 * n_args :]
    copies = [
        pltpu.make_async_copy(source, target, sems.at[i])
        for i, (source, target) in enumerate(zip(sources, staged))
    ]
    for copy in copies:
        copy.start()
    prior, _, cell, owner, slot, weight, station = staged[:7]
    _, latb, lond = prior.shape
    copies[0].wait()
    for r in range(latb):
        msg[r] = (prior[:, r, :] * shrink(STEPS[0][0])).astype(BF16)
    for copy in copies[2:7]:
        copy.wait()
    count = cell.shape[1]
    cells = cell[...]
    lon = cells % lond
    row = (cells // lond) % latb
    variable = cells // (lond * latb)
    rv = row * prior.shape[0] + variable
    key = owner[...] * slots + slot[...]
    alive = lax.broadcasted_iota(jnp.int32, (1, count), 1) < live[0]
    weights = jnp.where(alive, weight[...], 0.0)
    mine = lax.axis_index("band") * slots + lax.broadcasted_iota(jnp.int32, (1, count), 1)
    entry_msg[0:1] = key.astype(F32)
    entry_msg[1:2] = rv.astype(F32)
    entry_msg[2:3] = lon.astype(F32)
    entry_msg[3:4] = weights
    entry_msg[4:5] = station[...]
    entry_msg[5:6] = mine.astype(F32)
    entry_msg[6:8] = jnp.zeros((2, count), F32)
    columns = jnp.transpose(entry_msg[...])
    rv_col, lon_col = columns[:, 1:2], columns[:, 2:3]
    one_hot = jnp.where(rv_col == iota((count, latb * prior.shape[0]), 1), 1.0, 0.0).astype(BF16)
    current = jnp.concatenate([prior[:, r, :] for r in range(latb)], axis=0)
    picked = sum(dot(one_hot, part) for part in pieces(current, 2))
    at = jnp.sum(jnp.where(lon_col == iota((count, lond), 1), picked, 0.0), axis=1, keepdims=True)
    eye = iota((count, count), 0) == iota((count, count), 1)
    entry_msg[6:7] = weights * jnp.sum(jnp.where(eye, at, 0.0), axis=0, keepdims=True)
    copies[1].wait()
    for copy in copies[7:]:
        copy.wait()


def edges_into(edge_ref, state, rows, level):
    lane = lax.broadcasted_iota(jnp.int32, (1, LANES), 1)
    width = state.shape[2]
    edge = jnp.zeros(edge_ref.shape, F32)
    for r in range(rows):
        slab = state[r]
        edge = jnp.where(lane == r, slab[:, 0:1], edge)
        edge = jnp.where(lane == HALF + r, slab[:, width - 1 : width], edge)
    edge_ref[...] = (edge * shrink(level)).astype(BF16)


def extend_kernel(*refs, latb):
    prior, halo_a, halo_b = refs[:3]
    state, edge = refs[-2:]
    grow = 1.0 / shrink(STEPS[0][0])
    for r in range(latb):
        state[HALO + r] = prior[:, r, :]

    @pl.when(is_even("band"))
    def _():
        for r in range(latb):
            state[r] = halo_b[r].astype(F32) * grow
            state[HALO + latb + r] = halo_a[r].astype(F32) * grow

    @pl.when(jnp.logical_not(is_even("band")))
    def _():
        for r in range(latb):
            state[r] = halo_a[r].astype(F32) * grow
            state[HALO + latb + r] = halo_b[r].astype(F32) * grow

    edges_into(edge, state, 2 * HALO + latb, STEPS[0][0])


def noise_kernel(noise, after, noise_a, noise_b):
    latb = noise.shape[2]
    up = [(k, r) for k in range(HALO - 1) for r in range(1 + k, latb)]
    down = [(k, r) for k in range(HALO - 1) for r in range(0, latb - 1 - k)]

    @pl.when(is_even("band"))
    def _():
        for i in range(len(up)):
            noise_a[i] = noise[up[i][0], :, up[i][1], :].astype(BF16)
            noise_b[i] = noise[down[i][0], :, down[i][1], :].astype(BF16)

    @pl.when(jnp.logical_not(is_even("band")))
    def _():
        for i in range(len(up)):
            noise_a[i] = noise[down[i][0], :, down[i][1], :].astype(BF16)
            noise_b[i] = noise[up[i][0], :, up[i][1], :].astype(BF16)


def wide(column):
    return jnp.broadcast_to(column, (column.shape[0], LANES))


def one_hot(position, shape, dim):
    return jnp.where(position == iota(shape, dim), 1.0, 0.0).astype(BF16)


def own_kernel(msg, cols, pick, spread, *, variables, latb, lond):
    count = msg.shape[1]
    high = latb * variables
    col = jnp.transpose(msg[...])
    cols[0] = wide(col[:, 0:1])
    cols[1] = wide(col[:, 3:4])
    cols[2] = wide(col[:, 2:3])
    cols[3] = wide(col[:, 1:2] * lond + col[:, 2:3])
    cols[4] = wide(col[:, 5:6])
    pick[...] = one_hot(col[:, 1:2], (count, high), 1)
    spread[...] = one_hot(msg[1:2], (high, count), 0)


def tables_kernel(*refs, n_msgs, variables, latb):
    own_cols, msgs = refs[0], refs[1 : 1 + n_msgs]
    keys, near, seen, spread = refs[1 + n_msgs :]
    count = msgs[0].shape[1]
    even = is_even("band")
    low = jnp.where(even, msgs[2][...], msgs[1][...])
    up = jnp.where(even, msgs[1][...], msgs[2][...])
    for i in range(n_msgs):
        keys[:, i * count : (i + 1) * count] = msgs[i][...]
    for j, msg in enumerate((low, up)):
        col = jnp.transpose(msg)
        for i, source in enumerate((0, 3, 2)):
            near[i, j * count : (j + 1) * count] = wide(col[:, source : source + 1])
        spread[j] = one_hot(msg[1:2], (latb * variables, count), 0)
    for j in range(3):
        block = slice((j - 1) * count, j * count)
        key = near[0, block] if j else own_cols[0]
        acc = jnp.zeros((count, LANES), F32)
        for i in range(n_msgs):
            for part in range(count // LANES):
                at = slice(part * LANES, (part + 1) * LANES)
                acc = acc + jnp.where(key == msgs[i][5:6, at], msgs[i][4:5, at], 0.0)
        seen[j * count : (j + 1) * count] = wide(jnp.sum(acc, axis=1, keepdims=True))


def network_kernel(*refs, step, rows, latb, gather):
    state, edge_a, edge_b, noise, lift, conv, head, gain_1, gain_2 = refs[:9]
    if gather:
        pick, cols, target, at_entries, firsts, lifteds, sums, parts = refs[9:]
    else:
        target, firsts, lifteds, sums = refs[9:]
    level, drift, kick = STEPS[step]
    scale = shrink(level)
    out_halo = (rows - latb) // 2
    width = state.shape[2]
    channels = lift.shape[1]
    band = lax.axis_index("band")
    north = band == 0
    south = band == lax.axis_size("band") - 1

    lane = lax.broadcasted_iota(jnp.int32, (1, LANES), 1)
    even = is_even("wt")
    from_a, from_b = edge_a[...].astype(F32), edge_b[...].astype(F32)
    right = jnp.where(even, from_a, from_b)
    left = jnp.where(even, from_b, from_a)
    edge = pltpu.roll(jnp.where(lane < HALF, right, left), HALF, 1).astype(BF16)
    edge = silu_norm(dot(edge, lift[...], 0, 0), gain_1[...])

    sub = lax.broadcasted_iota(jnp.int32, (width, 1), 0)
    def first_row(r):
        lifted = dot((state[r] * scale).astype(BF16), lift[...], 0, 0)
        if 1 <= r <= rows:
            lifteds[(r - 1) * width : r * width] = lifted
        first = silu_norm(lifted, gain_1[...])
        before, after = edge[r : r + 1], edge[HALF + r : HALF + r + 1]
        outside = None
        if r < out_halo + 1:
            outside = north
        elif r >= out_halo + 1 + latb:
            outside = south
        if outside is not None:
            first = jnp.where(outside, 0.0, first)
            before = jnp.where(outside, 0.0, before)
            after = jnp.where(outside, 0.0, after)
        here = slice(r * width, (r + 1) * width)
        firsts[here, 0:channels] = jnp.where(sub == 0, before, pltpu.roll(first, 1, 0)).astype(BF16)
        firsts[here, channels : 2 * channels] = first.astype(BF16)
        firsts[here, 2 * channels : 3 * channels] = jnp.where(
            sub == width - 1, after, pltpu.roll(first, width - 1, 0)
        ).astype(BF16)

    def mix(start, stop):
        total = lifteds[start * width : stop * width]
        for p in range(3):
            total = total + dot(
                firsts[(start + p) * width : (stop + p) * width],
                conv[3 * channels * p : 3 * channels * (p + 1)],
            )
        sums[start * width : stop * width] = total

    def finish(start, stop):
        for i in range(start, stop):
            second = silu_norm(sums[i * width : (i + 1) * width], gain_2[...]).astype(BF16)
            moved = state[i + 1] + (drift / level) * dot(head[...], second, 1, 1)
            if out_halo <= i < out_halo + latb:
                moved = moved + kick * noise[step, :, i - out_halo, :]
            target[i] = moved

    bounds = [0]
    while bounds[-1] < rows:
        bounds.append(min(rows, bounds[-1] + CHUNK))
    made = 0
    for j, (start, stop) in enumerate(zip(bounds, bounds[1:])):
        for r in range(made, stop + 2):
            first_row(r)
        made = stop + 2
        mix(start, stop)
        if j + 2 < len(bounds):
            for r in range(made, bounds[j + 2] + 2):
                first_row(r)
            made = bounds[j + 2] + 2
        if j:
            finish(bounds[j - 1], start)
    finish(bounds[-2], rows)
    if gather:
        variables = state.shape[1]
        for r in range(latb):
            for j, part in enumerate(pieces(target[out_halo + r], 2)):
                parts[r * variables : (r + 1) * variables, j * width : (j + 1) * width] = part
        picked = dot(pick[...], parts[...])
        picked = picked[:, 0:width] + picked[:, width:]
        count = pick.shape[0]
        lon = jnp.concatenate([cols[2]] * (width // LANES), axis=1)
        at = jnp.sum(jnp.where(lon == iota((count, width), 1), picked, 0.0), axis=1, keepdims=True)
        at_entries[...] = jnp.broadcast_to(at, (count, LANES))


def matching(key, keys, values):
    count = values[0].shape[1]
    acc = jnp.zeros(key.shape, F32)
    for i, row in enumerate(values):
        for part in range(count // LANES):
            at = slice(part * LANES, (part + 1) * LANES)
            known = keys[0:1, i * count + part * LANES : i * count + (part + 1) * LANES]
            acc = acc + jnp.where(key == known, row[:, at], 0.0)
    return jnp.sum(acc, axis=1, keepdims=True)


def update_kernel(*refs, step, n_msgs, rows, latb, value_row):
    target, keys, cols, spread, near, seen, near_spread = refs[:7]
    values = [ref[value_row : value_row + 1] for ref in refs[7 : 7 + n_msgs]]
    rest = refs[7 + n_msgs :]
    last = step == len(STEPS) - 1
    count = values[0].shape[1]
    variables, width = target.shape[1], target.shape[2]
    out_halo = (rows - latb) // 2
    strength = obs_precision * STEPS[step][1]

    def columns_of(j):
        if j == 0:
            return cols[0], cols[1], cols[2]
        block = slice((j - 1) * count, j * count)
        return near[0, block], near[1, block], near[2, block]

    def column(j):
        key, weight, _ = columns_of(j)
        found = matching(key, keys, values)
        return strength * weight * (seen[j * count : (j + 1) * count] - found)

    def spread_rows(j, column_j, rows_from, rows_to):
        lon = jnp.concatenate([columns_of(j)[2]] * (width // LANES), axis=1)
        tall = jnp.concatenate([column_j] * (width // LANES), axis=1)
        value = jnp.where(lon == iota((count, width), 1), tall, 0.0)
        parts = jnp.concatenate(pieces(value, 2), axis=1)
        here = slice(rows_from * variables, rows_to * variables)
        both = dot(near_spread[j - 1, here] if j else spread[here], parts)
        return both[:, 0:width] + both[:, width:]

    mine = column(0)
    own = spread_rows(0, mine, 0, latb)
    if last:
        state_out, innov_out, state, innov, sems = rest
        for r in range(latb):
            state[:, r, :] = target[out_halo + r] + own[r * variables : (r + 1) * variables]
        state_copy = pltpu.make_async_copy(state, state_out, sems.at[0])
        state_copy.start()
        found = matching(cols[4], keys, values)
        eye = iota((count, count), 0) == iota((count, count), 1)
        innov[...] = keys[4:5, 0:count] - jnp.sum(jnp.where(eye, found, 0.0), axis=0, keepdims=True)
        innov_copy = pltpu.make_async_copy(innov, innov_out, sems.at[1])
        innov_copy.start()
        state_copy.wait()
        innov_copy.wait()
        return
    at_entries, halo_a, halo_b, state, edge, value = rest
    row_cell = keys[1:2, 0:count] * width + keys[2:3, 0:count]
    cell = jnp.concatenate([cols[3]] * (count // LANES), axis=1)
    tall = jnp.concatenate([mine] * (count // LANES), axis=1)
    before = jnp.concatenate([at_entries[...]] * (count // LANES), axis=1)
    eye = iota((count, count), 0) == iota((count, count), 1)
    total = jnp.where(cell == row_cell, tall, 0.0) + jnp.where(eye, before, 0.0)
    value[...] = jnp.broadcast_to(
        keys[3:4, 0:count] * jnp.sum(total, axis=0, keepdims=True), value.shape
    )
    for r in range(latb):
        state[out_halo + r] = target[out_halo + r] + own[r * variables : (r + 1) * variables]
    if out_halo:
        low = spread_rows(1, column(1), latb - out_halo, latb)
        up = spread_rows(2, column(2), 0, out_halo)
        base = sum(HALO - 1 - k for k in range(step))
        even = is_even("band")
        kick = STEPS[step][2]
        for r in range(out_halo):
            here = slice(r * variables, (r + 1) * variables)
            from_a, from_b = halo_a[base + r].astype(F32), halo_b[base + r].astype(F32)
            state[r] = target[r] + low[here] + kick * jnp.where(even, from_b, from_a)
            state[out_halo + latb + r] = (
                target[out_halo + latb + r] + up[here] + kick * jnp.where(even, from_a, from_b)
            )
    edges_into(edge, state, rows, STEPS[step + 1][0])


def swaps(count):
    first = [(i, i ^ 1) for i in range(count)]
    other = [(i, (i - 1) % count if i % 2 == 0 else (i + 1) % count) for i in range(count)]
    return first, other


def from_neighbours(block, axis):
    return [lax.ppermute(block, axis, route) for route in swaps(lax.axis_size(axis))]


def from_bands(block):
    count = lax.axis_size("band")
    found = [block] + from_neighbours(block, "band")
    reach = min(2 * REACH + 1, count)
    far = sorted({d % count for d in range(-reach, reach + 1)} - {0, 1, count - 1})
    for distance in far:
        route = [(i, (i + distance) % count) for i in range(count)]
        found.append(lax.ppermute(block, "band", route))
    return found


def per_device(
    prior_state, langevin_noise, station_values, entry_cell, entry_owner, entry_slot,
    entry_weight, live_counts, lift_weight, conv_weight, head_weight, first_gain, second_gain,
):
    variables, latb, lond = prior_state.shape
    count = entry_cell.shape[0]
    slots = station_values.shape[0]
    channels = lift_weight.shape[1]
    taps = conv_weight.reshape(-1, channels)
    gain_1, gain_2 = first_gain.reshape(1, -1), second_gain.reshape(1, -1)

    def row(a):
        return a.reshape(1, -1)

    taken = [
        prior_state, langevin_noise, row(entry_cell), row(entry_owner), row(entry_slot),
        row(entry_weight), row(station_values), taps, lift_weight, head_weight.T, gain_1, gain_2,
    ]
    *staged, msg, entry_msg = vmem_call(
        functools.partial(stage_kernel, n_args=len(taken), slots=slots),
        [(a.shape, a.dtype) for a in taken]
        + [((latb, variables, lond), BF16), ((8, count), F32)],
        live_counts, *taken,
        scalars=1,
        hbm_in=len(taken),
        scratch=[pltpu.SemaphoreType.DMA((len(taken),))],
    )
    prior_state, langevin_noise = staged[:2]
    taps, lift_weight, head_weight, gain_1, gain_2 = staged[7:]
    route_a, route_b = swaps(lax.axis_size("band"))
    route_b = [pair for pair in route_b if abs(pair[0] - pair[1]) == 1]
    halos = [lax.ppermute(msg, "band", route) for route in (route_a, route_b)]
    msgs = from_bands(entry_msg)
    n_msgs = len(msgs)
    high = latb * variables
    cols, pick, spread = vmem_call(
        functools.partial(own_kernel, variables=variables, latb=latb, lond=lond),
        [((5, count, LANES), F32), ((count, high), BF16), ((high, count), BF16)],
        entry_msg,
    )
    state, edge = vmem_call(
        functools.partial(extend_kernel, latb=latb),
        [((2 * HALO + latb, variables, lond), F32), ((variables, LANES), BF16)],
        prior_state, *halos, *msgs,
    )
    edges = from_neighbours(edge, "wt")
    slabs = ((sum(HALO - 1 - k for k in range(HALO - 1)), variables, lond), BF16)
    noise_a, noise_b = vmem_call(noise_kernel, [slabs, slabs], langevin_noise, edge)
    noise_halos = [lax.ppermute(noise_a, "band", route_a), lax.ppermute(noise_b, "band", route_b)]
    keys, near, seen, near_spread = vmem_call(
        functools.partial(tables_kernel, n_msgs=n_msgs, variables=variables, latb=latb),
        [
            ((8, n_msgs * count), F32),
            ((3, 2 * count, LANES), F32),
            ((3 * count, LANES), F32),
            ((2, high, count), BF16),
        ],
        cols, *msgs,
    )
    tables = (keys, cols, spread, near, seen, near_spread)
    values, value_row = msgs, 6
    for step in range(len(STEPS)):
        last = step == len(STEPS) - 1
        rows = latb + 2 * (HALO - 1 - step)
        network_out = [((rows, variables, lond), F32)]
        network_in = [
            state, *edges, langevin_noise,
            lift_weight, taps, head_weight, gain_1, gain_2,
        ]
        scratch = [
            pltpu.VMEM(((rows + 2) * lond, 3 * channels), BF16),
            pltpu.VMEM((rows * lond, channels), F32),
            pltpu.VMEM((rows * lond, channels), F32),
        ]
        if not last:
            network_out.append(((count, LANES), F32))
            network_in += [pick, cols]
            scratch.append(pltpu.VMEM((high, 2 * lond), BF16))
        found = vmem_call(
            functools.partial(network_kernel, step=step, rows=rows, latb=latb, gather=not last),
            network_out,
            *network_in,
            scratch=scratch,
            flops=4 * rows * lond * taps.size,
        )
        update = functools.partial(
            update_kernel, step=step, n_msgs=n_msgs, rows=rows, latb=latb, value_row=value_row
        )
        if last:
            outs = [((variables, latb, lond), F32), ((1, count), F32)]
            state, innov = vmem_call(
                update, outs, found[0], *tables, *values, hbm_out=True,
                scratch=[pltpu.VMEM(*out) for out in outs] + [pltpu.SemaphoreType.DMA((2,))],
            )
            return state, innov.reshape(-1)
        state, edge, value = vmem_call(
            update,
            [((rows, variables, lond), F32), ((variables, LANES), BF16), ((8, count), F32)],
            found[0], *tables, *values, found[1], *noise_halos,
        )
        values, value_row = from_bands(value), 0
        edges = from_neighbours(edge, "wt")


def solution(mesh):
    split = P(("groups", "band", "wt"))
    in_specs = (
        P("groups", "band", "wt"),
        P(None, "groups", "band", "wt"),
        split, split, split, split, split, split,
        P(), P(), P(), P(), P(),
    )
    out_specs = (P("groups", "band", "wt"), split)
    return jax.shard_map(
        per_device, mesh=mesh, in_specs=in_specs, out_specs=out_specs, check_vma=False
    )
```

time: 82.3 us -> 61.9 us (0.75)
  local copies, waits for them, and re-layouts: 11.1 us -> 0 us
  waiting for transfers between devices: 13.7 us -> 3.78 us
  starting transfers between devices: 30.1 us -> 31.2 us
    unnamed x31 -> x0, local copies, waits for them, and re-layouts: 11.1 us -> none
    ppermute x18 -> x16, waiting for transfers between devices: 13.6 us -> 2.69 us  [from_neighbours(): lax.ppermute(block, axis, route)]
    ppermute x2 -> x4, starting transfers between devices: 5.56 us -> 8.53 us  [the longest x2 6.57 us: per_device(): halos = [lax.ppermute(msg, 'band', route) for route in (route_a, route_b)]]
    ppermute x4, starting transfers between devices: 11 us -> 8.52 us  [from_bands(): found.append(lax.ppermute(block, 'band', route))]
    ppermute x4, waiting for transfers between devices: 0.04 us -> 1.08 us  [from_bands(): found.append(lax.ppermute(block, 'band', route))]
    ppermute x18 -> x16, starting transfers between devices: 13.6 us -> 14.1 us  [from_neighbours(): lax.ppermute(block, axis, route)]
    pallas_call x11 -> x13, Pallas kernels: 25.4 us -> 25.1 us  [vmem_call(): pl.pallas_call(kernel, out_shape=[out_type(shape, dtype) for shape, dtype...]
  transfers between devices with their start and end apart: 24 -> 24, of which waited for: 4 -> 5; matrix products, arithmetic and copies ran while one was open for 1% -> 0% of each run, Pallas kernels for 18% -> 30%
where the time goes in v2:
time: 61.9 us; the launch traced here: 61.7 us
  starting transfers between devices  31.2 us (50%)
  Pallas kernels  25.1 us (41%)
  waiting for transfers between devices  3.78 us (6%)
  between operations  1.67 us (3%)
    pallas_call x13, Pallas kernels, vmem_call(): pl.pallas_call(kernel, out_shape=[out_type(shape, dtype) for shape, dtype...  25.1 us
    ppermute x16, starting transfers between devices, from_neighbours(): lax.ppermute(block, axis, route)  14.1 us
    ppermute x4, starting transfers between devices, from_bands(): found.append(lax.ppermute(block, 'band', route))  8.52 us
    ppermute x2, starting transfers between devices, per_device(): halos = [lax.ppermute(msg, 'band', route) for route in (route_a, route_b)]  6.57 us
    ppermute x16, waiting for transfers between devices, from_neighbours(): lax.ppermute(block, axis, route)  2.69 us
  transfers between devices with their start and end apart: 24, of which 5 were waited for; matrix products, arithmetic and copies ran while one was open for 0% of the time, Pallas kernels for 30%

profile of v2, /device:TPU:0, one launch (start us, length us, event | category | flops | bytes accessed | tf_op | source)
XLA Modules:
  0.0 61.7 jit_solution(14934726420794931436)
XLA Ops:
  1.3 2.6 %shard_map.140 = (f32[64,4,256]{2,1,0:T(4,128)S(1)}, f32[4,64,4,256]{3,2,1,0:T(4,128)S(1)}, s32[1,256]{1,0:T(1,128)}, s32[1,256]{1,0:T(1,128)}, s32[1,256]{1,0:T...) custom-call(s32[1]{0:T(128)S(6)} %copy.15.refs_0_, ...), custom_call_target="tpu_custom_call" | custom-call | tf_op jit(solution)/shard_map/pallas_call | solution.py:50
  3.9 0.7 %collective-permute-start.1 = (bf16[4,64,256]{2,1,0:T(8,128)(2,1)S(1)}, bf16[4,64,256]{2,1,0:T(8,128)(2,1)S(1)}, u32[]{:S(2)}, u32[]{:S(2)}) collective-permute-start(bf16[4,64,256]{2,1,0:T(8,128)(2,1)S(1)} %get-tuple-element.40), channel_id=1, source_target_pairs={{4,8},{8,4},{5,9},{9,5},{6,10},{10,6},{7,11},{11,7},{20,24},{24,20... | collective-permute-start | bytes 393224 | tf_op jit(solution)/shard_map/ppermute | solution.py:460
  4.6 5.9 %collective-permute-start = (bf16[4,64,256]{2,1,0:T(8,128)(2,1)S(1)}, bf16[4,64,256]{2,1,0:T(8,128)(2,1)S(1)}, u32[]{:S(2)}, u32[]{:S(2)}) collective-permute-start(bf16[4,64,256]{2,1,0:T(8,128)(2,1)S(1)} %get-tuple-element.40), channel_id=1, source_target_pairs={{0,4},{4,0},{8,12},{12,8},{1,5},{5,1},{9,13},{13,9},{2,6},{6,2},{1... | collective-permute-start | bytes 393224 | tf_op jit(solution)/shard_map/ppermute | solution.py:460
  10.5 2.4 %collective-permute-start.3 = (f32[8,256]{1,0:T(8,128)S(1)}, f32[8,256]{1,0:T(8,128)S(1)}, u32[]{:S(2)}, u32[]{:S(2)}) collective-permute-start(f32[8,256]{1,0:T(8,128)S(1)} %get-tuple-element.41.refs_3_.msg.refs_1_.refs_7_), channel_id=1, source_target_pairs={{0,12},{4,8},{8,4},{12,0},{1,13},{5,9},{9,5},{13,1},{2,14},{6,10},... | collective-permute-start | bytes 24584 | tf_op jit(solution)/shard_map/ppermute | solution.py:415
  12.9 1.0 %collective-permute-start.2 = (f32[8,256]{1,0:T(8,128)S(1)}, f32[8,256]{1,0:T(8,128)S(1)}, u32[]{:S(2)}, u32[]{:S(2)}) collective-permute-start(f32[8,256]{1,0:T(8,128)S(1)} %get-tuple-element.41.refs_3_.msg.refs_1_.refs_7_), channel_id=1, source_target_pairs={{0,4},{4,0},{8,12},{12,8},{1,5},{5,1},{9,13},{13,9},{2,6},{6,2},{1... | collective-permute-start | bytes 24584 | tf_op jit(solution)/shard_map/ppermute | solution.py:415
  14.0 1.1 %collective-permute-done.4.refs_6_.refs_4_.refs_10_ = f32[8,256]{1,0:T(8,128)S(1)} collective-permute-done((f32[8,256]{1,0:T(8,128)S(1)}, f32[8,256]{1,0:T(8,128)S(1)}, u32[]{:S(2)}, u32[]{:S(2)}) %collective-permute-start.4) | collective-permute-done | bytes 8224 | tf_op jit(solution)/shard_map/ppermute | solution.py:425
  15.0 0.9 %collective-permute-done.3.refs_5_.refs_3_.refs_9_ = f32[8,256]{1,0:T(8,128)S(1)} collective-permute-done((f32[8,256]{1,0:T(8,128)S(1)}, f32[8,256]{1,0:T(8,128)S(1)}, u32[]{:S(2)}, u32[]{:S(2)}) %collective-permute-start.3) | collective-permute-done | bytes 8224 | tf_op jit(solution)/shard_map/ppermute | solution.py:415
  15.9 0.6 %collective-permute-done.2.refs_4_.refs_2_.refs_8_ = f32[8,256]{1,0:T(8,128)S(1)} collective-permute-done((f32[8,256]{1,0:T(8,128)S(1)}, f32[8,256]{1,0:T(8,128)S(1)}, u32[]{:S(2)}, u32[]{:S(2)}) %collective-permute-start.2) | collective-permute-done | bytes 8224 | tf_op jit(solution)/shard_map/ppermute | solution.py:415
  17.1 1.6 %collective-permute-start.5 = (bf16[64,128]{1,0:T(8,128)(2,1)S(1)}, bf16[64,128]{1,0:T(8,128)(2,1)S(1)}, u32[]{:S(2)}, u32[]{:S(2)}) collective-permute-start(bf16[64,128]{1,0:T(8,128)(2,1)S(1)} %get-tuple-element.43.after), channel_id=1, source_target_pairs={{0,1},{1,0},{2,3},{3,2},{4,5},{5,4},{6,7},{7,6},{8,9},{9,8},{10,11... | collective-permute-start | bytes 49160 | tf_op jit(solution)/shard_map/ppermute | solution.py:415
  19.2 0.6 %shard_map.144 = (f32[8,1024]{1,0:T(8,128)S(1)}, f32[3,512,128]{2,1,0:T(8,128)S(1)}, f32[768,128]{1,0:T(8,128)S(1)}, bf16[2,256,256]{2,1,0:T(8,128)(2,1)S(1)}) custom-call(f32[5,256,128]{2,1,0:T(8,128)S(1)} %get-tuple-element.51.refs_10_.refs_0_.refs_2_, f32[8,256]{1,0:T(8,128)S(1)} %get-tuple-element.41.refs_3_.msg.refs_1_.refs_7_, ...), custom_call_target="tpu_custom_call" | custom-call | tf_op jit(solution)/shard_map/pallas_call | solution.py:50
  19.8 0.8 %shard_map.145 = (bf16[6,64,256]{2,1,0:T(8,128)(2,1)S(1)}, bf16[6,64,256]{2,1,0:T(8,128)(2,1)S(1)}) custom-call(f32[4,64,4,256]{3,2,1,0:T(4,128)S(1)} %get-tuple-element.44.refs_3_.noise, bf16[64,128]{1,0:T(8,128)(2,1)S(1)} %get-tuple-element.43.after), custom_call_target="tpu_custom_call" | custom-call | tf_op jit(solution)/shard_map/pallas_call | solution.py:50
  20.6 1.1 %collective-permute-start.7 = (bf16[6,64,256]{2,1,0:T(8,128)(2,1)S(1)}, bf16[6,64,256]{2,1,0:T(8,128)(2,1)S(1)}, u32[]{:S(2)}, u32[]{:S(2)}) collective-permute-start(bf16[6,64,256]{2,1,0:T(8,128)(2,1)S(1)} %get-tuple-element.59), channel_id=1, source_target_pairs={{0,4},{4,0},{8,12},{12,8},{1,5},{5,1},{9,13},{13,9},{2,6},{6,2},{1... | collective-permute-start | bytes 589832 | tf_op jit(solution)/shard_map/ppermute | solution.py:477
  21.8 0.8 %collective-permute-start.8 = (bf16[6,64,256]{2,1,0:T(8,128)(2,1)S(1)}, bf16[6,64,256]{2,1,0:T(8,128)(2,1)S(1)}, u32[]{:S(2)}, u32[]{:S(2)}) collective-permute-start(bf16[6,64,256]{2,1,0:T(8,128)(2,1)S(1)} %get-tuple-element.60), channel_id=1, source_target_pairs={{4,8},{8,4},{5,9},{9,5},{6,10},{10,6},{7,11},{11,7},{20,24},{24,20... | collective-permute-start | bytes 589832 | tf_op jit(solution)/shard_map/ppermute | solution.py:477
  22.6 5.2 %shard_map.143 = (f32[10,64,256]{2,1,0:T(8,128)S(1)}, f32[256,128]{1,0:T(8,128)S(1)}) custom-call(f32[12,64,256]{2,1,0:T(8,128)S(1)} %get-tuple-element.42.refs_0_, bf16[64,128]{1,0:T(8,128)(2,1)S(1)} %collective-permute-done.5.refs_1_, bf16[64,128]{1,0:T(8,128)(2,1)S(1)} %collective-permute-done.6.refs_2_, ...), custom_call_target="tpu_custom_call" | custom-call | flops 6039797760 | tf_op jit(solution)/shard_map/pallas_call | solution.py:50
  27.9 0.9 %shard_map.146 = (f32[10,64,256]{2,1,0:T(8,128)S(1)}, bf16[64,128]{1,0:T(8,128)(2,1)S(1)}, f32[8,256]{1,0:T(8,128)S(1)}) custom-call(f32[10,64,256]{2,1,0:T(8,128)S(1)} %get-tuple-element.52.refs_0_, f32[8,1024]{1,0:T(8,128)S(1)} %get-tuple-element.53.refs_1_, f32[5,256,128]{2,1,0:T(8,128)S(1)} %get-tuple-element.51.refs_10_.refs_0_.refs_2_, ...), custom_call_target="tpu_custom_call" | custom-call | tf_op jit(solution)/shard_map/pallas_call | solution.py:50
  28.9 0.6 %collective-permute-start.9 = (bf16[64,128]{1,0:T(8,128)(2,1)S(1)}, bf16[64,128]{1,0:T(8,128)(2,1)S(1)}, u32[]{:S(2)}, u32[]{:S(2)}) collective-permute-start(bf16[64,128]{1,0:T(8,128)(2,1)S(1)} %get-tuple-element.62), channel_id=1, source_target_pairs={{0,1},{1,0},{2,3},{3,2},{4,5},{5,4},{6,7},{7,6},{8,9},{9,8},{10,11... | collective-permute-start | bytes 49160 | tf_op jit(solution)/shard_map/ppermute | solution.py:415
  29.5 3.7 %collective-permute-start.13 = (f32[8,256]{1,0:T(8,128)S(1)}, f32[8,256]{1,0:T(8,128)S(1)}, u32[]{:S(2)}, u32[]{:S(2)}) collective-permute-start(f32[8,256]{1,0:T(8,128)S(1)} %get-tuple-element.64.refs_7_), channel_id=1, source_target_pairs={{0,8},{4,12},{8,0},{12,4},{1,9},{5,13},{9,1},{13,5},{2,10},{6,14},... | collective-permute-start | bytes 24584 | tf_op jit(solution)/shard_map/ppermute | solution.py:425
  33.2 2.0 %collective-permute-start.12 = (f32[8,256]{1,0:T(8,128)S(1)}, f32[8,256]{1,0:T(8,128)S(1)}, u32[]{:S(2)}, u32[]{:S(2)}) collective-permute-start(f32[8,256]{1,0:T(8,128)S(1)} %get-tuple-element.64.refs_7_), channel_id=1, source_target_pairs={{0,12},{4,8},{8,4},{12,0},{1,13},{5,9},{9,5},{13,1},{2,14},{6,10},... | collective-permute-start | bytes 24584 | tf_op jit(solution)/shard_map/ppermute | solution.py:415
  35.1 4.6 %shard_map.147 = (f32[8,64,256]{2,1,0:T(8,128)S(1)}, f32[256,128]{1,0:T(8,128)S(1)}) custom-call(f32[10,64,256]{2,1,0:T(8,128)S(1)} %get-tuple-element.61.refs_0_, bf16[64,128]{1,0:T(8,128)(2,1)S(1)} %collective-permute-done.9.refs_1_, bf16[64,128]{1,0:T(8,128)(2,1)S(1)} %collective-permute-done.10.refs_2_, ...), custom_call_target="tpu_custom_call" | custom-call | flops 4831838208 | tf_op jit(solution)/shard_map/pallas_call | solution.py:50
  39.8 0.9 %shard_map.148 = (f32[8,64,256]{2,1,0:T(8,128)S(1)}, bf16[64,128]{1,0:T(8,128)(2,1)S(1)}, f32[8,256]{1,0:T(8,128)S(1)}) custom-call(f32[8,64,256]{2,1,0:T(8,128)S(1)} %get-tuple-element.63.refs_0_, f32[8,1024]{1,0:T(8,128)S(1)} %get-tuple-element.53.refs_1_, f32[5,256,128]{2,1,0:T(8,128)S(1)} %get-tuple-element.51.refs_10_.refs_0_.refs_2_, ...), custom_call_target="tpu_custom_call" | custom-call | tf_op jit(solution)/shard_map/pallas_call | solution.py:50
  40.7 0.6 collective-permute-start.15
  41.3 1.1 %collective-permute-start.14 = (bf16[64,128]{1,0:T(8,128)(2,1)S(1)}, bf16[64,128]{1,0:T(8,128)(2,1)S(1)}, u32[]{:S(2)}, u32[]{:S(2)}) collective-permute-start(bf16[64,128]{1,0:T(8,128)(2,1)S(1)} %get-tuple-element.67), channel_id=1, source_target_pairs={{0,1},{1,0},{2,3},{3,2},{4,5},{5,4},{6,7},{7,6},{8,9},{9,8},{10,11... | collective-permute-start | bytes 49160 | tf_op jit(solution)/shard_map/ppermute | solution.py:415
  42.4 2.4 %collective-permute-start.18 = (f32[8,256]{1,0:T(8,128)S(1)}, f32[8,256]{1,0:T(8,128)S(1)}, u32[]{:S(2)}, u32[]{:S(2)}) collective-permute-start(f32[8,256]{1,0:T(8,128)S(1)} %get-tuple-element.69.refs_7_), channel_id=1, source_target_pairs={{0,8},{4,12},{8,0},{12,4},{1,9},{5,13},{9,1},{13,5},{2,10},{6,14},... | collective-permute-start | bytes 24584 | tf_op jit(solution)/shard_map/ppermute | solution.py:425
  44.8 2.0 %collective-permute-start.17 = (f32[8,256]{1,0:T(8,128)S(1)}, f32[8,256]{1,0:T(8,128)S(1)}, u32[]{:S(2)}, u32[]{:S(2)}) collective-permute-start(f32[8,256]{1,0:T(8,128)S(1)} %get-tuple-element.69.refs_7_), channel_id=1, source_target_pairs={{0,12},{4,8},{8,4},{12,0},{1,13},{5,9},{9,5},{13,1},{2,14},{6,10},... | collective-permute-start | bytes 24584 | tf_op jit(solution)/shard_map/ppermute | solution.py:415
  46.8 4.0 %shard_map.149 = (f32[6,64,256]{2,1,0:T(8,128)S(1)}, f32[256,128]{1,0:T(8,128)S(1)}) custom-call(f32[8,64,256]{2,1,0:T(8,128)S(1)} %get-tuple-element.66.refs_0_, bf16[64,128]{1,0:T(8,128)(2,1)S(1)} %collective-permute-done.14.refs_1_, bf16[64,128]{1,0:T(8,128)(2,1)S(1)} %collective-permute-done.15.refs_2_, ...), custom_call_target="tpu_custom_call" | custom-call | flops 3623878656 | tf_op jit(solution)/shard_map/pallas_call | solution.py:50
  50.7 0.8 %shard_map.150 = (f32[6,64,256]{2,1,0:T(8,128)S(1)}, bf16[64,128]{1,0:T(8,128)(2,1)S(1)}, f32[8,256]{1,0:T(8,128)S(1)}) custom-call(f32[6,64,256]{2,1,0:T(8,128)S(1)} %get-tuple-element.68.refs_0_, f32[8,1024]{1,0:T(8,128)S(1)} %get-tuple-element.53.refs_1_, f32[5,256,128]{2,1,0:T(8,128)S(1)} %get-tuple-element.51.refs_10_.refs_0_.refs_2_, ...), custom_call_target="tpu_custom_call" | custom-call | tf_op jit(solution)/shard_map/pallas_call | solution.py:50
  51.7 0.6 %collective-permute-start.19 = (bf16[64,128]{1,0:T(8,128)(2,1)S(1)}, bf16[64,128]{1,0:T(8,128)(2,1)S(1)}, u32[]{:S(2)}, u32[]{:S(2)}) collective-permute-start(bf16[64,128]{1,0:T(8,128)(2,1)S(1)} %get-tuple-element.72), channel_id=1, source_target_pairs={{0,1},{1,0},{2,3},{3,2},{4,5},{5,4},{6,7},{7,6},{8,9},{9,8},{10,11... | collective-permute-start | bytes 49160 | tf_op jit(solution)/shard_map/ppermute | solution.py:415
  52.3 2.4 %collective-permute-start.23 = (f32[8,256]{1,0:T(8,128)S(1)}, f32[8,256]{1,0:T(8,128)S(1)}, u32[]{:S(2)}, u32[]{:S(2)}) collective-permute-start(f32[8,256]{1,0:T(8,128)S(1)} %get-tuple-element.73.refs_7_), channel_id=1, source_target_pairs={{0,8},{4,12},{8,0},{12,4},{1,9},{5,13},{9,1},{13,5},{2,10},{6,14},... | collective-permute-start | bytes 24584 | tf_op jit(solution)/shard_map/ppermute | solution.py:425
  54.7 2.0 %collective-permute-start.22 = (f32[8,256]{1,0:T(8,128)S(1)}, f32[8,256]{1,0:T(8,128)S(1)}, u32[]{:S(2)}, u32[]{:S(2)}) collective-permute-start(f32[8,256]{1,0:T(8,128)S(1)} %get-tuple-element.73.refs_7_), channel_id=1, source_target_pairs={{0,12},{4,8},{8,4},{12,0},{1,13},{5,9},{9,5},{13,1},{2,14},{6,10},... | collective-permute-start | bytes 24584 | tf_op jit(solution)/shard_map/ppermute | solution.py:415
  56.7 2.5 %shard_map.151.refs_0_ = f32[4,64,256]{2,1,0:T(8,128)S(1)} custom-call(f32[6,64,256]{2,1,0:T(8,128)S(1)} %get-tuple-element.71.refs_0_, bf16[64,128]{1,0:T(8,128)(2,1)S(1)} %collective-permute-done.19.refs_1_, bf16[64,128]{1,0:T(8,128)(2,1)S(1)} %collective-permute-done.20.refs_2_, f32[4,64,4,256]{3,2,1,0:T(4,128)S(1)} %get-tuple-element.44.refs_3_.noise, ...), custom_call_target="tpu_custom_call" | custom-call | flops 2415919104 | tf_op jit(solution)/shard_map/pallas_call | solution.py:50
  59.2 1.0 %collective-permute-done.22.refs_9_ = f32[8,256]{1,0:T(8,128)S(1)} collective-permute-done((f32[8,256]{1,0:T(8,128)S(1)}, f32[8,256]{1,0:T(8,128)S(1)}, u32[]{:S(2)}, u32[]{:S(2)}) %collective-permute-start.22) | collective-permute-done | bytes 8224 | tf_op jit(solution)/shard_map/ppermute | solution.py:415
  60.3 1.2 %shard_map.152 = (f32[64,4,256]{2,1,0:T(4,128)}, f32[1,256]{1,0:T(1,128)}) custom-call(f32[4,64,256]{2,1,0:T(8,128)S(1)} %shard_map.151.refs_0_, f32[8,1024]{1,0:T(8,128)S(1)} %get-tuple-element.53.refs_1_, f32[5,256,128]{2,1,0:T(8,128)S(1)} %get-tuple-element.51.refs_10_.refs_0_.refs_2_, bf16[256,256]{1,0:T(8,128)(2,1)S(1)} %get-tuple-element.54.refs_3_, ...), custom_call_target="tpu_custom_call" | custom-call | tf_op jit(solution)/shard_map/pallas_call | solution.py:50
  (29 shorter events, 1.4 us)
Async XLA Ops:
  3.9 12.7 %collective-permute-start.1 = (bf16[4,64,256]{2,1,0:T(8,128)(2,1)S(1)}, bf16[4,64,256]{2,1,0:T(8,128)(2,1)S(1)}, u32[]{:S(2)}, u32[]{:S(2)}) collective-permute-start(bf16[4,64,256]{2,1,0:T(8,128)(2,1)S(1)} %get-tuple-element.40), channel_id=1, source_target_pairs={{4,8},{8,4},{5,9},{9,5},{6,10},{10,6},{7,11},{11,7},{20,24},{24,20... | collective-permute-start | bytes 393224 | tf_op jit(solution)/shard_map/ppermute | solution.py:460
  4.6 12.0 %collective-permute-start = (bf16[4,64,256]{2,1,0:T(8,128)(2,1)S(1)}, bf16[4,64,256]{2,1,0:T(8,128)(2,1)S(1)}, u32[]{:S(2)}, u32[]{:S(2)}) collective-permute-start(bf16[4,64,256]{2,1,0:T(8,128)(2,1)S(1)} %get-tuple-element.40), channel_id=1, source_target_pairs={{0,4},{4,0},{8,12},{12,8},{1,5},{5,1},{9,13},{13,9},{2,6},{6,2},{1... | collective-permute-start | bytes 393224 | tf_op jit(solution)/shard_map/ppermute | solution.py:460
  10.5 4.6 %collective-permute-start.4 = (f32[8,256]{1,0:T(8,128)S(1)}, f32[8,256]{1,0:T(8,128)S(1)}, u32[]{:S(2)}, u32[]{:S(2)}) collective-permute-start(f32[8,256]{1,0:T(8,128)S(1)} %get-tuple-element.41.refs_3_.msg.refs_1_.refs_7_), channel_id=1, source_target_pairs={{0,8},{4,12},{8,0},{12,4},{1,9},{5,13},{9,1},{13,5},{2,10},{6,14},... | collective-permute-start | bytes 24584 | tf_op jit(solution)/shard_map/ppermute | solution.py:425
  10.5 5.4 %collective-permute-start.3 = (f32[8,256]{1,0:T(8,128)S(1)}, f32[8,256]{1,0:T(8,128)S(1)}, u32[]{:S(2)}, u32[]{:S(2)}) collective-permute-start(f32[8,256]{1,0:T(8,128)S(1)} %get-tuple-element.41.refs_3_.msg.refs_1_.refs_7_), channel_id=1, source_target_pairs={{0,12},{4,8},{8,4},{12,0},{1,13},{5,9},{9,5},{13,1},{2,14},{6,10},... | collective-permute-start | bytes 24584 | tf_op jit(solution)/shard_map/ppermute | solution.py:415
  12.9 3.7 %collective-permute-start.2 = (f32[8,256]{1,0:T(8,128)S(1)}, f32[8,256]{1,0:T(8,128)S(1)}, u32[]{:S(2)}, u32[]{:S(2)}) collective-permute-start(f32[8,256]{1,0:T(8,128)S(1)} %get-tuple-element.41.refs_3_.msg.refs_1_.refs_7_), channel_id=1, source_target_pairs={{0,4},{4,0},{8,12},{12,8},{1,5},{5,1},{9,13},{13,9},{2,6},{6,2},{1... | collective-permute-start | bytes 24584 | tf_op jit(solution)/shard_map/ppermute | solution.py:415
  17.0 5.6 %collective-permute-start.6 = (bf16[64,128]{1,0:T(8,128)(2,1)S(1)}, bf16[64,128]{1,0:T(8,128)(2,1)S(1)}, u32[]{:S(2)}, u32[]{:S(2)}) collective-permute-start(bf16[64,128]{1,0:T(8,128)(2,1)S(1)} %get-tuple-element.43.after), channel_id=1, source_target_pairs={{0,3},{1,2},{2,1},{3,0},{4,7},{5,6},{6,5},{7,4},{8,11},{9,10},{10,... | collective-permute-start | bytes 49160 | tf_op jit(solution)/shard_map/ppermute | solution.py:415
  17.1 5.5 %collective-permute-start.5 = (bf16[64,128]{1,0:T(8,128)(2,1)S(1)}, bf16[64,128]{1,0:T(8,128)(2,1)S(1)}, u32[]{:S(2)}, u32[]{:S(2)}) collective-permute-start(bf16[64,128]{1,0:T(8,128)(2,1)S(1)} %get-tuple-element.43.after), channel_id=1, source_target_pairs={{0,1},{1,0},{2,3},{3,2},{4,5},{5,4},{6,7},{7,6},{8,9},{9,8},{10,11... | collective-permute-start | bytes 49160 | tf_op jit(solution)/shard_map/ppermute | solution.py:415
  20.6 7.2 %collective-permute-start.7 = (bf16[6,64,256]{2,1,0:T(8,128)(2,1)S(1)}, bf16[6,64,256]{2,1,0:T(8,128)(2,1)S(1)}, u32[]{:S(2)}, u32[]{:S(2)}) collective-permute-start(bf16[6,64,256]{2,1,0:T(8,128)(2,1)S(1)} %get-tuple-element.59), channel_id=1, source_target_pairs={{0,4},{4,0},{8,12},{12,8},{1,5},{5,1},{9,13},{13,9},{2,6},{6,2},{1... | collective-permute-start | bytes 589832 | tf_op jit(solution)/shard_map/ppermute | solution.py:477
  21.8 6.1 %collective-permute-start.8 = (bf16[6,64,256]{2,1,0:T(8,128)(2,1)S(1)}, bf16[6,64,256]{2,1,0:T(8,128)(2,1)S(1)}, u32[]{:S(2)}, u32[]{:S(2)}) collective-permute-start(bf16[6,64,256]{2,1,0:T(8,128)(2,1)S(1)} %get-tuple-element.60), channel_id=1, source_target_pairs={{4,8},{8,4},{5,9},{9,5},{6,10},{10,6},{7,11},{11,7},{20,24},{24,20... | collective-permute-start | bytes 589832 | tf_op jit(solution)/shard_map/ppermute | solution.py:477
  28.8 6.3 %collective-permute-start.10 = (bf16[64,128]{1,0:T(8,128)(2,1)S(1)}, bf16[64,128]{1,0:T(8,128)(2,1)S(1)}, u32[]{:S(2)}, u32[]{:S(2)}) collective-permute-start(bf16[64,128]{1,0:T(8,128)(2,1)S(1)} %get-tuple-element.62), channel_id=1, source_target_pairs={{0,3},{1,2},{2,1},{3,0},{4,7},{5,6},{6,5},{7,4},{8,11},{9,10},{10,... | collective-permute-start | bytes 49160 | tf_op jit(solution)/shard_map/ppermute | solution.py:415
  28.9 6.3 %collective-permute-start.9 = (bf16[64,128]{1,0:T(8,128)(2,1)S(1)}, bf16[64,128]{1,0:T(8,128)(2,1)S(1)}, u32[]{:S(2)}, u32[]{:S(2)}) collective-permute-start(bf16[64,128]{1,0:T(8,128)(2,1)S(1)} %get-tuple-element.62), channel_id=1, source_target_pairs={{0,1},{1,0},{2,3},{3,2},{4,5},{5,4},{6,7},{7,6},{8,9},{9,8},{10,11... | collective-permute-start | bytes 49160 | tf_op jit(solution)/shard_map/ppermute | solution.py:415
  29.5 10.3 %collective-permute-start.13 = (f32[8,256]{1,0:T(8,128)S(1)}, f32[8,256]{1,0:T(8,128)S(1)}, u32[]{:S(2)}, u32[]{:S(2)}) collective-permute-start(f32[8,256]{1,0:T(8,128)S(1)} %get-tuple-element.64.refs_7_), channel_id=1, source_target_pairs={{0,8},{4,12},{8,0},{12,4},{1,9},{5,13},{9,1},{13,5},{2,10},{6,14},... | collective-permute-start | bytes 24584 | tf_op jit(solution)/shard_map/ppermute | solution.py:425
  33.2 6.6 %collective-permute-start.12 = (f32[8,256]{1,0:T(8,128)S(1)}, f32[8,256]{1,0:T(8,128)S(1)}, u32[]{:S(2)}, u32[]{:S(2)}) collective-permute-start(f32[8,256]{1,0:T(8,128)S(1)} %get-tuple-element.64.refs_7_), channel_id=1, source_target_pairs={{0,12},{4,8},{8,4},{12,0},{1,13},{5,9},{9,5},{13,1},{2,14},{6,10},... | collective-permute-start | bytes 24584 | tf_op jit(solution)/shard_map/ppermute | solution.py:415
  35.1 4.7 %collective-permute-start.11 = (f32[8,256]{1,0:T(8,128)S(1)}, f32[8,256]{1,0:T(8,128)S(1)}, u32[]{:S(2)}, u32[]{:S(2)}) collective-permute-start(f32[8,256]{1,0:T(8,128)S(1)} %get-tuple-element.64.refs_7_), channel_id=1, source_target_pairs={{0,4},{4,0},{8,12},{12,8},{1,5},{5,1},{9,13},{13,9},{2,6},{6,2},{1... | collective-permute-start | bytes 24584 | tf_op jit(solution)/shard_map/ppermute | solution.py:415
  40.7 6.1 %collective-permute-start.15 = (bf16[64,128]{1,0:T(8,128)(2,1)S(1)}, bf16[64,128]{1,0:T(8,128)(2,1)S(1)}, u32[]{:S(2)}, u32[]{:S(2)}) collective-permute-start(bf16[64,128]{1,0:T(8,128)(2,1)S(1)} %get-tuple-element.67), channel_id=1, source_target_pairs={{0,3},{1,2},{2,1},{3,0},{4,7},{5,6},{6,5},{7,4},{8,11},{9,10},{10,... | collective-permute-start | bytes 49160 | tf_op jit(solution)/shard_map/ppermute | solution.py:415
  41.3 5.5 %collective-permute-start.14 = (bf16[64,128]{1,0:T(8,128)(2,1)S(1)}, bf16[64,128]{1,0:T(8,128)(2,1)S(1)}, u32[]{:S(2)}, u32[]{:S(2)}) collective-permute-start(bf16[64,128]{1,0:T(8,128)(2,1)S(1)} %get-tuple-element.67), channel_id=1, source_target_pairs={{0,1},{1,0},{2,3},{3,2},{4,5},{5,4},{6,7},{7,6},{8,9},{9,8},{10,11... | collective-permute-start | bytes 49160 | tf_op jit(solution)/shard_map/ppermute | solution.py:415
  42.4 8.3 %collective-permute-start.18 = (f32[8,256]{1,0:T(8,128)S(1)}, f32[8,256]{1,0:T(8,128)S(1)}, u32[]{:S(2)}, u32[]{:S(2)}) collective-permute-start(f32[8,256]{1,0:T(8,128)S(1)} %get-tuple-element.69.refs_7_), channel_id=1, source_target_pairs={{0,8},{4,12},{8,0},{12,4},{1,9},{5,13},{9,1},{13,5},{2,10},{6,14},... | collective-permute-start | bytes 24584 | tf_op jit(solution)/shard_map/ppermute | solution.py:425
  44.8 5.9 %collective-permute-start.17 = (f32[8,256]{1,0:T(8,128)S(1)}, f32[8,256]{1,0:T(8,128)S(1)}, u32[]{:S(2)}, u32[]{:S(2)}) collective-permute-start(f32[8,256]{1,0:T(8,128)S(1)} %get-tuple-element.69.refs_7_), channel_id=1, source_target_pairs={{0,12},{4,8},{8,4},{12,0},{1,13},{5,9},{9,5},{13,1},{2,14},{6,10},... | collective-permute-start | bytes 24584 | tf_op jit(solution)/shard_map/ppermute | solution.py:415
  46.7 4.0 %collective-permute-start.16 = (f32[8,256]{1,0:T(8,128)S(1)}, f32[8,256]{1,0:T(8,128)S(1)}, u32[]{:S(2)}, u32[]{:S(2)}) collective-permute-start(f32[8,256]{1,0:T(8,128)S(1)} %get-tuple-element.69.refs_7_), channel_id=1, source_target_pairs={{0,4},{4,0},{8,12},{12,8},{1,5},{5,1},{9,13},{13,9},{2,6},{6,2},{1... | collective-permute-start | bytes 24584 | tf_op jit(solution)/shard_map/ppermute | solution.py:415
  51.6 5.1 %collective-permute-start.20 = (bf16[64,128]{1,0:T(8,128)(2,1)S(1)}, bf16[64,128]{1,0:T(8,128)(2,1)S(1)}, u32[]{:S(2)}, u32[]{:S(2)}) collective-permute-start(bf16[64,128]{1,0:T(8,128)(2,1)S(1)} %get-tuple-element.72), channel_id=1, source_target_pairs={{0,3},{1,2},{2,1},{3,0},{4,7},{5,6},{6,5},{7,4},{8,11},{9,10},{10,... | collective-permute-start | bytes 49160 | tf_op jit(solution)/shard_map/ppermute | solution.py:415
  51.7 5.0 %collective-permute-start.19 = (bf16[64,128]{1,0:T(8,128)(2,1)S(1)}, bf16[64,128]{1,0:T(8,128)(2,1)S(1)}, u32[]{:S(2)}, u32[]{:S(2)}) collective-permute-start(bf16[64,128]{1,0:T(8,128)(2,1)S(1)} %get-tuple-element.72), channel_id=1, source_target_pairs={{0,1},{1,0},{2,3},{3,2},{4,5},{5,4},{6,7},{7,6},{8,9},{9,8},{10,11... | collective-permute-start | bytes 49160 | tf_op jit(solution)/shard_map/ppermute | solution.py:415
  52.3 6.9 %collective-permute-start.23 = (f32[8,256]{1,0:T(8,128)S(1)}, f32[8,256]{1,0:T(8,128)S(1)}, u32[]{:S(2)}, u32[]{:S(2)}) collective-permute-start(f32[8,256]{1,0:T(8,128)S(1)} %get-tuple-element.73.refs_7_), channel_id=1, source_target_pairs={{0,8},{4,12},{8,0},{12,4},{1,9},{5,13},{9,1},{13,5},{2,10},{6,14},... | collective-permute-start | bytes 24584 | tf_op jit(solution)/shard_map/ppermute | solution.py:425
  54.7 5.4 %collective-permute-start.22 = (f32[8,256]{1,0:T(8,128)S(1)}, f32[8,256]{1,0:T(8,128)S(1)}, u32[]{:S(2)}, u32[]{:S(2)}) collective-permute-start(f32[8,256]{1,0:T(8,128)S(1)} %get-tuple-element.73.refs_7_), channel_id=1, source_target_pairs={{0,12},{4,8},{8,4},{12,0},{1,13},{5,9},{9,5},{13,1},{2,14},{6,10},... | collective-permute-start | bytes 24584 | tf_op jit(solution)/shard_map/ppermute | solution.py:415
  56.7 3.7 %collective-permute-start.21 = (f32[8,256]{1,0:T(8,128)S(1)}, f32[8,256]{1,0:T(8,128)S(1)}, u32[]{:S(2)}, u32[]{:S(2)}) collective-permute-start(f32[8,256]{1,0:T(8,128)S(1)} %get-tuple-element.73.refs_7_), channel_id=1, source_target_pairs={{0,4},{4,0},{8,12},{12,8},{1,5},{5,1},{9,13},{13,9},{2,6},{6,2},{1... | collective-permute-start | bytes 24584 | tf_op jit(solution)/shard_map/ppermute | solution.py:415

commit v3 on v2

--- a/solution.py
+++ b/solution.py
@@ -15,6 +15,7 @@
 LANES = 128
 HALF = 64
 CHUNK = 4
+PIECES = 3
 
 noise_levels = (1.0, 0.6, 0.3)
 obs_precision = 4.0
@@ -85,28 +86,66 @@
     return lax.rem(lax.axis_index(axis), 2) == 0
 
 
-def stage_kernel(*refs, n_args, slots):
-    live, sources, staged = refs[0], refs[1 : 1 + n_args], refs[1 + n_args : 1 + 2 * n_args]
-    msg, entry_msg, sems = refs[1 + 2 * n_args :]
+def start_all(pairs, sems):
     copies = [
         pltpu.make_async_copy(source, target, sems.at[i])
-        for i, (source, target) in enumerate(zip(sources, staged))
+        for i, (source, target) in enumerate(pairs)
     ]
     for copy in copies:
         copy.start()
-    prior, _, cell, owner, slot, weight, station = staged[:7]
-    _, latb, lond = prior.shape
-    copies[0].wait()
+    return copies
+
+
+def rows_of(source, target):
+    return [(source.at[:, r, :], target.at[r]) for r in range(target.shape[0])]
+
+
+def later_kernel(noise_in, *refs):
+    half = (len(refs) - 3) // 2
+    noise, noise_a, noise_b, sems = refs[half], *refs[-3:]
+    pairs = []
+    for k in range(noise.shape[0]):
+        pairs += rows_of(noise_in.at[k], noise.at[k])
+    pairs += list(zip(refs[:half], refs[half + 1 : -3]))
+    copies = start_all(pairs, sems)
+    for copy in copies:
+        copy.wait()
+    latb = noise.shape[1]
+    up = [(k, r) for k in range(HALO - 1) for r in range(1 + k, latb)]
+    down = [(k, r) for k in range(HALO - 1) for r in range(0, latb - 1 - k)]
+
+    @pl.when(is_even("band"))
+    def _():
+        for i in range(len(up)):
+            noise_a[i] = noise[up[i]].astype(BF16)
+            noise_b[i] = noise[down[i]].astype(BF16)
+
+    @pl.when(jnp.logical_not(is_even("band")))
+    def _():
+        for i in range(len(up)):
+            noise_a[i] = noise[down[i]].astype(BF16)
+            noise_b[i] = noise[up[i]].astype(BF16)
+
+
+def stage_kernel(*refs, slots):
+    live, prior_in, entries_in = refs[0], refs[1], refs[2:7]
+    prior, msg, copy_msg, entry_msg, *entries, sems = refs[7:]
+    latb, _, lond = prior.shape
+    copies = start_all(rows_of(prior_in, prior) + list(zip(entries_in, entries)), sems)
     for r in range(latb):
-        msg[r] = (prior[:, r, :] * shrink(STEPS[0][0])).astype(BF16)
-    for copy in copies[2:7]:
+        copies[r].wait()
+        slab = (prior[r] * shrink(STEPS[0][0])).astype(BF16)
+        msg[r] = slab
+        copy_msg[r] = slab
+    for copy in copies[latb:]:
         copy.wait()
+    cell, owner, slot, weight, station = entries
     count = cell.shape[1]
     cells = cell[...]
     lon = cells % lond
     row = (cells // lond) % latb
     variable = cells // (lond * latb)
-    rv = row * prior.shape[0] + variable
+    rv = row * prior.shape[1] + variable
     key = owner[...] * slots + slot[...]
     alive = lax.broadcasted_iota(jnp.int32, (1, count), 1) < live[0]
     weights = jnp.where(alive, weight[...], 0.0)
@@ -120,15 +159,15 @@
     entry_msg[6:8] = jnp.zeros((2, count), F32)
     columns = jnp.transpose(entry_msg[...])
     rv_col, lon_col = columns[:, 1:2], columns[:, 2:3]
-    one_hot = jnp.where(rv_col == iota((count, latb * prior.shape[0]), 1), 1.0, 0.0).astype(BF16)
-    current = jnp.concatenate([prior[:, r, :] for r in range(latb)], axis=0)
+    one_hot = jnp.where(rv_col == iota((count, latb * prior.shape[1]), 1), 1.0, 0.0).astype(BF16)
+    current = jnp.concatenate([prior[r] for r in range(latb)], axis=0)
     picked = sum(dot(one_hot, part) for part in pieces(current, 2))
     at = jnp.sum(jnp.where(lon_col == iota((count, lond), 1), picked, 0.0), axis=1, keepdims=True)
     eye = iota((count, count), 0) == iota((count, count), 1)
     entry_msg[6:7] = weights * jnp.sum(jnp.where(eye, at, 0.0), axis=0, keepdims=True)
-    copies[1].wait()
-    for copy in copies[7:]:
-        copy.wait()
+    high = jnp.concatenate([part.astype(F32) for part in pieces(entry_msg[...], PIECES)], axis=0)
+    msg[latb, 0 : 8 * PIECES] = high.astype(BF16)
+    copy_msg[latb, 0 : 8 * PIECES] = high.astype(BF16)
 
 
 def edges_into(edge_ref, state, rows, level):
@@ -142,44 +181,26 @@
     edge_ref[...] = (edge * shrink(level)).astype(BF16)
 
 
-def extend_kernel(*refs, latb):
-    prior, halo_a, halo_b = refs[:3]
-    state, edge = refs[-2:]
+def extend_kernel(prior, halo_a, halo_b, far, *refs, latb):
+    state, edge, msg_a, msg_b = refs[-4:]
     grow = 1.0 / shrink(STEPS[0][0])
+    band = lax.axis_index("band")
+    even = is_even("band")
     for r in range(latb):
-        state[HALO + r] = prior[:, r, :]
-
-    @pl.when(is_even("band"))
-    def _():
-        for r in range(latb):
-            state[r] = halo_b[r].astype(F32) * grow
-            state[HALO + latb + r] = halo_a[r].astype(F32) * grow
-
-    @pl.when(jnp.logical_not(is_even("band")))
-    def _():
-        for r in range(latb):
-            state[r] = halo_a[r].astype(F32) * grow
-            state[HALO + latb + r] = halo_b[r].astype(F32) * grow
-
+        from_a, from_b = halo_a[r].astype(F32) * grow, halo_b[r].astype(F32) * grow
+        state[r] = jnp.where(even, from_b, from_a)
+        state[HALO + r] = prior[r]
+        state[HALO + latb + r] = jnp.where(even, from_a, from_b)
     edges_into(edge, state, 2 * HALO + latb, STEPS[0][0])
-
-
-def noise_kernel(noise, after, noise_a, noise_b):
-    latb = noise.shape[2]
-    up = [(k, r) for k in range(HALO - 1) for r in range(1 + k, latb)]
-    down = [(k, r) for k in range(HALO - 1) for r in range(0, latb - 1 - k)]
-
-    @pl.when(is_even("band"))
-    def _():
-        for i in range(len(up)):
-            noise_a[i] = noise[up[i][0], :, up[i][1], :].astype(BF16)
-            noise_b[i] = noise[down[i][0], :, down[i][1], :].astype(BF16)
-
-    @pl.when(jnp.logical_not(is_even("band")))
-    def _():
-        for i in range(len(up)):
-            noise_a[i] = noise[down[i][0], :, down[i][1], :].astype(BF16)
-            noise_b[i] = noise[up[i][0], :, up[i][1], :].astype(BF16)
+    outer = jnp.logical_or(band == 0, band == lax.axis_size("band") - 1)
+    for halo, msg in ((halo_a, msg_a), (halo_b, msg_b)):
+        parts = halo[latb, 0 : 8 * PIECES].astype(F32)
+        whole = sum(parts[8 * i : 8 * i + 8] for i in range(PIECES))
+        msg[...] = jnp.where(outer, far[...], whole) if halo is halo_b else whole
+
+
+def pass_kernel(value, *refs):
+    refs[-1][...] = value[...]
 
 
 def wide(column):
@@ -205,7 +226,7 @@
 
 def tables_kernel(*refs, n_msgs, variables, latb):
     own_cols, msgs = refs[0], refs[1 : 1 + n_msgs]
-    keys, near, seen, spread = refs[1 + n_msgs :]
+    keys, near, seen, spread = refs[-4:]
     count = msgs[0].shape[1]
     even = is_even("band")
     low = jnp.where(even, msgs[2][...], msgs[1][...])
@@ -288,7 +309,7 @@
             second = silu_norm(sums[i * width : (i + 1) * width], gain_2[...]).astype(BF16)
             moved = state[i + 1] + (drift / level) * dot(head[...], second, 1, 1)
             if out_halo <= i < out_halo + latb:
-                moved = moved + kick * noise[step, :, i - out_halo, :]
+                moved = moved + kick * noise[step, i - out_halo]
             target[i] = moved
 
     bounds = [0]
@@ -366,16 +387,20 @@
     if last:
         state_out, innov_out, state, innov, sems = rest
         for r in range(latb):
-            state[:, r, :] = target[out_halo + r] + own[r * variables : (r + 1) * variables]
-        state_copy = pltpu.make_async_copy(state, state_out, sems.at[0])
-        state_copy.start()
+            state[r] = target[out_halo + r] + own[r * variables : (r + 1) * variables]
+        copies = [
+            pltpu.make_async_copy(state.at[r], state_out.at[:, r, :], sems.at[r])
+            for r in range(latb)
+        ]
+        for copy in copies:
+            copy.start()
         found = matching(cols[4], keys, values)
         eye = iota((count, count), 0) == iota((count, count), 1)
         innov[...] = keys[4:5, 0:count] - jnp.sum(jnp.where(eye, found, 0.0), axis=0, keepdims=True)
-        innov_copy = pltpu.make_async_copy(innov, innov_out, sems.at[1])
-        innov_copy.start()
-        state_copy.wait()
-        innov_copy.wait()
+        copies.append(pltpu.make_async_copy(innov, innov_out, sems.at[latb]))
+        copies[-1].start()
+        for copy in copies:
+            copy.wait()
         return
     at_entries, halo_a, halo_b, state, edge, value = rest
     row_cell = keys[1:2, 0:count] * width + keys[2:3, 0:count]
@@ -415,15 +440,18 @@
     return [lax.ppermute(block, axis, route) for route in swaps(lax.axis_size(axis))]
 
 
-def from_bands(block):
+def from_far(block):
     count = lax.axis_size("band")
-    found = [block] + from_neighbours(block, "band")
     reach = min(2 * REACH + 1, count)
-    far = sorted({d % count for d in range(-reach, reach + 1)} - {0, 1, count - 1})
-    for distance in far:
+    found = []
+    for distance in sorted({d % count for d in range(-reach, reach + 1)} - {0, 1, count - 1}):
         route = [(i, (i + distance) % count) for i in range(count)]
         found.append(lax.ppermute(block, "band", route))
     return found
+
+
+def from_bands(block):
+    return [block] + from_neighbours(block, "band") + from_far(block)
 
 
 def per_device(
@@ -440,41 +468,57 @@
     def row(a):
         return a.reshape(1, -1)
 
-    taken = [
-        prior_state, langevin_noise, row(entry_cell), row(entry_owner), row(entry_slot),
-        row(entry_weight), row(station_values), taps, lift_weight, head_weight.T, gain_1, gain_2,
+    entries = [
+        row(entry_cell), row(entry_owner), row(entry_slot), row(entry_weight), row(station_values),
     ]
-    *staged, msg, entry_msg = vmem_call(
-        functools.partial(stage_kernel, n_args=len(taken), slots=slots),
-        [(a.shape, a.dtype) for a in taken]
-        + [((latb, variables, lond), BF16), ((8, count), F32)],
-        live_counts, *taken,
+    message = ((latb + 1, variables, lond), BF16)
+    prior_state, msg, copy_msg, entry_msg = vmem_call(
+        functools.partial(stage_kernel, slots=slots),
+        [((latb, variables, lond), F32), message, message, ((8, count), F32)],
+        live_counts, prior_state, *entries,
         scalars=1,
-        hbm_in=len(taken),
-        scratch=[pltpu.SemaphoreType.DMA((len(taken),))],
-    )
-    prior_state, langevin_noise = staged[:2]
-    taps, lift_weight, head_weight, gain_1, gain_2 = staged[7:]
+        hbm_in=1 + len(entries),
+        scratch=[pltpu.VMEM(a.shape, a.dtype) for a in entries]
+        + [pltpu.SemaphoreType.DMA((latb + len(entries),))],
+    )
+    weights = [taps, lift_weight, head_weight.T, gain_1, gain_2]
+    slabs = ((sum(HALO - 1 - k for k in range(HALO - 1)), variables, lond), BF16)
+    langevin_noise, taps, lift_weight, head_weight, gain_1, gain_2, noise_a, noise_b = vmem_call(
+        later_kernel,
+        [((len(STEPS), latb, variables, lond), F32)]
+        + [(a.shape, a.dtype) for a in weights]
+        + [slabs, slabs],
+        langevin_noise, *weights,
+        hbm_in=1 + len(weights),
+        scratch=[pltpu.SemaphoreType.DMA((len(STEPS) * latb + len(weights),))],
+    )
     route_a, route_b = swaps(lax.axis_size("band"))
-    route_b = [pair for pair in route_b if abs(pair[0] - pair[1]) == 1]
-    halos = [lax.ppermute(msg, "band", route) for route in (route_a, route_b)]
-    msgs = from_bands(entry_msg)
-    n_msgs = len(msgs)
+    near_b = [pair for pair in route_b if abs(pair[0] - pair[1]) == 1]
+    far_b = [pair for pair in route_b if abs(pair[0] - pair[1]) != 1]
+    halos = [lax.ppermute(msg, "band", route_a), lax.ppermute(copy_msg, "band", near_b)]
+    around = lax.ppermute(entry_msg, "band", far_b)
+    others = from_far(entry_msg)
     high = latb * variables
     cols, pick, spread = vmem_call(
         functools.partial(own_kernel, variables=variables, latb=latb, lond=lond),
         [((5, count, LANES), F32), ((count, high), BF16), ((high, count), BF16)],
         entry_msg,
     )
-    state, edge = vmem_call(
+    state, edge, msg_a, msg_b = vmem_call(
         functools.partial(extend_kernel, latb=latb),
-        [((2 * HALO + latb, variables, lond), F32), ((variables, LANES), BF16)],
-        prior_state, *halos, *msgs,
-    )
+        [
+            ((2 * HALO + latb, variables, lond), F32),
+            ((variables, LANES), BF16),
+            ((8, count), F32),
+            ((8, count), F32),
+        ],
+        prior_state, *halos, around, noise_a, cols,
+    )
+    msgs = [entry_msg, msg_a, msg_b, *others]
+    n_msgs = len(msgs)
     edges = from_neighbours(edge, "wt")
-    slabs = ((sum(HALO - 1 - k for k in range(HALO - 1)), variables, lond), BF16)
-    noise_a, noise_b = vmem_call(noise_kernel, [slabs, slabs], langevin_noise, edge)
-    noise_halos = [lax.ppermute(noise_a, "band", route_a), lax.ppermute(noise_b, "band", route_b)]
+    (after_a,) = vmem_call(pass_kernel, [slabs], noise_a, *edges)
+    noise_halos = [lax.ppermute(after_a, "band", route_a), lax.ppermute(noise_b, "band", near_b)]
     keys, near, seen, near_spread = vmem_call(
         functools.partial(tables_kernel, n_msgs=n_msgs, variables=variables, latb=latb),
         [
@@ -483,7 +527,7 @@
             ((3 * count, LANES), F32),
             ((2, high, count), BF16),
         ],
-        cols, *msgs,
+        cols, *msgs, *noise_halos,
     )
     tables = (keys, cols, spread, near, seen, near_spread)
     values, value_row = msgs, 6
@@ -518,7 +562,11 @@
             outs = [((variables, latb, lond), F32), ((1, count), F32)]
             state, innov = vmem_call(
                 update, outs, found[0], *tables, *values, hbm_out=True,
-                scratch=[pltpu.VMEM(*out) for out in outs] + [pltpu.SemaphoreType.DMA((2,))],
+                scratch=[
+                    pltpu.VMEM((latb, variables, lond), F32),
+                    pltpu.VMEM((1, count), F32),
+                    pltpu.SemaphoreType.DMA((latb + 1,)),
+                ],
             )
             return state, innov.reshape(-1)
         state, edge, value = vmem_call(

time: 61.9 us -> 59.6 us (0.963)
  waiting for transfers between devices: 3.78 us -> 2.43 us
  starting transfers between devices: 31.2 us -> 30.3 us
    ppermute x16 -> x14, starting transfers between devices: 14.1 us -> 8.85 us  [from_neighbours(): lax.ppermute(block, axis, route)]
    ppermute x8 -> x9, starting transfers between devices: 17 us -> 21.5 us  [the longest x4 10.1 us: from_far(): found.append(lax.ppermute(block, 'band', route))]
    ppermute x16 -> x14, waiting for transfers between devices: 2.69 us -> 1.85 us  [from_neighbours(): lax.ppermute(block, axis, route)]
    pallas_call x13 -> x14, Pallas kernels: 25.1 us -> 24.9 us  [vmem_call(): pl.pallas_call(kernel, out_shape=[out_type(shape, dtype) for shape, dtype...]
  transfers between devices with their start and end apart: 24 -> 23, of which waited for: 5 -> 3; matrix products, arithmetic and copies ran while one was open for 0% -> 0% of each run, Pallas kernels for 30% -> 31%
where the time goes in v3:
time: 59.6 us; the launch traced here: 59.3 us
  starting transfers between devices  30.3 us (51%)
  Pallas kernels  24.9 us (42%)
  waiting for transfers between devices  2.43 us (4%)
  between operations  1.65 us (3%)
    pallas_call x14, Pallas kernels, vmem_call(): pl.pallas_call(kernel, out_shape=[out_type(shape, dtype) for shape, dtype...  24.9 us
    ppermute x4, starting transfers between devices, from_far(): found.append(lax.ppermute(block, 'band', route))  10.1 us
    ppermute x14, starting transfers between devices, from_neighbours(): lax.ppermute(block, axis, route)  8.85 us
    ppermute x1, starting transfers between devices, per_device(): around = lax.ppermute(entry_msg, 'band', far_b)  4.38 us
    ppermute x1, starting transfers between devices, per_device(): lax.ppermute(msg, 'band', route_a)  3.08 us
    ppermute x1, starting transfers between devices, per_device(): lax.ppermute(after_a, 'band', route_a)  2.61 us
    ppermute x14, waiting for transfers between devices, from_neighbours(): lax.ppermute(block, axis, route)  1.85 us
  transfers between devices with their start and end apart: 23, of which 3 were waited for; matrix products, arithmetic and copies ran while one was open for 0% of the time, Pallas kernels for 31%

profile of v3, /device:TPU:0, one launch (start us, length us, event | category | flops | bytes accessed | tf_op | source)
XLA Modules:
  0.0 59.3 jit_solution(5292490472927665765)
XLA Ops:
  1.3 1.6 %shard_map.140 = (f32[4,64,256]{2,1,0:T(8,128)S(1)}, bf16[5,64,256]{2,1,0:T(8,128)(2,1)S(1)}, bf16[5,64,256]{2,1,0:T(8,128)(2,1)S(1)}, f32[8,256]{1,0:T(8,128)S(1)}) custom-call(s32[1]{0:T(128)S(6)} %copy.15.refs_0_, f32[64,4,256]{2,1,0:T(4,128)} %refs_1_.2, s32[1,256]{1,0:T(1,128)} %bitcast.12, s32[1,256]{1,0:T(1,128)} %bitcast.13, s32[1,256]{1,0:T(1,128)} %bitcast.14, ...), custom_call_target="tpu_custom_call" | custom-call | tf_op jit(solution)/shard_map/pallas_call | solution.py:51
  2.9 3.1 %collective-permute-start = (bf16[5,64,256]{2,1,0:T(8,128)(2,1)S(1)}, bf16[5,64,256]{2,1,0:T(8,128)(2,1)S(1)}, u32[]{:S(2)}, u32[]{:S(2)}) collective-permute-start(bf16[5,64,256]{2,1,0:T(8,128)(2,1)S(1)} %get-tuple-element.43), channel_id=1, source_target_pairs={{0,4},{4,0},{8,12},{12,8},{1,5},{5,1},{9,13},{13,9},{2,6},{6,2},{1... | collective-permute-start | bytes 491528 | tf_op jit(solution)/shard_map/ppermute | solution.py:498
  6.0 0.7 %collective-permute-start.1 = (bf16[5,64,256]{2,1,0:T(8,128)(2,1)S(1)}, bf16[5,64,256]{2,1,0:T(8,128)(2,1)S(1)}, u32[]{:S(2)}, u32[]{:S(2)}) collective-permute-start(bf16[5,64,256]{2,1,0:T(8,128)(2,1)S(1)} %get-tuple-element.44), channel_id=1, source_target_pairs={{4,8},{8,4},{5,9},{9,5},{6,10},{10,6},{7,11},{11,7},{20,24},{24,20... | collective-permute-start | bytes 491528 | tf_op jit(solution)/shard_map/ppermute | solution.py:498
  6.6 4.4 %collective-permute-start.2 = (f32[8,256]{1,0:T(8,128)S(1)}, f32[8,256]{1,0:T(8,128)S(1)}, u32[]{:S(2)}, u32[]{:S(2)}) collective-permute-start(f32[8,256]{1,0:T(8,128)S(1)} %get-tuple-element.45.msg.refs_1_.refs_7_), channel_id=1, source_target_pairs={{0,12},{12,0},{1,13},{13,1},{2,14},{14,2},{3,15},{15,3},{16,28},{2... | collective-permute-start | bytes 24584 | tf_op jit(solution)/shard_map/ppermute | solution.py:499
  11.0 0.5 shard_map.142
  11.6 2.0 %shard_map.141 = (f32[4,4,64,256]{3,2,1,0:T(8,128)S(1)}, bf16[2304,256]{1,0:T(8,128)(2,1)S(1)}, bf16[64,256]{1,0:T(8,128)(2,1)S(1)}, bf16[64,256]{1,0:T(8,128)(2...) custom-call(f32[4,64,4,256]{3,2,1,0:T(4,128)} %noise_in.1, ...), custom_call_target="tpu_custom_call" | custom-call | tf_op jit(solution)/shard_map/pallas_call | solution.py:51
  13.5 0.6 collective-permute-done.2.far
  14.1 0.3 shard_map.143
  14.5 1.6 %collective-permute-start.3 = (bf16[64,128]{1,0:T(8,128)(2,1)S(1)}, bf16[64,128]{1,0:T(8,128)(2,1)S(1)}, u32[]{:S(2)}, u32[]{:S(2)}) collective-permute-start(bf16[64,128]{1,0:T(8,128)(2,1)S(1)} %get-tuple-element.49), channel_id=1, source_target_pairs={{0,1},{1,0},{2,3},{3,2},{4,5},{5,4},{6,7},{7,6},{8,9},{9,8},{10,11... | collective-permute-start | bytes 49160 | tf_op jit(solution)/shard_map/ppermute | solution.py:440
  16.1 2.2 %collective-permute-start.5 = (f32[8,256]{1,0:T(8,128)S(1)}, f32[8,256]{1,0:T(8,128)S(1)}, u32[]{:S(2)}, u32[]{:S(2)}) collective-permute-start(f32[8,256]{1,0:T(8,128)S(1)} %get-tuple-element.45.msg.refs_1_.refs_7_), channel_id=1, source_target_pairs={{0,8},{4,12},{8,0},{12,4},{1,9},{5,13},{9,1},{13,5},{2,10},{6,14},... | collective-permute-start | bytes 24584 | tf_op jit(solution)/shard_map/ppermute | solution.py:449
  18.3 0.7 %collective-permute-start.7 = (bf16[6,64,256]{2,1,0:T(8,128)(2,1)S(1)}, bf16[6,64,256]{2,1,0:T(8,128)(2,1)S(1)}, u32[]{:S(2)}, u32[]{:S(2)}) collective-permute-start(bf16[6,64,256]{2,1,0:T(8,128)(2,1)S(1)} %get-tuple-element.60), channel_id=1, source_target_pairs={{4,8},{8,4},{5,9},{9,5},{6,10},{10,6},{7,11},{11,7},{20,24},{24,20... | collective-permute-start | bytes 589832 | tf_op jit(solution)/shard_map/ppermute | solution.py:521
  19.0 2.6 %collective-permute-start.6 = (bf16[6,64,256]{2,1,0:T(8,128)(2,1)S(1)}, bf16[6,64,256]{2,1,0:T(8,128)(2,1)S(1)}, u32[]{:S(2)}, u32[]{:S(2)}) collective-permute-start(bf16[6,64,256]{2,1,0:T(8,128)(2,1)S(1)} %shard_map.145), channel_id=1, source_target_pairs={{0,4},{4,0},{8,12},{12,8},{1,5},{5,1},{9,13},{13,9},{2,6},{6,2},{1... | collective-permute-start | bytes 589832 | tf_op jit(solution)/shard_map/ppermute | solution.py:521
  21.6 5.1 %shard_map.144 = (f32[10,64,256]{2,1,0:T(8,128)S(1)}, f32[256,128]{1,0:T(8,128)S(1)}) custom-call(f32[12,64,256]{2,1,0:T(8,128)S(1)} %get-tuple-element.48.refs_0_, bf16[64,128]{1,0:T(8,128)(2,1)S(1)} %collective-permute-done.3.refs_1_.refs_0_, bf16[64,128]{1,0:T(8,128)(2,1)S(1)} %collective-permute-done.4.refs_2_.refs_1_, ...), custom_call_target="tpu_custom_call" | custom-call | flops 6039797760 | tf_op jit(solution)/shard_map/pallas_call | solution.py:51
  26.8 0.6 %shard_map.146 = (f32[8,1024]{1,0:T(8,128)S(1)}, f32[3,512,128]{2,1,0:T(8,128)S(1)}, f32[768,128]{1,0:T(8,128)S(1)}, bf16[2,256,256]{2,1,0:T(8,128)(2,1)S(1)}) custom-call(f32[5,256,128]{2,1,0:T(8,128)S(1)} %get-tuple-element.47.refs_1_.refs_10_.refs_0_.refs_2_, f32[8,256]{1,0:T(8,128)S(1)} %get-tuple-element.45.msg.refs_1_.refs_7_, ...), custom_call_target="tpu_custom_call" | custom-call | tf_op jit(solution)/shard_map/pallas_call | solution.py:51
  27.4 0.9 %shard_map.147 = (f32[10,64,256]{2,1,0:T(8,128)S(1)}, bf16[64,128]{1,0:T(8,128)(2,1)S(1)}, f32[8,256]{1,0:T(8,128)S(1)}) custom-call(f32[10,64,256]{2,1,0:T(8,128)S(1)} %get-tuple-element.57.refs_0_, f32[8,1024]{1,0:T(8,128)S(1)} %get-tuple-element.61.refs_1_, f32[5,256,128]{2,1,0:T(8,128)S(1)} %get-tuple-element.47.refs_1_.refs_10_.refs_0_.refs_2_, ...), custom_call_target="tpu_custom_call" | custom-call | tf_op jit(solution)/shard_map/pallas_call | solution.py:51
  28.4 0.6 %collective-permute-start.8 = (bf16[64,128]{1,0:T(8,128)(2,1)S(1)}, bf16[64,128]{1,0:T(8,128)(2,1)S(1)}, u32[]{:S(2)}, u32[]{:S(2)}) collective-permute-start(bf16[64,128]{1,0:T(8,128)(2,1)S(1)} %get-tuple-element.68), channel_id=1, source_target_pairs={{0,1},{1,0},{2,3},{3,2},{4,5},{5,4},{6,7},{7,6},{8,9},{9,8},{10,11... | collective-permute-start | bytes 49160 | tf_op jit(solution)/shard_map/ppermute | solution.py:440
  29.1 2.1 %collective-permute-start.12 = (f32[8,256]{1,0:T(8,128)S(1)}, f32[8,256]{1,0:T(8,128)S(1)}, u32[]{:S(2)}, u32[]{:S(2)}) collective-permute-start(f32[8,256]{1,0:T(8,128)S(1)} %get-tuple-element.70.refs_7_), channel_id=1, source_target_pairs={{0,8},{4,12},{8,0},{12,4},{1,9},{5,13},{9,1},{13,5},{2,10},{6,14},... | collective-permute-start | bytes 24584 | tf_op jit(solution)/shard_map/ppermute | solution.py:449
  31.2 1.3 %collective-permute-start.11 = (f32[8,256]{1,0:T(8,128)S(1)}, f32[8,256]{1,0:T(8,128)S(1)}, u32[]{:S(2)}, u32[]{:S(2)}) collective-permute-start(f32[8,256]{1,0:T(8,128)S(1)} %get-tuple-element.70.refs_7_), channel_id=1, source_target_pairs={{0,12},{4,8},{8,4},{12,0},{1,13},{5,9},{9,5},{13,1},{2,14},{6,10},... | collective-permute-start | bytes 24584 | tf_op jit(solution)/shard_map/ppermute | solution.py:440
  32.5 4.5 %shard_map.148 = (f32[8,64,256]{2,1,0:T(8,128)S(1)}, f32[256,128]{1,0:T(8,128)S(1)}) custom-call(f32[10,64,256]{2,1,0:T(8,128)S(1)} %get-tuple-element.67.refs_0_, bf16[64,128]{1,0:T(8,128)(2,1)S(1)} %collective-permute-done.8.refs_1_, bf16[64,128]{1,0:T(8,128)(2,1)S(1)} %collective-permute-done.9.refs_2_, f32[4,4,64,256]{3,2,1,0:T(8,128)S(1)} %get-tuple-element.50.refs_3_, ...), custom_call_target="tpu_custom_call" | custom-call | flops 4831838208 | tf_op jit(solution)/shard_map/pallas_call | solution.py:51
  37.1 0.9 %shard_map.149 = (f32[8,64,256]{2,1,0:T(8,128)S(1)}, bf16[64,128]{1,0:T(8,128)(2,1)S(1)}, f32[8,256]{1,0:T(8,128)S(1)}) custom-call(f32[8,64,256]{2,1,0:T(8,128)S(1)} %get-tuple-element.69.refs_0_, f32[8,1024]{1,0:T(8,128)S(1)} %get-tuple-element.61.refs_1_, f32[5,256,128]{2,1,0:T(8,128)S(1)} %get-tuple-element.47.refs_1_.refs_10_.refs_0_.refs_2_, ...), custom_call_target="tpu_custom_call" | custom-call | tf_op jit(solution)/shard_map/pallas_call | solution.py:51
  38.0 0.6 collective-permute-start.14
  38.6 1.1 %collective-permute-start.13 = (bf16[64,128]{1,0:T(8,128)(2,1)S(1)}, bf16[64,128]{1,0:T(8,128)(2,1)S(1)}, u32[]{:S(2)}, u32[]{:S(2)}) collective-permute-start(bf16[64,128]{1,0:T(8,128)(2,1)S(1)} %get-tuple-element.73), channel_id=1, source_target_pairs={{0,1},{1,0},{2,3},{3,2},{4,5},{5,4},{6,7},{7,6},{8,9},{9,8},{10,11... | collective-permute-start | bytes 49160 | tf_op jit(solution)/shard_map/ppermute | solution.py:440
  39.7 3.0 %collective-permute-start.17 = (f32[8,256]{1,0:T(8,128)S(1)}, f32[8,256]{1,0:T(8,128)S(1)}, u32[]{:S(2)}, u32[]{:S(2)}) collective-permute-start(f32[8,256]{1,0:T(8,128)S(1)} %get-tuple-element.75.refs_7_), channel_id=1, source_target_pairs={{0,8},{4,12},{8,0},{12,4},{1,9},{5,13},{9,1},{13,5},{2,10},{6,14},... | collective-permute-start | bytes 24584 | tf_op jit(solution)/shard_map/ppermute | solution.py:449
  42.7 1.4 %collective-permute-start.16 = (f32[8,256]{1,0:T(8,128)S(1)}, f32[8,256]{1,0:T(8,128)S(1)}, u32[]{:S(2)}, u32[]{:S(2)}) collective-permute-start(f32[8,256]{1,0:T(8,128)S(1)} %get-tuple-element.75.refs_7_), channel_id=1, source_target_pairs={{0,12},{4,8},{8,4},{12,0},{1,13},{5,9},{9,5},{13,1},{2,14},{6,10},... | collective-permute-start | bytes 24584 | tf_op jit(solution)/shard_map/ppermute | solution.py:440
  44.0 3.8 %shard_map.150 = (f32[6,64,256]{2,1,0:T(8,128)S(1)}, f32[256,128]{1,0:T(8,128)S(1)}) custom-call(f32[8,64,256]{2,1,0:T(8,128)S(1)} %get-tuple-element.72.refs_0_, bf16[64,128]{1,0:T(8,128)(2,1)S(1)} %collective-permute-done.13.refs_1_, bf16[64,128]{1,0:T(8,128)(2,1)S(1)} %collective-permute-done.14.refs_2_, f32[4,4,64,256]{3,2,1,0:T(8,128)S(1)} %get-tuple-element.50.refs_3_, ...), custom_call_target="tpu_custom_call" | custom-call | flops 3623878656 | tf_op jit(solution)/shard_map/pallas_call | solution.py:51
  48.1 0.8 %shard_map.151 = (f32[6,64,256]{2,1,0:T(8,128)S(1)}, bf16[64,128]{1,0:T(8,128)(2,1)S(1)}, f32[8,256]{1,0:T(8,128)S(1)}) custom-call(f32[6,64,256]{2,1,0:T(8,128)S(1)} %get-tuple-element.74.refs_0_, f32[8,1024]{1,0:T(8,128)S(1)} %get-tuple-element.61.refs_1_, f32[5,256,128]{2,1,0:T(8,128)S(1)} %get-tuple-element.47.refs_1_.refs_10_.refs_0_.refs_2_, ...), custom_call_target="tpu_custom_call" | custom-call | tf_op jit(solution)/shard_map/pallas_call | solution.py:51
  49.0 0.6 %collective-permute-start.18 = (bf16[64,128]{1,0:T(8,128)(2,1)S(1)}, bf16[64,128]{1,0:T(8,128)(2,1)S(1)}, u32[]{:S(2)}, u32[]{:S(2)}) collective-permute-start(bf16[64,128]{1,0:T(8,128)(2,1)S(1)} %get-tuple-element.78), channel_id=1, source_target_pairs={{0,1},{1,0},{2,3},{3,2},{4,5},{5,4},{6,7},{7,6},{8,9},{9,8},{10,11... | collective-permute-start | bytes 49160 | tf_op jit(solution)/shard_map/ppermute | solution.py:440
  49.7 2.8 %collective-permute-start.22 = (f32[8,256]{1,0:T(8,128)S(1)}, f32[8,256]{1,0:T(8,128)S(1)}, u32[]{:S(2)}, u32[]{:S(2)}) collective-permute-start(f32[8,256]{1,0:T(8,128)S(1)} %get-tuple-element.79.refs_7_), channel_id=1, source_target_pairs={{0,8},{4,12},{8,0},{12,4},{1,9},{5,13},{9,1},{13,5},{2,10},{6,14},... | collective-permute-start | bytes 24584 | tf_op jit(solution)/shard_map/ppermute | solution.py:449
  52.5 1.3 %collective-permute-start.21 = (f32[8,256]{1,0:T(8,128)S(1)}, f32[8,256]{1,0:T(8,128)S(1)}, u32[]{:S(2)}, u32[]{:S(2)}) collective-permute-start(f32[8,256]{1,0:T(8,128)S(1)} %get-tuple-element.79.refs_7_), channel_id=1, source_target_pairs={{0,12},{4,8},{8,4},{12,0},{1,13},{5,9},{9,5},{13,1},{2,14},{6,10},... | collective-permute-start | bytes 24584 | tf_op jit(solution)/shard_map/ppermute | solution.py:440
  53.9 2.5 %shard_map.152.refs_0_ = f32[4,64,256]{2,1,0:T(8,128)S(1)} custom-call(f32[6,64,256]{2,1,0:T(8,128)S(1)} %get-tuple-element.77.refs_0_, bf16[64,128]{1,0:T(8,128)(2,1)S(1)} %collective-permute-done.18.refs_1_, bf16[64,128]{1,0:T(8,128)(2,1)S(1)} %collective-permute-done.19.refs_2_, f32[4,4,64,256]{3,2,1,0:T(8,128)S(1)} %get-tuple-element.50.refs_3_, ...), custom_call_target="tpu_custom_call" | custom-call | flops 2415919104 | tf_op jit(solution)/shard_map/pallas_call | solution.py:51
  56.4 1.6 %collective-permute-done.21.refs_9_ = f32[8,256]{1,0:T(8,128)S(1)} collective-permute-done((f32[8,256]{1,0:T(8,128)S(1)}, f32[8,256]{1,0:T(8,128)S(1)}, u32[]{:S(2)}, u32[]{:S(2)}) %collective-permute-start.21) | collective-permute-done | bytes 8224 | tf_op jit(solution)/shard_map/ppermute | solution.py:440
  58.0 1.2 %shard_map.153 = (f32[64,4,256]{2,1,0:T(4,128)}, f32[1,256]{1,0:T(1,128)}) custom-call(f32[4,64,256]{2,1,0:T(8,128)S(1)} %shard_map.152.refs_0_, f32[8,1024]{1,0:T(8,128)S(1)} %get-tuple-element.61.refs_1_, f32[5,256,128]{2,1,0:T(8,128)S(1)} %get-tuple-element.47.refs_1_.refs_10_.refs_0_.refs_2_, bf16[256,256]{1,0:T(8,128)(2,1)S(1)} %get-tuple-element.62.refs_3_, ...), custom_call_target="tpu_custom_call" | custom-call | tf_op jit(solution)/shard_map/pallas_call | solution.py:51
  (28 shorter events, 0.6 us)
Async XLA Ops:
  2.9 11.2 %collective-permute-start = (bf16[5,64,256]{2,1,0:T(8,128)(2,1)S(1)}, bf16[5,64,256]{2,1,0:T(8,128)(2,1)S(1)}, u32[]{:S(2)}, u32[]{:S(2)}) collective-permute-start(bf16[5,64,256]{2,1,0:T(8,128)(2,1)S(1)} %get-tuple-element.43), channel_id=1, source_target_pairs={{0,4},{4,0},{8,12},{12,8},{1,5},{5,1},{9,13},{13,9},{2,6},{6,2},{1... | collective-permute-start | bytes 491528 | tf_op jit(solution)/shard_map/ppermute | solution.py:498
  6.0 8.1 %collective-permute-start.1 = (bf16[5,64,256]{2,1,0:T(8,128)(2,1)S(1)}, bf16[5,64,256]{2,1,0:T(8,128)(2,1)S(1)}, u32[]{:S(2)}, u32[]{:S(2)}) collective-permute-start(bf16[5,64,256]{2,1,0:T(8,128)(2,1)S(1)} %get-tuple-element.44), channel_id=1, source_target_pairs={{4,8},{8,4},{5,9},{9,5},{6,10},{10,6},{7,11},{11,7},{20,24},{24,20... | collective-permute-start | bytes 491528 | tf_op jit(solution)/shard_map/ppermute | solution.py:498
  6.6 7.4 %collective-permute-start.2 = (f32[8,256]{1,0:T(8,128)S(1)}, f32[8,256]{1,0:T(8,128)S(1)}, u32[]{:S(2)}, u32[]{:S(2)}) collective-permute-start(f32[8,256]{1,0:T(8,128)S(1)} %get-tuple-element.45.msg.refs_1_.refs_7_), channel_id=1, source_target_pairs={{0,12},{12,0},{1,13},{13,1},{2,14},{14,2},{3,15},{15,3},{16,28},{2... | collective-permute-start | bytes 24584 | tf_op jit(solution)/shard_map/ppermute | solution.py:499
  14.5 4.5 %collective-permute-start.4 = (bf16[64,128]{1,0:T(8,128)(2,1)S(1)}, bf16[64,128]{1,0:T(8,128)(2,1)S(1)}, u32[]{:S(2)}, u32[]{:S(2)}) collective-permute-start(bf16[64,128]{1,0:T(8,128)(2,1)S(1)} %get-tuple-element.49), channel_id=1, source_target_pairs={{0,3},{1,2},{2,1},{3,0},{4,7},{5,6},{6,5},{7,4},{8,11},{9,10},{10,... | collective-permute-start | bytes 49160 | tf_op jit(solution)/shard_map/ppermute | solution.py:440
  14.5 4.5 %collective-permute-start.3 = (bf16[64,128]{1,0:T(8,128)(2,1)S(1)}, bf16[64,128]{1,0:T(8,128)(2,1)S(1)}, u32[]{:S(2)}, u32[]{:S(2)}) collective-permute-start(bf16[64,128]{1,0:T(8,128)(2,1)S(1)} %get-tuple-element.49), channel_id=1, source_target_pairs={{0,1},{1,0},{2,3},{3,2},{4,5},{5,4},{6,7},{7,6},{8,9},{9,8},{10,11... | collective-permute-start | bytes 49160 | tf_op jit(solution)/shard_map/ppermute | solution.py:440
  16.1 10.6 %collective-permute-start.5 = (f32[8,256]{1,0:T(8,128)S(1)}, f32[8,256]{1,0:T(8,128)S(1)}, u32[]{:S(2)}, u32[]{:S(2)}) collective-permute-start(f32[8,256]{1,0:T(8,128)S(1)} %get-tuple-element.45.msg.refs_1_.refs_7_), channel_id=1, source_target_pairs={{0,8},{4,12},{8,0},{12,4},{1,9},{5,13},{9,1},{13,5},{2,10},{6,14},... | collective-permute-start | bytes 24584 | tf_op jit(solution)/shard_map/ppermute | solution.py:449
  18.3 8.5 %collective-permute-start.7 = (bf16[6,64,256]{2,1,0:T(8,128)(2,1)S(1)}, bf16[6,64,256]{2,1,0:T(8,128)(2,1)S(1)}, u32[]{:S(2)}, u32[]{:S(2)}) collective-permute-start(bf16[6,64,256]{2,1,0:T(8,128)(2,1)S(1)} %get-tuple-element.60), channel_id=1, source_target_pairs={{4,8},{8,4},{5,9},{9,5},{6,10},{10,6},{7,11},{11,7},{20,24},{24,20... | collective-permute-start | bytes 589832 | tf_op jit(solution)/shard_map/ppermute | solution.py:521
  19.0 7.8 %collective-permute-start.6 = (bf16[6,64,256]{2,1,0:T(8,128)(2,1)S(1)}, bf16[6,64,256]{2,1,0:T(8,128)(2,1)S(1)}, u32[]{:S(2)}, u32[]{:S(2)}) collective-permute-start(bf16[6,64,256]{2,1,0:T(8,128)(2,1)S(1)} %shard_map.145), channel_id=1, source_target_pairs={{0,4},{4,0},{8,12},{12,8},{1,5},{5,1},{9,13},{13,9},{2,6},{6,2},{1... | collective-permute-start | bytes 589832 | tf_op jit(solution)/shard_map/ppermute | solution.py:521
  28.3 4.2 %collective-permute-start.9 = (bf16[64,128]{1,0:T(8,128)(2,1)S(1)}, bf16[64,128]{1,0:T(8,128)(2,1)S(1)}, u32[]{:S(2)}, u32[]{:S(2)}) collective-permute-start(bf16[64,128]{1,0:T(8,128)(2,1)S(1)} %get-tuple-element.68), channel_id=1, source_target_pairs={{0,3},{1,2},{2,1},{3,0},{4,7},{5,6},{6,5},{7,4},{8,11},{9,10},{10,... | collective-permute-start | bytes 49160 | tf_op jit(solution)/shard_map/ppermute | solution.py:440
  28.4 4.1 %collective-permute-start.8 = (bf16[64,128]{1,0:T(8,128)(2,1)S(1)}, bf16[64,128]{1,0:T(8,128)(2,1)S(1)}, u32[]{:S(2)}, u32[]{:S(2)}) collective-permute-start(bf16[64,128]{1,0:T(8,128)(2,1)S(1)} %get-tuple-element.68), channel_id=1, source_target_pairs={{0,1},{1,0},{2,3},{3,2},{4,5},{5,4},{6,7},{7,6},{8,9},{9,8},{10,11... | collective-permute-start | bytes 49160 | tf_op jit(solution)/shard_map/ppermute | solution.py:440
  29.1 8.0 %collective-permute-start.12 = (f32[8,256]{1,0:T(8,128)S(1)}, f32[8,256]{1,0:T(8,128)S(1)}, u32[]{:S(2)}, u32[]{:S(2)}) collective-permute-start(f32[8,256]{1,0:T(8,128)S(1)} %get-tuple-element.70.refs_7_), channel_id=1, source_target_pairs={{0,8},{4,12},{8,0},{12,4},{1,9},{5,13},{9,1},{13,5},{2,10},{6,14},... | collective-permute-start | bytes 24584 | tf_op jit(solution)/shard_map/ppermute | solution.py:449
  31.2 5.9 %collective-permute-start.11 = (f32[8,256]{1,0:T(8,128)S(1)}, f32[8,256]{1,0:T(8,128)S(1)}, u32[]{:S(2)}, u32[]{:S(2)}) collective-permute-start(f32[8,256]{1,0:T(8,128)S(1)} %get-tuple-element.70.refs_7_), channel_id=1, source_target_pairs={{0,12},{4,8},{8,4},{12,0},{1,13},{5,9},{9,5},{13,1},{2,14},{6,10},... | collective-permute-start | bytes 24584 | tf_op jit(solution)/shard_map/ppermute | solution.py:440
  32.5 4.6 %collective-permute-start.10 = (f32[8,256]{1,0:T(8,128)S(1)}, f32[8,256]{1,0:T(8,128)S(1)}, u32[]{:S(2)}, u32[]{:S(2)}) collective-permute-start(f32[8,256]{1,0:T(8,128)S(1)} %get-tuple-element.70.refs_7_), channel_id=1, source_target_pairs={{0,4},{4,0},{8,12},{12,8},{1,5},{5,1},{9,13},{13,9},{2,6},{6,2},{1... | collective-permute-start | bytes 24584 | tf_op jit(solution)/shard_map/ppermute | solution.py:440
  38.0 6.0 %collective-permute-start.14 = (bf16[64,128]{1,0:T(8,128)(2,1)S(1)}, bf16[64,128]{1,0:T(8,128)(2,1)S(1)}, u32[]{:S(2)}, u32[]{:S(2)}) collective-permute-start(bf16[64,128]{1,0:T(8,128)(2,1)S(1)} %get-tuple-element.73), channel_id=1, source_target_pairs={{0,3},{1,2},{2,1},{3,0},{4,7},{5,6},{6,5},{7,4},{8,11},{9,10},{10,... | collective-permute-start | bytes 49160 | tf_op jit(solution)/shard_map/ppermute | solution.py:440
  38.6 5.5 %collective-permute-start.13 = (bf16[64,128]{1,0:T(8,128)(2,1)S(1)}, bf16[64,128]{1,0:T(8,128)(2,1)S(1)}, u32[]{:S(2)}, u32[]{:S(2)}) collective-permute-start(bf16[64,128]{1,0:T(8,128)(2,1)S(1)} %get-tuple-element.73), channel_id=1, source_target_pairs={{0,1},{1,0},{2,3},{3,2},{4,5},{5,4},{6,7},{7,6},{8,9},{9,8},{10,11... | collective-permute-start | bytes 49160 | tf_op jit(solution)/shard_map/ppermute | solution.py:440
  39.7 8.2 %collective-permute-start.17 = (f32[8,256]{1,0:T(8,128)S(1)}, f32[8,256]{1,0:T(8,128)S(1)}, u32[]{:S(2)}, u32[]{:S(2)}) collective-permute-start(f32[8,256]{1,0:T(8,128)S(1)} %get-tuple-element.75.refs_7_), channel_id=1, source_target_pairs={{0,8},{4,12},{8,0},{12,4},{1,9},{5,13},{9,1},{13,5},{2,10},{6,14},... | collective-permute-start | bytes 24584 | tf_op jit(solution)/shard_map/ppermute | solution.py:449
  42.7 5.4 %collective-permute-start.16 = (f32[8,256]{1,0:T(8,128)S(1)}, f32[8,256]{1,0:T(8,128)S(1)}, u32[]{:S(2)}, u32[]{:S(2)}) collective-permute-start(f32[8,256]{1,0:T(8,128)S(1)} %get-tuple-element.75.refs_7_), channel_id=1, source_target_pairs={{0,12},{4,8},{8,4},{12,0},{1,13},{5,9},{9,5},{13,1},{2,14},{6,10},... | collective-permute-start | bytes 24584 | tf_op jit(solution)/shard_map/ppermute | solution.py:440
  44.0 4.1 %collective-permute-start.15 = (f32[8,256]{1,0:T(8,128)S(1)}, f32[8,256]{1,0:T(8,128)S(1)}, u32[]{:S(2)}, u32[]{:S(2)}) collective-permute-start(f32[8,256]{1,0:T(8,128)S(1)} %get-tuple-element.75.refs_7_), channel_id=1, source_target_pairs={{0,4},{4,0},{8,12},{12,8},{1,5},{5,1},{9,13},{13,9},{2,6},{6,2},{1... | collective-permute-start | bytes 24584 | tf_op jit(solution)/shard_map/ppermute | solution.py:440
  49.0 4.9 %collective-permute-start.19 = (bf16[64,128]{1,0:T(8,128)(2,1)S(1)}, bf16[64,128]{1,0:T(8,128)(2,1)S(1)}, u32[]{:S(2)}, u32[]{:S(2)}) collective-permute-start(bf16[64,128]{1,0:T(8,128)(2,1)S(1)} %get-tuple-element.78), channel_id=1, source_target_pairs={{0,3},{1,2},{2,1},{3,0},{4,7},{5,6},{6,5},{7,4},{8,11},{9,10},{10,... | collective-permute-start | bytes 49160 | tf_op jit(solution)/shard_map/ppermute | solution.py:440
  49.0 4.8 %collective-permute-start.18 = (bf16[64,128]{1,0:T(8,128)(2,1)S(1)}, bf16[64,128]{1,0:T(8,128)(2,1)S(1)}, u32[]{:S(2)}, u32[]{:S(2)}) collective-permute-start(bf16[64,128]{1,0:T(8,128)(2,1)S(1)} %get-tuple-element.78), channel_id=1, source_target_pairs={{0,1},{1,0},{2,3},{3,2},{4,5},{5,4},{6,7},{7,6},{8,9},{9,8},{10,11... | collective-permute-start | bytes 49160 | tf_op jit(solution)/shard_map/ppermute | solution.py:440
  49.7 6.7 %collective-permute-start.22 = (f32[8,256]{1,0:T(8,128)S(1)}, f32[8,256]{1,0:T(8,128)S(1)}, u32[]{:S(2)}, u32[]{:S(2)}) collective-permute-start(f32[8,256]{1,0:T(8,128)S(1)} %get-tuple-element.79.refs_7_), channel_id=1, source_target_pairs={{0,8},{4,12},{8,0},{12,4},{1,9},{5,13},{9,1},{13,5},{2,10},{6,14},... | collective-permute-start | bytes 24584 | tf_op jit(solution)/shard_map/ppermute | solution.py:449
  52.5 5.4 %collective-permute-start.21 = (f32[8,256]{1,0:T(8,128)S(1)}, f32[8,256]{1,0:T(8,128)S(1)}, u32[]{:S(2)}, u32[]{:S(2)}) collective-permute-start(f32[8,256]{1,0:T(8,128)S(1)} %get-tuple-element.79.refs_7_), channel_id=1, source_target_pairs={{0,12},{4,8},{8,4},{12,0},{1,13},{5,9},{9,5},{13,1},{2,14},{6,10},... | collective-permute-start | bytes 24584 | tf_op jit(solution)/shard_map/ppermute | solution.py:440
  53.9 4.1 %collective-permute-start.20 = (f32[8,256]{1,0:T(8,128)S(1)}, f32[8,256]{1,0:T(8,128)S(1)}, u32[]{:S(2)}, u32[]{:S(2)}) collective-permute-start(f32[8,256]{1,0:T(8,128)S(1)} %get-tuple-element.79.refs_7_), channel_id=1, source_target_pairs={{0,4},{4,0},{8,12},{12,8},{1,5},{5,1},{9,13},{13,9},{2,6},{6,2},{1... | collective-permute-start | bytes 24584 | tf_op jit(solution)/shard_map/ppermute | solution.py:440

commit v4 on v3

v4 whole, which is shorter than its diff:
```python
import functools
import math

import jax
import jax.numpy as jnp
from jax import lax
from jax.experimental import pallas as pl
from jax.experimental.pallas import tpu as pltpu
from jax.sharding import PartitionSpec as P

F32 = jnp.float32
BF16 = jnp.bfloat16
REACH = 2
LANES = 128
PIECES = 3

noise_levels = (1.0, 0.6, 0.3)
obs_precision = 4.0
step_factor = 0.1


def sub_steps():
    steps = []
    for section in range(2):
        upper, lower = noise_levels[section], noise_levels[section + 1]
        spread = upper * upper - lower * lower
        steps.append((upper, spread, math.sqrt(spread)))
        factor = step_factor * lower * lower
        steps.append((lower, factor, math.sqrt(2.0 * factor)))
    return steps


STEPS = sub_steps()


def shrink(level):
    return 1.0 / math.sqrt(1.0 + level * level)


def vmem_call(kernel, outs, *args, scratch=(), scalars=0, hbm_in=0, hbm_out=False, flops=0):
    args = list(args)
    for i in range(scalars, len(args)):
        place = pltpu.HBM if i < scalars + hbm_in else pltpu.VMEM
        args[i] = pltpu.with_memory_space_constraint(args[i], place)
    smem = pl.BlockSpec(memory_space=pltpu.SMEM)
    vmem, hbm = pl.BlockSpec(memory_space=pltpu.VMEM), pl.BlockSpec(memory_space=pltpu.HBM)
    out_type = jax.ShapeDtypeStruct if hbm_out else pltpu.VMEM
    return pl.pallas_call(
        kernel,
        out_shape=[out_type(shape, dtype) for shape, dtype in outs],
        in_specs=[smem] * scalars + [hbm] * hbm_in + [vmem] * (len(args) - scalars - hbm_in),
        out_specs=[hbm if hbm_out else vmem] * len(outs),
        scratch_shapes=list(scratch),
        cost_estimate=pl.CostEstimate(flops=flops, bytes_accessed=0, transcendentals=0),
        compiler_params=pltpu.CompilerParams(vmem_limit_bytes=48 * 2**20),
    )(*args)


def dot(a, b, ca=1, cb=0):
    return lax.dot_general(a, b, (((ca,), (cb,)), ((), ())), preferred_element_type=F32)


def pieces(x, count):
    out = []
    for _ in range(count):
        part = x.astype(BF16)
        out.append(part)
        x = x - part.astype(F32)
    return out


def iota(shape, dim):
    return lax.broadcasted_iota(jnp.int32, shape, dim).astype(F32)


def silu_norm(values, gain):
    power = jnp.mean(values * values, axis=1, keepdims=True)
    half = values * (0.5 * lax.rsqrt(power + 1e-06)) * gain
    return half + half * jnp.tanh(half)


def row_order(latb):
    return [*range(1, latb - 1), 0, latb - 1]


def is_even(axis):
    return lax.rem(lax.axis_index(axis), 2) == 0


def start_all(pairs, sems):
    copies = [
        pltpu.make_async_copy(source, target, sems.at[i])
        for i, (source, target) in enumerate(pairs)
    ]
    for copy in copies:
        copy.start()
    return copies


def rows_of(source, target):
    return [(source.at[:, r, :], target.at[r]) for r in range(target.shape[0])]


def later_kernel(noise_in, *refs):
    half = (len(refs) - 2) // 2
    noise, sems = refs[half], refs[-1]
    pairs = []
    for k in range(noise.shape[0]):
        pairs += rows_of(noise_in.at[k], noise.at[k])
    pairs += list(zip(refs[:half], refs[half + 1 : -1]))
    for copy in start_all(pairs, sems):
        copy.wait()


def stage_kernel(*refs, slots):
    live, prior_in, entries_in = refs[0], refs[1], refs[2:7]
    prior, edge, entry_msg, *entries, sems = refs[7:]
    latb, _, lond = prior.shape
    copies = start_all(rows_of(prior_in, prior) + list(zip(entries_in, entries)), sems)
    for copy in copies[:latb]:
        copy.wait()
    edges_into(edge, prior, latb, STEPS[0][0])
    for copy in copies[latb:]:
        copy.wait()
    cell, owner, slot, weight, station = entries
    count = cell.shape[1]
    cells = cell[...]
    lon = cells % lond
    row = (cells // lond) % latb
    row = jnp.where(row == 0, latb - 2, jnp.where(row == latb - 1, row, row - 1))
    variable = cells // (lond * latb)
    rv = row * prior.shape[1] + variable
    key = owner[...] * slots + slot[...]
    alive = lax.broadcasted_iota(jnp.int32, (1, count), 1) < live[0]
    weights = jnp.where(alive, weight[...], 0.0)
    mine = lax.axis_index("band") * slots + lax.broadcasted_iota(jnp.int32, (1, count), 1)
    entry_msg[0:1] = key.astype(F32)
    entry_msg[1:2] = rv.astype(F32)
    entry_msg[2:3] = lon.astype(F32)
    entry_msg[3:4] = weights
    entry_msg[4:5] = station[...]
    entry_msg[5:6] = mine.astype(F32)
    entry_msg[6:8] = jnp.zeros((2, count), F32)
    columns = jnp.transpose(entry_msg[...])
    rv_col, lon_col = columns[:, 1:2], columns[:, 2:3]
    one_hot = jnp.where(rv_col == iota((count, latb * prior.shape[1]), 1), 1.0, 0.0).astype(BF16)
    current = jnp.concatenate([prior[r] for r in row_order(latb)], axis=0)
    picked = sum(dot(one_hot, part) for part in pieces(current, 2))
    at = jnp.sum(jnp.where(lon_col == iota((count, lond), 1), picked, 0.0), axis=1, keepdims=True)
    eye = iota((count, count), 0) == iota((count, count), 1)
    entry_msg[6:7] = weights * jnp.sum(jnp.where(eye, at, 0.0), axis=0, keepdims=True)


def edges_into(edge_ref, state, rows, level):
    lane = lax.broadcasted_iota(jnp.int32, (1, LANES), 1)
    variables, width = state.shape[1:]
    edge = jnp.zeros((variables, LANES), F32)
    for r in range(rows):
        slab = state[r]
        edge = jnp.where(lane == r, slab[:, 0:1], edge)
        edge = jnp.where(lane == rows + r, slab[:, width - 1 : width], edge)
    edge = (edge * shrink(level)).astype(BF16).astype(F32)
    edge_ref[...] = jnp.transpose(jnp.concatenate([edge] * (LANES // variables), axis=0))[0 : 2 * rows]


def from_sides(axis, from_a, from_b):
    even = is_even(axis)
    return jnp.where(even, from_b, from_a), jnp.where(even, from_a, from_b)


def message_kernel(state, edge_a, edge_b, value, msg_a, msg_b, *, level, used):
    latb, variables, width = state.shape
    even = is_even("band")
    left, right = from_sides("wt", edge_a[...], edge_b[...])
    parts = [part.astype(F32) for part in pieces(value[0:used], PIECES)]
    padding = jnp.zeros((msg_a.shape[0] - variables - PIECES * used - 1, width), F32)
    below, above = [
        jnp.concatenate(
            [
                state[r] * shrink(level),
                *parts,
                jnp.concatenate([left[latb + r : latb + r + 1], right[r : r + 1]], axis=1),
                padding,
            ],
            axis=0,
        )
        for r in (0, latb - 1)
    ]
    msg_a[...] = jnp.where(even, above, below).astype(BF16)
    msg_b[...] = jnp.where(even, below, above).astype(BF16)


def unpacked(msg, variables, used):
    packed = msg[variables:].astype(F32)
    return sum(packed[used * i : used * (i + 1)] for i in range(PIECES))


def wide(column):
    return jnp.broadcast_to(column, (column.shape[0], LANES))


def one_hot(position, shape, dim):
    return jnp.where(position == iota(shape, dim), 1.0, 0.0).astype(BF16)


def own_kernel(msg, cols, pick, spread, *, variables, latb, lond):
    count = msg.shape[1]
    high = latb * variables
    col = jnp.transpose(msg[...])
    cols[0] = wide(col[:, 0:1])
    cols[1] = wide(col[:, 3:4])
    cols[2] = wide(col[:, 2:3])
    cols[3] = wide(col[:, 1:2] * lond + col[:, 2:3])
    cols[4] = wide(col[:, 5:6])
    pick[...] = one_hot(col[:, 1:2], (count, high), 1)
    spread[...] = one_hot(msg[1:2], (high, count), 0)


def tables_kernel(cols, own, msg_a, msg_b, *refs, variables):
    far, keys, seen = refs[:-2], refs[-2], refs[-1]
    count = own.shape[1]
    msgs = [own[...], *(unpacked(msg, variables, 8) for msg in (msg_a, msg_b))]
    msgs += [ref[...] for ref in far]
    for i, msg in enumerate(msgs):
        keys[:, i * count : (i + 1) * count] = msg
    acc = jnp.zeros((count, LANES), F32)
    for msg in msgs:
        for part in range(count // LANES):
            at = slice(part * LANES, (part + 1) * LANES)
            acc = acc + jnp.where(cols[0] == msg[5:6, at], msg[4:5, at], 0.0)
    seen[...] = wide(jnp.sum(acc, axis=1, keepdims=True))


def first_row(scaled, before, after, lift, gain):
    lifted = dot(scaled, lift[...], 0, 0)
    first = silu_norm(lifted, gain[...])
    width = first.shape[0]
    sub = lax.broadcasted_iota(jnp.int32, (width, 1), 0)
    shifted = [
        jnp.where(sub == 0, before, pltpu.roll(first, 1, 0)),
        first,
        jnp.where(sub == width - 1, after, pltpu.roll(first, width - 1, 0)),
    ]
    return lifted, [x.astype(BF16) for x in shifted]


def picked_from(rows, pick, lon, parts):
    variables, width = rows[0].shape
    for r, row in enumerate(rows):
        for j, part in enumerate(pieces(row, 2)):
            parts[r * variables : (r + 1) * variables, j * width : (j + 1) * width] = part
    picked = dot(pick, parts[...])
    picked = picked[:, 0:width] + picked[:, width:]
    lons = jnp.concatenate([lon] * (width // LANES), axis=1)
    spots = jnp.where(lons == iota((lon.shape[0], width), 1), picked, 0.0)
    return wide(jnp.sum(spots, axis=1, keepdims=True))


def inner_kernel(
    state, edge_a, edge_b, noise, lift, conv, head, gain_1, gain_2, pick, cols,
    middle, sums, at_entries, firsts, total, parts, *, step,
):
    level, drift, kick = STEPS[step]
    latb, _, width = state.shape
    channels = lift.shape[1]
    variables = state.shape[1]
    left, right = from_sides("wt", edge_a[...], edge_b[...])
    edge = jnp.concatenate([left, right], axis=0)[:, 0:variables].astype(BF16)
    edge = silu_norm(dot(edge, lift[...]), gain_1[...])
    for r in range(latb):
        lifted, shifted = first_row(
            (state[r] * shrink(level)).astype(BF16),
            edge[latb + r : latb + r + 1], edge[2 * latb + r : 2 * latb + r + 1], lift, gain_1,
        )
        here = slice(r * width, (r + 1) * width)
        total[here] = lifted
        for q in range(3):
            firsts[here, q * channels : (q + 1) * channels] = shifted[q]
    deep = 3 * channels
    inside = (latb - 1) * width
    total[...] += dot(firsts[...], conv[deep : 2 * deep])
    total[width:] += dot(firsts[0:inside], conv[0:deep])
    total[0:inside] += dot(firsts[width:], conv[2 * deep :])
    sums[0] = total[0:width]
    sums[1] = total[inside:]
    for r in range(1, latb - 1):
        second = silu_norm(total[r * width : (r + 1) * width], gain_2[...]).astype(BF16)
        score = dot(head[...], second, 1, 1)
        middle[r - 1] = state[r] + (drift / level) * score + kick * noise[step, r]
    done = (latb - 2) * variables
    at_entries[...] = picked_from(
        [middle[r] for r in range(latb - 2)], pick[:, 0:done], cols[2], parts
    )


def outer_kernel(*refs, step, gather, used):
    state, msg_a, msg_b, middle, sums, noise, lift, conv, head, gain_1, gain_2 = refs[:11]
    if gather:
        pick, cols, before, target, at_entries, parts = refs[11:]
    else:
        (target,) = refs[11:]
    level, drift, kick = STEPS[step]
    latb, variables, width = state.shape
    channels = lift.shape[1]
    deep = 3 * channels
    band = lax.axis_index("band")
    beyond = (band == 0, band == lax.axis_size("band") - 1)
    near = from_sides("band", msg_a[...].astype(F32), msg_b[...].astype(F32))
    spot = variables + PIECES * used
    corner = [side[spot : spot + 1, at : at + LANES] for side in near for at in (0, LANES)]
    corner = jnp.concatenate([*corner, jnp.zeros((12, LANES), F32)], axis=0)
    edge = silu_norm(dot(corner[:, 0:variables].astype(BF16), lift[...]), gain_1[...])
    for r in range(1, latb - 1):
        target[r] = middle[r - 1]
    for i, (r, p) in enumerate(((0, 0), (latb - 1, 2))):
        _, shifted = first_row(
            near[i][0:variables].astype(BF16),
            edge[2 * i : 2 * i + 1], edge[2 * i + 1 : 2 * i + 2], lift, gain_1,
        )
        first = jnp.where(beyond[i], 0.0, jnp.concatenate(shifted, axis=1).astype(F32)).astype(BF16)
        mixed = sums[i] + dot(first, conv[p * deep : (p + 1) * deep])
        second = silu_norm(mixed, gain_2[...]).astype(BF16)
        score = dot(head[...], second, 1, 1)
        target[r] = state[r] + (drift / level) * score + kick * noise[step, r]
    if gather:
        done = (latb - 2) * variables
        at_entries[...] = before[...] + picked_from(
            [target[0], target[latb - 1]], pick[:, done:], cols[2], parts
        )


def matching(key, keys, values):
    count = values[0].shape[1]
    acc = jnp.zeros(key.shape, F32)
    for i, row in enumerate(values):
        for part in range(count // LANES):
            at = slice(part * LANES, (part + 1) * LANES)
            known = keys[0:1, i * count + part * LANES : i * count + (part + 1) * LANES]
            acc = acc + jnp.where(key == known, row[:, at], 0.0)
    return jnp.sum(acc, axis=1, keepdims=True)


def update_kernel(*refs, step, n_far, value_row, used):
    target, keys, cols, spread, seen, own, msg_a, msg_b = refs[:8]
    far, rest = refs[8 : 8 + n_far], refs[8 + n_far :]
    here = slice(value_row, value_row + 1)
    count = own.shape[1]
    latb, variables, width = target.shape
    values = [own[here], *(unpacked(msg, variables, used)[here] for msg in (msg_a, msg_b))]
    values += [ref[here] for ref in far]
    found = matching(cols[0], keys, values)
    mine = obs_precision * STEPS[step][1] * cols[1] * (seen[...] - found)
    lon = jnp.concatenate([cols[2]] * (width // LANES), axis=1)
    tall = jnp.concatenate([mine] * (width // LANES), axis=1)
    spots = jnp.where(lon == iota((count, width), 1), tall, 0.0)
    both = dot(spread[...], jnp.concatenate(pieces(spots, 2), axis=1))
    added = both[:, 0:width] + both[:, width:]
    place = {r: slice(i * variables, (i + 1) * variables) for i, r in enumerate(row_order(latb))}
    eye = iota((count, count), 0) == iota((count, count), 1)
    if step == len(STEPS) - 1:
        state_out, innov_out, state, innov, sems = rest
        for r in range(latb):
            state[r] = target[r] + added[place[r]]
        copies = [
            pltpu.make_async_copy(state.at[r], state_out.at[:, r, :], sems.at[r])
            for r in range(latb)
        ]
        for copy in copies:
            copy.start()
        found = matching(cols[4], keys, values)
        innov[...] = keys[4:5, 0:count] - jnp.sum(jnp.where(eye, found, 0.0), axis=0, keepdims=True)
        copies.append(pltpu.make_async_copy(innov, innov_out, sems.at[latb]))
        copies[-1].start()
        for copy in copies:
            copy.wait()
        return
    at_entries, state, edge, value = rest
    for r in range(latb):
        state[r] = target[r] + added[place[r]]
    edges_into(edge, state, latb, STEPS[step + 1][0])
    row_cell = keys[1:2, 0:count] * width + keys[2:3, 0:count]
    cell = jnp.concatenate([cols[3]] * (count // LANES), axis=1)
    tall = jnp.concatenate([mine] * (count // LANES), axis=1)
    before = jnp.concatenate([at_entries[...]] * (count // LANES), axis=1)
    total = jnp.where(cell == row_cell, tall, 0.0) + jnp.where(eye, before, 0.0)
    value[...] = jnp.broadcast_to(
        keys[3:4, 0:count] * jnp.sum(total, axis=0, keepdims=True), value.shape
    )


def swaps(count):
    first = [(i, i ^ 1) for i in range(count)]
    other = [(i, (i - 1) % count if i % 2 == 0 else (i + 1) % count) for i in range(count)]
    return first, other


def from_neighbours(block, axis):
    return [lax.ppermute(block, axis, route) for route in swaps(lax.axis_size(axis))]


def from_far(block):
    count = lax.axis_size("band")
    reach = min(2 * REACH, count)
    found = []
    for distance in sorted({d % count for d in range(-reach, reach + 1)} - {0, 1, count - 1}):
        route = [(i, (i + distance) % count) for i in range(count)]
        found.append(lax.ppermute(block, "band", route))
    return found


def per_device(
    prior_state, langevin_noise, station_values, entry_cell, entry_owner, entry_slot,
    entry_weight, live_counts, lift_weight, conv_weight, head_weight, first_gain, second_gain,
):
    variables, latb, lond = prior_state.shape
    count = entry_cell.shape[0]
    slots = station_values.shape[0]
    channels = lift_weight.shape[1]
    taps = conv_weight.reshape(-1, channels)
    gain_1, gain_2 = first_gain.reshape(1, -1), second_gain.reshape(1, -1)

    def row(a):
        return a.reshape(1, -1)

    entries = [
        row(entry_cell), row(entry_owner), row(entry_slot), row(entry_weight), row(station_values),
    ]
    state, edge, value = vmem_call(
        functools.partial(stage_kernel, slots=slots),
        [((latb, variables, lond), F32), ((2 * latb, LANES), F32), ((8, count), F32)],
        live_counts, prior_state, *entries,
        scalars=1,
        hbm_in=1 + len(entries),
        scratch=[pltpu.VMEM(a.shape, a.dtype) for a in entries]
        + [pltpu.SemaphoreType.DMA((latb + len(entries),))],
    )
    weights = [taps, lift_weight, head_weight.T, gain_1, gain_2]
    noise, taps, *weights = vmem_call(
        later_kernel,
        [((len(STEPS), latb, variables, lond), F32)] + [(a.shape, a.dtype) for a in weights],
        langevin_noise, *weights,
        hbm_in=1 + len(weights),
        scratch=[pltpu.SemaphoreType.DMA((len(STEPS) * latb + len(weights),))],
    )
    weights = [weights[0], taps, *weights[1:]]
    high = latb * variables
    cols, pick, spread = vmem_call(
        functools.partial(own_kernel, variables=variables, latb=latb, lond=lond),
        [((5, count, LANES), F32), ((count, high), BF16), ((high, count), BF16)],
        value,
    )
    route_a, route_b = swaps(lax.axis_size("band"))
    whole = ((latb, variables, lond), F32)
    value_row, used = 6, 8
    for step in range(len(STEPS)):
        last = step == len(STEPS) - 1
        far = from_far(value)
        edges = from_neighbours(edge, "wt")
        msg_a, msg_b = vmem_call(
            functools.partial(message_kernel, level=STEPS[step][0], used=used),
            [((variables + (32 if used == 8 else 16), lond), BF16)] * 2,
            state, *edges, value,
        )
        msg_a, msg_b = lax.ppermute(msg_a, "band", route_a), lax.ppermute(msg_b, "band", route_b)
        middle, sums, before = vmem_call(
            functools.partial(inner_kernel, step=step),
            [
                ((latb - 2, variables, lond), F32),
                ((2, lond, channels), F32),
                ((count, LANES), F32),
            ],
            state, *edges, noise, *weights, pick, cols,
            scratch=[
                pltpu.VMEM((latb * lond, 3 * channels), BF16),
                pltpu.VMEM((latb * lond, channels), F32),
                pltpu.VMEM(((latb - 2) * variables, 2 * lond), BF16),
            ],
            flops=4 * latb * lond * taps.size,
        )
        if step == 0:
            keys, seen = vmem_call(
                functools.partial(tables_kernel, variables=variables),
                [((8, (3 + len(far)) * count), F32), ((count, LANES), F32)],
                cols, value, msg_a, msg_b, *far,
            )
        outer_in = [state, msg_a, msg_b, middle, sums, noise, *weights]
        outer = functools.partial(outer_kernel, step=step, gather=not last, used=used)
        update = functools.partial(
            update_kernel, step=step, n_far=len(far), value_row=value_row, used=used
        )
        given = [keys, cols, spread, seen, value, msg_a, msg_b, *far]
        if last:
            (target,) = vmem_call(outer, [whole], *outer_in)
            state, innov = vmem_call(
                update, [((variables, latb, lond), F32), ((1, count), F32)], target, *given,
                hbm_out=True,
                scratch=[
                    pltpu.VMEM(*whole),
                    pltpu.VMEM((1, count), F32),
                    pltpu.SemaphoreType.DMA((latb + 1,)),
                ],
            )
            return state, innov.reshape(-1)
        target, at_entries = vmem_call(
            outer, [whole, ((count, LANES), F32)], *outer_in, pick, cols, before,
            scratch=[pltpu.VMEM((2 * variables, 2 * lond), BF16)],
        )
        state, edge, value = vmem_call(
            update, [whole, ((2 * latb, LANES), F32), ((8, count), F32)],
            target, *given, at_entries,
        )
        value_row, used = 0, 1


def solution(mesh):
    split = P(("groups", "band", "wt"))
    in_specs = (
        P("groups", "band", "wt"),
        P(None, "groups", "band", "wt"),
        split, split, split, split, split, split,
        P(), P(), P(), P(), P(),
    )
    out_specs = (P("groups", "band", "wt"), split)
    return jax.shard_map(
        per_device, mesh=mesh, in_specs=in_specs, out_specs=out_specs, check_vma=False
    )
```

time: 59.6 us -> 58.3 us (0.978)
  starting transfers between devices: 30.3 us -> 17.2 us
  waiting for transfers between devices: 2.43 us -> 14.5 us
    ppermute x5 -> x8, waiting for transfers between devices: 0.57 us -> 8.63 us  [the longest x4 8.62 us: per_device(): lax.ppermute(msg_b, 'band', route_b)]
    ppermute x4, starting transfers between devices: 10.1 us -> 4.03 us  [from_far(): found.append(lax.ppermute(block, 'band', route))]
    ppermute x14 -> x8, waiting for transfers between devices: 1.85 us -> 5.9 us  [from_neighbours(): lax.ppermute(block, axis, route)]
    ppermute x14 -> x8, starting transfers between devices: 8.85 us -> 5.22 us  [from_neighbours(): lax.ppermute(block, axis, route)]
    ppermute x5 -> x8, starting transfers between devices: 11.4 us -> 7.9 us  [the longest x4 4.98 us: per_device(): lax.ppermute(msg_b, 'band', route_b)]
    pallas_call x14 -> x20, Pallas kernels: 24.9 us -> 24.6 us  [vmem_call(): pl.pallas_call(kernel, out_shape=[out_type(shape, dtype) for shape, dtype...]
  transfers between devices with their start and end apart: 23 -> 20, of which waited for: 3 -> 9; matrix products, arithmetic and copies ran while one was open for 0% -> 0% of each run, Pallas kernels for 31% -> 31%
where the time goes in v4:
time: 58.3 us; the launch traced here: 58.1 us
  Pallas kernels  24.6 us (42%)
  starting transfers between devices  17.2 us (30%)
  waiting for transfers between devices  14.5 us (25%)
  between operations  1.8 us (3%)
    pallas_call x20, Pallas kernels, vmem_call(): pl.pallas_call(kernel, out_shape=[out_type(shape, dtype) for shape, dtype...  24.6 us
    ppermute x4, waiting for transfers between devices, per_device(): lax.ppermute(msg_b, 'band', route_b)  8.62 us
    ppermute x8, waiting for transfers between devices, from_neighbours(): lax.ppermute(block, axis, route)  5.9 us
    ppermute x8, starting transfers between devices, from_neighbours(): lax.ppermute(block, axis, route)  5.22 us
    ppermute x4, starting transfers between devices, per_device(): lax.ppermute(msg_b, 'band', route_b)  4.98 us
    ppermute x4, starting transfers between devices, from_far(): found.append(lax.ppermute(block, 'band', route))  4.03 us
    ppermute x4, starting transfers between devices, per_device(): lax.ppermute(msg_a, 'band', route_a)  2.92 us
  transfers between devices with their start and end apart: 20, of which 9 were waited for; matrix products, arithmetic and copies ran while one was open for 0% of the time, Pallas kernels for 31%

profile of v4, /device:TPU:0, one launch (start us, length us, event | category | flops | bytes accessed | tf_op | source)
XLA Modules:
  0.0 58.1 jit_solution(8774031923016982721)
XLA Ops:
  1.3 1.8 %shard_map.140 = (f32[4,64,256]{2,1,0:T(8,128)S(1)}, f32[8,128]{1,0:T(8,128)S(1)}, f32[8,256]{1,0:T(8,128)S(1)}) custom-call(s32[1]{0:T(128)S(6)} %copy.15.refs_0_, f32[64,4,256]{2,1,0:T(4,128)} %refs_1_.2, s32[1,256]{1,0:T(1,128)} %bitcast.12, s32[1,256]{1,0:T(1,128)} %bitcast.13, s32[1,256]{1,0:T(1,128)} %bitcast.14, f32[1,256]{1,0:T(1,128)} %bitcast.15, ...), custom_call_target="tpu_custom_call" | custom-call | tf_op jit(solution)/shard_map/pallas_call | solution.py:48
  3.6 2.6 %collective-permute-start.1 = (f32[8,128]{1,0:T(8,128)S(1)}, f32[8,128]{1,0:T(8,128)S(1)}, u32[]{:S(2)}, u32[]{:S(2)}) collective-permute-start(f32[8,128]{1,0:T(8,128)S(1)} %get-tuple-element.53), channel_id=1, source_target_pairs={{0,3},{1,2},{2,1},{3,0},{4,7},{5,6},{6,5},{7,4},{8,11},{9,10},{10,... | collective-permute-start | bytes 12296 | tf_op jit(solution)/shard_map/ppermute | solution.py:398
  6.2 2.6 %collective-permute-start.4 = (f32[8,256]{1,0:T(8,128)S(1)}, f32[8,256]{1,0:T(8,128)S(1)}, u32[]{:S(2)}, u32[]{:S(2)}) collective-permute-start(f32[8,256]{1,0:T(8,128)S(1)} %get-tuple-element.54.value.msg.own.refs_5_), channel_id=1, source_target_pairs={{0,8},{4,12},{8,0},{12,4},{1,9},{5,13},{9,1},{13,5},{2,10},{6,14},... | collective-permute-start | bytes 24584 | tf_op jit(solution)/shard_map/ppermute | solution.py:407
  9.3 1.9 %shard_map.142 = (f32[4,4,64,256]{3,2,1,0:T(8,128)S(1)}, bf16[2304,256]{1,0:T(8,128)(2,1)S(1)}, bf16[64,256]{1,0:T(8,128)(2,1)S(1)}, bf16[64,256]{1,0:T(8,128)(2...) custom-call(f32[4,64,4,256]{3,2,1,0:T(4,128)} %noise_in.1, bf16[2304,256]{1,0:T(8,128)(2,1)} %bitcast.10, ...), custom_call_target="tpu_custom_call" | custom-call | tf_op jit(solution)/shard_map/pallas_call | solution.py:48
  11.3 1.6 %collective-permute-start.2 = (bf16[96,256]{1,0:T(8,128)(2,1)S(1)}, bf16[96,256]{1,0:T(8,128)(2,1)S(1)}, u32[]{:S(2)}, u32[]{:S(2)}) collective-permute-start(bf16[96,256]{1,0:T(8,128)(2,1)S(1)} %get-tuple-element.55), channel_id=1, source_target_pairs={{0,4},{4,0},{8,12},{12,8},{1,5},{5,1},{9,13},{13,9},{2,6},{6,2},{1... | collective-permute-start | bytes 147464 | tf_op jit(solution)/shard_map/ppermute | solution.py:464
  13.2 2.3 %shard_map.144 = (f32[2,64,256]{2,1,0:T(8,128)S(1)}, f32[2,256,256]{2,1,0:T(8,128)S(1)}, f32[256,128]{1,0:T(8,128)S(1)}) custom-call(f32[4,64,256]{2,1,0:T(8,128)S(1)} %get-tuple-element.52.state.refs_0_, f32[8,128]{1,0:T(8,128)S(1)} %collective-permute-done.edge_a, f32[8,128]{1,0:T(8,128)S(1)} %collective-permute-done.1.edge_b, ...), custom_call_target="tpu_custom_call" | custom-call | flops 2415919104 | tf_op jit(solution)/shard_map/pallas_call | solution.py:48
  15.5 3.4 %collective-permute-done.3.refs_2_.msg_b.refs_7_ = bf16[96,256]{1,0:T(8,128)(2,1)S(1)} collective-permute-done((bf16[96,256]{1,0:T(8,128)(2,1)S(1)}, bf16[96,256]{1,0:T(8,128)(2,1)S(1)}, u32[]{:S(2)}, u32[]{:S(2)}) %collective-permute-start.3) | collective-permute-done | bytes 49184 | tf_op jit(solution)/shard_map/ppermute | solution.py:464
  19.0 2.0 %shard_map.145 = (f32[4,64,256]{2,1,0:T(8,128)S(1)}, f32[256,128]{1,0:T(8,128)S(1)}) custom-call(f32[4,64,256]{2,1,0:T(8,128)S(1)} %get-tuple-element.52.state.refs_0_, bf16[96,256]{1,0:T(8,128)(2,1)S(1)} %collective-permute-done.2.refs_1_.msg_a.refs_6_, bf16[96,256]{1,0:T(8,128)(2,1)S(1)} %collective-permute-done.3.refs_2_.msg_b.refs_7_, ...), custom_call_target="tpu_custom_call" | custom-call | tf_op jit(solution)/shard_map/pallas_call | solution.py:48
  21.0 0.6 shard_map.147
  21.6 0.7 %collective-permute-start.6 = (f32[8,128]{1,0:T(8,128)S(1)}, f32[8,128]{1,0:T(8,128)S(1)}, u32[]{:S(2)}, u32[]{:S(2)}) collective-permute-start(f32[8,128]{1,0:T(8,128)S(1)} %get-tuple-element.74), channel_id=1, source_target_pairs={{0,3},{1,2},{2,1},{3,0},{4,7},{5,6},{6,5},{7,4},{8,11},{9,10},{10,... | collective-permute-start | bytes 12296 | tf_op jit(solution)/shard_map/ppermute | solution.py:398
  22.8 1.9 %collective-permute-done.6.edge_b = f32[8,128]{1,0:T(8,128)S(1)} collective-permute-done((f32[8,128]{1,0:T(8,128)S(1)}, f32[8,128]{1,0:T(8,128)S(1)}, u32[]{:S(2)}, u32[]{:S(2)}) %collective-permute-start.6) | collective-permute-done | bytes 4128 | tf_op jit(solution)/shard_map/ppermute | solution.py:398
  24.8 1.9 %collective-permute-start.8 = (bf16[80,256]{1,0:T(8,128)(2,1)S(1)}, bf16[80,256]{1,0:T(8,128)(2,1)S(1)}, u32[]{:S(2)}, u32[]{:S(2)}) collective-permute-start(bf16[80,256]{1,0:T(8,128)(2,1)S(1)} %get-tuple-element.77), channel_id=1, source_target_pairs={{0,12},{4,8},{8,4},{12,0},{1,13},{5,9},{9,5},{13,1},{2,14},{6,10},... | collective-permute-start | bytes 122888 | tf_op jit(solution)/shard_map/ppermute | solution.py:464
  26.8 2.3 %shard_map.149 = (f32[2,64,256]{2,1,0:T(8,128)S(1)}, f32[2,256,256]{2,1,0:T(8,128)S(1)}, f32[256,128]{1,0:T(8,128)S(1)}) custom-call(f32[4,64,256]{2,1,0:T(8,128)S(1)} %get-tuple-element.73.state.refs_0_, f32[8,128]{1,0:T(8,128)S(1)} %collective-permute-done.5.edge_a, f32[8,128]{1,0:T(8,128)S(1)} %collective-permute-done.6.edge_b, ...), custom_call_target="tpu_custom_call" | custom-call | flops 2415919104 | tf_op jit(solution)/shard_map/pallas_call | solution.py:48
  29.1 1.7 %collective-permute-done.8.refs_2_.refs_7_ = bf16[80,256]{1,0:T(8,128)(2,1)S(1)} collective-permute-done((bf16[80,256]{1,0:T(8,128)(2,1)S(1)}, bf16[80,256]{1,0:T(8,128)(2,1)S(1)}, u32[]{:S(2)}, u32[]{:S(2)}) %collective-permute-start.8) | collective-permute-done | bytes 40992 | tf_op jit(solution)/shard_map/ppermute | solution.py:464
  30.8 2.0 %shard_map.150 = (f32[4,64,256]{2,1,0:T(8,128)S(1)}, f32[256,128]{1,0:T(8,128)S(1)}) custom-call(f32[4,64,256]{2,1,0:T(8,128)S(1)} %get-tuple-element.73.state.refs_0_, bf16[80,256]{1,0:T(8,128)(2,1)S(1)} %collective-permute-done.7.refs_1_.refs_6_, bf16[80,256]{1,0:T(8,128)(2,1)S(1)} %collective-permute-done.8.refs_2_.refs_7_, ...), custom_call_target="tpu_custom_call" | custom-call | tf_op jit(solution)/shard_map/pallas_call | solution.py:48
  32.7 0.6 shard_map.151
  33.4 0.7 %collective-permute-start.11 = (f32[8,128]{1,0:T(8,128)S(1)}, f32[8,128]{1,0:T(8,128)S(1)}, u32[]{:S(2)}, u32[]{:S(2)}) collective-permute-start(f32[8,128]{1,0:T(8,128)S(1)} %get-tuple-element.84), channel_id=1, source_target_pairs={{0,3},{1,2},{2,1},{3,0},{4,7},{5,6},{6,5},{7,4},{8,11},{9,10},{10,... | collective-permute-start | bytes 12296 | tf_op jit(solution)/shard_map/ppermute | solution.py:398
  34.5 1.9 %collective-permute-done.11.edge_b = f32[8,128]{1,0:T(8,128)S(1)} collective-permute-done((f32[8,128]{1,0:T(8,128)S(1)}, f32[8,128]{1,0:T(8,128)S(1)}, u32[]{:S(2)}, u32[]{:S(2)}) %collective-permute-start.11) | collective-permute-done | bytes 4128 | tf_op jit(solution)/shard_map/ppermute | solution.py:398
  36.5 1.0 %collective-permute-start.12 = (bf16[80,256]{1,0:T(8,128)(2,1)S(1)}, bf16[80,256]{1,0:T(8,128)(2,1)S(1)}, u32[]{:S(2)}, u32[]{:S(2)}) collective-permute-start(bf16[80,256]{1,0:T(8,128)(2,1)S(1)} %get-tuple-element.86), channel_id=1, source_target_pairs={{0,4},{4,0},{8,12},{12,8},{1,5},{5,1},{9,13},{13,9},{2,6},{6,2},{1... | collective-permute-start | bytes 122888 | tf_op jit(solution)/shard_map/ppermute | solution.py:464
  37.5 1.0 %collective-permute-start.13 = (bf16[80,256]{1,0:T(8,128)(2,1)S(1)}, bf16[80,256]{1,0:T(8,128)(2,1)S(1)}, u32[]{:S(2)}, u32[]{:S(2)}) collective-permute-start(bf16[80,256]{1,0:T(8,128)(2,1)S(1)} %get-tuple-element.87), channel_id=1, source_target_pairs={{0,12},{4,8},{8,4},{12,0},{1,13},{5,9},{9,5},{13,1},{2,14},{6,10},... | collective-permute-start | bytes 122888 | tf_op jit(solution)/shard_map/ppermute | solution.py:464
  38.5 2.3 %shard_map.153 = (f32[2,64,256]{2,1,0:T(8,128)S(1)}, f32[2,256,256]{2,1,0:T(8,128)S(1)}, f32[256,128]{1,0:T(8,128)S(1)}) custom-call(f32[4,64,256]{2,1,0:T(8,128)S(1)} %get-tuple-element.83.state.refs_0_, f32[8,128]{1,0:T(8,128)S(1)} %collective-permute-done.10.edge_a, f32[8,128]{1,0:T(8,128)S(1)} %collective-permute-done.11.edge_b, ...), custom_call_target="tpu_custom_call" | custom-call | flops 2415919104 | tf_op jit(solution)/shard_map/pallas_call | solution.py:48
  40.8 2.5 %collective-permute-done.13.refs_2_.refs_7_ = bf16[80,256]{1,0:T(8,128)(2,1)S(1)} collective-permute-done((bf16[80,256]{1,0:T(8,128)(2,1)S(1)}, bf16[80,256]{1,0:T(8,128)(2,1)S(1)}, u32[]{:S(2)}, u32[]{:S(2)}) %collective-permute-start.13) | collective-permute-done | bytes 40992 | tf_op jit(solution)/shard_map/ppermute | solution.py:464
  43.3 2.0 %shard_map.154 = (f32[4,64,256]{2,1,0:T(8,128)S(1)}, f32[256,128]{1,0:T(8,128)S(1)}) custom-call(f32[4,64,256]{2,1,0:T(8,128)S(1)} %get-tuple-element.83.state.refs_0_, bf16[80,256]{1,0:T(8,128)(2,1)S(1)} %collective-permute-done.12.refs_1_.refs_6_, bf16[80,256]{1,0:T(8,128)(2,1)S(1)} %collective-permute-done.13.refs_2_.refs_7_, ...), custom_call_target="tpu_custom_call" | custom-call | tf_op jit(solution)/shard_map/pallas_call | solution.py:48
  45.4 0.6 shard_map.155
  46.1 0.7 %collective-permute-start.16 = (f32[8,128]{1,0:T(8,128)S(1)}, f32[8,128]{1,0:T(8,128)S(1)}, u32[]{:S(2)}, u32[]{:S(2)}) collective-permute-start(f32[8,128]{1,0:T(8,128)S(1)} %get-tuple-element.94), channel_id=1, source_target_pairs={{0,3},{1,2},{2,1},{3,0},{4,7},{5,6},{6,5},{7,4},{8,11},{9,10},{10,... | collective-permute-start | bytes 12296 | tf_op jit(solution)/shard_map/ppermute | solution.py:398
  46.7 1.4 %collective-permute-start.19 = (f32[8,256]{1,0:T(8,128)S(1)}, f32[8,256]{1,0:T(8,128)S(1)}, u32[]{:S(2)}, u32[]{:S(2)}) collective-permute-start(f32[8,256]{1,0:T(8,128)S(1)} %get-tuple-element.95.value.refs_5_), channel_id=1, source_target_pairs={{0,8},{4,12},{8,0},{12,4},{1,9},{5,13},{9,1},{13,5},{2,10},{6,14},... | collective-permute-start | bytes 24584 | tf_op jit(solution)/shard_map/ppermute | solution.py:407
  48.2 1.0 %collective-permute-done.16.edge_b = f32[8,128]{1,0:T(8,128)S(1)} collective-permute-done((f32[8,128]{1,0:T(8,128)S(1)}, f32[8,128]{1,0:T(8,128)S(1)}, u32[]{:S(2)}, u32[]{:S(2)}) %collective-permute-start.16) | collective-permute-done | bytes 4128 | tf_op jit(solution)/shard_map/ppermute | solution.py:398
  49.4 1.8 %collective-permute-start.18 = (bf16[80,256]{1,0:T(8,128)(2,1)S(1)}, bf16[80,256]{1,0:T(8,128)(2,1)S(1)}, u32[]{:S(2)}, u32[]{:S(2)}) collective-permute-start(bf16[80,256]{1,0:T(8,128)(2,1)S(1)} %get-tuple-element.97), channel_id=1, source_target_pairs={{0,12},{4,8},{8,4},{12,0},{1,13},{5,9},{9,5},{13,1},{2,14},{6,10},... | collective-permute-start | bytes 122888 | tf_op jit(solution)/shard_map/ppermute | solution.py:464
  51.2 2.9 %shard_map.157 = (f32[2,64,256]{2,1,0:T(8,128)S(1)}, f32[2,256,256]{2,1,0:T(8,128)S(1)}, f32[256,128]{1,0:T(8,128)}) custom-call(f32[4,64,256]{2,1,0:T(8,128)S(1)} %get-tuple-element.93.state.refs_0_, f32[8,128]{1,0:T(8,128)S(1)} %collective-permute-done.15.edge_a, f32[8,128]{1,0:T(8,128)S(1)} %collective-permute-done.16.edge_b, ...), custom_call_target="tpu_custom_call" | custom-call | flops 2415919104 | tf_op jit(solution)/shard_map/pallas_call | solution.py:48
  54.2 1.1 %collective-permute-done.18.refs_2_.refs_7_ = bf16[80,256]{1,0:T(8,128)(2,1)S(1)} collective-permute-done((bf16[80,256]{1,0:T(8,128)(2,1)S(1)}, bf16[80,256]{1,0:T(8,128)(2,1)S(1)}, u32[]{:S(2)}, u32[]{:S(2)}) %collective-permute-start.18) | collective-permute-done | bytes 40992 | tf_op jit(solution)/shard_map/ppermute | solution.py:464
  55.3 1.4 %shard_map.158.refs_0_ = f32[4,64,256]{2,1,0:T(8,128)S(1)} custom-call(f32[4,64,256]{2,1,0:T(8,128)S(1)} %get-tuple-element.93.state.refs_0_, bf16[80,256]{1,0:T(8,128)(2,1)S(1)} %collective-permute-done.17.refs_1_.refs_6_, bf16[80,256]{1,0:T(8,128)(2,1)S(1)} %collective-permute-done.18.refs_2_.refs_7_, f32[2,64,256]{2,1,0:T(8,128)S(1)} %get-tuple-element.98.refs_3_, ...), custom_call_target="tpu_custom_call" | custom-call | tf_op jit(solution)/shard_map/pallas_call | solution.py:48
  56.7 1.2 %shard_map.159 = (f32[64,4,256]{2,1,0:T(4,128)}, f32[1,256]{1,0:T(1,128)}) custom-call(f32[4,64,256]{2,1,0:T(8,128)S(1)} %shard_map.158.refs_0_, f32[8,1024]{1,0:T(8,128)S(1)} %get-tuple-element.69.refs_1_, f32[5,256,128]{2,1,0:T(8,128)S(1)} %get-tuple-element.64.cols.refs_12_.refs_2_, bf16[256,256]{1,0:T(8,128)(2,1)S(1)} %get-tuple-element.70.refs_3_, ...), custom_call_target="tpu_custom_call" | custom-call | tf_op jit(solution)/shard_map/pallas_call | solution.py:48
  (28 shorter events, 3.0 us)
Async XLA Ops:
  3.1 8.2 %collective-permute-start = (f32[8,128]{1,0:T(8,128)S(1)}, f32[8,128]{1,0:T(8,128)S(1)}, u32[]{:S(2)}, u32[]{:S(2)}) collective-permute-start(f32[8,128]{1,0:T(8,128)S(1)} %get-tuple-element.53), channel_id=1, source_target_pairs={{0,1},{1,0},{2,3},{3,2},{4,5},{5,4},{6,7},{7,6},{8,9},{9,8},{10,11... | collective-permute-start | bytes 12296 | tf_op jit(solution)/shard_map/ppermute | solution.py:398
  3.6 7.7 %collective-permute-start.1 = (f32[8,128]{1,0:T(8,128)S(1)}, f32[8,128]{1,0:T(8,128)S(1)}, u32[]{:S(2)}, u32[]{:S(2)}) collective-permute-start(f32[8,128]{1,0:T(8,128)S(1)} %get-tuple-element.53), channel_id=1, source_target_pairs={{0,3},{1,2},{2,1},{3,0},{4,7},{5,6},{6,5},{7,4},{8,11},{9,10},{10,... | collective-permute-start | bytes 12296 | tf_op jit(solution)/shard_map/ppermute | solution.py:398
  6.2 9.3 %collective-permute-start.4 = (f32[8,256]{1,0:T(8,128)S(1)}, f32[8,256]{1,0:T(8,128)S(1)}, u32[]{:S(2)}, u32[]{:S(2)}) collective-permute-start(f32[8,256]{1,0:T(8,128)S(1)} %get-tuple-element.54.value.msg.own.refs_5_), channel_id=1, source_target_pairs={{0,8},{4,12},{8,0},{12,4},{1,9},{5,13},{9,1},{13,5},{2,10},{6,14},... | collective-permute-start | bytes 24584 | tf_op jit(solution)/shard_map/ppermute | solution.py:407
  11.3 4.2 %collective-permute-start.2 = (bf16[96,256]{1,0:T(8,128)(2,1)S(1)}, bf16[96,256]{1,0:T(8,128)(2,1)S(1)}, u32[]{:S(2)}, u32[]{:S(2)}) collective-permute-start(bf16[96,256]{1,0:T(8,128)(2,1)S(1)} %get-tuple-element.55), channel_id=1, source_target_pairs={{0,4},{4,0},{8,12},{12,8},{1,5},{5,1},{9,13},{13,9},{2,6},{6,2},{1... | collective-permute-start | bytes 147464 | tf_op jit(solution)/shard_map/ppermute | solution.py:464
  13.0 5.9 %collective-permute-start.3 = (bf16[96,256]{1,0:T(8,128)(2,1)S(1)}, bf16[96,256]{1,0:T(8,128)(2,1)S(1)}, u32[]{:S(2)}, u32[]{:S(2)}) collective-permute-start(bf16[96,256]{1,0:T(8,128)(2,1)S(1)} %get-tuple-element.56), channel_id=1, source_target_pairs={{0,12},{4,8},{8,4},{12,0},{1,13},{5,9},{9,5},{13,1},{2,14},{6,10},... | collective-permute-start | bytes 147464 | tf_op jit(solution)/shard_map/ppermute | solution.py:464
  21.6 1.2 %collective-permute-start.5 = (f32[8,128]{1,0:T(8,128)S(1)}, f32[8,128]{1,0:T(8,128)S(1)}, u32[]{:S(2)}, u32[]{:S(2)}) collective-permute-start(f32[8,128]{1,0:T(8,128)S(1)} %get-tuple-element.74), channel_id=1, source_target_pairs={{0,1},{1,0},{2,3},{3,2},{4,5},{5,4},{6,7},{7,6},{8,9},{9,8},{10,11... | collective-permute-start | bytes 12296 | tf_op jit(solution)/shard_map/ppermute | solution.py:398
  21.6 3.1 %collective-permute-start.6 = (f32[8,128]{1,0:T(8,128)S(1)}, f32[8,128]{1,0:T(8,128)S(1)}, u32[]{:S(2)}, u32[]{:S(2)}) collective-permute-start(f32[8,128]{1,0:T(8,128)S(1)} %get-tuple-element.74), channel_id=1, source_target_pairs={{0,3},{1,2},{2,1},{3,0},{4,7},{5,6},{6,5},{7,4},{8,11},{9,10},{10,... | collective-permute-start | bytes 12296 | tf_op jit(solution)/shard_map/ppermute | solution.py:398
  22.3 10.5 %collective-permute-start.9 = (f32[8,256]{1,0:T(8,128)S(1)}, f32[8,256]{1,0:T(8,128)S(1)}, u32[]{:S(2)}, u32[]{:S(2)}) collective-permute-start(f32[8,256]{1,0:T(8,128)S(1)} %get-tuple-element.75.value.refs_5_), channel_id=1, source_target_pairs={{0,8},{4,12},{8,0},{12,4},{1,9},{5,13},{9,1},{13,5},{2,10},{6,14},... | collective-permute-start | bytes 24584 | tf_op jit(solution)/shard_map/ppermute | solution.py:407
  24.8 4.3 %collective-permute-start.7 = (bf16[80,256]{1,0:T(8,128)(2,1)S(1)}, bf16[80,256]{1,0:T(8,128)(2,1)S(1)}, u32[]{:S(2)}, u32[]{:S(2)}) collective-permute-start(bf16[80,256]{1,0:T(8,128)(2,1)S(1)} %get-tuple-element.76), channel_id=1, source_target_pairs={{0,4},{4,0},{8,12},{12,8},{1,5},{5,1},{9,13},{13,9},{2,6},{6,2},{1... | collective-permute-start | bytes 122888 | tf_op jit(solution)/shard_map/ppermute | solution.py:464
  24.8 5.9 %collective-permute-start.8 = (bf16[80,256]{1,0:T(8,128)(2,1)S(1)}, bf16[80,256]{1,0:T(8,128)(2,1)S(1)}, u32[]{:S(2)}, u32[]{:S(2)}) collective-permute-start(bf16[80,256]{1,0:T(8,128)(2,1)S(1)} %get-tuple-element.77), channel_id=1, source_target_pairs={{0,12},{4,8},{8,4},{12,0},{1,13},{5,9},{9,5},{13,1},{2,14},{6,10},... | collective-permute-start | bytes 122888 | tf_op jit(solution)/shard_map/ppermute | solution.py:464
  33.3 1.2 %collective-permute-start.10 = (f32[8,128]{1,0:T(8,128)S(1)}, f32[8,128]{1,0:T(8,128)S(1)}, u32[]{:S(2)}, u32[]{:S(2)}) collective-permute-start(f32[8,128]{1,0:T(8,128)S(1)} %get-tuple-element.84), channel_id=1, source_target_pairs={{0,1},{1,0},{2,3},{3,2},{4,5},{5,4},{6,7},{7,6},{8,9},{9,8},{10,11... | collective-permute-start | bytes 12296 | tf_op jit(solution)/shard_map/ppermute | solution.py:398
  33.4 3.1 %collective-permute-start.11 = (f32[8,128]{1,0:T(8,128)S(1)}, f32[8,128]{1,0:T(8,128)S(1)}, u32[]{:S(2)}, u32[]{:S(2)}) collective-permute-start(f32[8,128]{1,0:T(8,128)S(1)} %get-tuple-element.84), channel_id=1, source_target_pairs={{0,3},{1,2},{2,1},{3,0},{4,7},{5,6},{6,5},{7,4},{8,11},{9,10},{10,... | collective-permute-start | bytes 12296 | tf_op jit(solution)/shard_map/ppermute | solution.py:398
  34.0 11.4 %collective-permute-start.14 = (f32[8,256]{1,0:T(8,128)S(1)}, f32[8,256]{1,0:T(8,128)S(1)}, u32[]{:S(2)}, u32[]{:S(2)}) collective-permute-start(f32[8,256]{1,0:T(8,128)S(1)} %get-tuple-element.85.value.refs_5_), channel_id=1, source_target_pairs={{0,8},{4,12},{8,0},{12,4},{1,9},{5,13},{9,1},{13,5},{2,10},{6,14},... | collective-permute-start | bytes 24584 | tf_op jit(solution)/shard_map/ppermute | solution.py:407
  36.5 4.3 %collective-permute-start.12 = (bf16[80,256]{1,0:T(8,128)(2,1)S(1)}, bf16[80,256]{1,0:T(8,128)(2,1)S(1)}, u32[]{:S(2)}, u32[]{:S(2)}) collective-permute-start(bf16[80,256]{1,0:T(8,128)(2,1)S(1)} %get-tuple-element.86), channel_id=1, source_target_pairs={{0,4},{4,0},{8,12},{12,8},{1,5},{5,1},{9,13},{13,9},{2,6},{6,2},{1... | collective-permute-start | bytes 122888 | tf_op jit(solution)/shard_map/ppermute | solution.py:464
  37.5 5.8 %collective-permute-start.13 = (bf16[80,256]{1,0:T(8,128)(2,1)S(1)}, bf16[80,256]{1,0:T(8,128)(2,1)S(1)}, u32[]{:S(2)}, u32[]{:S(2)}) collective-permute-start(bf16[80,256]{1,0:T(8,128)(2,1)S(1)} %get-tuple-element.87), channel_id=1, source_target_pairs={{0,12},{4,8},{8,4},{12,0},{1,13},{5,9},{9,5},{13,1},{2,14},{6,10},... | collective-permute-start | bytes 122888 | tf_op jit(solution)/shard_map/ppermute | solution.py:464
  46.0 2.1 %collective-permute-start.15 = (f32[8,128]{1,0:T(8,128)S(1)}, f32[8,128]{1,0:T(8,128)S(1)}, u32[]{:S(2)}, u32[]{:S(2)}) collective-permute-start(f32[8,128]{1,0:T(8,128)S(1)} %get-tuple-element.94), channel_id=1, source_target_pairs={{0,1},{1,0},{2,3},{3,2},{4,5},{5,4},{6,7},{7,6},{8,9},{9,8},{10,11... | collective-permute-start | bytes 12296 | tf_op jit(solution)/shard_map/ppermute | solution.py:398
  46.1 3.1 %collective-permute-start.16 = (f32[8,128]{1,0:T(8,128)S(1)}, f32[8,128]{1,0:T(8,128)S(1)}, u32[]{:S(2)}, u32[]{:S(2)}) collective-permute-start(f32[8,128]{1,0:T(8,128)S(1)} %get-tuple-element.94), channel_id=1, source_target_pairs={{0,3},{1,2},{2,1},{3,0},{4,7},{5,6},{6,5},{7,4},{8,11},{9,10},{10,... | collective-permute-start | bytes 12296 | tf_op jit(solution)/shard_map/ppermute | solution.py:398
  46.7 10.0 %collective-permute-start.19 = (f32[8,256]{1,0:T(8,128)S(1)}, f32[8,256]{1,0:T(8,128)S(1)}, u32[]{:S(2)}, u32[]{:S(2)}) collective-permute-start(f32[8,256]{1,0:T(8,128)S(1)} %get-tuple-element.95.value.refs_5_), channel_id=1, source_target_pairs={{0,8},{4,12},{8,0},{12,4},{1,9},{5,13},{9,1},{13,5},{2,10},{6,14},... | collective-permute-start | bytes 24584 | tf_op jit(solution)/shard_map/ppermute | solution.py:407
  49.2 5.0 %collective-permute-start.17 = (bf16[80,256]{1,0:T(8,128)(2,1)S(1)}, bf16[80,256]{1,0:T(8,128)(2,1)S(1)}, u32[]{:S(2)}, u32[]{:S(2)}) collective-permute-start(bf16[80,256]{1,0:T(8,128)(2,1)S(1)} %get-tuple-element.96), channel_id=1, source_target_pairs={{0,4},{4,0},{8,12},{12,8},{1,5},{5,1},{9,13},{13,9},{2,6},{6,2},{1... | collective-permute-start | bytes 122888 | tf_op jit(solution)/shard_map/ppermute | solution.py:464
  49.4 5.8 %collective-permute-start.18 = (bf16[80,256]{1,0:T(8,128)(2,1)S(1)}, bf16[80,256]{1,0:T(8,128)(2,1)S(1)}, u32[]{:S(2)}, u32[]{:S(2)}) collective-permute-start(bf16[80,256]{1,0:T(8,128)(2,1)S(1)} %get-tuple-element.97), channel_id=1, source_target_pairs={{0,12},{4,8},{8,4},{12,0},{1,13},{5,9},{9,5},{13,1},{2,14},{6,10},... | collective-permute-start | bytes 122888 | tf_op jit(solution)/shard_map/ppermute | solution.py:464

commit v5 on v4

--- a/solution.py
+++ b/solution.py
@@ -244,21 +244,9 @@
     return lifted, [x.astype(BF16) for x in shifted]
 
 
-def picked_from(rows, pick, lon, parts):
-    variables, width = rows[0].shape
-    for r, row in enumerate(rows):
-        for j, part in enumerate(pieces(row, 2)):
-            parts[r * variables : (r + 1) * variables, j * width : (j + 1) * width] = part
-    picked = dot(pick, parts[...])
-    picked = picked[:, 0:width] + picked[:, width:]
-    lons = jnp.concatenate([lon] * (width // LANES), axis=1)
-    spots = jnp.where(lons == iota((lon.shape[0], width), 1), picked, 0.0)
-    return wide(jnp.sum(spots, axis=1, keepdims=True))
-
-
 def inner_kernel(
-    state, edge_a, edge_b, noise, lift, conv, head, gain_1, gain_2, pick, cols,
-    middle, sums, at_entries, firsts, total, parts, *, step,
+    state, edge_a, edge_b, noise, lift, conv, head, gain_1, gain_2,
+    middle, sums, firsts, total, *, step,
 ):
     level, drift, kick = STEPS[step]
     latb, _, width = state.shape
@@ -287,46 +275,22 @@
         second = silu_norm(total[r * width : (r + 1) * width], gain_2[...]).astype(BF16)
         score = dot(head[...], second, 1, 1)
         middle[r - 1] = state[r] + (drift / level) * score + kick * noise[step, r]
-    done = (latb - 2) * variables
-    at_entries[...] = picked_from(
-        [middle[r] for r in range(latb - 2)], pick[:, 0:done], cols[2], parts
-    )
-
-
-def outer_kernel(*refs, step, gather, used):
-    state, msg_a, msg_b, middle, sums, noise, lift, conv, head, gain_1, gain_2 = refs[:11]
-    if gather:
-        pick, cols, before, target, at_entries, parts = refs[11:]
-    else:
-        (target,) = refs[11:]
-    level, drift, kick = STEPS[step]
+
+
+def value_kernel(state, keys, cols, pick, value, parts):
     latb, variables, width = state.shape
-    channels = lift.shape[1]
-    deep = 3 * channels
-    band = lax.axis_index("band")
-    beyond = (band == 0, band == lax.axis_size("band") - 1)
-    near = from_sides("band", msg_a[...].astype(F32), msg_b[...].astype(F32))
-    spot = variables + PIECES * used
-    corner = [side[spot : spot + 1, at : at + LANES] for side in near for at in (0, LANES)]
-    corner = jnp.concatenate([*corner, jnp.zeros((12, LANES), F32)], axis=0)
-    edge = silu_norm(dot(corner[:, 0:variables].astype(BF16), lift[...]), gain_1[...])
-    for r in range(1, latb - 1):
-        target[r] = middle[r - 1]
-    for i, (r, p) in enumerate(((0, 0), (latb - 1, 2))):
-        _, shifted = first_row(
-            near[i][0:variables].astype(BF16),
-            edge[2 * i : 2 * i + 1], edge[2 * i + 1 : 2 * i + 2], lift, gain_1,
-        )
-        first = jnp.where(beyond[i], 0.0, jnp.concatenate(shifted, axis=1).astype(F32)).astype(BF16)
-        mixed = sums[i] + dot(first, conv[p * deep : (p + 1) * deep])
-        second = silu_norm(mixed, gain_2[...]).astype(BF16)
-        score = dot(head[...], second, 1, 1)
-        target[r] = state[r] + (drift / level) * score + kick * noise[step, r]
-    if gather:
-        done = (latb - 2) * variables
-        at_entries[...] = before[...] + picked_from(
-            [target[0], target[latb - 1]], pick[:, done:], cols[2], parts
-        )
+    count = pick.shape[0]
+    for i, r in enumerate(row_order(latb)):
+        for j, part in enumerate(pieces(state[r], 2)):
+            parts[i * variables : (i + 1) * variables, j * width : (j + 1) * width] = part
+    picked = dot(pick[...], parts[...])
+    picked = picked[:, 0:width] + picked[:, width:]
+    lon = jnp.concatenate([cols[2]] * (width // LANES), axis=1)
+    spots = jnp.where(lon == iota((count, width), 1), picked, 0.0)
+    at = jnp.sum(spots, axis=1, keepdims=True)
+    eye = iota((count, count), 0) == iota((count, count), 1)
+    row = keys[3:4, 0:count] * jnp.sum(jnp.where(eye, at, 0.0), axis=0, keepdims=True)
+    value[...] = jnp.broadcast_to(row, value.shape)
 
 
 def matching(key, keys, values):
@@ -341,51 +305,64 @@
 
 
 def update_kernel(*refs, step, n_far, value_row, used):
-    target, keys, cols, spread, seen, own, msg_a, msg_b = refs[:8]
-    far, rest = refs[8 : 8 + n_far], refs[8 + n_far :]
+    state, middle, sums, noise, lift, conv, head, gain_1, gain_2 = refs[:9]
+    keys, cols, spread, seen, own, msg_a, msg_b = refs[9:16]
+    far, rest = refs[16 : 16 + n_far], refs[16 + n_far :]
+    level, drift, kick = STEPS[step]
+    latb, variables, width = state.shape
+    deep = 3 * lift.shape[1]
+    count = own.shape[1]
+
+    near = from_sides("band", msg_a[...].astype(F32), msg_b[...].astype(F32))
+    spot = variables + PIECES * used
+    corner = [side[spot : spot + 1, at : at + LANES] for side in near for at in (0, LANES)]
+    corner = jnp.concatenate([*corner, jnp.zeros((12, LANES), F32)], axis=0)
+    edge = silu_norm(dot(corner[:, 0:variables].astype(BF16), lift[...]), gain_1[...])
+
     here = slice(value_row, value_row + 1)
-    count = own.shape[1]
-    latb, variables, width = target.shape
     values = [own[here], *(unpacked(msg, variables, used)[here] for msg in (msg_a, msg_b))]
     values += [ref[here] for ref in far]
     found = matching(cols[0], keys, values)
-    mine = obs_precision * STEPS[step][1] * cols[1] * (seen[...] - found)
+    mine = obs_precision * drift * cols[1] * (seen[...] - found)
     lon = jnp.concatenate([cols[2]] * (width // LANES), axis=1)
     tall = jnp.concatenate([mine] * (width // LANES), axis=1)
     spots = jnp.where(lon == iota((count, width), 1), tall, 0.0)
     both = dot(spread[...], jnp.concatenate(pieces(spots, 2), axis=1))
     added = both[:, 0:width] + both[:, width:]
     place = {r: slice(i * variables, (i + 1) * variables) for i, r in enumerate(row_order(latb))}
+    moved = {r: middle[r - 1] + added[place[r]] for r in range(1, latb - 1)}
+
+    band = lax.axis_index("band")
+    beyond = (band == 0, band == lax.axis_size("band") - 1)
+    for i, (r, p) in enumerate(((0, 0), (latb - 1, 2))):
+        _, shifted = first_row(
+            near[i][0:variables].astype(BF16),
+            edge[2 * i : 2 * i + 1], edge[2 * i + 1 : 2 * i + 2], lift, gain_1,
+        )
+        first = jnp.where(beyond[i], 0.0, jnp.concatenate(shifted, axis=1).astype(F32)).astype(BF16)
+        mixed = sums[i] + dot(first, conv[p * deep : (p + 1) * deep])
+        second = silu_norm(mixed, gain_2[...]).astype(BF16)
+        score = dot(head[...], second, 1, 1)
+        moved[r] = state[r] + (drift / level) * score + kick * noise[step, r] + added[place[r]]
+
+    if step < len(STEPS) - 1:
+        after, border = rest
+        for r in range(latb):
+            after[r] = moved[r]
+        edges_into(border, after, latb, STEPS[step + 1][0])
+        return
+    state_out, innov_out, after, innov, sems = rest
+    found = matching(cols[4], keys, values)
     eye = iota((count, count), 0) == iota((count, count), 1)
-    if step == len(STEPS) - 1:
-        state_out, innov_out, state, innov, sems = rest
-        for r in range(latb):
-            state[r] = target[r] + added[place[r]]
-        copies = [
-            pltpu.make_async_copy(state.at[r], state_out.at[:, r, :], sems.at[r])
-            for r in range(latb)
-        ]
-        for copy in copies:
-            copy.start()
-        found = matching(cols[4], keys, values)
-        innov[...] = keys[4:5, 0:count] - jnp.sum(jnp.where(eye, found, 0.0), axis=0, keepdims=True)
-        copies.append(pltpu.make_async_copy(innov, innov_out, sems.at[latb]))
+    innov[...] = keys[4:5, 0:count] - jnp.sum(jnp.where(eye, found, 0.0), axis=0, keepdims=True)
+    copies = [pltpu.make_async_copy(innov, innov_out, sems.at[latb])]
+    copies[0].start()
+    for r in row_order(latb):
+        after[r] = moved[r]
+        copies.append(pltpu.make_async_copy(after.at[r], state_out.at[:, r, :], sems.at[r]))
         copies[-1].start()
-        for copy in copies:
-            copy.wait()
-        return
-    at_entries, state, edge, value = rest
-    for r in range(latb):
-        state[r] = target[r] + added[place[r]]
-    edges_into(edge, state, latb, STEPS[step + 1][0])
-    row_cell = keys[1:2, 0:count] * width + keys[2:3, 0:count]
-    cell = jnp.concatenate([cols[3]] * (count // LANES), axis=1)
-    tall = jnp.concatenate([mine] * (count // LANES), axis=1)
-    before = jnp.concatenate([at_entries[...]] * (count // LANES), axis=1)
-    total = jnp.where(cell == row_cell, tall, 0.0) + jnp.where(eye, before, 0.0)
-    value[...] = jnp.broadcast_to(
-        keys[3:4, 0:count] * jnp.sum(total, axis=0, keepdims=True), value.shape
-    )
+    for copy in copies:
+        copy.wait()
 
 
 def swaps(count):
@@ -462,18 +439,13 @@
             state, *edges, value,
         )
         msg_a, msg_b = lax.ppermute(msg_a, "band", route_a), lax.ppermute(msg_b, "band", route_b)
-        middle, sums, before = vmem_call(
+        middle, sums = vmem_call(
             functools.partial(inner_kernel, step=step),
-            [
-                ((latb - 2, variables, lond), F32),
-                ((2, lond, channels), F32),
-                ((count, LANES), F32),
-            ],
-            state, *edges, noise, *weights, pick, cols,
+            [((latb - 2, variables, lond), F32), ((2, lond, channels), F32)],
+            state, *edges, noise, *weights,
             scratch=[
                 pltpu.VMEM((latb * lond, 3 * channels), BF16),
                 pltpu.VMEM((latb * lond, channels), F32),
-                pltpu.VMEM(((latb - 2) * variables, 2 * lond), BF16),
             ],
             flops=4 * latb * lond * taps.size,
         )
@@ -483,16 +455,14 @@
                 [((8, (3 + len(far)) * count), F32), ((count, LANES), F32)],
                 cols, value, msg_a, msg_b, *far,
             )
-        outer_in = [state, msg_a, msg_b, middle, sums, noise, *weights]
-        outer = functools.partial(outer_kernel, step=step, gather=not last, used=used)
         update = functools.partial(
             update_kernel, step=step, n_far=len(far), value_row=value_row, used=used
         )
-        given = [keys, cols, spread, seen, value, msg_a, msg_b, *far]
+        given = [state, middle, sums, noise, *weights]
+        given += [keys, cols, spread, seen, value, msg_a, msg_b, *far]
         if last:
-            (target,) = vmem_call(outer, [whole], *outer_in)
             state, innov = vmem_call(
-                update, [((variables, latb, lond), F32), ((1, count), F32)], target, *given,
+                update, [((variables, latb, lond), F32), ((1, count), F32)], *given,
                 hbm_out=True,
                 scratch=[
                     pltpu.VMEM(*whole),
@@ -501,13 +471,10 @@
                 ],
             )
             return state, innov.reshape(-1)
-        target, at_entries = vmem_call(
-            outer, [whole, ((count, LANES), F32)], *outer_in, pick, cols, before,
-            scratch=[pltpu.VMEM((2 * variables, 2 * lond), BF16)],
-        )
-        state, edge, value = vmem_call(
-            update, [whole, ((2 * latb, LANES), F32), ((8, count), F32)],
-            target, *given, at_entries,
+        state, edge = vmem_call(update, [whole, ((2 * latb, LANES), F32)], *given)
+        (value,) = vmem_call(
+            value_kernel, [((8, count), F32)], state, keys, cols, pick,
+            scratch=[pltpu.VMEM((high, 2 * lond), BF16)],
         )
         value_row, used = 0, 1
 

time: 58.3 us -> 55.7 us (0.955)
  Pallas kernels: 24.6 us -> 20.8 us
  waiting for transfers between devices: 14.5 us -> 15.4 us
    pallas_call x20 -> x19, Pallas kernels: 24.6 us -> 20.8 us  [vmem_call(): pl.pallas_call(kernel, out_shape=[out_type(shape, dtype) for shape, dtype...]
    ppermute x4, starting transfers between devices: 4.03 us -> 3.06 us  [from_far(): found.append(lax.ppermute(block, 'band', route))]
    ppermute x4, starting transfers between devices: 2.92 us -> 3.77 us  [per_device(): lax.ppermute(msg_a, 'band', route_a)]
    ppermute x4, waiting for transfers between devices: 8.62 us -> 9.42 us  [per_device(): lax.ppermute(msg_b, 'band', route_b)]
  transfers between devices with their start and end apart: 20 -> 20, of which waited for: 9 -> 8; matrix products, arithmetic and copies ran while one was open for 0% -> 0% of each run, Pallas kernels for 31% -> 21%
where the time goes in v5:
time: 55.7 us; the launch traced here: 55.5 us
  Pallas kernels  20.8 us (37%)
  starting transfers between devices  17.6 us (32%)
  waiting for transfers between devices  15.4 us (28%)
  between operations  1.64 us (3%)
    pallas_call x19, Pallas kernels, vmem_call(): pl.pallas_call(kernel, out_shape=[out_type(shape, dtype) for shape, dtype...  20.8 us
    ppermute x4, waiting for transfers between devices, per_device(): lax.ppermute(msg_b, 'band', route_b)  9.42 us
    ppermute x8, waiting for transfers between devices, from_neighbours(): lax.ppermute(block, axis, route)  5.67 us
    ppermute x4, starting transfers between devices, per_device(): lax.ppermute(msg_b, 'band', route_b)  5.52 us
    ppermute x8, starting transfers between devices, from_neighbours(): lax.ppermute(block, axis, route)  5.28 us
    ppermute x4, starting transfers between devices, per_device(): lax.ppermute(msg_a, 'band', route_a)  3.77 us
    ppermute x4, starting transfers between devices, from_far(): found.append(lax.ppermute(block, 'band', route))  3.06 us
  transfers between devices with their start and end apart: 20, of which 8 were waited for; matrix products, arithmetic and copies ran while one was open for 0% of the time, Pallas kernels for 21%

profile of v5, /device:TPU:0, one launch (start us, length us, event | category | flops | bytes accessed | tf_op | source)
XLA Modules:
  0.0 55.5 jit_solution(8648893140856204873)
XLA Ops:
  1.3 1.8 %shard_map.140 = (f32[4,64,256]{2,1,0:T(8,128)S(1)}, f32[8,128]{1,0:T(8,128)S(1)}, f32[8,256]{1,0:T(8,128)S(1)}) custom-call(s32[1]{0:T(128)S(6)} %copy.15.refs_0_, f32[64,4,256]{2,1,0:T(4,128)} %refs_1_.2, s32[1,256]{1,0:T(1,128)} %bitcast.12, s32[1,256]{1,0:T(1,128)} %bitcast.13, s32[1,256]{1,0:T(1,128)} %bitcast.14, f32[1,256]{1,0:T(1,128)} %bitcast.15, ...), custom_call_target="tpu_custom_call" | custom-call | tf_op jit(solution)/shard_map/pallas_call | solution.py:48
  3.1 2.4 %collective-permute-start.1 = (f32[8,128]{1,0:T(8,128)S(1)}, f32[8,128]{1,0:T(8,128)S(1)}, u32[]{:S(2)}, u32[]{:S(2)}) collective-permute-start(f32[8,128]{1,0:T(8,128)S(1)} %get-tuple-element.41), channel_id=1, source_target_pairs={{0,3},{1,2},{2,1},{3,0},{4,7},{5,6},{6,5},{7,4},{8,11},{9,10},{10,... | collective-permute-start | bytes 12296 | tf_op jit(solution)/shard_map/ppermute | solution.py:375
  5.5 0.7 %collective-permute-start = (f32[8,128]{1,0:T(8,128)S(1)}, f32[8,128]{1,0:T(8,128)S(1)}, u32[]{:S(2)}, u32[]{:S(2)}) collective-permute-start(f32[8,128]{1,0:T(8,128)S(1)} %get-tuple-element.41), channel_id=1, source_target_pairs={{0,1},{1,0},{2,3},{3,2},{4,5},{5,4},{6,7},{7,6},{8,9},{9,8},{10,11... | collective-permute-start | bytes 12296 | tf_op jit(solution)/shard_map/ppermute | solution.py:375
  6.2 2.6 %collective-permute-start.4 = (f32[8,256]{1,0:T(8,128)S(1)}, f32[8,256]{1,0:T(8,128)S(1)}, u32[]{:S(2)}, u32[]{:S(2)}) collective-permute-start(f32[8,256]{1,0:T(8,128)S(1)} %get-tuple-element.50.msg.value.own.refs_13_), channel_id=1, source_target_pairs={{0,8},{4,12},{8,0},{12,4},{1,9},{5,13},{9,1},{13,5},{2,10},{6,14},... | collective-permute-start | bytes 24584 | tf_op jit(solution)/shard_map/ppermute | solution.py:384
  8.8 0.5 shard_map.143
  9.3 1.9 %shard_map.141 = (f32[4,4,64,256]{3,2,1,0:T(8,128)S(1)}, bf16[2304,256]{1,0:T(8,128)(2,1)S(1)}, bf16[64,256]{1,0:T(8,128)(2,1)S(1)}, bf16[64,256]{1,0:T(8,128)(2...) custom-call(f32[4,64,4,256]{3,2,1,0:T(4,128)} %noise_in.1, bf16[2304,256]{1,0:T(8,128)(2,1)} %bitcast.10, ...), custom_call_target="tpu_custom_call" | custom-call | tf_op jit(solution)/shard_map/pallas_call | solution.py:48
  11.3 1.6 %collective-permute-start.2 = (bf16[96,256]{1,0:T(8,128)(2,1)S(1)}, bf16[96,256]{1,0:T(8,128)(2,1)S(1)}, u32[]{:S(2)}, u32[]{:S(2)}) collective-permute-start(bf16[96,256]{1,0:T(8,128)(2,1)S(1)} %get-tuple-element.52), channel_id=1, source_target_pairs={{0,4},{4,0},{8,12},{12,8},{1,5},{5,1},{9,13},{13,9},{2,6},{6,2},{1... | collective-permute-start | bytes 147464 | tf_op jit(solution)/shard_map/ppermute | solution.py:441
  13.2 2.0 %shard_map.142 = (f32[2,64,256]{2,1,0:T(8,128)S(1)}, f32[2,256,256]{2,1,0:T(8,128)S(1)}) custom-call(f32[4,64,256]{2,1,0:T(8,128)S(1)} %get-tuple-element.40.state.refs_0_, f32[8,128]{1,0:T(8,128)S(1)} %collective-permute-done.edge_a, f32[8,128]{1,0:T(8,128)S(1)} %collective-permute-done.1.edge_b, f32[4,4,64,256]{3,2,1,0:T(8,128)S(1)} %get-tuple-element.42.noise.refs_3_, ...), custom_call_target="tpu_custom_call" | custom-call | flops 2415919104 | tf_op jit(solution)/shard_map/pallas_call | solution.py:48
  15.5 3.4 %collective-permute-done.3.msg_b.refs_15_ = bf16[96,256]{1,0:T(8,128)(2,1)S(1)} collective-permute-done((bf16[96,256]{1,0:T(8,128)(2,1)S(1)}, bf16[96,256]{1,0:T(8,128)(2,1)S(1)}, u32[]{:S(2)}, u32[]{:S(2)}) %collective-permute-start.3) | collective-permute-done | bytes 49184 | tf_op jit(solution)/shard_map/ppermute | solution.py:441
  19.0 1.7 %shard_map.146 = (f32[4,64,256]{2,1,0:T(8,128)S(1)}, f32[8,128]{1,0:T(8,128)S(1)}) custom-call(f32[4,64,256]{2,1,0:T(8,128)S(1)} %get-tuple-element.40.state.refs_0_, f32[2,64,256]{2,1,0:T(8,128)S(1)} %get-tuple-element.48.refs_1_, f32[2,256,256]{2,1,0:T(8,128)S(1)} %get-tuple-element.49.refs_2_, f32[4,4,64,256]{3,2,1,0:T(8,128)S(1)} %get-tuple-element.42.noise.refs_3_, ...), custom_call_target="tpu_custom_call" | custom-call | tf_op jit(solution)/shard_map/pallas_call | solution.py:48
  20.8 0.6 %collective-permute-start.5 = (f32[8,128]{1,0:T(8,128)S(1)}, f32[8,128]{1,0:T(8,128)S(1)}, u32[]{:S(2)}, u32[]{:S(2)}) collective-permute-start(f32[8,128]{1,0:T(8,128)S(1)} %get-tuple-element.58), channel_id=1, source_target_pairs={{0,1},{1,0},{2,3},{3,2},{4,5},{5,4},{6,7},{7,6},{8,9},{9,8},{10,11... | collective-permute-start | bytes 12296 | tf_op jit(solution)/shard_map/ppermute | solution.py:375
  21.4 0.3 shard_map.148.value.refs_13_
  21.8 2.0 %collective-permute-done.6.edge_b = f32[8,128]{1,0:T(8,128)S(1)} collective-permute-done((f32[8,128]{1,0:T(8,128)S(1)}, f32[8,128]{1,0:T(8,128)S(1)}, u32[]{:S(2)}, u32[]{:S(2)}) %collective-permute-start.6) | collective-permute-done | bytes 4128 | tf_op jit(solution)/shard_map/ppermute | solution.py:375
  23.9 2.4 %collective-permute-start.8 = (bf16[80,256]{1,0:T(8,128)(2,1)S(1)}, bf16[80,256]{1,0:T(8,128)(2,1)S(1)}, u32[]{:S(2)}, u32[]{:S(2)}) collective-permute-start(bf16[80,256]{1,0:T(8,128)(2,1)S(1)} %get-tuple-element.63), channel_id=1, source_target_pairs={{0,12},{4,8},{8,4},{12,0},{1,13},{5,9},{9,5},{13,1},{2,14},{6,10},... | collective-permute-start | bytes 122888 | tf_op jit(solution)/shard_map/ppermute | solution.py:441
  26.3 2.0 %shard_map.147 = (f32[2,64,256]{2,1,0:T(8,128)S(1)}, f32[2,256,256]{2,1,0:T(8,128)S(1)}) custom-call(f32[4,64,256]{2,1,0:T(8,128)S(1)} %get-tuple-element.57.state.refs_0_, f32[8,128]{1,0:T(8,128)S(1)} %collective-permute-done.5.edge_a, f32[8,128]{1,0:T(8,128)S(1)} %collective-permute-done.6.edge_b, f32[4,4,64,256]{3,2,1,0:T(8,128)S(1)} %get-tuple-element.42.noise.refs_3_, ...), custom_call_target="tpu_custom_call" | custom-call | flops 2415919104 | tf_op jit(solution)/shard_map/pallas_call | solution.py:48
  28.3 1.5 %collective-permute-done.8.refs_15_ = bf16[80,256]{1,0:T(8,128)(2,1)S(1)} collective-permute-done((bf16[80,256]{1,0:T(8,128)(2,1)S(1)}, bf16[80,256]{1,0:T(8,128)(2,1)S(1)}, u32[]{:S(2)}, u32[]{:S(2)}) %collective-permute-start.8) | collective-permute-done | bytes 40992 | tf_op jit(solution)/shard_map/ppermute | solution.py:441
  29.8 1.7 %shard_map.150 = (f32[4,64,256]{2,1,0:T(8,128)S(1)}, f32[8,128]{1,0:T(8,128)S(1)}) custom-call(f32[4,64,256]{2,1,0:T(8,128)S(1)} %get-tuple-element.57.state.refs_0_, f32[2,64,256]{2,1,0:T(8,128)S(1)} %get-tuple-element.59.refs_1_, f32[2,256,256]{2,1,0:T(8,128)S(1)} %get-tuple-element.60.refs_2_, f32[4,4,64,256]{3,2,1,0:T(8,128)S(1)} %get-tuple-element.42.noise.refs_3_, ...), custom_call_target="tpu_custom_call" | custom-call | tf_op jit(solution)/shard_map/pallas_call | solution.py:48
  31.5 0.7 %collective-permute-start.10 = (f32[8,128]{1,0:T(8,128)S(1)}, f32[8,128]{1,0:T(8,128)S(1)}, u32[]{:S(2)}, u32[]{:S(2)}) collective-permute-start(f32[8,128]{1,0:T(8,128)S(1)} %get-tuple-element.65), channel_id=1, source_target_pairs={{0,1},{1,0},{2,3},{3,2},{4,5},{5,4},{6,7},{7,6},{8,9},{9,8},{10,11... | collective-permute-start | bytes 12296 | tf_op jit(solution)/shard_map/ppermute | solution.py:375
  32.2 0.3 shard_map.152.value.refs_13_
  32.7 1.9 %collective-permute-done.11.edge_b = f32[8,128]{1,0:T(8,128)S(1)} collective-permute-done((f32[8,128]{1,0:T(8,128)S(1)}, f32[8,128]{1,0:T(8,128)S(1)}, u32[]{:S(2)}, u32[]{:S(2)}) %collective-permute-start.11) | collective-permute-done | bytes 4128 | tf_op jit(solution)/shard_map/ppermute | solution.py:375
  34.6 1.9 %collective-permute-start.12 = (bf16[80,256]{1,0:T(8,128)(2,1)S(1)}, bf16[80,256]{1,0:T(8,128)(2,1)S(1)}, u32[]{:S(2)}, u32[]{:S(2)}) collective-permute-start(bf16[80,256]{1,0:T(8,128)(2,1)S(1)} %get-tuple-element.68), channel_id=1, source_target_pairs={{0,4},{4,0},{8,12},{12,8},{1,5},{5,1},{9,13},{13,9},{2,6},{6,2},{1... | collective-permute-start | bytes 122888 | tf_op jit(solution)/shard_map/ppermute | solution.py:441
  36.5 0.6 %collective-permute-start.13 = (bf16[80,256]{1,0:T(8,128)(2,1)S(1)}, bf16[80,256]{1,0:T(8,128)(2,1)S(1)}, u32[]{:S(2)}, u32[]{:S(2)}) collective-permute-start(bf16[80,256]{1,0:T(8,128)(2,1)S(1)} %get-tuple-element.69), channel_id=1, source_target_pairs={{0,12},{4,8},{8,4},{12,0},{1,13},{5,9},{9,5},{13,1},{2,14},{6,10},... | collective-permute-start | bytes 122888 | tf_op jit(solution)/shard_map/ppermute | solution.py:441
  37.1 2.0 %shard_map.151 = (f32[2,64,256]{2,1,0:T(8,128)S(1)}, f32[2,256,256]{2,1,0:T(8,128)S(1)}) custom-call(f32[4,64,256]{2,1,0:T(8,128)S(1)} %get-tuple-element.64.state.refs_0_, f32[8,128]{1,0:T(8,128)S(1)} %collective-permute-done.10.edge_a, f32[8,128]{1,0:T(8,128)S(1)} %collective-permute-done.11.edge_b, f32[4,4,64,256]{3,2,1,0:T(8,128)S(1)} %get-tuple-element.42.noise.refs_3_, ...), custom_call_target="tpu_custom_call" | custom-call | flops 2415919104 | tf_op jit(solution)/shard_map/pallas_call | solution.py:48
  39.1 3.2 %collective-permute-done.13.refs_15_ = bf16[80,256]{1,0:T(8,128)(2,1)S(1)} collective-permute-done((bf16[80,256]{1,0:T(8,128)(2,1)S(1)}, bf16[80,256]{1,0:T(8,128)(2,1)S(1)}, u32[]{:S(2)}, u32[]{:S(2)}) %collective-permute-start.13) | collective-permute-done | bytes 40992 | tf_op jit(solution)/shard_map/ppermute | solution.py:441
  42.3 1.7 %shard_map.154 = (f32[4,64,256]{2,1,0:T(8,128)S(1)}, f32[8,128]{1,0:T(8,128)S(1)}) custom-call(f32[4,64,256]{2,1,0:T(8,128)S(1)} %get-tuple-element.64.state.refs_0_, f32[2,64,256]{2,1,0:T(8,128)S(1)} %get-tuple-element.66.refs_1_, f32[2,256,256]{2,1,0:T(8,128)S(1)} %get-tuple-element.67.refs_2_, f32[4,4,64,256]{3,2,1,0:T(8,128)S(1)} %get-tuple-element.42.noise.refs_3_, ...), custom_call_target="tpu_custom_call" | custom-call | tf_op jit(solution)/shard_map/pallas_call | solution.py:48
  44.0 0.6 %collective-permute-start.15 = (f32[8,128]{1,0:T(8,128)S(1)}, f32[8,128]{1,0:T(8,128)S(1)}, u32[]{:S(2)}, u32[]{:S(2)}) collective-permute-start(f32[8,128]{1,0:T(8,128)S(1)} %get-tuple-element.71), channel_id=1, source_target_pairs={{0,1},{1,0},{2,3},{3,2},{4,5},{5,4},{6,7},{7,6},{8,9},{9,8},{10,11... | collective-permute-start | bytes 12296 | tf_op jit(solution)/shard_map/ppermute | solution.py:375
  44.6 0.3 shard_map.156.value.refs_13_
  45.2 1.8 %collective-permute-done.16.edge_b = f32[8,128]{1,0:T(8,128)S(1)} collective-permute-done((f32[8,128]{1,0:T(8,128)S(1)}, f32[8,128]{1,0:T(8,128)S(1)}, u32[]{:S(2)}, u32[]{:S(2)}) %collective-permute-start.16) | collective-permute-done | bytes 4128 | tf_op jit(solution)/shard_map/ppermute | solution.py:375
  47.2 2.3 %collective-permute-start.18 = (bf16[80,256]{1,0:T(8,128)(2,1)S(1)}, bf16[80,256]{1,0:T(8,128)(2,1)S(1)}, u32[]{:S(2)}, u32[]{:S(2)}) collective-permute-start(bf16[80,256]{1,0:T(8,128)(2,1)S(1)} %get-tuple-element.75), channel_id=1, source_target_pairs={{0,12},{4,8},{8,4},{12,0},{1,13},{5,9},{9,5},{13,1},{2,14},{6,10},... | collective-permute-start | bytes 122888 | tf_op jit(solution)/shard_map/ppermute | solution.py:441
  49.5 2.1 %shard_map.155 = (f32[2,64,256]{2,1,0:T(8,128)S(1)}, f32[2,256,256]{2,1,0:T(8,128)S(1)}) custom-call(f32[4,64,256]{2,1,0:T(8,128)S(1)} %get-tuple-element.70.state.refs_0_, f32[8,128]{1,0:T(8,128)S(1)} %collective-permute-done.15.edge_a, f32[8,128]{1,0:T(8,128)S(1)} %collective-permute-done.16.edge_b, f32[4,4,64,256]{3,2,1,0:T(8,128)S(1)} %get-tuple-element.42.noise.refs_3_, ...), custom_call_target="tpu_custom_call" | custom-call | flops 2415919104 | tf_op jit(solution)/shard_map/pallas_call | solution.py:48
  51.7 1.3 %collective-permute-done.18.refs_15_ = bf16[80,256]{1,0:T(8,128)(2,1)S(1)} collective-permute-done((bf16[80,256]{1,0:T(8,128)(2,1)S(1)}, bf16[80,256]{1,0:T(8,128)(2,1)S(1)}, u32[]{:S(2)}, u32[]{:S(2)}) %collective-permute-start.18) | collective-permute-done | bytes 40992 | tf_op jit(solution)/shard_map/ppermute | solution.py:441
  53.0 2.2 %shard_map.158 = (f32[64,4,256]{2,1,0:T(4,128)}, f32[1,256]{1,0:T(1,128)}) custom-call(f32[4,64,256]{2,1,0:T(8,128)S(1)} %get-tuple-element.70.state.refs_0_, f32[2,64,256]{2,1,0:T(8,128)S(1)} %get-tuple-element.72.refs_1_, f32[2,256,256]{2,1,0:T(8,128)S(1)} %get-tuple-element.73.refs_2_, f32[4,4,64,256]{3,2,1,0:T(8,128)S(1)} %get-tuple-element.42.noise.refs_3_, ...), custom_call_target="tpu_custom_call" | custom-call | tf_op jit(solution)/shard_map/pallas_call | solution.py:48
  (27 shorter events, 1.8 us)
Async XLA Ops:
  3.1 8.2 %collective-permute-start.1 = (f32[8,128]{1,0:T(8,128)S(1)}, f32[8,128]{1,0:T(8,128)S(1)}, u32[]{:S(2)}, u32[]{:S(2)}) collective-permute-start(f32[8,128]{1,0:T(8,128)S(1)} %get-tuple-element.41), channel_id=1, source_target_pairs={{0,3},{1,2},{2,1},{3,0},{4,7},{5,6},{6,5},{7,4},{8,11},{9,10},{10,... | collective-permute-start | bytes 12296 | tf_op jit(solution)/shard_map/ppermute | solution.py:375
  5.5 5.7 %collective-permute-start = (f32[8,128]{1,0:T(8,128)S(1)}, f32[8,128]{1,0:T(8,128)S(1)}, u32[]{:S(2)}, u32[]{:S(2)}) collective-permute-start(f32[8,128]{1,0:T(8,128)S(1)} %get-tuple-element.41), channel_id=1, source_target_pairs={{0,1},{1,0},{2,3},{3,2},{4,5},{5,4},{6,7},{7,6},{8,9},{9,8},{10,11... | collective-permute-start | bytes 12296 | tf_op jit(solution)/shard_map/ppermute | solution.py:375
  6.2 8.9 %collective-permute-start.4 = (f32[8,256]{1,0:T(8,128)S(1)}, f32[8,256]{1,0:T(8,128)S(1)}, u32[]{:S(2)}, u32[]{:S(2)}) collective-permute-start(f32[8,256]{1,0:T(8,128)S(1)} %get-tuple-element.50.msg.value.own.refs_13_), channel_id=1, source_target_pairs={{0,8},{4,12},{8,0},{12,4},{1,9},{5,13},{9,1},{13,5},{2,10},{6,14},... | collective-permute-start | bytes 24584 | tf_op jit(solution)/shard_map/ppermute | solution.py:384
  11.3 4.2 %collective-permute-start.2 = (bf16[96,256]{1,0:T(8,128)(2,1)S(1)}, bf16[96,256]{1,0:T(8,128)(2,1)S(1)}, u32[]{:S(2)}, u32[]{:S(2)}) collective-permute-start(bf16[96,256]{1,0:T(8,128)(2,1)S(1)} %get-tuple-element.52), channel_id=1, source_target_pairs={{0,4},{4,0},{8,12},{12,8},{1,5},{5,1},{9,13},{13,9},{2,6},{6,2},{1... | collective-permute-start | bytes 147464 | tf_op jit(solution)/shard_map/ppermute | solution.py:441
  13.0 5.9 %collective-permute-start.3 = (bf16[96,256]{1,0:T(8,128)(2,1)S(1)}, bf16[96,256]{1,0:T(8,128)(2,1)S(1)}, u32[]{:S(2)}, u32[]{:S(2)}) collective-permute-start(bf16[96,256]{1,0:T(8,128)(2,1)S(1)} %get-tuple-element.53), channel_id=1, source_target_pairs={{0,12},{4,8},{8,4},{12,0},{1,13},{5,9},{9,5},{13,1},{2,14},{6,10},... | collective-permute-start | bytes 147464 | tf_op jit(solution)/shard_map/ppermute | solution.py:441
  20.7 3.1 %collective-permute-start.6 = (f32[8,128]{1,0:T(8,128)S(1)}, f32[8,128]{1,0:T(8,128)S(1)}, u32[]{:S(2)}, u32[]{:S(2)}) collective-permute-start(f32[8,128]{1,0:T(8,128)S(1)} %get-tuple-element.58), channel_id=1, source_target_pairs={{0,3},{1,2},{2,1},{3,0},{4,7},{5,6},{6,5},{7,4},{8,11},{9,10},{10,... | collective-permute-start | bytes 12296 | tf_op jit(solution)/shard_map/ppermute | solution.py:375
  20.8 3.0 %collective-permute-start.5 = (f32[8,128]{1,0:T(8,128)S(1)}, f32[8,128]{1,0:T(8,128)S(1)}, u32[]{:S(2)}, u32[]{:S(2)}) collective-permute-start(f32[8,128]{1,0:T(8,128)S(1)} %get-tuple-element.58), channel_id=1, source_target_pairs={{0,1},{1,0},{2,3},{3,2},{4,5},{5,4},{6,7},{7,6},{8,9},{9,8},{10,11... | collective-permute-start | bytes 12296 | tf_op jit(solution)/shard_map/ppermute | solution.py:375
  21.7 6.5 %collective-permute-start.9 = (f32[8,256]{1,0:T(8,128)S(1)}, f32[8,256]{1,0:T(8,128)S(1)}, u32[]{:S(2)}, u32[]{:S(2)}) collective-permute-start(f32[8,256]{1,0:T(8,128)S(1)} %shard_map.148.value.refs_13_), channel_id=1, source_target_pairs={{0,8},{4,12},{8,0},{12,4},{1,9},{5,13},{9,1},{13,5},{2,10},{6,14},... | collective-permute-start | bytes 24584 | tf_op jit(solution)/shard_map/ppermute | solution.py:384
  23.8 4.4 %collective-permute-start.7 = (bf16[80,256]{1,0:T(8,128)(2,1)S(1)}, bf16[80,256]{1,0:T(8,128)(2,1)S(1)}, u32[]{:S(2)}, u32[]{:S(2)}) collective-permute-start(bf16[80,256]{1,0:T(8,128)(2,1)S(1)} %get-tuple-element.62), channel_id=1, source_target_pairs={{0,4},{4,0},{8,12},{12,8},{1,5},{5,1},{9,13},{13,9},{2,6},{6,2},{1... | collective-permute-start | bytes 122888 | tf_op jit(solution)/shard_map/ppermute | solution.py:441
  23.9 5.9 %collective-permute-start.8 = (bf16[80,256]{1,0:T(8,128)(2,1)S(1)}, bf16[80,256]{1,0:T(8,128)(2,1)S(1)}, u32[]{:S(2)}, u32[]{:S(2)}) collective-permute-start(bf16[80,256]{1,0:T(8,128)(2,1)S(1)} %get-tuple-element.63), channel_id=1, source_target_pairs={{0,12},{4,8},{8,4},{12,0},{1,13},{5,9},{9,5},{13,1},{2,14},{6,10},... | collective-permute-start | bytes 122888 | tf_op jit(solution)/shard_map/ppermute | solution.py:441
  31.5 3.1 %collective-permute-start.11 = (f32[8,128]{1,0:T(8,128)S(1)}, f32[8,128]{1,0:T(8,128)S(1)}, u32[]{:S(2)}, u32[]{:S(2)}) collective-permute-start(f32[8,128]{1,0:T(8,128)S(1)} %get-tuple-element.65), channel_id=1, source_target_pairs={{0,3},{1,2},{2,1},{3,0},{4,7},{5,6},{6,5},{7,4},{8,11},{9,10},{10,... | collective-permute-start | bytes 12296 | tf_op jit(solution)/shard_map/ppermute | solution.py:375
  31.5 3.0 %collective-permute-start.10 = (f32[8,128]{1,0:T(8,128)S(1)}, f32[8,128]{1,0:T(8,128)S(1)}, u32[]{:S(2)}, u32[]{:S(2)}) collective-permute-start(f32[8,128]{1,0:T(8,128)S(1)} %get-tuple-element.65), channel_id=1, source_target_pairs={{0,1},{1,0},{2,3},{3,2},{4,5},{5,4},{6,7},{7,6},{8,9},{9,8},{10,11... | collective-permute-start | bytes 12296 | tf_op jit(solution)/shard_map/ppermute | solution.py:375
  32.5 6.5 %collective-permute-start.14 = (f32[8,256]{1,0:T(8,128)S(1)}, f32[8,256]{1,0:T(8,128)S(1)}, u32[]{:S(2)}, u32[]{:S(2)}) collective-permute-start(f32[8,256]{1,0:T(8,128)S(1)} %shard_map.152.value.refs_13_), channel_id=1, source_target_pairs={{0,8},{4,12},{8,0},{12,4},{1,9},{5,13},{9,1},{13,5},{2,10},{6,14},... | collective-permute-start | bytes 24584 | tf_op jit(solution)/shard_map/ppermute | solution.py:384
  34.6 4.5 %collective-permute-start.12 = (bf16[80,256]{1,0:T(8,128)(2,1)S(1)}, bf16[80,256]{1,0:T(8,128)(2,1)S(1)}, u32[]{:S(2)}, u32[]{:S(2)}) collective-permute-start(bf16[80,256]{1,0:T(8,128)(2,1)S(1)} %get-tuple-element.68), channel_id=1, source_target_pairs={{0,4},{4,0},{8,12},{12,8},{1,5},{5,1},{9,13},{13,9},{2,6},{6,2},{1... | collective-permute-start | bytes 122888 | tf_op jit(solution)/shard_map/ppermute | solution.py:441
  36.5 5.8 %collective-permute-start.13 = (bf16[80,256]{1,0:T(8,128)(2,1)S(1)}, bf16[80,256]{1,0:T(8,128)(2,1)S(1)}, u32[]{:S(2)}, u32[]{:S(2)}) collective-permute-start(bf16[80,256]{1,0:T(8,128)(2,1)S(1)} %get-tuple-element.69), channel_id=1, source_target_pairs={{0,12},{4,8},{8,4},{12,0},{1,13},{5,9},{9,5},{13,1},{2,14},{6,10},... | collective-permute-start | bytes 122888 | tf_op jit(solution)/shard_map/ppermute | solution.py:441
  43.9 3.1 %collective-permute-start.16 = (f32[8,128]{1,0:T(8,128)S(1)}, f32[8,128]{1,0:T(8,128)S(1)}, u32[]{:S(2)}, u32[]{:S(2)}) collective-permute-start(f32[8,128]{1,0:T(8,128)S(1)} %get-tuple-element.71), channel_id=1, source_target_pairs={{0,3},{1,2},{2,1},{3,0},{4,7},{5,6},{6,5},{7,4},{8,11},{9,10},{10,... | collective-permute-start | bytes 12296 | tf_op jit(solution)/shard_map/ppermute | solution.py:375
  44.0 3.0 %collective-permute-start.15 = (f32[8,128]{1,0:T(8,128)S(1)}, f32[8,128]{1,0:T(8,128)S(1)}, u32[]{:S(2)}, u32[]{:S(2)}) collective-permute-start(f32[8,128]{1,0:T(8,128)S(1)} %get-tuple-element.71), channel_id=1, source_target_pairs={{0,1},{1,0},{2,3},{3,2},{4,5},{5,4},{6,7},{7,6},{8,9},{9,8},{10,11... | collective-permute-start | bytes 12296 | tf_op jit(solution)/shard_map/ppermute | solution.py:375
  45.0 6.7 %collective-permute-start.19 = (f32[8,256]{1,0:T(8,128)S(1)}, f32[8,256]{1,0:T(8,128)S(1)}, u32[]{:S(2)}, u32[]{:S(2)}) collective-permute-start(f32[8,256]{1,0:T(8,128)S(1)} %shard_map.156.value.refs_13_), channel_id=1, source_target_pairs={{0,8},{4,12},{8,0},{12,4},{1,9},{5,13},{9,1},{13,5},{2,10},{6,14},... | collective-permute-start | bytes 24584 | tf_op jit(solution)/shard_map/ppermute | solution.py:384
  47.1 4.6 %collective-permute-start.17 = (bf16[80,256]{1,0:T(8,128)(2,1)S(1)}, bf16[80,256]{1,0:T(8,128)(2,1)S(1)}, u32[]{:S(2)}, u32[]{:S(2)}) collective-permute-start(bf16[80,256]{1,0:T(8,128)(2,1)S(1)} %get-tuple-element.74), channel_id=1, source_target_pairs={{0,4},{4,0},{8,12},{12,8},{1,5},{5,1},{9,13},{13,9},{2,6},{6,2},{1... | collective-permute-start | bytes 122888 | tf_op jit(solution)/shard_map/ppermute | solution.py:441
  47.2 5.8 %collective-permute-start.18 = (bf16[80,256]{1,0:T(8,128)(2,1)S(1)}, bf16[80,256]{1,0:T(8,128)(2,1)S(1)}, u32[]{:S(2)}, u32[]{:S(2)}) collective-permute-start(bf16[80,256]{1,0:T(8,128)(2,1)S(1)} %get-tuple-element.75), channel_id=1, source_target_pairs={{0,12},{4,8},{8,4},{12,0},{1,13},{5,9},{9,5},{13,1},{2,14},{6,10},... | collective-permute-start | bytes 122888 | tf_op jit(solution)/shard_map/ppermute | solution.py:441

commit v6 on v5

--- a/solution.py
+++ b/solution.py
@@ -168,12 +168,13 @@
     return jnp.where(even, from_b, from_a), jnp.where(even, from_a, from_b)
 
 
-def message_kernel(state, edge_a, edge_b, value, msg_a, msg_b, *, level, used):
+def message_kernel(state, edge_a, edge_b, value, *refs, level, used, first):
+    msg = refs[-1]
     latb, variables, width = state.shape
     even = is_even("band")
     left, right = from_sides("wt", edge_a[...], edge_b[...])
     parts = [part.astype(F32) for part in pieces(value[0:used], PIECES)]
-    padding = jnp.zeros((msg_a.shape[0] - variables - PIECES * used - 1, width), F32)
+    padding = jnp.zeros((msg.shape[0] - variables - PIECES * used - 1, width), F32)
     below, above = [
         jnp.concatenate(
             [
@@ -186,8 +187,8 @@
         )
         for r in (0, latb - 1)
     ]
-    msg_a[...] = jnp.where(even, above, below).astype(BF16)
-    msg_b[...] = jnp.where(even, below, above).astype(BF16)
+    upward = even if first else jnp.logical_not(even)
+    msg[...] = jnp.where(upward, above, below).astype(BF16)
 
 
 def unpacked(msg, variables, used):
@@ -433,11 +434,11 @@
         last = step == len(STEPS) - 1
         far = from_far(value)
         edges = from_neighbours(edge, "wt")
-        msg_a, msg_b = vmem_call(
-            functools.partial(message_kernel, level=STEPS[step][0], used=used),
-            [((variables + (32 if used == 8 else 16), lond), BF16)] * 2,
-            state, *edges, value,
-        )
+        message = [((variables + (32 if used == 8 else 16), lond), BF16)]
+        make = functools.partial(message_kernel, level=STEPS[step][0], used=used)
+        given = [state, *edges, value]
+        (msg_b,) = vmem_call(functools.partial(make, first=False), message, *given)
+        (msg_a,) = vmem_call(functools.partial(make, first=True), message, *given, msg_b)
         msg_a, msg_b = lax.ppermute(msg_a, "band", route_a), lax.ppermute(msg_b, "band", route_b)
         middle, sums = vmem_call(
             functools.partial(inner_kernel, step=step),

time: 55.7 us -> 53.5 us (0.961)
  waiting for transfers between devices: 15.4 us -> 12 us
  starting transfers between devices: 17.6 us -> 18.8 us
    ppermute x4, waiting for transfers between devices: 9.42 us -> 0.01 us  [per_device(): lax.ppermute(msg_b, 'band', route_b)]
    ppermute x4, waiting for transfers between devices: 0.32 us -> 8.76 us  [per_device(): lax.ppermute(msg_a, 'band', route_a)]
    ppermute x4, starting transfers between devices: 3.77 us -> 0.53 us  [per_device(): lax.ppermute(msg_a, 'band', route_a)]
    ppermute x8, waiting for transfers between devices: 5.67 us -> 3.23 us  [from_neighbours(): lax.ppermute(block, axis, route)]
    ppermute x4, starting transfers between devices: 3.06 us -> 5.3 us  [from_far(): found.append(lax.ppermute(block, 'band', route))]
    ppermute x4, starting transfers between devices: 5.52 us -> 7.47 us  [per_device(): lax.ppermute(msg_b, 'band', route_b)]
    pallas_call x19 -> x23, Pallas kernels: 20.8 us -> 20.9 us  [vmem_call(): pl.pallas_call(kernel, out_shape=[out_type(shape, dtype) for shape, dtype...]
  transfers between devices with their start and end apart: 20 -> 20, of which waited for: 8 -> 7; matrix products, arithmetic and copies ran while one was open for 0% -> 0% of each run, Pallas kernels for 21% -> 22%
where the time goes in v6:
time: 53.5 us; the launch traced here: 53.3 us
  Pallas kernels  20.9 us (39%)
  starting transfers between devices  18.8 us (35%)
  waiting for transfers between devices  12 us (22%)
  between operations  1.62 us (3%)
    pallas_call x23, Pallas kernels, vmem_call(): pl.pallas_call(kernel, out_shape=[out_type(shape, dtype) for shape, dtype...  20.9 us
    ppermute x4, waiting for transfers between devices, per_device(): lax.ppermute(msg_a, 'band', route_a)  8.76 us
    ppermute x4, starting transfers between devices, per_device(): lax.ppermute(msg_b, 'band', route_b)  7.47 us
    ppermute x8, starting transfers between devices, from_neighbours(): lax.ppermute(block, axis, route)  5.48 us
    ppermute x4, starting transfers between devices, from_far(): found.append(lax.ppermute(block, 'band', route))  5.3 us
    ppermute x8, waiting for transfers between devices, from_neighbours(): lax.ppermute(block, axis, route)  3.23 us
  transfers between devices with their start and end apart: 20, of which 7 were waited for; matrix products, arithmetic and copies ran while one was open for 0% of the time, Pallas kernels for 22%

profile of v6, /device:TPU:0, one launch (start us, length us, event | category | flops | bytes accessed | tf_op | source)
XLA Modules:
  0.0 53.3 jit_solution(18209994090465867055)
XLA Ops:
  1.3 1.8 %shard_map.140 = (f32[4,64,256]{2,1,0:T(8,128)S(1)}, f32[8,128]{1,0:T(8,128)S(1)}, f32[8,256]{1,0:T(8,128)S(1)}) custom-call(s32[1]{0:T(128)S(6)} %copy.15.refs_0_, f32[64,4,256]{2,1,0:T(4,128)} %refs_1_.2, s32[1,256]{1,0:T(1,128)} %bitcast.12, s32[1,256]{1,0:T(1,128)} %bitcast.13, s32[1,256]{1,0:T(1,128)} %bitcast.14, f32[1,256]{1,0:T(1,128)} %bitcast.15, ...), custom_call_target="tpu_custom_call" | custom-call | tf_op jit(solution)/shard_map/pallas_call | solution.py:48
  3.1 2.4 %collective-permute-start.1 = (f32[8,128]{1,0:T(8,128)S(1)}, f32[8,128]{1,0:T(8,128)S(1)}, u32[]{:S(2)}, u32[]{:S(2)}) collective-permute-start(f32[8,128]{1,0:T(8,128)S(1)} %get-tuple-element.33), channel_id=1, source_target_pairs={{0,3},{1,2},{2,1},{3,0},{4,7},{5,6},{6,5},{7,4},{8,11},{9,10},{10,... | collective-permute-start | bytes 12296 | tf_op jit(solution)/shard_map/ppermute | solution.py:376
  5.5 0.7 %collective-permute-start = (f32[8,128]{1,0:T(8,128)S(1)}, f32[8,128]{1,0:T(8,128)S(1)}, u32[]{:S(2)}, u32[]{:S(2)}) collective-permute-start(f32[8,128]{1,0:T(8,128)S(1)} %get-tuple-element.33), channel_id=1, source_target_pairs={{0,1},{1,0},{2,3},{3,2},{4,5},{5,4},{6,7},{7,6},{8,9},{9,8},{10,11... | collective-permute-start | bytes 12296 | tf_op jit(solution)/shard_map/ppermute | solution.py:376
  6.2 2.6 %collective-permute-start.4 = (f32[8,256]{1,0:T(8,128)S(1)}, f32[8,256]{1,0:T(8,128)S(1)}, u32[]{:S(2)}, u32[]{:S(2)}) collective-permute-start(f32[8,256]{1,0:T(8,128)S(1)} %get-tuple-element.42.msg.value.own.refs_13_), channel_id=1, source_target_pairs={{0,8},{4,12},{8,0},{12,4},{1,9},{5,13},{9,1},{13,5},{2,10},{6,14},... | collective-permute-start | bytes 24584 | tf_op jit(solution)/shard_map/ppermute | solution.py:385
  8.8 0.5 shard_map.143
  9.3 1.9 %shard_map.141 = (f32[4,4,64,256]{3,2,1,0:T(8,128)S(1)}, bf16[2304,256]{1,0:T(8,128)(2,1)S(1)}, bf16[64,256]{1,0:T(8,128)(2,1)S(1)}, bf16[64,256]{1,0:T(8,128)(2...) custom-call(f32[4,64,4,256]{3,2,1,0:T(4,128)} %noise_in.1, bf16[2304,256]{1,0:T(8,128)(2,1)} %bitcast.10, ...), custom_call_target="tpu_custom_call" | custom-call | tf_op jit(solution)/shard_map/pallas_call | solution.py:48
  11.3 1.4 %collective-permute-start.3 = (bf16[96,256]{1,0:T(8,128)(2,1)S(1)}, bf16[96,256]{1,0:T(8,128)(2,1)S(1)}, u32[]{:S(2)}, u32[]{:S(2)}) collective-permute-start(bf16[96,256]{1,0:T(8,128)(2,1)S(1)} %shard_map.144.refs_0_), channel_id=1, source_target_pairs={{0,12},{4,8},{8,4},{12,0},{1,13},{5,9},{9,5},{13,1},{2,14},{6,10},... | collective-permute-start | bytes 147464 | tf_op jit(solution)/shard_map/ppermute | solution.py:442
  13.1 2.0 %shard_map.142 = (f32[2,64,256]{2,1,0:T(8,128)S(1)}, f32[2,256,256]{2,1,0:T(8,128)S(1)}) custom-call(f32[4,64,256]{2,1,0:T(8,128)S(1)} %get-tuple-element.32.state.refs_0_, f32[8,128]{1,0:T(8,128)S(1)} %collective-permute-done.edge_a, f32[8,128]{1,0:T(8,128)S(1)} %collective-permute-done.1.edge_b, f32[4,4,64,256]{3,2,1,0:T(8,128)S(1)} %get-tuple-element.34.noise.refs_3_, ...), custom_call_target="tpu_custom_call" | custom-call | flops 2415919104 | tf_op jit(solution)/shard_map/pallas_call | solution.py:48
  15.0 2.4 %collective-permute-done.2.msg_a.refs_14_ = bf16[96,256]{1,0:T(8,128)(2,1)S(1)} collective-permute-done((bf16[96,256]{1,0:T(8,128)(2,1)S(1)}, bf16[96,256]{1,0:T(8,128)(2,1)S(1)}, u32[]{:S(2)}, u32[]{:S(2)}) %collective-permute-start.2) | collective-permute-done | bytes 49184 | tf_op jit(solution)/shard_map/ppermute | solution.py:442
  17.6 1.7 %shard_map.147 = (f32[4,64,256]{2,1,0:T(8,128)S(1)}, f32[8,128]{1,0:T(8,128)S(1)}) custom-call(f32[4,64,256]{2,1,0:T(8,128)S(1)} %get-tuple-element.32.state.refs_0_, f32[2,64,256]{2,1,0:T(8,128)S(1)} %get-tuple-element.40.refs_1_, f32[2,256,256]{2,1,0:T(8,128)S(1)} %get-tuple-element.41.refs_2_, f32[4,4,64,256]{3,2,1,0:T(8,128)S(1)} %get-tuple-element.34.noise.refs_3_, ...), custom_call_target="tpu_custom_call" | custom-call | tf_op jit(solution)/shard_map/pallas_call | solution.py:48
  19.4 0.6 %collective-permute-start.5 = (f32[8,128]{1,0:T(8,128)S(1)}, f32[8,128]{1,0:T(8,128)S(1)}, u32[]{:S(2)}, u32[]{:S(2)}) collective-permute-start(f32[8,128]{1,0:T(8,128)S(1)} %get-tuple-element.48), channel_id=1, source_target_pairs={{0,1},{1,0},{2,3},{3,2},{4,5},{5,4},{6,7},{7,6},{8,9},{9,8},{10,11... | collective-permute-start | bytes 12296 | tf_op jit(solution)/shard_map/ppermute | solution.py:376
  20.0 0.3 shard_map.149.value.refs_13_
  20.3 1.2 %collective-permute-start.9 = (f32[8,256]{1,0:T(8,128)S(1)}, f32[8,256]{1,0:T(8,128)S(1)}, u32[]{:S(2)}, u32[]{:S(2)}) collective-permute-start(f32[8,256]{1,0:T(8,128)S(1)} %shard_map.149.value.refs_13_), channel_id=1, source_target_pairs={{0,8},{4,12},{8,0},{12,4},{1,9},{5,13},{9,1},{13,5},{2,10},{6,14},... | collective-permute-start | bytes 24584 | tf_op jit(solution)/shard_map/ppermute | solution.py:385
  21.5 0.8 %collective-permute-done.6.edge_b = f32[8,128]{1,0:T(8,128)S(1)} collective-permute-done((f32[8,128]{1,0:T(8,128)S(1)}, f32[8,128]{1,0:T(8,128)S(1)}, u32[]{:S(2)}, u32[]{:S(2)}) %collective-permute-start.6) | collective-permute-done | bytes 4128 | tf_op jit(solution)/shard_map/ppermute | solution.py:376
  22.4 2.0 %collective-permute-start.8 = (bf16[80,256]{1,0:T(8,128)(2,1)S(1)}, bf16[80,256]{1,0:T(8,128)(2,1)S(1)}, u32[]{:S(2)}, u32[]{:S(2)}) collective-permute-start(bf16[80,256]{1,0:T(8,128)(2,1)S(1)} %shard_map.150.refs_0_), channel_id=1, source_target_pairs={{0,12},{4,8},{8,4},{12,0},{1,13},{5,9},{9,5},{13,1},{2,14},{6,10},... | collective-permute-start | bytes 122888 | tf_op jit(solution)/shard_map/ppermute | solution.py:442
  24.5 2.0 %shard_map.148 = (f32[2,64,256]{2,1,0:T(8,128)S(1)}, f32[2,256,256]{2,1,0:T(8,128)S(1)}) custom-call(f32[4,64,256]{2,1,0:T(8,128)S(1)} %get-tuple-element.47.state.refs_0_, f32[8,128]{1,0:T(8,128)S(1)} %collective-permute-done.5.edge_a, f32[8,128]{1,0:T(8,128)S(1)} %collective-permute-done.6.edge_b, f32[4,4,64,256]{3,2,1,0:T(8,128)S(1)} %get-tuple-element.34.noise.refs_3_, ...), custom_call_target="tpu_custom_call" | custom-call | flops 2415919104 | tf_op jit(solution)/shard_map/pallas_call | solution.py:48
  26.5 2.2 %collective-permute-done.7.refs_14_ = bf16[80,256]{1,0:T(8,128)(2,1)S(1)} collective-permute-done((bf16[80,256]{1,0:T(8,128)(2,1)S(1)}, bf16[80,256]{1,0:T(8,128)(2,1)S(1)}, u32[]{:S(2)}, u32[]{:S(2)}) %collective-permute-start.7) | collective-permute-done | bytes 40992 | tf_op jit(solution)/shard_map/ppermute | solution.py:442
  28.7 1.7 %shard_map.152 = (f32[4,64,256]{2,1,0:T(8,128)S(1)}, f32[8,128]{1,0:T(8,128)S(1)}) custom-call(f32[4,64,256]{2,1,0:T(8,128)S(1)} %get-tuple-element.47.state.refs_0_, f32[2,64,256]{2,1,0:T(8,128)S(1)} %get-tuple-element.49.refs_1_, f32[2,256,256]{2,1,0:T(8,128)S(1)} %get-tuple-element.50.refs_2_, f32[4,4,64,256]{3,2,1,0:T(8,128)S(1)} %get-tuple-element.34.noise.refs_3_, ...), custom_call_target="tpu_custom_call" | custom-call | tf_op jit(solution)/shard_map/pallas_call | solution.py:48
  30.5 0.8 %collective-permute-start.10 = (f32[8,128]{1,0:T(8,128)S(1)}, f32[8,128]{1,0:T(8,128)S(1)}, u32[]{:S(2)}, u32[]{:S(2)}) collective-permute-start(f32[8,128]{1,0:T(8,128)S(1)} %get-tuple-element.53), channel_id=1, source_target_pairs={{0,1},{1,0},{2,3},{3,2},{4,5},{5,4},{6,7},{7,6},{8,9},{9,8},{10,11... | collective-permute-start | bytes 12296 | tf_op jit(solution)/shard_map/ppermute | solution.py:376
  31.5 0.7 %collective-permute-start.14 = (f32[8,256]{1,0:T(8,128)S(1)}, f32[8,256]{1,0:T(8,128)S(1)}, u32[]{:S(2)}, u32[]{:S(2)}) collective-permute-start(f32[8,256]{1,0:T(8,128)S(1)} %shard_map.154.value.refs_13_), channel_id=1, source_target_pairs={{0,8},{4,12},{8,0},{12,4},{1,9},{5,13},{9,1},{13,5},{2,10},{6,14},... | collective-permute-start | bytes 24584 | tf_op jit(solution)/shard_map/ppermute | solution.py:385
  32.3 1.2 %collective-permute-done.11.edge_b = f32[8,128]{1,0:T(8,128)S(1)} collective-permute-done((f32[8,128]{1,0:T(8,128)S(1)}, f32[8,128]{1,0:T(8,128)S(1)}, u32[]{:S(2)}, u32[]{:S(2)}) %collective-permute-start.11) | collective-permute-done | bytes 4128 | tf_op jit(solution)/shard_map/ppermute | solution.py:376
  33.5 2.0 %collective-permute-start.13 = (bf16[80,256]{1,0:T(8,128)(2,1)S(1)}, bf16[80,256]{1,0:T(8,128)(2,1)S(1)}, u32[]{:S(2)}, u32[]{:S(2)}) collective-permute-start(bf16[80,256]{1,0:T(8,128)(2,1)S(1)} %shard_map.155.refs_0_), channel_id=1, source_target_pairs={{0,12},{4,8},{8,4},{12,0},{1,13},{5,9},{9,5},{13,1},{2,14},{6,10},... | collective-permute-start | bytes 122888 | tf_op jit(solution)/shard_map/ppermute | solution.py:442
  35.6 2.0 %shard_map.153 = (f32[2,64,256]{2,1,0:T(8,128)S(1)}, f32[2,256,256]{2,1,0:T(8,128)S(1)}) custom-call(f32[4,64,256]{2,1,0:T(8,128)S(1)} %get-tuple-element.52.state.refs_0_, f32[8,128]{1,0:T(8,128)S(1)} %collective-permute-done.10.edge_a, f32[8,128]{1,0:T(8,128)S(1)} %collective-permute-done.11.edge_b, f32[4,4,64,256]{3,2,1,0:T(8,128)S(1)} %get-tuple-element.34.noise.refs_3_, ...), custom_call_target="tpu_custom_call" | custom-call | flops 2415919104 | tf_op jit(solution)/shard_map/pallas_call | solution.py:48
  37.6 2.2 %collective-permute-done.12.refs_14_ = bf16[80,256]{1,0:T(8,128)(2,1)S(1)} collective-permute-done((bf16[80,256]{1,0:T(8,128)(2,1)S(1)}, bf16[80,256]{1,0:T(8,128)(2,1)S(1)}, u32[]{:S(2)}, u32[]{:S(2)}) %collective-permute-start.12) | collective-permute-done | bytes 40992 | tf_op jit(solution)/shard_map/ppermute | solution.py:442
  39.8 1.7 %shard_map.157 = (f32[4,64,256]{2,1,0:T(8,128)S(1)}, f32[8,128]{1,0:T(8,128)S(1)}) custom-call(f32[4,64,256]{2,1,0:T(8,128)S(1)} %get-tuple-element.52.state.refs_0_, f32[2,64,256]{2,1,0:T(8,128)S(1)} %get-tuple-element.54.refs_1_, f32[2,256,256]{2,1,0:T(8,128)S(1)} %get-tuple-element.55.refs_2_, f32[4,4,64,256]{3,2,1,0:T(8,128)S(1)} %get-tuple-element.34.noise.refs_3_, ...), custom_call_target="tpu_custom_call" | custom-call | tf_op jit(solution)/shard_map/pallas_call | solution.py:48
  41.6 0.8 %collective-permute-start.15 = (f32[8,128]{1,0:T(8,128)S(1)}, f32[8,128]{1,0:T(8,128)S(1)}, u32[]{:S(2)}, u32[]{:S(2)}) collective-permute-start(f32[8,128]{1,0:T(8,128)S(1)} %get-tuple-element.57), channel_id=1, source_target_pairs={{0,1},{1,0},{2,3},{3,2},{4,5},{5,4},{6,7},{7,6},{8,9},{9,8},{10,11... | collective-permute-start | bytes 12296 | tf_op jit(solution)/shard_map/ppermute | solution.py:376
  42.6 0.7 %collective-permute-start.19 = (f32[8,256]{1,0:T(8,128)S(1)}, f32[8,256]{1,0:T(8,128)S(1)}, u32[]{:S(2)}, u32[]{:S(2)}) collective-permute-start(f32[8,256]{1,0:T(8,128)S(1)} %shard_map.159.value.refs_13_), channel_id=1, source_target_pairs={{0,8},{4,12},{8,0},{12,4},{1,9},{5,13},{9,1},{13,5},{2,10},{6,14},... | collective-permute-start | bytes 24584 | tf_op jit(solution)/shard_map/ppermute | solution.py:385
  43.4 1.2 %collective-permute-done.16.edge_b = f32[8,128]{1,0:T(8,128)S(1)} collective-permute-done((f32[8,128]{1,0:T(8,128)S(1)}, f32[8,128]{1,0:T(8,128)S(1)}, u32[]{:S(2)}, u32[]{:S(2)}) %collective-permute-start.16) | collective-permute-done | bytes 4128 | tf_op jit(solution)/shard_map/ppermute | solution.py:376
  44.6 2.0 %collective-permute-start.18 = (bf16[80,256]{1,0:T(8,128)(2,1)S(1)}, bf16[80,256]{1,0:T(8,128)(2,1)S(1)}, u32[]{:S(2)}, u32[]{:S(2)}) collective-permute-start(bf16[80,256]{1,0:T(8,128)(2,1)S(1)} %shard_map.160.refs_0_), channel_id=1, source_target_pairs={{0,12},{4,8},{8,4},{12,0},{1,13},{5,9},{9,5},{13,1},{2,14},{6,10},... | collective-permute-start | bytes 122888 | tf_op jit(solution)/shard_map/ppermute | solution.py:442
  46.7 2.2 %shard_map.158 = (f32[2,64,256]{2,1,0:T(8,128)S(1)}, f32[2,256,256]{2,1,0:T(8,128)S(1)}) custom-call(f32[4,64,256]{2,1,0:T(8,128)S(1)} %get-tuple-element.56.state.refs_0_, f32[8,128]{1,0:T(8,128)S(1)} %collective-permute-done.15.edge_a, f32[8,128]{1,0:T(8,128)S(1)} %collective-permute-done.16.edge_b, f32[4,4,64,256]{3,2,1,0:T(8,128)S(1)} %get-tuple-element.34.noise.refs_3_, ...), custom_call_target="tpu_custom_call" | custom-call | flops 2415919104 | tf_op jit(solution)/shard_map/pallas_call | solution.py:48
  48.9 2.0 %collective-permute-done.17.refs_14_ = bf16[80,256]{1,0:T(8,128)(2,1)S(1)} collective-permute-done((bf16[80,256]{1,0:T(8,128)(2,1)S(1)}, bf16[80,256]{1,0:T(8,128)(2,1)S(1)}, u32[]{:S(2)}, u32[]{:S(2)}) %collective-permute-start.17) | collective-permute-done | bytes 40992 | tf_op jit(solution)/shard_map/ppermute | solution.py:442
  50.9 2.2 %shard_map.162 = (f32[64,4,256]{2,1,0:T(4,128)}, f32[1,256]{1,0:T(1,128)}) custom-call(f32[4,64,256]{2,1,0:T(8,128)S(1)} %get-tuple-element.56.state.refs_0_, f32[2,64,256]{2,1,0:T(8,128)S(1)} %get-tuple-element.58.refs_1_, f32[2,256,256]{2,1,0:T(8,128)S(1)} %get-tuple-element.59.refs_2_, f32[4,4,64,256]{3,2,1,0:T(8,128)S(1)} %get-tuple-element.34.noise.refs_3_, ...), custom_call_target="tpu_custom_call" | custom-call | tf_op jit(solution)/shard_map/pallas_call | solution.py:48
  (31 shorter events, 1.8 us)
Async XLA Ops:
  3.1 8.2 %collective-permute-start.1 = (f32[8,128]{1,0:T(8,128)S(1)}, f32[8,128]{1,0:T(8,128)S(1)}, u32[]{:S(2)}, u32[]{:S(2)}) collective-permute-start(f32[8,128]{1,0:T(8,128)S(1)} %get-tuple-element.33), channel_id=1, source_target_pairs={{0,3},{1,2},{2,1},{3,0},{4,7},{5,6},{6,5},{7,4},{8,11},{9,10},{10,... | collective-permute-start | bytes 12296 | tf_op jit(solution)/shard_map/ppermute | solution.py:376
  5.5 5.7 %collective-permute-start = (f32[8,128]{1,0:T(8,128)S(1)}, f32[8,128]{1,0:T(8,128)S(1)}, u32[]{:S(2)}, u32[]{:S(2)}) collective-permute-start(f32[8,128]{1,0:T(8,128)S(1)} %get-tuple-element.33), channel_id=1, source_target_pairs={{0,1},{1,0},{2,3},{3,2},{4,5},{5,4},{6,7},{7,6},{8,9},{9,8},{10,11... | collective-permute-start | bytes 12296 | tf_op jit(solution)/shard_map/ppermute | solution.py:376
  6.2 8.8 %collective-permute-start.4 = (f32[8,256]{1,0:T(8,128)S(1)}, f32[8,256]{1,0:T(8,128)S(1)}, u32[]{:S(2)}, u32[]{:S(2)}) collective-permute-start(f32[8,256]{1,0:T(8,128)S(1)} %get-tuple-element.42.msg.value.own.refs_13_), channel_id=1, source_target_pairs={{0,8},{4,12},{8,0},{12,4},{1,9},{5,13},{9,1},{13,5},{2,10},{6,14},... | collective-permute-start | bytes 24584 | tf_op jit(solution)/shard_map/ppermute | solution.py:385
  11.3 6.1 %collective-permute-start.3 = (bf16[96,256]{1,0:T(8,128)(2,1)S(1)}, bf16[96,256]{1,0:T(8,128)(2,1)S(1)}, u32[]{:S(2)}, u32[]{:S(2)}) collective-permute-start(bf16[96,256]{1,0:T(8,128)(2,1)S(1)} %shard_map.144.refs_0_), channel_id=1, source_target_pairs={{0,12},{4,8},{8,4},{12,0},{1,13},{5,9},{9,5},{13,1},{2,14},{6,10},... | collective-permute-start | bytes 147464 | tf_op jit(solution)/shard_map/ppermute | solution.py:442
  12.7 4.7 %collective-permute-start.2 = (bf16[96,256]{1,0:T(8,128)(2,1)S(1)}, bf16[96,256]{1,0:T(8,128)(2,1)S(1)}, u32[]{:S(2)}, u32[]{:S(2)}) collective-permute-start(bf16[96,256]{1,0:T(8,128)(2,1)S(1)} %shard_map.145), channel_id=1, source_target_pairs={{0,4},{4,0},{8,12},{12,8},{1,5},{5,1},{9,13},{13,9},{2,6},{6,2},{1... | collective-permute-start | bytes 147464 | tf_op jit(solution)/shard_map/ppermute | solution.py:442
  19.3 3.1 %collective-permute-start.6 = (f32[8,128]{1,0:T(8,128)S(1)}, f32[8,128]{1,0:T(8,128)S(1)}, u32[]{:S(2)}, u32[]{:S(2)}) collective-permute-start(f32[8,128]{1,0:T(8,128)S(1)} %get-tuple-element.48), channel_id=1, source_target_pairs={{0,3},{1,2},{2,1},{3,0},{4,7},{5,6},{6,5},{7,4},{8,11},{9,10},{10,... | collective-permute-start | bytes 12296 | tf_op jit(solution)/shard_map/ppermute | solution.py:376
  19.4 3.0 %collective-permute-start.5 = (f32[8,128]{1,0:T(8,128)S(1)}, f32[8,128]{1,0:T(8,128)S(1)}, u32[]{:S(2)}, u32[]{:S(2)}) collective-permute-start(f32[8,128]{1,0:T(8,128)S(1)} %get-tuple-element.48), channel_id=1, source_target_pairs={{0,1},{1,0},{2,3},{3,2},{4,5},{5,4},{6,7},{7,6},{8,9},{9,8},{10,11... | collective-permute-start | bytes 12296 | tf_op jit(solution)/shard_map/ppermute | solution.py:376
  20.3 6.2 %collective-permute-start.9 = (f32[8,256]{1,0:T(8,128)S(1)}, f32[8,256]{1,0:T(8,128)S(1)}, u32[]{:S(2)}, u32[]{:S(2)}) collective-permute-start(f32[8,256]{1,0:T(8,128)S(1)} %shard_map.149.value.refs_13_), channel_id=1, source_target_pairs={{0,8},{4,12},{8,0},{12,4},{1,9},{5,13},{9,1},{13,5},{2,10},{6,14},... | collective-permute-start | bytes 24584 | tf_op jit(solution)/shard_map/ppermute | solution.py:385
  22.4 6.3 %collective-permute-start.8 = (bf16[80,256]{1,0:T(8,128)(2,1)S(1)}, bf16[80,256]{1,0:T(8,128)(2,1)S(1)}, u32[]{:S(2)}, u32[]{:S(2)}) collective-permute-start(bf16[80,256]{1,0:T(8,128)(2,1)S(1)} %shard_map.150.refs_0_), channel_id=1, source_target_pairs={{0,12},{4,8},{8,4},{12,0},{1,13},{5,9},{9,5},{13,1},{2,14},{6,10},... | collective-permute-start | bytes 122888 | tf_op jit(solution)/shard_map/ppermute | solution.py:442
  24.5 4.3 %collective-permute-start.7 = (bf16[80,256]{1,0:T(8,128)(2,1)S(1)}, bf16[80,256]{1,0:T(8,128)(2,1)S(1)}, u32[]{:S(2)}, u32[]{:S(2)}) collective-permute-start(bf16[80,256]{1,0:T(8,128)(2,1)S(1)} %shard_map.151), channel_id=1, source_target_pairs={{0,4},{4,0},{8,12},{12,8},{1,5},{5,1},{9,13},{13,9},{2,6},{6,2},{1... | collective-permute-start | bytes 122888 | tf_op jit(solution)/shard_map/ppermute | solution.py:442
  30.4 3.1 %collective-permute-start.11 = (f32[8,128]{1,0:T(8,128)S(1)}, f32[8,128]{1,0:T(8,128)S(1)}, u32[]{:S(2)}, u32[]{:S(2)}) collective-permute-start(f32[8,128]{1,0:T(8,128)S(1)} %get-tuple-element.53), channel_id=1, source_target_pairs={{0,3},{1,2},{2,1},{3,0},{4,7},{5,6},{6,5},{7,4},{8,11},{9,10},{10,... | collective-permute-start | bytes 12296 | tf_op jit(solution)/shard_map/ppermute | solution.py:376
  30.5 3.0 %collective-permute-start.10 = (f32[8,128]{1,0:T(8,128)S(1)}, f32[8,128]{1,0:T(8,128)S(1)}, u32[]{:S(2)}, u32[]{:S(2)}) collective-permute-start(f32[8,128]{1,0:T(8,128)S(1)} %get-tuple-element.53), channel_id=1, source_target_pairs={{0,1},{1,0},{2,3},{3,2},{4,5},{5,4},{6,7},{7,6},{8,9},{9,8},{10,11... | collective-permute-start | bytes 12296 | tf_op jit(solution)/shard_map/ppermute | solution.py:376
  31.5 6.1 %collective-permute-start.14 = (f32[8,256]{1,0:T(8,128)S(1)}, f32[8,256]{1,0:T(8,128)S(1)}, u32[]{:S(2)}, u32[]{:S(2)}) collective-permute-start(f32[8,256]{1,0:T(8,128)S(1)} %shard_map.154.value.refs_13_), channel_id=1, source_target_pairs={{0,8},{4,12},{8,0},{12,4},{1,9},{5,13},{9,1},{13,5},{2,10},{6,14},... | collective-permute-start | bytes 24584 | tf_op jit(solution)/shard_map/ppermute | solution.py:385
  33.5 6.3 %collective-permute-start.13 = (bf16[80,256]{1,0:T(8,128)(2,1)S(1)}, bf16[80,256]{1,0:T(8,128)(2,1)S(1)}, u32[]{:S(2)}, u32[]{:S(2)}) collective-permute-start(bf16[80,256]{1,0:T(8,128)(2,1)S(1)} %shard_map.155.refs_0_), channel_id=1, source_target_pairs={{0,12},{4,8},{8,4},{12,0},{1,13},{5,9},{9,5},{13,1},{2,14},{6,10},... | collective-permute-start | bytes 122888 | tf_op jit(solution)/shard_map/ppermute | solution.py:442
  35.6 4.3 %collective-permute-start.12 = (bf16[80,256]{1,0:T(8,128)(2,1)S(1)}, bf16[80,256]{1,0:T(8,128)(2,1)S(1)}, u32[]{:S(2)}, u32[]{:S(2)}) collective-permute-start(bf16[80,256]{1,0:T(8,128)(2,1)S(1)} %shard_map.156), channel_id=1, source_target_pairs={{0,4},{4,0},{8,12},{12,8},{1,5},{5,1},{9,13},{13,9},{2,6},{6,2},{1... | collective-permute-start | bytes 122888 | tf_op jit(solution)/shard_map/ppermute | solution.py:442
  41.5 3.1 %collective-permute-start.16 = (f32[8,128]{1,0:T(8,128)S(1)}, f32[8,128]{1,0:T(8,128)S(1)}, u32[]{:S(2)}, u32[]{:S(2)}) collective-permute-start(f32[8,128]{1,0:T(8,128)S(1)} %get-tuple-element.57), channel_id=1, source_target_pairs={{0,3},{1,2},{2,1},{3,0},{4,7},{5,6},{6,5},{7,4},{8,11},{9,10},{10,... | collective-permute-start | bytes 12296 | tf_op jit(solution)/shard_map/ppermute | solution.py:376
  41.6 3.0 %collective-permute-start.15 = (f32[8,128]{1,0:T(8,128)S(1)}, f32[8,128]{1,0:T(8,128)S(1)}, u32[]{:S(2)}, u32[]{:S(2)}) collective-permute-start(f32[8,128]{1,0:T(8,128)S(1)} %get-tuple-element.57), channel_id=1, source_target_pairs={{0,1},{1,0},{2,3},{3,2},{4,5},{5,4},{6,7},{7,6},{8,9},{9,8},{10,11... | collective-permute-start | bytes 12296 | tf_op jit(solution)/shard_map/ppermute | solution.py:376
  42.6 6.3 %collective-permute-start.19 = (f32[8,256]{1,0:T(8,128)S(1)}, f32[8,256]{1,0:T(8,128)S(1)}, u32[]{:S(2)}, u32[]{:S(2)}) collective-permute-start(f32[8,256]{1,0:T(8,128)S(1)} %shard_map.159.value.refs_13_), channel_id=1, source_target_pairs={{0,8},{4,12},{8,0},{12,4},{1,9},{5,13},{9,1},{13,5},{2,10},{6,14},... | collective-permute-start | bytes 24584 | tf_op jit(solution)/shard_map/ppermute | solution.py:385
  44.6 6.3 %collective-permute-start.18 = (bf16[80,256]{1,0:T(8,128)(2,1)S(1)}, bf16[80,256]{1,0:T(8,128)(2,1)S(1)}, u32[]{:S(2)}, u32[]{:S(2)}) collective-permute-start(bf16[80,256]{1,0:T(8,128)(2,1)S(1)} %shard_map.160.refs_0_), channel_id=1, source_target_pairs={{0,12},{4,8},{8,4},{12,0},{1,13},{5,9},{9,5},{13,1},{2,14},{6,10},... | collective-permute-start | bytes 122888 | tf_op jit(solution)/shard_map/ppermute | solution.py:442
  46.7 4.3 %collective-permute-start.17 = (bf16[80,256]{1,0:T(8,128)(2,1)S(1)}, bf16[80,256]{1,0:T(8,128)(2,1)S(1)}, u32[]{:S(2)}, u32[]{:S(2)}) collective-permute-start(bf16[80,256]{1,0:T(8,128)(2,1)S(1)} %shard_map.161), channel_id=1, source_target_pairs={{0,4},{4,0},{8,12},{12,8},{1,5},{5,1},{9,13},{13,9},{2,6},{6,2},{1... | collective-permute-start | bytes 122888 | tf_op jit(solution)/shard_map/ppermute | solution.py:442

commit v7 on v6

--- a/solution.py
+++ b/solution.py
@@ -102,12 +102,12 @@
 
 
 def later_kernel(noise_in, *refs):
-    half = (len(refs) - 2) // 2
-    noise, sems = refs[half], refs[-1]
+    half = (len(refs) - 3) // 2
+    noise, sems = refs[half + 1], refs[-1]
     pairs = []
     for k in range(noise.shape[0]):
         pairs += rows_of(noise_in.at[k], noise.at[k])
-    pairs += list(zip(refs[:half], refs[half + 1 : -1]))
+    pairs += list(zip(refs[:half], refs[half + 2 : -1]))
     for copy in start_all(pairs, sems):
         copy.wait()
 
@@ -204,7 +204,7 @@
     return jnp.where(position == iota(shape, dim), 1.0, 0.0).astype(BF16)
 
 
-def own_kernel(msg, cols, pick, spread, *, variables, latb, lond):
+def own_kernel(msg, after, cols, pick, spread, *, variables, latb, lond):
     count = msg.shape[1]
     high = latb * variables
     col = jnp.transpose(msg[...])
@@ -412,21 +412,7 @@
         scratch=[pltpu.VMEM(a.shape, a.dtype) for a in entries]
         + [pltpu.SemaphoreType.DMA((latb + len(entries),))],
     )
-    weights = [taps, lift_weight, head_weight.T, gain_1, gain_2]
-    noise, taps, *weights = vmem_call(
-        later_kernel,
-        [((len(STEPS), latb, variables, lond), F32)] + [(a.shape, a.dtype) for a in weights],
-        langevin_noise, *weights,
-        hbm_in=1 + len(weights),
-        scratch=[pltpu.SemaphoreType.DMA((len(STEPS) * latb + len(weights),))],
-    )
-    weights = [weights[0], taps, *weights[1:]]
     high = latb * variables
-    cols, pick, spread = vmem_call(
-        functools.partial(own_kernel, variables=variables, latb=latb, lond=lond),
-        [((5, count, LANES), F32), ((count, high), BF16), ((high, count), BF16)],
-        value,
-    )
     route_a, route_b = swaps(lax.axis_size("band"))
     whole = ((latb, variables, lond), F32)
     value_row, used = 6, 8
@@ -439,6 +425,21 @@
         given = [state, *edges, value]
         (msg_b,) = vmem_call(functools.partial(make, first=False), message, *given)
         (msg_a,) = vmem_call(functools.partial(make, first=True), message, *given, msg_b)
+        if step == 0:
+            weights = [taps, lift_weight, head_weight.T, gain_1, gain_2]
+            noise, taps, *weights = vmem_call(
+                later_kernel,
+                [((len(STEPS), latb, variables, lond), F32)] + [(a.shape, a.dtype) for a in weights],
+                langevin_noise, *weights, msg_a,
+                hbm_in=1 + len(weights),
+                scratch=[pltpu.SemaphoreType.DMA((len(STEPS) * latb + len(weights),))],
+            )
+            weights = [weights[0], taps, *weights[1:]]
+            cols, pick, spread = vmem_call(
+                functools.partial(own_kernel, variables=variables, latb=latb, lond=lond),
+                [((5, count, LANES), F32), ((count, high), BF16), ((high, count), BF16)],
+                value, msg_a,
+            )
         msg_a, msg_b = lax.ppermute(msg_a, "band", route_a), lax.ppermute(msg_b, "band", route_b)
         middle, sums = vmem_call(
             functools.partial(inner_kernel, step=step),

time: 53.5 us -> 53.2 us (level)
  waiting for transfers between devices: 12 us -> 9.18 us
  starting transfers between devices: 18.8 us -> 21.3 us
    ppermute x4, waiting for transfers between devices: 8.76 us -> 6.72 us  [per_device(): lax.ppermute(msg_a, 'band', route_a)]
    ppermute x4, starting transfers between devices: 7.47 us -> 9.43 us  [per_device(): lax.ppermute(msg_b, 'band', route_b)]
    ppermute x8, waiting for transfers between devices: 3.23 us -> 2.43 us  [from_neighbours(): lax.ppermute(block, axis, route)]
    ppermute x8, starting transfers between devices: 5.48 us -> 6.19 us  [from_neighbours(): lax.ppermute(block, axis, route)]
  transfers between devices with their start and end apart: 20 -> 20, of which waited for: 7 -> 6; matrix products, arithmetic and copies ran while one was open for 0% -> 0% of each run, Pallas kernels for 22% -> 22%
where the time goes in v7:
time: 53.2 us; the launch traced here: 53 us
  starting transfers between devices  21.3 us (40%)
  Pallas kernels  20.9 us (39%)
  waiting for transfers between devices  9.18 us (17%)
  between operations  1.62 us (3%)
    pallas_call x23, Pallas kernels, vmem_call(): pl.pallas_call(kernel, out_shape=[out_type(shape, dtype) for shape, dtype...  20.9 us
    ppermute x4, starting transfers between devices, per_device(): lax.ppermute(msg_b, 'band', route_b)  9.43 us
    ppermute x4, waiting for transfers between devices, per_device(): lax.ppermute(msg_a, 'band', route_a)  6.72 us
    ppermute x8, starting transfers between devices, from_neighbours(): lax.ppermute(block, axis, route)  6.19 us
    ppermute x4, starting transfers between devices, from_far(): found.append(lax.ppermute(block, 'band', route))  5.4 us
    ppermute x8, waiting for transfers between devices, from_neighbours(): lax.ppermute(block, axis, route)  2.43 us
  transfers between devices with their start and end apart: 20, of which 6 were waited for; matrix products, arithmetic and copies ran while one was open for 0% of the time, Pallas kernels for 22%

profile of v7, /device:TPU:0, one launch (start us, length us, event | category | flops | bytes accessed | tf_op | source)
XLA Modules:
  0.0 53.0 jit_solution(6079470128134898023)
XLA Ops:
  1.3 1.8 %shard_map.140 = (f32[4,64,256]{2,1,0:T(8,128)S(1)}, f32[8,128]{1,0:T(8,128)S(1)}, f32[8,256]{1,0:T(8,128)S(1)}) custom-call(s32[1]{0:T(128)S(6)} %copy.15.refs_0_, f32[64,4,256]{2,1,0:T(4,128)} %refs_1_.2, s32[1,256]{1,0:T(1,128)} %bitcast.12, s32[1,256]{1,0:T(1,128)} %bitcast.13, s32[1,256]{1,0:T(1,128)} %bitcast.14, f32[1,256]{1,0:T(1,128)} %bitcast.15, ...), custom_call_target="tpu_custom_call" | custom-call | tf_op jit(solution)/shard_map/pallas_call | solution.py:48
  3.1 2.4 %collective-permute-start.1 = (f32[8,128]{1,0:T(8,128)S(1)}, f32[8,128]{1,0:T(8,128)S(1)}, u32[]{:S(2)}, u32[]{:S(2)}) collective-permute-start(f32[8,128]{1,0:T(8,128)S(1)} %get-tuple-element.33), channel_id=1, source_target_pairs={{0,3},{1,2},{2,1},{3,0},{4,7},{5,6},{6,5},{7,4},{8,11},{9,10},{10,... | collective-permute-start | bytes 12296 | tf_op jit(solution)/shard_map/ppermute | solution.py:376
  5.5 0.7 %collective-permute-start = (f32[8,128]{1,0:T(8,128)S(1)}, f32[8,128]{1,0:T(8,128)S(1)}, u32[]{:S(2)}, u32[]{:S(2)}) collective-permute-start(f32[8,128]{1,0:T(8,128)S(1)} %get-tuple-element.33), channel_id=1, source_target_pairs={{0,1},{1,0},{2,3},{3,2},{4,5},{5,4},{6,7},{7,6},{8,9},{9,8},{10,11... | collective-permute-start | bytes 12296 | tf_op jit(solution)/shard_map/ppermute | solution.py:376
  6.2 2.6 %collective-permute-start.4 = (f32[8,256]{1,0:T(8,128)S(1)}, f32[8,256]{1,0:T(8,128)S(1)}, u32[]{:S(2)}, u32[]{:S(2)}) collective-permute-start(f32[8,256]{1,0:T(8,128)S(1)} %get-tuple-element.34.value.msg.own.refs_13_), channel_id=1, source_target_pairs={{0,8},{4,12},{8,0},{12,4},{1,9},{5,13},{9,1},{13,5},{2,10},{6,14},... | collective-permute-start | bytes 24584 | tf_op jit(solution)/shard_map/ppermute | solution.py:385
  8.8 2.5 %collective-permute-start.3 = (bf16[96,256]{1,0:T(8,128)(2,1)S(1)}, bf16[96,256]{1,0:T(8,128)(2,1)S(1)}, u32[]{:S(2)}, u32[]{:S(2)}) collective-permute-start(bf16[96,256]{1,0:T(8,128)(2,1)S(1)} %shard_map.141.refs_0_), channel_id=1, source_target_pairs={{0,12},{4,8},{8,4},{12,0},{1,13},{5,9},{9,5},{13,1},{2,14},{6,10},... | collective-permute-start | bytes 147464 | tf_op jit(solution)/shard_map/ppermute | solution.py:443
  11.4 1.9 %shard_map.143 = (f32[4,4,64,256]{3,2,1,0:T(8,128)S(1)}, bf16[2304,256]{1,0:T(8,128)(2,1)S(1)}, bf16[64,256]{1,0:T(8,128)(2,1)S(1)}, bf16[64,256]{1,0:T(8,128)(2...) custom-call(f32[4,64,4,256]{3,2,1,0:T(4,128)} %noise_in.1, bf16[2304,256]{1,0:T(8,128)(2,1)} %bitcast.10, ...), custom_call_target="tpu_custom_call" | custom-call | tf_op jit(solution)/shard_map/pallas_call | solution.py:48
  13.4 2.0 %shard_map.144 = (f32[2,64,256]{2,1,0:T(8,128)S(1)}, f32[2,256,256]{2,1,0:T(8,128)S(1)}) custom-call(f32[4,64,256]{2,1,0:T(8,128)S(1)} %get-tuple-element.32.state.refs_0_, f32[8,128]{1,0:T(8,128)S(1)} %collective-permute-done.edge_a, f32[8,128]{1,0:T(8,128)S(1)} %collective-permute-done.1.edge_b, f32[4,4,64,256]{3,2,1,0:T(8,128)S(1)} %get-tuple-element.35.noise.refs_3_, ...), custom_call_target="tpu_custom_call" | custom-call | flops 2415919104 | tf_op jit(solution)/shard_map/pallas_call | solution.py:48
  15.4 0.5 shard_map.145
  16.1 1.7 %shard_map.147 = (f32[4,64,256]{2,1,0:T(8,128)S(1)}, f32[8,128]{1,0:T(8,128)S(1)}) custom-call(f32[4,64,256]{2,1,0:T(8,128)S(1)} %get-tuple-element.32.state.refs_0_, f32[2,64,256]{2,1,0:T(8,128)S(1)} %get-tuple-element.41.refs_1_, f32[2,256,256]{2,1,0:T(8,128)S(1)} %get-tuple-element.42.refs_2_, f32[4,4,64,256]{3,2,1,0:T(8,128)S(1)} %get-tuple-element.35.noise.refs_3_, ...), custom_call_target="tpu_custom_call" | custom-call | tf_op jit(solution)/shard_map/pallas_call | solution.py:48
  17.7 1.0 %collective-permute-start.6 = (f32[8,128]{1,0:T(8,128)S(1)}, f32[8,128]{1,0:T(8,128)S(1)}, u32[]{:S(2)}, u32[]{:S(2)}) collective-permute-start(f32[8,128]{1,0:T(8,128)S(1)} %get-tuple-element.48), channel_id=1, source_target_pairs={{0,3},{1,2},{2,1},{3,0},{4,7},{5,6},{6,5},{7,4},{8,11},{9,10},{10,... | collective-permute-start | bytes 12296 | tf_op jit(solution)/shard_map/ppermute | solution.py:376
  18.8 0.7 %collective-permute-start.5 = (f32[8,128]{1,0:T(8,128)S(1)}, f32[8,128]{1,0:T(8,128)S(1)}, u32[]{:S(2)}, u32[]{:S(2)}) collective-permute-start(f32[8,128]{1,0:T(8,128)S(1)} %get-tuple-element.48), channel_id=1, source_target_pairs={{0,1},{1,0},{2,3},{3,2},{4,5},{5,4},{6,7},{7,6},{8,9},{9,8},{10,11... | collective-permute-start | bytes 12296 | tf_op jit(solution)/shard_map/ppermute | solution.py:376
  19.4 0.3 shard_map.149.value.refs_13_
  19.8 1.0 %collective-permute-start.9 = (f32[8,256]{1,0:T(8,128)S(1)}, f32[8,256]{1,0:T(8,128)S(1)}, u32[]{:S(2)}, u32[]{:S(2)}) collective-permute-start(f32[8,256]{1,0:T(8,128)S(1)} %shard_map.149.value.refs_13_), channel_id=1, source_target_pairs={{0,8},{4,12},{8,0},{12,4},{1,9},{5,13},{9,1},{13,5},{2,10},{6,14},... | collective-permute-start | bytes 24584 | tf_op jit(solution)/shard_map/ppermute | solution.py:385
  20.9 3.4 %collective-permute-start.8 = (bf16[80,256]{1,0:T(8,128)(2,1)S(1)}, bf16[80,256]{1,0:T(8,128)(2,1)S(1)}, u32[]{:S(2)}, u32[]{:S(2)}) collective-permute-start(bf16[80,256]{1,0:T(8,128)(2,1)S(1)} %shard_map.150.refs_0_), channel_id=1, source_target_pairs={{0,12},{4,8},{8,4},{12,0},{1,13},{5,9},{9,5},{13,1},{2,14},{6,10},... | collective-permute-start | bytes 122888 | tf_op jit(solution)/shard_map/ppermute | solution.py:443
  24.4 2.0 %shard_map.148 = (f32[2,64,256]{2,1,0:T(8,128)S(1)}, f32[2,256,256]{2,1,0:T(8,128)S(1)}) custom-call(f32[4,64,256]{2,1,0:T(8,128)S(1)} %get-tuple-element.47.state.refs_0_, f32[8,128]{1,0:T(8,128)S(1)} %collective-permute-done.5.edge_a, f32[8,128]{1,0:T(8,128)S(1)} %collective-permute-done.6.edge_b, f32[4,4,64,256]{3,2,1,0:T(8,128)S(1)} %get-tuple-element.35.noise.refs_3_, ...), custom_call_target="tpu_custom_call" | custom-call | flops 2415919104 | tf_op jit(solution)/shard_map/pallas_call | solution.py:48
  26.4 2.0 %collective-permute-done.7.refs_14_ = bf16[80,256]{1,0:T(8,128)(2,1)S(1)} collective-permute-done((bf16[80,256]{1,0:T(8,128)(2,1)S(1)}, bf16[80,256]{1,0:T(8,128)(2,1)S(1)}, u32[]{:S(2)}, u32[]{:S(2)}) %collective-permute-start.7) | collective-permute-done | bytes 40992 | tf_op jit(solution)/shard_map/ppermute | solution.py:443
  28.4 1.7 %shard_map.152 = (f32[4,64,256]{2,1,0:T(8,128)S(1)}, f32[8,128]{1,0:T(8,128)S(1)}) custom-call(f32[4,64,256]{2,1,0:T(8,128)S(1)} %get-tuple-element.47.state.refs_0_, f32[2,64,256]{2,1,0:T(8,128)S(1)} %get-tuple-element.49.refs_1_, f32[2,256,256]{2,1,0:T(8,128)S(1)} %get-tuple-element.50.refs_2_, f32[4,4,64,256]{3,2,1,0:T(8,128)S(1)} %get-tuple-element.35.noise.refs_3_, ...), custom_call_target="tpu_custom_call" | custom-call | tf_op jit(solution)/shard_map/pallas_call | solution.py:48
  30.1 0.6 %collective-permute-start.10 = (f32[8,128]{1,0:T(8,128)S(1)}, f32[8,128]{1,0:T(8,128)S(1)}, u32[]{:S(2)}, u32[]{:S(2)}) collective-permute-start(f32[8,128]{1,0:T(8,128)S(1)} %get-tuple-element.53), channel_id=1, source_target_pairs={{0,1},{1,0},{2,3},{3,2},{4,5},{5,4},{6,7},{7,6},{8,9},{9,8},{10,11... | collective-permute-start | bytes 12296 | tf_op jit(solution)/shard_map/ppermute | solution.py:376
  31.1 1.2 %collective-permute-start.14 = (f32[8,256]{1,0:T(8,128)S(1)}, f32[8,256]{1,0:T(8,128)S(1)}, u32[]{:S(2)}, u32[]{:S(2)}) collective-permute-start(f32[8,256]{1,0:T(8,128)S(1)} %shard_map.154.value.refs_13_), channel_id=1, source_target_pairs={{0,8},{4,12},{8,0},{12,4},{1,9},{5,13},{9,1},{13,5},{2,10},{6,14},... | collective-permute-start | bytes 24584 | tf_op jit(solution)/shard_map/ppermute | solution.py:385
  32.2 0.9 %collective-permute-done.11.edge_b = f32[8,128]{1,0:T(8,128)S(1)} collective-permute-done((f32[8,128]{1,0:T(8,128)S(1)}, f32[8,128]{1,0:T(8,128)S(1)}, u32[]{:S(2)}, u32[]{:S(2)}) %collective-permute-start.11) | collective-permute-done | bytes 4128 | tf_op jit(solution)/shard_map/ppermute | solution.py:376
  33.2 1.8 %collective-permute-start.13 = (bf16[80,256]{1,0:T(8,128)(2,1)S(1)}, bf16[80,256]{1,0:T(8,128)(2,1)S(1)}, u32[]{:S(2)}, u32[]{:S(2)}) collective-permute-start(bf16[80,256]{1,0:T(8,128)(2,1)S(1)} %shard_map.155.refs_0_), channel_id=1, source_target_pairs={{0,12},{4,8},{8,4},{12,0},{1,13},{5,9},{9,5},{13,1},{2,14},{6,10},... | collective-permute-start | bytes 122888 | tf_op jit(solution)/shard_map/ppermute | solution.py:443
  35.1 2.0 %shard_map.153 = (f32[2,64,256]{2,1,0:T(8,128)S(1)}, f32[2,256,256]{2,1,0:T(8,128)S(1)}) custom-call(f32[4,64,256]{2,1,0:T(8,128)S(1)} %get-tuple-element.52.state.refs_0_, f32[8,128]{1,0:T(8,128)S(1)} %collective-permute-done.10.edge_a, f32[8,128]{1,0:T(8,128)S(1)} %collective-permute-done.11.edge_b, f32[4,4,64,256]{3,2,1,0:T(8,128)S(1)} %get-tuple-element.35.noise.refs_3_, ...), custom_call_target="tpu_custom_call" | custom-call | flops 2415919104 | tf_op jit(solution)/shard_map/pallas_call | solution.py:48
  37.0 2.4 %collective-permute-done.12.refs_14_ = bf16[80,256]{1,0:T(8,128)(2,1)S(1)} collective-permute-done((bf16[80,256]{1,0:T(8,128)(2,1)S(1)}, bf16[80,256]{1,0:T(8,128)(2,1)S(1)}, u32[]{:S(2)}, u32[]{:S(2)}) %collective-permute-start.12) | collective-permute-done | bytes 40992 | tf_op jit(solution)/shard_map/ppermute | solution.py:443
  39.5 1.7 %shard_map.157 = (f32[4,64,256]{2,1,0:T(8,128)S(1)}, f32[8,128]{1,0:T(8,128)S(1)}) custom-call(f32[4,64,256]{2,1,0:T(8,128)S(1)} %get-tuple-element.52.state.refs_0_, f32[2,64,256]{2,1,0:T(8,128)S(1)} %get-tuple-element.54.refs_1_, f32[2,256,256]{2,1,0:T(8,128)S(1)} %get-tuple-element.55.refs_2_, f32[4,4,64,256]{3,2,1,0:T(8,128)S(1)} %get-tuple-element.35.noise.refs_3_, ...), custom_call_target="tpu_custom_call" | custom-call | tf_op jit(solution)/shard_map/pallas_call | solution.py:48
  41.2 0.6 %collective-permute-start.15 = (f32[8,128]{1,0:T(8,128)S(1)}, f32[8,128]{1,0:T(8,128)S(1)}, u32[]{:S(2)}, u32[]{:S(2)}) collective-permute-start(f32[8,128]{1,0:T(8,128)S(1)} %get-tuple-element.57), channel_id=1, source_target_pairs={{0,1},{1,0},{2,3},{3,2},{4,5},{5,4},{6,7},{7,6},{8,9},{9,8},{10,11... | collective-permute-start | bytes 12296 | tf_op jit(solution)/shard_map/ppermute | solution.py:376
  41.9 0.3 shard_map.159.value.refs_13_
  42.2 0.6 %collective-permute-start.19 = (f32[8,256]{1,0:T(8,128)S(1)}, f32[8,256]{1,0:T(8,128)S(1)}, u32[]{:S(2)}, u32[]{:S(2)}) collective-permute-start(f32[8,256]{1,0:T(8,128)S(1)} %shard_map.159.value.refs_13_), channel_id=1, source_target_pairs={{0,8},{4,12},{8,0},{12,4},{1,9},{5,13},{9,1},{13,5},{2,10},{6,14},... | collective-permute-start | bytes 24584 | tf_op jit(solution)/shard_map/ppermute | solution.py:385
  42.8 1.4 %collective-permute-done.16.edge_b = f32[8,128]{1,0:T(8,128)S(1)} collective-permute-done((f32[8,128]{1,0:T(8,128)S(1)}, f32[8,128]{1,0:T(8,128)S(1)}, u32[]{:S(2)}, u32[]{:S(2)}) %collective-permute-start.16) | collective-permute-done | bytes 4128 | tf_op jit(solution)/shard_map/ppermute | solution.py:376
  44.3 1.8 %collective-permute-start.18 = (bf16[80,256]{1,0:T(8,128)(2,1)S(1)}, bf16[80,256]{1,0:T(8,128)(2,1)S(1)}, u32[]{:S(2)}, u32[]{:S(2)}) collective-permute-start(bf16[80,256]{1,0:T(8,128)(2,1)S(1)} %shard_map.160.refs_0_), channel_id=1, source_target_pairs={{0,12},{4,8},{8,4},{12,0},{1,13},{5,9},{9,5},{13,1},{2,14},{6,10},... | collective-permute-start | bytes 122888 | tf_op jit(solution)/shard_map/ppermute | solution.py:443
  46.2 2.1 %shard_map.158 = (f32[2,64,256]{2,1,0:T(8,128)S(1)}, f32[2,256,256]{2,1,0:T(8,128)S(1)}) custom-call(f32[4,64,256]{2,1,0:T(8,128)S(1)} %get-tuple-element.56.state.refs_0_, f32[8,128]{1,0:T(8,128)S(1)} %collective-permute-done.15.edge_a, f32[8,128]{1,0:T(8,128)S(1)} %collective-permute-done.16.edge_b, f32[4,4,64,256]{3,2,1,0:T(8,128)S(1)} %get-tuple-element.35.noise.refs_3_, ...), custom_call_target="tpu_custom_call" | custom-call | flops 2415919104 | tf_op jit(solution)/shard_map/pallas_call | solution.py:48
  48.3 2.3 %collective-permute-done.17.refs_14_ = bf16[80,256]{1,0:T(8,128)(2,1)S(1)} collective-permute-done((bf16[80,256]{1,0:T(8,128)(2,1)S(1)}, bf16[80,256]{1,0:T(8,128)(2,1)S(1)}, u32[]{:S(2)}, u32[]{:S(2)}) %collective-permute-start.17) | collective-permute-done | bytes 40992 | tf_op jit(solution)/shard_map/ppermute | solution.py:443
  50.6 2.2 %shard_map.162 = (f32[64,4,256]{2,1,0:T(4,128)}, f32[1,256]{1,0:T(1,128)}) custom-call(f32[4,64,256]{2,1,0:T(8,128)S(1)} %get-tuple-element.56.state.refs_0_, f32[2,64,256]{2,1,0:T(8,128)S(1)} %get-tuple-element.58.refs_1_, f32[2,256,256]{2,1,0:T(8,128)S(1)} %get-tuple-element.59.refs_2_, f32[4,4,64,256]{3,2,1,0:T(8,128)S(1)} %get-tuple-element.35.noise.refs_3_, ...), custom_call_target="tpu_custom_call" | custom-call | tf_op jit(solution)/shard_map/pallas_call | solution.py:48
  (31 shorter events, 1.3 us)
Async XLA Ops:
  3.1 5.7 %collective-permute-start.1 = (f32[8,128]{1,0:T(8,128)S(1)}, f32[8,128]{1,0:T(8,128)S(1)}, u32[]{:S(2)}, u32[]{:S(2)}) collective-permute-start(f32[8,128]{1,0:T(8,128)S(1)} %get-tuple-element.33), channel_id=1, source_target_pairs={{0,3},{1,2},{2,1},{3,0},{4,7},{5,6},{6,5},{7,4},{8,11},{9,10},{10,... | collective-permute-start | bytes 12296 | tf_op jit(solution)/shard_map/ppermute | solution.py:376
  5.5 3.3 %collective-permute-start = (f32[8,128]{1,0:T(8,128)S(1)}, f32[8,128]{1,0:T(8,128)S(1)}, u32[]{:S(2)}, u32[]{:S(2)}) collective-permute-start(f32[8,128]{1,0:T(8,128)S(1)} %get-tuple-element.33), channel_id=1, source_target_pairs={{0,1},{1,0},{2,3},{3,2},{4,5},{5,4},{6,7},{7,6},{8,9},{9,8},{10,11... | collective-permute-start | bytes 12296 | tf_op jit(solution)/shard_map/ppermute | solution.py:376
  6.2 9.7 %collective-permute-start.4 = (f32[8,256]{1,0:T(8,128)S(1)}, f32[8,256]{1,0:T(8,128)S(1)}, u32[]{:S(2)}, u32[]{:S(2)}) collective-permute-start(f32[8,256]{1,0:T(8,128)S(1)} %get-tuple-element.34.value.msg.own.refs_13_), channel_id=1, source_target_pairs={{0,8},{4,12},{8,0},{12,4},{1,9},{5,13},{9,1},{13,5},{2,10},{6,14},... | collective-permute-start | bytes 24584 | tf_op jit(solution)/shard_map/ppermute | solution.py:385
  8.8 7.1 %collective-permute-start.3 = (bf16[96,256]{1,0:T(8,128)(2,1)S(1)}, bf16[96,256]{1,0:T(8,128)(2,1)S(1)}, u32[]{:S(2)}, u32[]{:S(2)}) collective-permute-start(bf16[96,256]{1,0:T(8,128)(2,1)S(1)} %shard_map.141.refs_0_), channel_id=1, source_target_pairs={{0,12},{4,8},{8,4},{12,0},{1,13},{5,9},{9,5},{13,1},{2,14},{6,10},... | collective-permute-start | bytes 147464 | tf_op jit(solution)/shard_map/ppermute | solution.py:443
  11.4 4.5 %collective-permute-start.2 = (bf16[96,256]{1,0:T(8,128)(2,1)S(1)}, bf16[96,256]{1,0:T(8,128)(2,1)S(1)}, u32[]{:S(2)}, u32[]{:S(2)}) collective-permute-start(bf16[96,256]{1,0:T(8,128)(2,1)S(1)} %shard_map.142.refs_5_.after), channel_id=1, source_target_pairs={{0,4},{4,0},{8,12},{12,8},{1,5},{5,1},{9,13},{13,9},{2,6},{6,2},{1... | collective-permute-start | bytes 147464 | tf_op jit(solution)/shard_map/ppermute | solution.py:443
  17.7 3.1 %collective-permute-start.6 = (f32[8,128]{1,0:T(8,128)S(1)}, f32[8,128]{1,0:T(8,128)S(1)}, u32[]{:S(2)}, u32[]{:S(2)}) collective-permute-start(f32[8,128]{1,0:T(8,128)S(1)} %get-tuple-element.48), channel_id=1, source_target_pairs={{0,3},{1,2},{2,1},{3,0},{4,7},{5,6},{6,5},{7,4},{8,11},{9,10},{10,... | collective-permute-start | bytes 12296 | tf_op jit(solution)/shard_map/ppermute | solution.py:376
  18.8 2.1 %collective-permute-start.5 = (f32[8,128]{1,0:T(8,128)S(1)}, f32[8,128]{1,0:T(8,128)S(1)}, u32[]{:S(2)}, u32[]{:S(2)}) collective-permute-start(f32[8,128]{1,0:T(8,128)S(1)} %get-tuple-element.48), channel_id=1, source_target_pairs={{0,1},{1,0},{2,3},{3,2},{4,5},{5,4},{6,7},{7,6},{8,9},{9,8},{10,11... | collective-permute-start | bytes 12296 | tf_op jit(solution)/shard_map/ppermute | solution.py:376
  19.8 6.6 %collective-permute-start.9 = (f32[8,256]{1,0:T(8,128)S(1)}, f32[8,256]{1,0:T(8,128)S(1)}, u32[]{:S(2)}, u32[]{:S(2)}) collective-permute-start(f32[8,256]{1,0:T(8,128)S(1)} %shard_map.149.value.refs_13_), channel_id=1, source_target_pairs={{0,8},{4,12},{8,0},{12,4},{1,9},{5,13},{9,1},{13,5},{2,10},{6,14},... | collective-permute-start | bytes 24584 | tf_op jit(solution)/shard_map/ppermute | solution.py:385
  20.9 7.5 %collective-permute-start.8 = (bf16[80,256]{1,0:T(8,128)(2,1)S(1)}, bf16[80,256]{1,0:T(8,128)(2,1)S(1)}, u32[]{:S(2)}, u32[]{:S(2)}) collective-permute-start(bf16[80,256]{1,0:T(8,128)(2,1)S(1)} %shard_map.150.refs_0_), channel_id=1, source_target_pairs={{0,12},{4,8},{8,4},{12,0},{1,13},{5,9},{9,5},{13,1},{2,14},{6,10},... | collective-permute-start | bytes 122888 | tf_op jit(solution)/shard_map/ppermute | solution.py:443
  24.3 4.1 %collective-permute-start.7 = (bf16[80,256]{1,0:T(8,128)(2,1)S(1)}, bf16[80,256]{1,0:T(8,128)(2,1)S(1)}, u32[]{:S(2)}, u32[]{:S(2)}) collective-permute-start(bf16[80,256]{1,0:T(8,128)(2,1)S(1)} %shard_map.151), channel_id=1, source_target_pairs={{0,4},{4,0},{8,12},{12,8},{1,5},{5,1},{9,13},{13,9},{2,6},{6,2},{1... | collective-permute-start | bytes 122888 | tf_op jit(solution)/shard_map/ppermute | solution.py:443
  30.0 3.1 %collective-permute-start.11 = (f32[8,128]{1,0:T(8,128)S(1)}, f32[8,128]{1,0:T(8,128)S(1)}, u32[]{:S(2)}, u32[]{:S(2)}) collective-permute-start(f32[8,128]{1,0:T(8,128)S(1)} %get-tuple-element.53), channel_id=1, source_target_pairs={{0,3},{1,2},{2,1},{3,0},{4,7},{5,6},{6,5},{7,4},{8,11},{9,10},{10,... | collective-permute-start | bytes 12296 | tf_op jit(solution)/shard_map/ppermute | solution.py:376
  30.1 3.0 %collective-permute-start.10 = (f32[8,128]{1,0:T(8,128)S(1)}, f32[8,128]{1,0:T(8,128)S(1)}, u32[]{:S(2)}, u32[]{:S(2)}) collective-permute-start(f32[8,128]{1,0:T(8,128)S(1)} %get-tuple-element.53), channel_id=1, source_target_pairs={{0,1},{1,0},{2,3},{3,2},{4,5},{5,4},{6,7},{7,6},{8,9},{9,8},{10,11... | collective-permute-start | bytes 12296 | tf_op jit(solution)/shard_map/ppermute | solution.py:376
  31.1 6.0 %collective-permute-start.14 = (f32[8,256]{1,0:T(8,128)S(1)}, f32[8,256]{1,0:T(8,128)S(1)}, u32[]{:S(2)}, u32[]{:S(2)}) collective-permute-start(f32[8,256]{1,0:T(8,128)S(1)} %shard_map.154.value.refs_13_), channel_id=1, source_target_pairs={{0,8},{4,12},{8,0},{12,4},{1,9},{5,13},{9,1},{13,5},{2,10},{6,14},... | collective-permute-start | bytes 24584 | tf_op jit(solution)/shard_map/ppermute | solution.py:385
  33.2 6.3 %collective-permute-start.13 = (bf16[80,256]{1,0:T(8,128)(2,1)S(1)}, bf16[80,256]{1,0:T(8,128)(2,1)S(1)}, u32[]{:S(2)}, u32[]{:S(2)}) collective-permute-start(bf16[80,256]{1,0:T(8,128)(2,1)S(1)} %shard_map.155.refs_0_), channel_id=1, source_target_pairs={{0,12},{4,8},{8,4},{12,0},{1,13},{5,9},{9,5},{13,1},{2,14},{6,10},... | collective-permute-start | bytes 122888 | tf_op jit(solution)/shard_map/ppermute | solution.py:443
  35.0 4.5 %collective-permute-start.12 = (bf16[80,256]{1,0:T(8,128)(2,1)S(1)}, bf16[80,256]{1,0:T(8,128)(2,1)S(1)}, u32[]{:S(2)}, u32[]{:S(2)}) collective-permute-start(bf16[80,256]{1,0:T(8,128)(2,1)S(1)} %shard_map.156), channel_id=1, source_target_pairs={{0,4},{4,0},{8,12},{12,8},{1,5},{5,1},{9,13},{13,9},{2,6},{6,2},{1... | collective-permute-start | bytes 122888 | tf_op jit(solution)/shard_map/ppermute | solution.py:443
  41.1 3.1 %collective-permute-start.16 = (f32[8,128]{1,0:T(8,128)S(1)}, f32[8,128]{1,0:T(8,128)S(1)}, u32[]{:S(2)}, u32[]{:S(2)}) collective-permute-start(f32[8,128]{1,0:T(8,128)S(1)} %get-tuple-element.57), channel_id=1, source_target_pairs={{0,3},{1,2},{2,1},{3,0},{4,7},{5,6},{6,5},{7,4},{8,11},{9,10},{10,... | collective-permute-start | bytes 12296 | tf_op jit(solution)/shard_map/ppermute | solution.py:376
  41.2 3.0 %collective-permute-start.15 = (f32[8,128]{1,0:T(8,128)S(1)}, f32[8,128]{1,0:T(8,128)S(1)}, u32[]{:S(2)}, u32[]{:S(2)}) collective-permute-start(f32[8,128]{1,0:T(8,128)S(1)} %get-tuple-element.57), channel_id=1, source_target_pairs={{0,1},{1,0},{2,3},{3,2},{4,5},{5,4},{6,7},{7,6},{8,9},{9,8},{10,11... | collective-permute-start | bytes 12296 | tf_op jit(solution)/shard_map/ppermute | solution.py:376
  42.2 6.1 %collective-permute-start.19 = (f32[8,256]{1,0:T(8,128)S(1)}, f32[8,256]{1,0:T(8,128)S(1)}, u32[]{:S(2)}, u32[]{:S(2)}) collective-permute-start(f32[8,256]{1,0:T(8,128)S(1)} %shard_map.159.value.refs_13_), channel_id=1, source_target_pairs={{0,8},{4,12},{8,0},{12,4},{1,9},{5,13},{9,1},{13,5},{2,10},{6,14},... | collective-permute-start | bytes 24584 | tf_op jit(solution)/shard_map/ppermute | solution.py:385
  44.3 6.3 %collective-permute-start.18 = (bf16[80,256]{1,0:T(8,128)(2,1)S(1)}, bf16[80,256]{1,0:T(8,128)(2,1)S(1)}, u32[]{:S(2)}, u32[]{:S(2)}) collective-permute-start(bf16[80,256]{1,0:T(8,128)(2,1)S(1)} %shard_map.160.refs_0_), channel_id=1, source_target_pairs={{0,12},{4,8},{8,4},{12,0},{1,13},{5,9},{9,5},{13,1},{2,14},{6,10},... | collective-permute-start | bytes 122888 | tf_op jit(solution)/shard_map/ppermute | solution.py:443
  46.1 4.5 %collective-permute-start.17 = (bf16[80,256]{1,0:T(8,128)(2,1)S(1)}, bf16[80,256]{1,0:T(8,128)(2,1)S(1)}, u32[]{:S(2)}, u32[]{:S(2)}) collective-permute-start(bf16[80,256]{1,0:T(8,128)(2,1)S(1)} %shard_map.161), channel_id=1, source_target_pairs={{0,4},{4,0},{8,12},{12,8},{1,5},{5,1},{9,13},{13,9},{2,6},{6,2},{1... | collective-permute-start | bytes 122888 | tf_op jit(solution)/shard_map/ppermute | solution.py:443

commit v8 on v7

--- a/solution.py
+++ b/solution.py
@@ -475,7 +475,7 @@
             return state, innov.reshape(-1)
         state, edge = vmem_call(update, [whole, ((2 * latb, LANES), F32)], *given)
         (value,) = vmem_call(
-            value_kernel, [((8, count), F32)], state, keys, cols, pick,
+            value_kernel, [((1, count), F32)], state, keys, cols, pick,
             scratch=[pltpu.VMEM((high, 2 * lond), BF16)],
         )
         value_row, used = 0, 1

time: 53.2 us -> 53.2 us (level)
  no operation moved by 1% of the time
where the time goes in v8:
time: 53.2 us; the launch traced here: 53 us
  starting transfers between devices  21.3 us (40%)
  Pallas kernels  20.9 us (39%)
  waiting for transfers between devices  9.18 us (17%)
  between operations  1.62 us (3%)
    pallas_call x23, Pallas kernels, vmem_call(): pl.pallas_call(kernel, out_shape=[out_type(shape, dtype) for shape, dtype...  20.9 us
    ppermute x4, starting transfers between devices, per_device(): lax.ppermute(msg_b, 'band', route_b)  9.43 us
    ppermute x4, waiting for transfers between devices, per_device(): lax.ppermute(msg_a, 'band', route_a)  6.71 us
    ppermute x8, starting transfers between devices, from_neighbours(): lax.ppermute(block, axis, route)  6.18 us
    ppermute x4, starting transfers between devices, from_far(): found.append(lax.ppermute(block, 'band', route))  5.4 us
    ppermute x8, waiting for transfers between devices, from_neighbours(): lax.ppermute(block, axis, route)  2.45 us
  transfers between devices with their start and end apart: 20, of which 6 were waited for; matrix products, arithmetic and copies ran while one was open for 0% of the time, Pallas kernels for 22%

profile of v8, /device:TPU:0, one launch (start us, length us, event | category | flops | bytes accessed | tf_op | source)
XLA Modules:
  0.0 53.0 jit_solution(11628269750727161003)
XLA Ops:
  1.3 1.8 %shard_map.140 = (f32[4,64,256]{2,1,0:T(8,128)S(1)}, f32[8,128]{1,0:T(8,128)S(1)}, f32[8,256]{1,0:T(8,128)S(1)}) custom-call(s32[1]{0:T(128)S(6)} %copy.15.refs_0_, f32[64,4,256]{2,1,0:T(4,128)} %refs_1_.2, s32[1,256]{1,0:T(1,128)} %bitcast.12, s32[1,256]{1,0:T(1,128)} %bitcast.13, s32[1,256]{1,0:T(1,128)} %bitcast.14, f32[1,256]{1,0:T(1,128)} %bitcast.15, ...), custom_call_target="tpu_custom_call" | custom-call | tf_op jit(solution)/shard_map/pallas_call | solution.py:48
  3.1 2.4 %collective-permute-start.1 = (f32[8,128]{1,0:T(8,128)S(1)}, f32[8,128]{1,0:T(8,128)S(1)}, u32[]{:S(2)}, u32[]{:S(2)}) collective-permute-start(f32[8,128]{1,0:T(8,128)S(1)} %get-tuple-element.33), channel_id=1, source_target_pairs={{0,3},{1,2},{2,1},{3,0},{4,7},{5,6},{6,5},{7,4},{8,11},{9,10},{10,... | collective-permute-start | bytes 12296 | tf_op jit(solution)/shard_map/ppermute | solution.py:376
  5.5 0.7 %collective-permute-start = (f32[8,128]{1,0:T(8,128)S(1)}, f32[8,128]{1,0:T(8,128)S(1)}, u32[]{:S(2)}, u32[]{:S(2)}) collective-permute-start(f32[8,128]{1,0:T(8,128)S(1)} %get-tuple-element.33), channel_id=1, source_target_pairs={{0,1},{1,0},{2,3},{3,2},{4,5},{5,4},{6,7},{7,6},{8,9},{9,8},{10,11... | collective-permute-start | bytes 12296 | tf_op jit(solution)/shard_map/ppermute | solution.py:376
  6.2 2.6 %collective-permute-start.4 = (f32[8,256]{1,0:T(8,128)S(1)}, f32[8,256]{1,0:T(8,128)S(1)}, u32[]{:S(2)}, u32[]{:S(2)}) collective-permute-start(f32[8,256]{1,0:T(8,128)S(1)} %get-tuple-element.34.value.msg.own.refs_13_), channel_id=1, source_target_pairs={{0,8},{4,12},{8,0},{12,4},{1,9},{5,13},{9,1},{13,5},{2,10},{6,14},... | collective-permute-start | bytes 24584 | tf_op jit(solution)/shard_map/ppermute | solution.py:385
  8.8 2.5 %collective-permute-start.3 = (bf16[96,256]{1,0:T(8,128)(2,1)S(1)}, bf16[96,256]{1,0:T(8,128)(2,1)S(1)}, u32[]{:S(2)}, u32[]{:S(2)}) collective-permute-start(bf16[96,256]{1,0:T(8,128)(2,1)S(1)} %shard_map.141.refs_0_), channel_id=1, source_target_pairs={{0,12},{4,8},{8,4},{12,0},{1,13},{5,9},{9,5},{13,1},{2,14},{6,10},... | collective-permute-start | bytes 147464 | tf_op jit(solution)/shard_map/ppermute | solution.py:443
  11.4 1.9 %shard_map.143 = (f32[4,4,64,256]{3,2,1,0:T(8,128)S(1)}, bf16[2304,256]{1,0:T(8,128)(2,1)S(1)}, bf16[64,256]{1,0:T(8,128)(2,1)S(1)}, bf16[64,256]{1,0:T(8,128)(2...) custom-call(f32[4,64,4,256]{3,2,1,0:T(4,128)} %noise_in.1, bf16[2304,256]{1,0:T(8,128)(2,1)} %bitcast.10, ...), custom_call_target="tpu_custom_call" | custom-call | tf_op jit(solution)/shard_map/pallas_call | solution.py:48
  13.4 2.0 %shard_map.144 = (f32[2,64,256]{2,1,0:T(8,128)S(1)}, f32[2,256,256]{2,1,0:T(8,128)S(1)}) custom-call(f32[4,64,256]{2,1,0:T(8,128)S(1)} %get-tuple-element.32.state.refs_0_, f32[8,128]{1,0:T(8,128)S(1)} %collective-permute-done.edge_a, f32[8,128]{1,0:T(8,128)S(1)} %collective-permute-done.1.edge_b, f32[4,4,64,256]{3,2,1,0:T(8,128)S(1)} %get-tuple-element.35.noise.refs_3_, ...), custom_call_target="tpu_custom_call" | custom-call | flops 2415919104 | tf_op jit(solution)/shard_map/pallas_call | solution.py:48
  15.3 0.5 shard_map.145
  16.1 1.7 %shard_map.147 = (f32[4,64,256]{2,1,0:T(8,128)S(1)}, f32[8,128]{1,0:T(8,128)S(1)}) custom-call(f32[4,64,256]{2,1,0:T(8,128)S(1)} %get-tuple-element.32.state.refs_0_, f32[2,64,256]{2,1,0:T(8,128)S(1)} %get-tuple-element.41.refs_1_, f32[2,256,256]{2,1,0:T(8,128)S(1)} %get-tuple-element.42.refs_2_, f32[4,4,64,256]{3,2,1,0:T(8,128)S(1)} %get-tuple-element.35.noise.refs_3_, ...), custom_call_target="tpu_custom_call" | custom-call | tf_op jit(solution)/shard_map/pallas_call | solution.py:48
  17.7 1.0 %collective-permute-start.6 = (f32[8,128]{1,0:T(8,128)S(1)}, f32[8,128]{1,0:T(8,128)S(1)}, u32[]{:S(2)}, u32[]{:S(2)}) collective-permute-start(f32[8,128]{1,0:T(8,128)S(1)} %get-tuple-element.48), channel_id=1, source_target_pairs={{0,3},{1,2},{2,1},{3,0},{4,7},{5,6},{6,5},{7,4},{8,11},{9,10},{10,... | collective-permute-start | bytes 12296 | tf_op jit(solution)/shard_map/ppermute | solution.py:376
  18.8 0.7 %collective-permute-start.5 = (f32[8,128]{1,0:T(8,128)S(1)}, f32[8,128]{1,0:T(8,128)S(1)}, u32[]{:S(2)}, u32[]{:S(2)}) collective-permute-start(f32[8,128]{1,0:T(8,128)S(1)} %get-tuple-element.48), channel_id=1, source_target_pairs={{0,1},{1,0},{2,3},{3,2},{4,5},{5,4},{6,7},{7,6},{8,9},{9,8},{10,11... | collective-permute-start | bytes 12296 | tf_op jit(solution)/shard_map/ppermute | solution.py:376
  19.5 0.3 shard_map.149.value.refs_13_
  19.8 1.0 %collective-permute-start.9 = (f32[1,256]{1,0:T(1,128)S(1)}, f32[1,256]{1,0:T(1,128)S(1)}, u32[]{:S(2)}, u32[]{:S(2)}) collective-permute-start(f32[1,256]{1,0:T(1,128)S(1)} %shard_map.149.value.refs_13_), channel_id=1, source_target_pairs={{0,8},{4,12},{8,0},{12,4},{1,9},{5,13},{9,1},{13,5},{2,10},{6,14},... | collective-permute-start | bytes 3080 | tf_op jit(solution)/shard_map/ppermute | solution.py:385
  20.9 3.4 %collective-permute-start.8 = (bf16[80,256]{1,0:T(8,128)(2,1)S(1)}, bf16[80,256]{1,0:T(8,128)(2,1)S(1)}, u32[]{:S(2)}, u32[]{:S(2)}) collective-permute-start(bf16[80,256]{1,0:T(8,128)(2,1)S(1)} %shard_map.150.refs_0_), channel_id=1, source_target_pairs={{0,12},{4,8},{8,4},{12,0},{1,13},{5,9},{9,5},{13,1},{2,14},{6,10},... | collective-permute-start | bytes 122888 | tf_op jit(solution)/shard_map/ppermute | solution.py:443
  24.4 2.0 %shard_map.148 = (f32[2,64,256]{2,1,0:T(8,128)S(1)}, f32[2,256,256]{2,1,0:T(8,128)S(1)}) custom-call(f32[4,64,256]{2,1,0:T(8,128)S(1)} %get-tuple-element.47.state.refs_0_, f32[8,128]{1,0:T(8,128)S(1)} %collective-permute-done.5.edge_a, f32[8,128]{1,0:T(8,128)S(1)} %collective-permute-done.6.edge_b, f32[4,4,64,256]{3,2,1,0:T(8,128)S(1)} %get-tuple-element.35.noise.refs_3_, ...), custom_call_target="tpu_custom_call" | custom-call | flops 2415919104 | tf_op jit(solution)/shard_map/pallas_call | solution.py:48
  26.4 2.0 %collective-permute-done.7.refs_14_ = bf16[80,256]{1,0:T(8,128)(2,1)S(1)} collective-permute-done((bf16[80,256]{1,0:T(8,128)(2,1)S(1)}, bf16[80,256]{1,0:T(8,128)(2,1)S(1)}, u32[]{:S(2)}, u32[]{:S(2)}) %collective-permute-start.7) | collective-permute-done | bytes 40992 | tf_op jit(solution)/shard_map/ppermute | solution.py:443
  28.4 1.7 %shard_map.152 = (f32[4,64,256]{2,1,0:T(8,128)S(1)}, f32[8,128]{1,0:T(8,128)S(1)}) custom-call(f32[4,64,256]{2,1,0:T(8,128)S(1)} %get-tuple-element.47.state.refs_0_, f32[2,64,256]{2,1,0:T(8,128)S(1)} %get-tuple-element.49.refs_1_, f32[2,256,256]{2,1,0:T(8,128)S(1)} %get-tuple-element.50.refs_2_, f32[4,4,64,256]{3,2,1,0:T(8,128)S(1)} %get-tuple-element.35.noise.refs_3_, ...), custom_call_target="tpu_custom_call" | custom-call | tf_op jit(solution)/shard_map/pallas_call | solution.py:48
  30.1 0.6 %collective-permute-start.10 = (f32[8,128]{1,0:T(8,128)S(1)}, f32[8,128]{1,0:T(8,128)S(1)}, u32[]{:S(2)}, u32[]{:S(2)}) collective-permute-start(f32[8,128]{1,0:T(8,128)S(1)} %get-tuple-element.53), channel_id=1, source_target_pairs={{0,1},{1,0},{2,3},{3,2},{4,5},{5,4},{6,7},{7,6},{8,9},{9,8},{10,11... | collective-permute-start | bytes 12296 | tf_op jit(solution)/shard_map/ppermute | solution.py:376
  30.7 0.3 shard_map.154.value.refs_13_
  31.0 1.2 %collective-permute-start.14 = (f32[1,256]{1,0:T(1,128)S(1)}, f32[1,256]{1,0:T(1,128)S(1)}, u32[]{:S(2)}, u32[]{:S(2)}) collective-permute-start(f32[1,256]{1,0:T(1,128)S(1)} %shard_map.154.value.refs_13_), channel_id=1, source_target_pairs={{0,8},{4,12},{8,0},{12,4},{1,9},{5,13},{9,1},{13,5},{2,10},{6,14},... | collective-permute-start | bytes 3080 | tf_op jit(solution)/shard_map/ppermute | solution.py:385
  32.2 0.9 %collective-permute-done.11.edge_b = f32[8,128]{1,0:T(8,128)S(1)} collective-permute-done((f32[8,128]{1,0:T(8,128)S(1)}, f32[8,128]{1,0:T(8,128)S(1)}, u32[]{:S(2)}, u32[]{:S(2)}) %collective-permute-start.11) | collective-permute-done | bytes 4128 | tf_op jit(solution)/shard_map/ppermute | solution.py:376
  33.2 1.8 %collective-permute-start.13 = (bf16[80,256]{1,0:T(8,128)(2,1)S(1)}, bf16[80,256]{1,0:T(8,128)(2,1)S(1)}, u32[]{:S(2)}, u32[]{:S(2)}) collective-permute-start(bf16[80,256]{1,0:T(8,128)(2,1)S(1)} %shard_map.155.refs_0_), channel_id=1, source_target_pairs={{0,12},{4,8},{8,4},{12,0},{1,13},{5,9},{9,5},{13,1},{2,14},{6,10},... | collective-permute-start | bytes 122888 | tf_op jit(solution)/shard_map/ppermute | solution.py:443
  35.1 2.0 %shard_map.153 = (f32[2,64,256]{2,1,0:T(8,128)S(1)}, f32[2,256,256]{2,1,0:T(8,128)S(1)}) custom-call(f32[4,64,256]{2,1,0:T(8,128)S(1)} %get-tuple-element.52.state.refs_0_, f32[8,128]{1,0:T(8,128)S(1)} %collective-permute-done.10.edge_a, f32[8,128]{1,0:T(8,128)S(1)} %collective-permute-done.11.edge_b, f32[4,4,64,256]{3,2,1,0:T(8,128)S(1)} %get-tuple-element.35.noise.refs_3_, ...), custom_call_target="tpu_custom_call" | custom-call | flops 2415919104 | tf_op jit(solution)/shard_map/pallas_call | solution.py:48
  37.0 2.4 %collective-permute-done.12.refs_14_ = bf16[80,256]{1,0:T(8,128)(2,1)S(1)} collective-permute-done((bf16[80,256]{1,0:T(8,128)(2,1)S(1)}, bf16[80,256]{1,0:T(8,128)(2,1)S(1)}, u32[]{:S(2)}, u32[]{:S(2)}) %collective-permute-start.12) | collective-permute-done | bytes 40992 | tf_op jit(solution)/shard_map/ppermute | solution.py:443
  39.5 1.7 %shard_map.157 = (f32[4,64,256]{2,1,0:T(8,128)S(1)}, f32[8,128]{1,0:T(8,128)S(1)}) custom-call(f32[4,64,256]{2,1,0:T(8,128)S(1)} %get-tuple-element.52.state.refs_0_, f32[2,64,256]{2,1,0:T(8,128)S(1)} %get-tuple-element.54.refs_1_, f32[2,256,256]{2,1,0:T(8,128)S(1)} %get-tuple-element.55.refs_2_, f32[4,4,64,256]{3,2,1,0:T(8,128)S(1)} %get-tuple-element.35.noise.refs_3_, ...), custom_call_target="tpu_custom_call" | custom-call | tf_op jit(solution)/shard_map/pallas_call | solution.py:48
  41.2 0.6 %collective-permute-start.15 = (f32[8,128]{1,0:T(8,128)S(1)}, f32[8,128]{1,0:T(8,128)S(1)}, u32[]{:S(2)}, u32[]{:S(2)}) collective-permute-start(f32[8,128]{1,0:T(8,128)S(1)} %get-tuple-element.57), channel_id=1, source_target_pairs={{0,1},{1,0},{2,3},{3,2},{4,5},{5,4},{6,7},{7,6},{8,9},{9,8},{10,11... | collective-permute-start | bytes 12296 | tf_op jit(solution)/shard_map/ppermute | solution.py:376
  42.2 0.6 %collective-permute-start.19 = (f32[1,256]{1,0:T(1,128)S(1)}, f32[1,256]{1,0:T(1,128)S(1)}, u32[]{:S(2)}, u32[]{:S(2)}) collective-permute-start(f32[1,256]{1,0:T(1,128)S(1)} %shard_map.159.value.refs_13_), channel_id=1, source_target_pairs={{0,8},{4,12},{8,0},{12,4},{1,9},{5,13},{9,1},{13,5},{2,10},{6,14},... | collective-permute-start | bytes 3080 | tf_op jit(solution)/shard_map/ppermute | solution.py:385
  42.8 1.4 %collective-permute-done.16.edge_b = f32[8,128]{1,0:T(8,128)S(1)} collective-permute-done((f32[8,128]{1,0:T(8,128)S(1)}, f32[8,128]{1,0:T(8,128)S(1)}, u32[]{:S(2)}, u32[]{:S(2)}) %collective-permute-start.16) | collective-permute-done | bytes 4128 | tf_op jit(solution)/shard_map/ppermute | solution.py:376
  44.3 1.8 %collective-permute-start.18 = (bf16[80,256]{1,0:T(8,128)(2,1)S(1)}, bf16[80,256]{1,0:T(8,128)(2,1)S(1)}, u32[]{:S(2)}, u32[]{:S(2)}) collective-permute-start(bf16[80,256]{1,0:T(8,128)(2,1)S(1)} %shard_map.160.refs_0_), channel_id=1, source_target_pairs={{0,12},{4,8},{8,4},{12,0},{1,13},{5,9},{9,5},{13,1},{2,14},{6,10},... | collective-permute-start | bytes 122888 | tf_op jit(solution)/shard_map/ppermute | solution.py:443
  46.1 2.1 %shard_map.158 = (f32[2,64,256]{2,1,0:T(8,128)S(1)}, f32[2,256,256]{2,1,0:T(8,128)S(1)}) custom-call(f32[4,64,256]{2,1,0:T(8,128)S(1)} %get-tuple-element.56.state.refs_0_, f32[8,128]{1,0:T(8,128)S(1)} %collective-permute-done.15.edge_a, f32[8,128]{1,0:T(8,128)S(1)} %collective-permute-done.16.edge_b, f32[4,4,64,256]{3,2,1,0:T(8,128)S(1)} %get-tuple-element.35.noise.refs_3_, ...), custom_call_target="tpu_custom_call" | custom-call | flops 2415919104 | tf_op jit(solution)/shard_map/pallas_call | solution.py:48
  48.3 2.3 %collective-permute-done.17.refs_14_ = bf16[80,256]{1,0:T(8,128)(2,1)S(1)} collective-permute-done((bf16[80,256]{1,0:T(8,128)(2,1)S(1)}, bf16[80,256]{1,0:T(8,128)(2,1)S(1)}, u32[]{:S(2)}, u32[]{:S(2)}) %collective-permute-start.17) | collective-permute-done | bytes 40992 | tf_op jit(solution)/shard_map/ppermute | solution.py:443
  50.6 2.3 %shard_map.162 = (f32[64,4,256]{2,1,0:T(4,128)}, f32[1,256]{1,0:T(1,128)}) custom-call(f32[4,64,256]{2,1,0:T(8,128)S(1)} %get-tuple-element.56.state.refs_0_, f32[2,64,256]{2,1,0:T(8,128)S(1)} %get-tuple-element.58.refs_1_, f32[2,256,256]{2,1,0:T(8,128)S(1)} %get-tuple-element.59.refs_2_, f32[4,4,64,256]{3,2,1,0:T(8,128)S(1)} %get-tuple-element.35.noise.refs_3_, ...), custom_call_target="tpu_custom_call" | custom-call | tf_op jit(solution)/shard_map/pallas_call | solution.py:48
  (31 shorter events, 1.3 us)
Async XLA Ops:
  3.1 5.7 %collective-permute-start.1 = (f32[8,128]{1,0:T(8,128)S(1)}, f32[8,128]{1,0:T(8,128)S(1)}, u32[]{:S(2)}, u32[]{:S(2)}) collective-permute-start(f32[8,128]{1,0:T(8,128)S(1)} %get-tuple-element.33), channel_id=1, source_target_pairs={{0,3},{1,2},{2,1},{3,0},{4,7},{5,6},{6,5},{7,4},{8,11},{9,10},{10,... | collective-permute-start | bytes 12296 | tf_op jit(solution)/shard_map/ppermute | solution.py:376
  5.5 3.3 %collective-permute-start = (f32[8,128]{1,0:T(8,128)S(1)}, f32[8,128]{1,0:T(8,128)S(1)}, u32[]{:S(2)}, u32[]{:S(2)}) collective-permute-start(f32[8,128]{1,0:T(8,128)S(1)} %get-tuple-element.33), channel_id=1, source_target_pairs={{0,1},{1,0},{2,3},{3,2},{4,5},{5,4},{6,7},{7,6},{8,9},{9,8},{10,11... | collective-permute-start | bytes 12296 | tf_op jit(solution)/shard_map/ppermute | solution.py:376
  6.2 9.7 %collective-permute-start.4 = (f32[8,256]{1,0:T(8,128)S(1)}, f32[8,256]{1,0:T(8,128)S(1)}, u32[]{:S(2)}, u32[]{:S(2)}) collective-permute-start(f32[8,256]{1,0:T(8,128)S(1)} %get-tuple-element.34.value.msg.own.refs_13_), channel_id=1, source_target_pairs={{0,8},{4,12},{8,0},{12,4},{1,9},{5,13},{9,1},{13,5},{2,10},{6,14},... | collective-permute-start | bytes 24584 | tf_op jit(solution)/shard_map/ppermute | solution.py:385
  8.8 7.1 %collective-permute-start.3 = (bf16[96,256]{1,0:T(8,128)(2,1)S(1)}, bf16[96,256]{1,0:T(8,128)(2,1)S(1)}, u32[]{:S(2)}, u32[]{:S(2)}) collective-permute-start(bf16[96,256]{1,0:T(8,128)(2,1)S(1)} %shard_map.141.refs_0_), channel_id=1, source_target_pairs={{0,12},{4,8},{8,4},{12,0},{1,13},{5,9},{9,5},{13,1},{2,14},{6,10},... | collective-permute-start | bytes 147464 | tf_op jit(solution)/shard_map/ppermute | solution.py:443
  11.4 4.5 %collective-permute-start.2 = (bf16[96,256]{1,0:T(8,128)(2,1)S(1)}, bf16[96,256]{1,0:T(8,128)(2,1)S(1)}, u32[]{:S(2)}, u32[]{:S(2)}) collective-permute-start(bf16[96,256]{1,0:T(8,128)(2,1)S(1)} %shard_map.142.refs_5_.after), channel_id=1, source_target_pairs={{0,4},{4,0},{8,12},{12,8},{1,5},{5,1},{9,13},{13,9},{2,6},{6,2},{1... | collective-permute-start | bytes 147464 | tf_op jit(solution)/shard_map/ppermute | solution.py:443
  17.7 3.1 %collective-permute-start.6 = (f32[8,128]{1,0:T(8,128)S(1)}, f32[8,128]{1,0:T(8,128)S(1)}, u32[]{:S(2)}, u32[]{:S(2)}) collective-permute-start(f32[8,128]{1,0:T(8,128)S(1)} %get-tuple-element.48), channel_id=1, source_target_pairs={{0,3},{1,2},{2,1},{3,0},{4,7},{5,6},{6,5},{7,4},{8,11},{9,10},{10,... | collective-permute-start | bytes 12296 | tf_op jit(solution)/shard_map/ppermute | solution.py:376
  18.8 2.1 %collective-permute-start.5 = (f32[8,128]{1,0:T(8,128)S(1)}, f32[8,128]{1,0:T(8,128)S(1)}, u32[]{:S(2)}, u32[]{:S(2)}) collective-permute-start(f32[8,128]{1,0:T(8,128)S(1)} %get-tuple-element.48), channel_id=1, source_target_pairs={{0,1},{1,0},{2,3},{3,2},{4,5},{5,4},{6,7},{7,6},{8,9},{9,8},{10,11... | collective-permute-start | bytes 12296 | tf_op jit(solution)/shard_map/ppermute | solution.py:376
  19.8 6.6 %collective-permute-start.9 = (f32[1,256]{1,0:T(1,128)S(1)}, f32[1,256]{1,0:T(1,128)S(1)}, u32[]{:S(2)}, u32[]{:S(2)}) collective-permute-start(f32[1,256]{1,0:T(1,128)S(1)} %shard_map.149.value.refs_13_), channel_id=1, source_target_pairs={{0,8},{4,12},{8,0},{12,4},{1,9},{5,13},{9,1},{13,5},{2,10},{6,14},... | collective-permute-start | bytes 3080 | tf_op jit(solution)/shard_map/ppermute | solution.py:385
  20.9 7.5 %collective-permute-start.8 = (bf16[80,256]{1,0:T(8,128)(2,1)S(1)}, bf16[80,256]{1,0:T(8,128)(2,1)S(1)}, u32[]{:S(2)}, u32[]{:S(2)}) collective-permute-start(bf16[80,256]{1,0:T(8,128)(2,1)S(1)} %shard_map.150.refs_0_), channel_id=1, source_target_pairs={{0,12},{4,8},{8,4},{12,0},{1,13},{5,9},{9,5},{13,1},{2,14},{6,10},... | collective-permute-start | bytes 122888 | tf_op jit(solution)/shard_map/ppermute | solution.py:443
  24.3 4.1 %collective-permute-start.7 = (bf16[80,256]{1,0:T(8,128)(2,1)S(1)}, bf16[80,256]{1,0:T(8,128)(2,1)S(1)}, u32[]{:S(2)}, u32[]{:S(2)}) collective-permute-start(bf16[80,256]{1,0:T(8,128)(2,1)S(1)} %shard_map.151), channel_id=1, source_target_pairs={{0,4},{4,0},{8,12},{12,8},{1,5},{5,1},{9,13},{13,9},{2,6},{6,2},{1... | collective-permute-start | bytes 122888 | tf_op jit(solution)/shard_map/ppermute | solution.py:443
  30.0 3.1 %collective-permute-start.11 = (f32[8,128]{1,0:T(8,128)S(1)}, f32[8,128]{1,0:T(8,128)S(1)}, u32[]{:S(2)}, u32[]{:S(2)}) collective-permute-start(f32[8,128]{1,0:T(8,128)S(1)} %get-tuple-element.53), channel_id=1, source_target_pairs={{0,3},{1,2},{2,1},{3,0},{4,7},{5,6},{6,5},{7,4},{8,11},{9,10},{10,... | collective-permute-start | bytes 12296 | tf_op jit(solution)/shard_map/ppermute | solution.py:376
  30.1 3.0 %collective-permute-start.10 = (f32[8,128]{1,0:T(8,128)S(1)}, f32[8,128]{1,0:T(8,128)S(1)}, u32[]{:S(2)}, u32[]{:S(2)}) collective-permute-start(f32[8,128]{1,0:T(8,128)S(1)} %get-tuple-element.53), channel_id=1, source_target_pairs={{0,1},{1,0},{2,3},{3,2},{4,5},{5,4},{6,7},{7,6},{8,9},{9,8},{10,11... | collective-permute-start | bytes 12296 | tf_op jit(solution)/shard_map/ppermute | solution.py:376
  31.0 6.0 %collective-permute-start.14 = (f32[1,256]{1,0:T(1,128)S(1)}, f32[1,256]{1,0:T(1,128)S(1)}, u32[]{:S(2)}, u32[]{:S(2)}) collective-permute-start(f32[1,256]{1,0:T(1,128)S(1)} %shard_map.154.value.refs_13_), channel_id=1, source_target_pairs={{0,8},{4,12},{8,0},{12,4},{1,9},{5,13},{9,1},{13,5},{2,10},{6,14},... | collective-permute-start | bytes 3080 | tf_op jit(solution)/shard_map/ppermute | solution.py:385
  33.2 6.3 %collective-permute-start.13 = (bf16[80,256]{1,0:T(8,128)(2,1)S(1)}, bf16[80,256]{1,0:T(8,128)(2,1)S(1)}, u32[]{:S(2)}, u32[]{:S(2)}) collective-permute-start(bf16[80,256]{1,0:T(8,128)(2,1)S(1)} %shard_map.155.refs_0_), channel_id=1, source_target_pairs={{0,12},{4,8},{8,4},{12,0},{1,13},{5,9},{9,5},{13,1},{2,14},{6,10},... | collective-permute-start | bytes 122888 | tf_op jit(solution)/shard_map/ppermute | solution.py:443
  35.0 4.5 %collective-permute-start.12 = (bf16[80,256]{1,0:T(8,128)(2,1)S(1)}, bf16[80,256]{1,0:T(8,128)(2,1)S(1)}, u32[]{:S(2)}, u32[]{:S(2)}) collective-permute-start(bf16[80,256]{1,0:T(8,128)(2,1)S(1)} %shard_map.156), channel_id=1, source_target_pairs={{0,4},{4,0},{8,12},{12,8},{1,5},{5,1},{9,13},{13,9},{2,6},{6,2},{1... | collective-permute-start | bytes 122888 | tf_op jit(solution)/shard_map/ppermute | solution.py:443
  41.1 3.1 %collective-permute-start.16 = (f32[8,128]{1,0:T(8,128)S(1)}, f32[8,128]{1,0:T(8,128)S(1)}, u32[]{:S(2)}, u32[]{:S(2)}) collective-permute-start(f32[8,128]{1,0:T(8,128)S(1)} %get-tuple-element.57), channel_id=1, source_target_pairs={{0,3},{1,2},{2,1},{3,0},{4,7},{5,6},{6,5},{7,4},{8,11},{9,10},{10,... | collective-permute-start | bytes 12296 | tf_op jit(solution)/shard_map/ppermute | solution.py:376
  41.2 3.0 %collective-permute-start.15 = (f32[8,128]{1,0:T(8,128)S(1)}, f32[8,128]{1,0:T(8,128)S(1)}, u32[]{:S(2)}, u32[]{:S(2)}) collective-permute-start(f32[8,128]{1,0:T(8,128)S(1)} %get-tuple-element.57), channel_id=1, source_target_pairs={{0,1},{1,0},{2,3},{3,2},{4,5},{5,4},{6,7},{7,6},{8,9},{9,8},{10,11... | collective-permute-start | bytes 12296 | tf_op jit(solution)/shard_map/ppermute | solution.py:376
  42.2 6.1 %collective-permute-start.19 = (f32[1,256]{1,0:T(1,128)S(1)}, f32[1,256]{1,0:T(1,128)S(1)}, u32[]{:S(2)}, u32[]{:S(2)}) collective-permute-start(f32[1,256]{1,0:T(1,128)S(1)} %shard_map.159.value.refs_13_), channel_id=1, source_target_pairs={{0,8},{4,12},{8,0},{12,4},{1,9},{5,13},{9,1},{13,5},{2,10},{6,14},... | collective-permute-start | bytes 3080 | tf_op jit(solution)/shard_map/ppermute | solution.py:385
  44.3 6.3 %collective-permute-start.18 = (bf16[80,256]{1,0:T(8,128)(2,1)S(1)}, bf16[80,256]{1,0:T(8,128)(2,1)S(1)}, u32[]{:S(2)}, u32[]{:S(2)}) collective-permute-start(bf16[80,256]{1,0:T(8,128)(2,1)S(1)} %shard_map.160.refs_0_), channel_id=1, source_target_pairs={{0,12},{4,8},{8,4},{12,0},{1,13},{5,9},{9,5},{13,1},{2,14},{6,10},... | collective-permute-start | bytes 122888 | tf_op jit(solution)/shard_map/ppermute | solution.py:443
  46.1 4.5 %collective-permute-start.17 = (bf16[80,256]{1,0:T(8,128)(2,1)S(1)}, bf16[80,256]{1,0:T(8,128)(2,1)S(1)}, u32[]{:S(2)}, u32[]{:S(2)}) collective-permute-start(bf16[80,256]{1,0:T(8,128)(2,1)S(1)} %shard_map.161), channel_id=1, source_target_pairs={{0,4},{4,0},{8,12},{12,8},{1,5},{5,1},{9,13},{13,9},{2,6},{6,2},{1... | collective-permute-start | bytes 122888 | tf_op jit(solution)/shard_map/ppermute | solution.py:443

commit v9 on v7

--- a/solution.py
+++ b/solution.py
@@ -340,8 +340,8 @@
             near[i][0:variables].astype(BF16),
             edge[2 * i : 2 * i + 1], edge[2 * i + 1 : 2 * i + 2], lift, gain_1,
         )
-        first = jnp.where(beyond[i], 0.0, jnp.concatenate(shifted, axis=1).astype(F32)).astype(BF16)
-        mixed = sums[i] + dot(first, conv[p * deep : (p + 1) * deep])
+        share = dot(jnp.concatenate(shifted, axis=1), conv[p * deep : (p + 1) * deep])
+        mixed = sums[i] + jnp.where(beyond[i], 0.0, share)
         second = silu_norm(mixed, gain_2[...]).astype(BF16)
         score = dot(head[...], second, 1, 1)
         moved[r] = state[r] + (drift / level) * score + kick * noise[step, r] + added[place[r]]

time: 53.2 us -> 53.2 us (level)
  no operation moved by 1% of the time
where the time goes in v9:
time: 53.2 us; the launch traced here: 53 us
  starting transfers between devices  21.3 us (40%)
  Pallas kernels  20.9 us (39%)
  waiting for transfers between devices  9.16 us (17%)
  between operations  1.62 us (3%)
    pallas_call x23, Pallas kernels, vmem_call(): pl.pallas_call(kernel, out_shape=[out_type(shape, dtype) for shape, dtype...  20.9 us
    ppermute x4, starting transfers between devices, per_device(): lax.ppermute(msg_b, 'band', route_b)  9.43 us
    ppermute x4, waiting for transfers between devices, per_device(): lax.ppermute(msg_a, 'band', route_a)  6.71 us
    ppermute x8, starting transfers between devices, from_neighbours(): lax.ppermute(block, axis, route)  6.19 us
    ppermute x4, starting transfers between devices, from_far(): found.append(lax.ppermute(block, 'band', route))  5.39 us
    ppermute x8, waiting for transfers between devices, from_neighbours(): lax.ppermute(block, axis, route)  2.43 us
  transfers between devices with their start and end apart: 20, of which 6 were waited for; matrix products, arithmetic and copies ran while one was open for 0% of the time, Pallas kernels for 22%

profile of v9, /device:TPU:0, one launch (start us, length us, event | category | flops | bytes accessed | tf_op | source)
XLA Modules:
  0.0 53.0 jit_solution(2224836393432807651)
XLA Ops:
  1.3 1.8 %shard_map.140 = (f32[4,64,256]{2,1,0:T(8,128)S(1)}, f32[8,128]{1,0:T(8,128)S(1)}, f32[8,256]{1,0:T(8,128)S(1)}) custom-call(s32[1]{0:T(128)S(6)} %copy.15.refs_0_, f32[64,4,256]{2,1,0:T(4,128)} %refs_1_.2, s32[1,256]{1,0:T(1,128)} %bitcast.12, s32[1,256]{1,0:T(1,128)} %bitcast.13, s32[1,256]{1,0:T(1,128)} %bitcast.14, f32[1,256]{1,0:T(1,128)} %bitcast.15, ...), custom_call_target="tpu_custom_call" | custom-call | tf_op jit(solution)/shard_map/pallas_call | solution.py:48
  3.1 2.4 %collective-permute-start.1 = (f32[8,128]{1,0:T(8,128)S(1)}, f32[8,128]{1,0:T(8,128)S(1)}, u32[]{:S(2)}, u32[]{:S(2)}) collective-permute-start(f32[8,128]{1,0:T(8,128)S(1)} %get-tuple-element.33), channel_id=1, source_target_pairs={{0,3},{1,2},{2,1},{3,0},{4,7},{5,6},{6,5},{7,4},{8,11},{9,10},{10,... | collective-permute-start | bytes 12296 | tf_op jit(solution)/shard_map/ppermute | solution.py:376
  5.5 0.7 %collective-permute-start = (f32[8,128]{1,0:T(8,128)S(1)}, f32[8,128]{1,0:T(8,128)S(1)}, u32[]{:S(2)}, u32[]{:S(2)}) collective-permute-start(f32[8,128]{1,0:T(8,128)S(1)} %get-tuple-element.33), channel_id=1, source_target_pairs={{0,1},{1,0},{2,3},{3,2},{4,5},{5,4},{6,7},{7,6},{8,9},{9,8},{10,11... | collective-permute-start | bytes 12296 | tf_op jit(solution)/shard_map/ppermute | solution.py:376
  6.2 2.6 %collective-permute-start.4 = (f32[8,256]{1,0:T(8,128)S(1)}, f32[8,256]{1,0:T(8,128)S(1)}, u32[]{:S(2)}, u32[]{:S(2)}) collective-permute-start(f32[8,256]{1,0:T(8,128)S(1)} %get-tuple-element.34.value.msg.own.refs_13_), channel_id=1, source_target_pairs={{0,8},{4,12},{8,0},{12,4},{1,9},{5,13},{9,1},{13,5},{2,10},{6,14},... | collective-permute-start | bytes 24584 | tf_op jit(solution)/shard_map/ppermute | solution.py:385
  8.8 2.5 %collective-permute-start.3 = (bf16[96,256]{1,0:T(8,128)(2,1)S(1)}, bf16[96,256]{1,0:T(8,128)(2,1)S(1)}, u32[]{:S(2)}, u32[]{:S(2)}) collective-permute-start(bf16[96,256]{1,0:T(8,128)(2,1)S(1)} %shard_map.141.refs_0_), channel_id=1, source_target_pairs={{0,12},{4,8},{8,4},{12,0},{1,13},{5,9},{9,5},{13,1},{2,14},{6,10},... | collective-permute-start | bytes 147464 | tf_op jit(solution)/shard_map/ppermute | solution.py:443
  11.4 1.9 %shard_map.143 = (f32[4,4,64,256]{3,2,1,0:T(8,128)S(1)}, bf16[2304,256]{1,0:T(8,128)(2,1)S(1)}, bf16[64,256]{1,0:T(8,128)(2,1)S(1)}, bf16[64,256]{1,0:T(8,128)(2...) custom-call(f32[4,64,4,256]{3,2,1,0:T(4,128)} %noise_in.1, bf16[2304,256]{1,0:T(8,128)(2,1)} %bitcast.10, ...), custom_call_target="tpu_custom_call" | custom-call | tf_op jit(solution)/shard_map/pallas_call | solution.py:48
  13.4 2.0 %shard_map.144 = (f32[2,64,256]{2,1,0:T(8,128)S(1)}, f32[2,256,256]{2,1,0:T(8,128)S(1)}) custom-call(f32[4,64,256]{2,1,0:T(8,128)S(1)} %get-tuple-element.32.state.refs_0_, f32[8,128]{1,0:T(8,128)S(1)} %collective-permute-done.edge_a, f32[8,128]{1,0:T(8,128)S(1)} %collective-permute-done.1.edge_b, f32[4,4,64,256]{3,2,1,0:T(8,128)S(1)} %get-tuple-element.35.noise.refs_3_, ...), custom_call_target="tpu_custom_call" | custom-call | flops 2415919104 | tf_op jit(solution)/shard_map/pallas_call | solution.py:48
  15.4 0.5 shard_map.145
  16.1 1.7 %shard_map.147 = (f32[4,64,256]{2,1,0:T(8,128)S(1)}, f32[8,128]{1,0:T(8,128)S(1)}) custom-call(f32[4,64,256]{2,1,0:T(8,128)S(1)} %get-tuple-element.32.state.refs_0_, f32[2,64,256]{2,1,0:T(8,128)S(1)} %get-tuple-element.41.refs_1_, f32[2,256,256]{2,1,0:T(8,128)S(1)} %get-tuple-element.42.refs_2_, f32[4,4,64,256]{3,2,1,0:T(8,128)S(1)} %get-tuple-element.35.noise.refs_3_, ...), custom_call_target="tpu_custom_call" | custom-call | tf_op jit(solution)/shard_map/pallas_call | solution.py:48
  17.7 1.0 %collective-permute-start.6 = (f32[8,128]{1,0:T(8,128)S(1)}, f32[8,128]{1,0:T(8,128)S(1)}, u32[]{:S(2)}, u32[]{:S(2)}) collective-permute-start(f32[8,128]{1,0:T(8,128)S(1)} %get-tuple-element.48), channel_id=1, source_target_pairs={{0,3},{1,2},{2,1},{3,0},{4,7},{5,6},{6,5},{7,4},{8,11},{9,10},{10,... | collective-permute-start | bytes 12296 | tf_op jit(solution)/shard_map/ppermute | solution.py:376
  18.8 0.7 %collective-permute-start.5 = (f32[8,128]{1,0:T(8,128)S(1)}, f32[8,128]{1,0:T(8,128)S(1)}, u32[]{:S(2)}, u32[]{:S(2)}) collective-permute-start(f32[8,128]{1,0:T(8,128)S(1)} %get-tuple-element.48), channel_id=1, source_target_pairs={{0,1},{1,0},{2,3},{3,2},{4,5},{5,4},{6,7},{7,6},{8,9},{9,8},{10,11... | collective-permute-start | bytes 12296 | tf_op jit(solution)/shard_map/ppermute | solution.py:376
  19.4 0.3 shard_map.149.value.refs_13_
  19.8 1.0 %collective-permute-start.9 = (f32[8,256]{1,0:T(8,128)S(1)}, f32[8,256]{1,0:T(8,128)S(1)}, u32[]{:S(2)}, u32[]{:S(2)}) collective-permute-start(f32[8,256]{1,0:T(8,128)S(1)} %shard_map.149.value.refs_13_), channel_id=1, source_target_pairs={{0,8},{4,12},{8,0},{12,4},{1,9},{5,13},{9,1},{13,5},{2,10},{6,14},... | collective-permute-start | bytes 24584 | tf_op jit(solution)/shard_map/ppermute | solution.py:385
  20.9 3.4 %collective-permute-start.8 = (bf16[80,256]{1,0:T(8,128)(2,1)S(1)}, bf16[80,256]{1,0:T(8,128)(2,1)S(1)}, u32[]{:S(2)}, u32[]{:S(2)}) collective-permute-start(bf16[80,256]{1,0:T(8,128)(2,1)S(1)} %shard_map.150.refs_0_), channel_id=1, source_target_pairs={{0,12},{4,8},{8,4},{12,0},{1,13},{5,9},{9,5},{13,1},{2,14},{6,10},... | collective-permute-start | bytes 122888 | tf_op jit(solution)/shard_map/ppermute | solution.py:443
  24.4 2.0 %shard_map.148 = (f32[2,64,256]{2,1,0:T(8,128)S(1)}, f32[2,256,256]{2,1,0:T(8,128)S(1)}) custom-call(f32[4,64,256]{2,1,0:T(8,128)S(1)} %get-tuple-element.47.state.refs_0_, f32[8,128]{1,0:T(8,128)S(1)} %collective-permute-done.5.edge_a, f32[8,128]{1,0:T(8,128)S(1)} %collective-permute-done.6.edge_b, f32[4,4,64,256]{3,2,1,0:T(8,128)S(1)} %get-tuple-element.35.noise.refs_3_, ...), custom_call_target="tpu_custom_call" | custom-call | flops 2415919104 | tf_op jit(solution)/shard_map/pallas_call | solution.py:48
  26.4 2.0 %collective-permute-done.7.refs_14_ = bf16[80,256]{1,0:T(8,128)(2,1)S(1)} collective-permute-done((bf16[80,256]{1,0:T(8,128)(2,1)S(1)}, bf16[80,256]{1,0:T(8,128)(2,1)S(1)}, u32[]{:S(2)}, u32[]{:S(2)}) %collective-permute-start.7) | collective-permute-done | bytes 40992 | tf_op jit(solution)/shard_map/ppermute | solution.py:443
  28.4 1.7 %shard_map.152 = (f32[4,64,256]{2,1,0:T(8,128)S(1)}, f32[8,128]{1,0:T(8,128)S(1)}) custom-call(f32[4,64,256]{2,1,0:T(8,128)S(1)} %get-tuple-element.47.state.refs_0_, f32[2,64,256]{2,1,0:T(8,128)S(1)} %get-tuple-element.49.refs_1_, f32[2,256,256]{2,1,0:T(8,128)S(1)} %get-tuple-element.50.refs_2_, f32[4,4,64,256]{3,2,1,0:T(8,128)S(1)} %get-tuple-element.35.noise.refs_3_, ...), custom_call_target="tpu_custom_call" | custom-call | tf_op jit(solution)/shard_map/pallas_call | solution.py:48
  30.1 0.6 %collective-permute-start.10 = (f32[8,128]{1,0:T(8,128)S(1)}, f32[8,128]{1,0:T(8,128)S(1)}, u32[]{:S(2)}, u32[]{:S(2)}) collective-permute-start(f32[8,128]{1,0:T(8,128)S(1)} %get-tuple-element.53), channel_id=1, source_target_pairs={{0,1},{1,0},{2,3},{3,2},{4,5},{5,4},{6,7},{7,6},{8,9},{9,8},{10,11... | collective-permute-start | bytes 12296 | tf_op jit(solution)/shard_map/ppermute | solution.py:376
  31.0 1.2 %collective-permute-start.14 = (f32[8,256]{1,0:T(8,128)S(1)}, f32[8,256]{1,0:T(8,128)S(1)}, u32[]{:S(2)}, u32[]{:S(2)}) collective-permute-start(f32[8,256]{1,0:T(8,128)S(1)} %shard_map.154.value.refs_13_), channel_id=1, source_target_pairs={{0,8},{4,12},{8,0},{12,4},{1,9},{5,13},{9,1},{13,5},{2,10},{6,14},... | collective-permute-start | bytes 24584 | tf_op jit(solution)/shard_map/ppermute | solution.py:385
  32.2 0.9 %collective-permute-done.11.edge_b = f32[8,128]{1,0:T(8,128)S(1)} collective-permute-done((f32[8,128]{1,0:T(8,128)S(1)}, f32[8,128]{1,0:T(8,128)S(1)}, u32[]{:S(2)}, u32[]{:S(2)}) %collective-permute-start.11) | collective-permute-done | bytes 4128 | tf_op jit(solution)/shard_map/ppermute | solution.py:376
  33.2 1.8 %collective-permute-start.13 = (bf16[80,256]{1,0:T(8,128)(2,1)S(1)}, bf16[80,256]{1,0:T(8,128)(2,1)S(1)}, u32[]{:S(2)}, u32[]{:S(2)}) collective-permute-start(bf16[80,256]{1,0:T(8,128)(2,1)S(1)} %shard_map.155.refs_0_), channel_id=1, source_target_pairs={{0,12},{4,8},{8,4},{12,0},{1,13},{5,9},{9,5},{13,1},{2,14},{6,10},... | collective-permute-start | bytes 122888 | tf_op jit(solution)/shard_map/ppermute | solution.py:443
  35.0 2.0 %shard_map.153 = (f32[2,64,256]{2,1,0:T(8,128)S(1)}, f32[2,256,256]{2,1,0:T(8,128)S(1)}) custom-call(f32[4,64,256]{2,1,0:T(8,128)S(1)} %get-tuple-element.52.state.refs_0_, f32[8,128]{1,0:T(8,128)S(1)} %collective-permute-done.10.edge_a, f32[8,128]{1,0:T(8,128)S(1)} %collective-permute-done.11.edge_b, f32[4,4,64,256]{3,2,1,0:T(8,128)S(1)} %get-tuple-element.35.noise.refs_3_, ...), custom_call_target="tpu_custom_call" | custom-call | flops 2415919104 | tf_op jit(solution)/shard_map/pallas_call | solution.py:48
  37.0 2.4 %collective-permute-done.12.refs_14_ = bf16[80,256]{1,0:T(8,128)(2,1)S(1)} collective-permute-done((bf16[80,256]{1,0:T(8,128)(2,1)S(1)}, bf16[80,256]{1,0:T(8,128)(2,1)S(1)}, u32[]{:S(2)}, u32[]{:S(2)}) %collective-permute-start.12) | collective-permute-done | bytes 40992 | tf_op jit(solution)/shard_map/ppermute | solution.py:443
  39.5 1.7 %shard_map.157 = (f32[4,64,256]{2,1,0:T(8,128)S(1)}, f32[8,128]{1,0:T(8,128)S(1)}) custom-call(f32[4,64,256]{2,1,0:T(8,128)S(1)} %get-tuple-element.52.state.refs_0_, f32[2,64,256]{2,1,0:T(8,128)S(1)} %get-tuple-element.54.refs_1_, f32[2,256,256]{2,1,0:T(8,128)S(1)} %get-tuple-element.55.refs_2_, f32[4,4,64,256]{3,2,1,0:T(8,128)S(1)} %get-tuple-element.35.noise.refs_3_, ...), custom_call_target="tpu_custom_call" | custom-call | tf_op jit(solution)/shard_map/pallas_call | solution.py:48
  41.2 0.6 %collective-permute-start.15 = (f32[8,128]{1,0:T(8,128)S(1)}, f32[8,128]{1,0:T(8,128)S(1)}, u32[]{:S(2)}, u32[]{:S(2)}) collective-permute-start(f32[8,128]{1,0:T(8,128)S(1)} %get-tuple-element.57), channel_id=1, source_target_pairs={{0,1},{1,0},{2,3},{3,2},{4,5},{5,4},{6,7},{7,6},{8,9},{9,8},{10,11... | collective-permute-start | bytes 12296 | tf_op jit(solution)/shard_map/ppermute | solution.py:376
  41.8 0.3 shard_map.159.value.refs_13_
  42.2 0.6 %collective-permute-start.19 = (f32[8,256]{1,0:T(8,128)S(1)}, f32[8,256]{1,0:T(8,128)S(1)}, u32[]{:S(2)}, u32[]{:S(2)}) collective-permute-start(f32[8,256]{1,0:T(8,128)S(1)} %shard_map.159.value.refs_13_), channel_id=1, source_target_pairs={{0,8},{4,12},{8,0},{12,4},{1,9},{5,13},{9,1},{13,5},{2,10},{6,14},... | collective-permute-start | bytes 24584 | tf_op jit(solution)/shard_map/ppermute | solution.py:385
  42.8 1.4 %collective-permute-done.16.edge_b = f32[8,128]{1,0:T(8,128)S(1)} collective-permute-done((f32[8,128]{1,0:T(8,128)S(1)}, f32[8,128]{1,0:T(8,128)S(1)}, u32[]{:S(2)}, u32[]{:S(2)}) %collective-permute-start.16) | collective-permute-done | bytes 4128 | tf_op jit(solution)/shard_map/ppermute | solution.py:376
  44.3 1.8 %collective-permute-start.18 = (bf16[80,256]{1,0:T(8,128)(2,1)S(1)}, bf16[80,256]{1,0:T(8,128)(2,1)S(1)}, u32[]{:S(2)}, u32[]{:S(2)}) collective-permute-start(bf16[80,256]{1,0:T(8,128)(2,1)S(1)} %shard_map.160.refs_0_), channel_id=1, source_target_pairs={{0,12},{4,8},{8,4},{12,0},{1,13},{5,9},{9,5},{13,1},{2,14},{6,10},... | collective-permute-start | bytes 122888 | tf_op jit(solution)/shard_map/ppermute | solution.py:443
  46.1 2.1 %shard_map.158 = (f32[2,64,256]{2,1,0:T(8,128)S(1)}, f32[2,256,256]{2,1,0:T(8,128)S(1)}) custom-call(f32[4,64,256]{2,1,0:T(8,128)S(1)} %get-tuple-element.56.state.refs_0_, f32[8,128]{1,0:T(8,128)S(1)} %collective-permute-done.15.edge_a, f32[8,128]{1,0:T(8,128)S(1)} %collective-permute-done.16.edge_b, f32[4,4,64,256]{3,2,1,0:T(8,128)S(1)} %get-tuple-element.35.noise.refs_3_, ...), custom_call_target="tpu_custom_call" | custom-call | flops 2415919104 | tf_op jit(solution)/shard_map/pallas_call | solution.py:48
  48.3 2.3 %collective-permute-done.17.refs_14_ = bf16[80,256]{1,0:T(8,128)(2,1)S(1)} collective-permute-done((bf16[80,256]{1,0:T(8,128)(2,1)S(1)}, bf16[80,256]{1,0:T(8,128)(2,1)S(1)}, u32[]{:S(2)}, u32[]{:S(2)}) %collective-permute-start.17) | collective-permute-done | bytes 40992 | tf_op jit(solution)/shard_map/ppermute | solution.py:443
  50.6 2.2 %shard_map.162 = (f32[64,4,256]{2,1,0:T(4,128)}, f32[1,256]{1,0:T(1,128)}) custom-call(f32[4,64,256]{2,1,0:T(8,128)S(1)} %get-tuple-element.56.state.refs_0_, f32[2,64,256]{2,1,0:T(8,128)S(1)} %get-tuple-element.58.refs_1_, f32[2,256,256]{2,1,0:T(8,128)S(1)} %get-tuple-element.59.refs_2_, f32[4,4,64,256]{3,2,1,0:T(8,128)S(1)} %get-tuple-element.35.noise.refs_3_, ...), custom_call_target="tpu_custom_call" | custom-call | tf_op jit(solution)/shard_map/pallas_call | solution.py:48
  (31 shorter events, 1.3 us)
Async XLA Ops:
  3.1 5.7 %collective-permute-start.1 = (f32[8,128]{1,0:T(8,128)S(1)}, f32[8,128]{1,0:T(8,128)S(1)}, u32[]{:S(2)}, u32[]{:S(2)}) collective-permute-start(f32[8,128]{1,0:T(8,128)S(1)} %get-tuple-element.33), channel_id=1, source_target_pairs={{0,3},{1,2},{2,1},{3,0},{4,7},{5,6},{6,5},{7,4},{8,11},{9,10},{10,... | collective-permute-start | bytes 12296 | tf_op jit(solution)/shard_map/ppermute | solution.py:376
  5.5 3.3 %collective-permute-start = (f32[8,128]{1,0:T(8,128)S(1)}, f32[8,128]{1,0:T(8,128)S(1)}, u32[]{:S(2)}, u32[]{:S(2)}) collective-permute-start(f32[8,128]{1,0:T(8,128)S(1)} %get-tuple-element.33), channel_id=1, source_target_pairs={{0,1},{1,0},{2,3},{3,2},{4,5},{5,4},{6,7},{7,6},{8,9},{9,8},{10,11... | collective-permute-start | bytes 12296 | tf_op jit(solution)/shard_map/ppermute | solution.py:376
  6.2 9.7 %collective-permute-start.4 = (f32[8,256]{1,0:T(8,128)S(1)}, f32[8,256]{1,0:T(8,128)S(1)}, u32[]{:S(2)}, u32[]{:S(2)}) collective-permute-start(f32[8,256]{1,0:T(8,128)S(1)} %get-tuple-element.34.value.msg.own.refs_13_), channel_id=1, source_target_pairs={{0,8},{4,12},{8,0},{12,4},{1,9},{5,13},{9,1},{13,5},{2,10},{6,14},... | collective-permute-start | bytes 24584 | tf_op jit(solution)/shard_map/ppermute | solution.py:385
  8.8 7.1 %collective-permute-start.3 = (bf16[96,256]{1,0:T(8,128)(2,1)S(1)}, bf16[96,256]{1,0:T(8,128)(2,1)S(1)}, u32[]{:S(2)}, u32[]{:S(2)}) collective-permute-start(bf16[96,256]{1,0:T(8,128)(2,1)S(1)} %shard_map.141.refs_0_), channel_id=1, source_target_pairs={{0,12},{4,8},{8,4},{12,0},{1,13},{5,9},{9,5},{13,1},{2,14},{6,10},... | collective-permute-start | bytes 147464 | tf_op jit(solution)/shard_map/ppermute | solution.py:443
  11.4 4.5 %collective-permute-start.2 = (bf16[96,256]{1,0:T(8,128)(2,1)S(1)}, bf16[96,256]{1,0:T(8,128)(2,1)S(1)}, u32[]{:S(2)}, u32[]{:S(2)}) collective-permute-start(bf16[96,256]{1,0:T(8,128)(2,1)S(1)} %shard_map.142.refs_5_.after), channel_id=1, source_target_pairs={{0,4},{4,0},{8,12},{12,8},{1,5},{5,1},{9,13},{13,9},{2,6},{6,2},{1... | collective-permute-start | bytes 147464 | tf_op jit(solution)/shard_map/ppermute | solution.py:443
  17.7 3.1 %collective-permute-start.6 = (f32[8,128]{1,0:T(8,128)S(1)}, f32[8,128]{1,0:T(8,128)S(1)}, u32[]{:S(2)}, u32[]{:S(2)}) collective-permute-start(f32[8,128]{1,0:T(8,128)S(1)} %get-tuple-element.48), channel_id=1, source_target_pairs={{0,3},{1,2},{2,1},{3,0},{4,7},{5,6},{6,5},{7,4},{8,11},{9,10},{10,... | collective-permute-start | bytes 12296 | tf_op jit(solution)/shard_map/ppermute | solution.py:376
  18.8 2.1 %collective-permute-start.5 = (f32[8,128]{1,0:T(8,128)S(1)}, f32[8,128]{1,0:T(8,128)S(1)}, u32[]{:S(2)}, u32[]{:S(2)}) collective-permute-start(f32[8,128]{1,0:T(8,128)S(1)} %get-tuple-element.48), channel_id=1, source_target_pairs={{0,1},{1,0},{2,3},{3,2},{4,5},{5,4},{6,7},{7,6},{8,9},{9,8},{10,11... | collective-permute-start | bytes 12296 | tf_op jit(solution)/shard_map/ppermute | solution.py:376
  19.8 6.6 %collective-permute-start.9 = (f32[8,256]{1,0:T(8,128)S(1)}, f32[8,256]{1,0:T(8,128)S(1)}, u32[]{:S(2)}, u32[]{:S(2)}) collective-permute-start(f32[8,256]{1,0:T(8,128)S(1)} %shard_map.149.value.refs_13_), channel_id=1, source_target_pairs={{0,8},{4,12},{8,0},{12,4},{1,9},{5,13},{9,1},{13,5},{2,10},{6,14},... | collective-permute-start | bytes 24584 | tf_op jit(solution)/shard_map/ppermute | solution.py:385
  20.9 7.5 %collective-permute-start.8 = (bf16[80,256]{1,0:T(8,128)(2,1)S(1)}, bf16[80,256]{1,0:T(8,128)(2,1)S(1)}, u32[]{:S(2)}, u32[]{:S(2)}) collective-permute-start(bf16[80,256]{1,0:T(8,128)(2,1)S(1)} %shard_map.150.refs_0_), channel_id=1, source_target_pairs={{0,12},{4,8},{8,4},{12,0},{1,13},{5,9},{9,5},{13,1},{2,14},{6,10},... | collective-permute-start | bytes 122888 | tf_op jit(solution)/shard_map/ppermute | solution.py:443
  24.3 4.1 %collective-permute-start.7 = (bf16[80,256]{1,0:T(8,128)(2,1)S(1)}, bf16[80,256]{1,0:T(8,128)(2,1)S(1)}, u32[]{:S(2)}, u32[]{:S(2)}) collective-permute-start(bf16[80,256]{1,0:T(8,128)(2,1)S(1)} %shard_map.151), channel_id=1, source_target_pairs={{0,4},{4,0},{8,12},{12,8},{1,5},{5,1},{9,13},{13,9},{2,6},{6,2},{1... | collective-permute-start | bytes 122888 | tf_op jit(solution)/shard_map/ppermute | solution.py:443
  30.0 3.1 %collective-permute-start.11 = (f32[8,128]{1,0:T(8,128)S(1)}, f32[8,128]{1,0:T(8,128)S(1)}, u32[]{:S(2)}, u32[]{:S(2)}) collective-permute-start(f32[8,128]{1,0:T(8,128)S(1)} %get-tuple-element.53), channel_id=1, source_target_pairs={{0,3},{1,2},{2,1},{3,0},{4,7},{5,6},{6,5},{7,4},{8,11},{9,10},{10,... | collective-permute-start | bytes 12296 | tf_op jit(solution)/shard_map/ppermute | solution.py:376
  30.1 3.0 %collective-permute-start.10 = (f32[8,128]{1,0:T(8,128)S(1)}, f32[8,128]{1,0:T(8,128)S(1)}, u32[]{:S(2)}, u32[]{:S(2)}) collective-permute-start(f32[8,128]{1,0:T(8,128)S(1)} %get-tuple-element.53), channel_id=1, source_target_pairs={{0,1},{1,0},{2,3},{3,2},{4,5},{5,4},{6,7},{7,6},{8,9},{9,8},{10,11... | collective-permute-start | bytes 12296 | tf_op jit(solution)/shard_map/ppermute | solution.py:376
  31.0 6.0 %collective-permute-start.14 = (f32[8,256]{1,0:T(8,128)S(1)}, f32[8,256]{1,0:T(8,128)S(1)}, u32[]{:S(2)}, u32[]{:S(2)}) collective-permute-start(f32[8,256]{1,0:T(8,128)S(1)} %shard_map.154.value.refs_13_), channel_id=1, source_target_pairs={{0,8},{4,12},{8,0},{12,4},{1,9},{5,13},{9,1},{13,5},{2,10},{6,14},... | collective-permute-start | bytes 24584 | tf_op jit(solution)/shard_map/ppermute | solution.py:385
  33.2 6.3 %collective-permute-start.13 = (bf16[80,256]{1,0:T(8,128)(2,1)S(1)}, bf16[80,256]{1,0:T(8,128)(2,1)S(1)}, u32[]{:S(2)}, u32[]{:S(2)}) collective-permute-start(bf16[80,256]{1,0:T(8,128)(2,1)S(1)} %shard_map.155.refs_0_), channel_id=1, source_target_pairs={{0,12},{4,8},{8,4},{12,0},{1,13},{5,9},{9,5},{13,1},{2,14},{6,10},... | collective-permute-start | bytes 122888 | tf_op jit(solution)/shard_map/ppermute | solution.py:443
  35.0 4.5 %collective-permute-start.12 = (bf16[80,256]{1,0:T(8,128)(2,1)S(1)}, bf16[80,256]{1,0:T(8,128)(2,1)S(1)}, u32[]{:S(2)}, u32[]{:S(2)}) collective-permute-start(bf16[80,256]{1,0:T(8,128)(2,1)S(1)} %shard_map.156), channel_id=1, source_target_pairs={{0,4},{4,0},{8,12},{12,8},{1,5},{5,1},{9,13},{13,9},{2,6},{6,2},{1... | collective-permute-start | bytes 122888 | tf_op jit(solution)/shard_map/ppermute | solution.py:443
  41.1 3.1 %collective-permute-start.16 = (f32[8,128]{1,0:T(8,128)S(1)}, f32[8,128]{1,0:T(8,128)S(1)}, u32[]{:S(2)}, u32[]{:S(2)}) collective-permute-start(f32[8,128]{1,0:T(8,128)S(1)} %get-tuple-element.57), channel_id=1, source_target_pairs={{0,3},{1,2},{2,1},{3,0},{4,7},{5,6},{6,5},{7,4},{8,11},{9,10},{10,... | collective-permute-start | bytes 12296 | tf_op jit(solution)/shard_map/ppermute | solution.py:376
  41.2 3.0 %collective-permute-start.15 = (f32[8,128]{1,0:T(8,128)S(1)}, f32[8,128]{1,0:T(8,128)S(1)}, u32[]{:S(2)}, u32[]{:S(2)}) collective-permute-start(f32[8,128]{1,0:T(8,128)S(1)} %get-tuple-element.57), channel_id=1, source_target_pairs={{0,1},{1,0},{2,3},{3,2},{4,5},{5,4},{6,7},{7,6},{8,9},{9,8},{10,11... | collective-permute-start | bytes 12296 | tf_op jit(solution)/shard_map/ppermute | solution.py:376
  42.2 6.1 %collective-permute-start.19 = (f32[8,256]{1,0:T(8,128)S(1)}, f32[8,256]{1,0:T(8,128)S(1)}, u32[]{:S(2)}, u32[]{:S(2)}) collective-permute-start(f32[8,256]{1,0:T(8,128)S(1)} %shard_map.159.value.refs_13_), channel_id=1, source_target_pairs={{0,8},{4,12},{8,0},{12,4},{1,9},{5,13},{9,1},{13,5},{2,10},{6,14},... | collective-permute-start | bytes 24584 | tf_op jit(solution)/shard_map/ppermute | solution.py:385
  44.3 6.3 %collective-permute-start.18 = (bf16[80,256]{1,0:T(8,128)(2,1)S(1)}, bf16[80,256]{1,0:T(8,128)(2,1)S(1)}, u32[]{:S(2)}, u32[]{:S(2)}) collective-permute-start(bf16[80,256]{1,0:T(8,128)(2,1)S(1)} %shard_map.160.refs_0_), channel_id=1, source_target_pairs={{0,12},{4,8},{8,4},{12,0},{1,13},{5,9},{9,5},{13,1},{2,14},{6,10},... | collective-permute-start | bytes 122888 | tf_op jit(solution)/shard_map/ppermute | solution.py:443
  46.1 4.5 %collective-permute-start.17 = (bf16[80,256]{1,0:T(8,128)(2,1)S(1)}, bf16[80,256]{1,0:T(8,128)(2,1)S(1)}, u32[]{:S(2)}, u32[]{:S(2)}) collective-permute-start(bf16[80,256]{1,0:T(8,128)(2,1)S(1)} %shard_map.161), channel_id=1, source_target_pairs={{0,4},{4,0},{8,12},{12,8},{1,5},{5,1},{9,13},{13,9},{2,6},{6,2},{1... | collective-permute-start | bytes 122888 | tf_op jit(solution)/shard_map/ppermute | solution.py:443
